TPU v7x, 1024 devices: a whole 4x4x32 slice. The times are simulated.
1024 devices in a mesh: row: 8 (over z_lo), col: 16 (over x, z_hi), layer: 8 (over y, core).
Axes of the slice: x: 4, y: 4, z: 32 (z_hi: 4, z_lo: 8; z = z_hi * 8 + z_lo), core: 2. Of those that a mesh axis runs over, the one named last changes fastest.
Arguments:
- tiles: bfloat16 [8, 16, 8, 8, 1, 128, 128], P('row', 'col', 'layer'), may hold values from -2 to 2
- pair_a: int32 [8, 16, 8, 16, 16, 2], P('row', 'col', 'layer'), may hold values from 0 to 8, as said below
- pair_b: int32 [8, 16, 8, 16, 16, 2], P('row', 'col', 'layer'), may hold values from 0 to 64, as said below
Outputs:
- product: float32 [8, 16, 16, 128, 128], P('row', 'col', 'layer')
Inputs may be any that keep to these rules, and one draw needn't show every extreme that they name: `pair_a`: the value 8 marks an empty product slot. For each result tile and column of the grid the live slots come first and there is at least one; in every device's list some result tile has all 2 slots live for one column and another has one. `pair_b`: equals 64 exactly where pair_a marks an empty slot.
All inputs are finite; a program needn't handle non-finite values.
Results may differ from a plain program's by a relative error of at most 0.0003.
Values may be sent and summed in bfloat16 or wider, within the bound.
No kernel may reach another device: no remote copies, remote signals or barrier semaphores. Data moves between devices by JAX's collectives and lax.ppermute only.
A program may use at most 32 MiB of HBM per device.

v0:
```python
import jax
import jax.numpy as jnp
from jax import lax
from jax.sharding import PartitionSpec as P


def on_device(tiles, pair_a, pair_b):
    layers = lax.axis_size("layer")
    per_bucket = tiles.shape[4]
    width = tiles.shape[5]
    per_dev = layers * per_bucket
    routed = lax.all_to_all(tiles, "layer", split_axis=3, concat_axis=2, tiled=True)
    column = lax.all_gather(routed, "row", axis=0, tiled=True)
    column = column.reshape(-1, width, width)
    blank = jnp.zeros((1, width, width), jnp.bfloat16)
    column = jnp.concatenate([column, blank], axis=0)
    left_list = pair_a[0, 0, 0]
    right_list = pair_b[0, 0, 0]
    results = left_list.shape[0]
    slots = left_list.shape[2]
    panel = lax.all_gather(tiles, "col", axis=1, tiled=True)
    count = panel.shape[1]
    flat = panel.reshape(count * per_dev, width, width)
    flat = jnp.concatenate([flat, blank], axis=0)
    source = jnp.arange(count, dtype=jnp.int32)[None, :, None]
    index_a = jnp.where(left_list < per_dev, source * per_dev + left_list, count * per_dev)
    index_a = index_a.reshape(results, count * slots)
    index_b = right_list.reshape(results, count * slots)

    def one_result(indices):
        left_tiles = flat[indices[0]]
        right_tiles = column[indices[1]]
        return jnp.einsum(
            "pik,pkj->ij", left_tiles, right_tiles, preferred_element_type=jnp.float32
        )

    partial_value = lax.map(one_result, (index_a, index_b))
    return lax.psum_scatter(partial_value[None, None], "layer", scatter_dimension=2, tiled=True)


def solution(mesh):
    return jax.shard_map(
        on_device,
        mesh=mesh,
        in_specs=(
            P("row", "col", "layer", None, None, None, None),
            P("row", "col", "layer", None, None, None),
            P("row", "col", "layer", None, None, None),
        ),
        out_specs=P("row", "col", "layer", None, None),
        check_vma=False,
    )
```

profile of v0, /device:TPU:1, one launch (start us, length us, event | category | flops | bytes accessed | tf_op | source)
XLA Modules:
  0.0 508.0 jit_solution(11203784930309092298)
XLA Ops:
  6.5 24.7 %all_to_all.12 = bf16[1,1,1,8,1,128,128]{6,5,4,2,1,0,3:T(8,128)(2,1)} all-to-all(bf16[1,1,1,8,1,128,128]{6,5,4,2,1,0,3:T(8,128)(2,1)} %bitcast.44), channel_id=1, replica_groups=mesh['row'=8,'col'=16,'layer'=8] {'layer'}, dimensions={3} | all-to-all | bytes 524288 | tf_op jit(solution)/shard_map/all_to_all | solution.py:12
  31.2 0.0 all-gather.4.cloned.1.call-start
  31.3 0.7 all-gather.4.cloned.1.call-update
  32.1 0.8 copy.10
  32.9 0.1 add.42
  32.9 0.1 add.43
  33.0 0.1 add_select_fusion
  33.1 0.1 copy.15
  33.2 0.8 copy.12
  34.0 0.1 copy.16
  34.0 67.4 %all-gather.6.cloned.1.call-done = bf16[8,1,1,8,1,128,128]{6,5,4,3,2,1,0:T(8,128)(2,1)} async-done(((bf16[1,1,1,8,1,128,128]{6,5,4,3,2,1,0:T(8,128)(2,1)}), bf16[8,1,1,8,1,128,128]{6,5,4,3,2,1,0:T(8,128)(2,1)}) %all-gather.6.cloned.1.call-update) | async-done | bytes 2097168 | tf_op jit(solution)/shard_map/all_gather | solution.py:13
  101.4 3.2 concatenate.7
  104.7 251.0 %all-gather.4.cloned.1.call-done = bf16[1,16,1,8,1,128,128]{6,5,4,3,2,0,1:T(8,128)(2,1)} async-done(((bf16[1,1,1,8,1,128,128]{6,5,4,3,2,0,1:T(8,128)(2,1)}), bf16[1,16,1,8,1,128,128]{6,5,4,3,2,0,1:T(8,128)(2,1)}) %all-gather.4.cloned.1.call-update) | async-done | bytes 4194320 | tf_op jit(solution)/shard_map/all_gather | solution.py:21
  355.7 5.7 %concatenate.6 = bf16[129,128,128]{2,1,0:T(8,128)(2,1)} pad(bf16[128,128,128]{2,1,0:T(8,128)(2,1)} %bitcast.41, bf16[]{:T(256)} %constant.8.clone.1), padding=0_1x0_0x0_0 | pad | bytes 8421378 | tf_op jit(solution)/shard_map/concatenate | solution.py:24
  361.4 102.3 %while.10 = (s32[]{:T(128)}, f32[16,128,128]{2,1,0:T(8,128)}, s32[16,32]{1,0:T(8,128)S(1)}, bf16[129,128,128]{2,1,0:T(8,128)(2,1)}, s32[16,32]{1,0:T(8,128)S(1)}, /*index=5*/bf16[65,128,128]{2,1,0:T(8,128)(2,1)}, s32[]{:T(128)}) while((s32[]{:T(128)}, f32[16,128,128]{2,1,0:T(8,128)}, s32[16,32]{1,0:T(8,128)S(1)}, ...), condition=%wide.region_1.2_spmd, body=%wide.region_0.1_spmd.sunk | while | flops 134219968 | bytes 6366801 | solution.py:37
  361.5 2.9 gather_fusion
  364.4 2.3 gather_fusion.1
  366.8 1.1 fusion.14
  367.8 2.9 gather_fusion
  370.8 2.3 gather_fusion.1
  373.2 1.0 fusion.14
  374.2 2.9 gather_fusion
  377.2 2.3 gather_fusion.1
  379.6 1.1 fusion.14
  380.6 2.9 gather_fusion
  383.6 2.3 gather_fusion.1
  386.0 1.1 fusion.14
  387.0 2.9 gather_fusion
  390.0 2.3 gather_fusion.1
  392.4 1.1 fusion.14
  393.4 2.9 gather_fusion
  396.4 2.3 gather_fusion.1
  398.7 1.1 fusion.14
  399.8 2.9 gather_fusion
  402.8 2.3 gather_fusion.1
  405.1 1.1 fusion.14
  406.2 2.9 gather_fusion
  409.2 2.3 gather_fusion.1
  411.5 1.1 fusion.14
  412.6 2.9 gather_fusion
  415.6 2.3 gather_fusion.1
  417.9 1.1 fusion.14
  419.0 2.9 gather_fusion
  422.0 2.3 gather_fusion.1
  424.3 1.0 fusion.14
  425.4 2.9 gather_fusion
  428.4 2.3 gather_fusion.1
  430.7 1.0 fusion.14
  431.8 2.9 gather_fusion
  434.7 2.3 gather_fusion.1
  437.1 1.1 fusion.14
  438.2 2.9 gather_fusion
  441.1 2.3 gather_fusion.1
  443.5 1.1 fusion.14
  444.6 2.9 gather_fusion
  447.5 2.3 gather_fusion.1
  449.9 1.1 fusion.14
  451.0 2.9 gather_fusion
  453.9 2.3 gather_fusion.1
  456.3 1.1 fusion.14
  457.4 2.9 gather_fusion
  460.4 2.3 gather_fusion.1
  462.7 1.1 fusion.14
  463.8 37.7 %reduce-scatter.2.cloned.1.call-done = f32[1,1,2,128,128]{4,3,2,1,0:T(8,128)} async-done(((f32[1,1,16,128,128]{4,3,2,1,0:T(8,128)}), f32[1,1,2,128,128]{4,3,2,1,0:T(8,128)}) %reduce-scatter.2.cloned.1.call-update) | async-done | bytes 131088 | tf_op jit(solution)/shard_map/reduce_scatter | solution.py:38
  (54 shorter events, 0.4 us)
Async XLA Ops:
  6.5 94.9 %all-gather.6.cloned.1.call-start = ((), (), s32[]{:S(2)}) async-start(), calls=%async_computation.4 | async-start | bytes 2359296 | tf_op jit(solution)/shard_map/all_gather | solution.py:13
  31.2 324.5 %all-gather.4.cloned.1.call-start = ((), (), s32[]{:S(2)}) async-start(), calls=%async_computation.2 | async-start | bytes 4456448 | tf_op jit(solution)/shard_map/all_gather | solution.py:21
  32.0 469.5 %reduce-scatter.2.cloned.1.call-start = ((), (), s32[]{:S(2)}) async-start(), calls=%async_computation.3 | async-start | bytes 1179648 | tf_op jit(solution)/shard_map/reduce_scatter | solution.py:38
Sparse Core Ops, SparseCore 0:
  31.4 69.9 all-gather.5
  105.6 250.0 all-gather.3
  463.9 37.5 reduce-scatter.1
where the time goes:
time: 509 us; the launch traced here: 508 us
  waiting for transfers between devices  357 us (70%)
  local copies, waits for them, and re-layouts  95.6 us (19%)
  blocking collectives  24.7 us (5%)
  matrix products  16.9 us (3%)
  between operations  13.1 us (3%)
    all_gather x1, waiting for transfers between devices, on_device(): panel = lax.all_gather(tiles, 'col', axis=1, tiled=True)  251 us
    all_gather x1, waiting for transfers between devices, on_device(): column = lax.all_gather(routed, 'row', axis=0, tiled=True)  67.4 us
    gather x16, local copies, waits for them, and re-layouts, one_result(): left_tiles = flat[indices[0]]  47.1 us
    reduce_scatter x1, waiting for transfers between devices, on_device(): lax.psum_scatter(partial_value[None, None], 'layer', scatter_dimension=2,...  37.7 us
    gather x16, local copies, waits for them, and re-layouts, one_result(): right_tiles = column[indices[1]]  37.6 us
    all_to_all x1, blocking collectives, on_device(): lax.all_to_all(tiles, 'layer', split_axis=3, concat_axis=2, tiled=True)  24.7 us
    dot_general x16, matrix products, one_result(): jnp.einsum('pik,pkj->ij', left_tiles, right_tiles, preferred_element_type...  16.9 us
  transfers between devices with their start and end apart: 3, of which 3 were waited for; matrix products, arithmetic and copies ran while one was open for 1% of the time, Pallas kernels for 0%

commit v1 on v0

v1 whole, which is shorter than its diff:
```python
import functools

import jax
import jax.numpy as jnp
from jax import lax
from jax.experimental import pallas as pl
from jax.experimental.pallas import tpu as pltpu
from jax.sharding import Mesh
from jax.sharding import PartitionSpec as P

X, ZH, Y, CORE, ROW = 4, 4, 4, 2, 8
S, SLOTS, R, BS = 8, 2, 16, 128
COLS = X * ZH


def ring(n, k):
    return [(i, (i + k) % n) for i in range(n)]


def products(groups, first, place, left, right, *refs):
    parts = [len(g[2]) for g in groups]
    refs = list(refs)
    a_hbm = []
    for n in parts:
        a_hbm.append(refs[:n])
        refs = refs[n:]
    b_own, refs = refs[0], refs[1:]
    b_right, refs = refs[: ROW - 1], refs[ROW - 1 :]
    b_left, refs = refs[: ROW - 1], refs[ROW - 1 :]
    if first:
        out, a_all, b_all, a_sem, b_sem = refs
        before = None
    else:
        before, keep, send, a_all, b_all, a_sem, b_sem = refs
    x, zh, row, core, y = (place[k] for k in range(5))

    def b_copy(src, dst, s):
        return pltpu.make_async_copy(src, b_all.at[pl.ds(dst * S, S)], b_sem.at[s])

    copies = []
    n = 0
    for g, group in enumerate(groups):
        for part, (start, size) in zip(a_hbm[g], group[2]):
            copies.append(pltpu.make_async_copy(part, a_all.at[pl.ds(g * S + start, size)], a_sem.at[n]))
            n += 1
    for c in copies:
        c.start()
    b_copy(b_own, row, 0).start()
    for s in range(1, ROW):
        source = lax.rem(row - s + ROW, ROW)

        @pl.when(row >= s)
        def _(s=s, source=source):
            b_copy(b_right[s - 1], source, s).start()

        @pl.when(row < s)
        def _(s=s, source=source):
            b_copy(b_left[ROW - s - 1], source, s).start()

    zero = len(groups) * S
    a_all[zero] = jnp.zeros((BS, BS), jnp.bfloat16)
    for c in copies:
        c.wait()
    for s in range(ROW):
        b_copy(b_own, lax.rem(row - s + ROW, ROW), s).wait()

    def one(r):
        total = None if first else before[r]
        for g, (dx, dz, _) in enumerate(groups):
            c = lax.rem(x + dx, X) * ZH + lax.rem(zh + dz, ZH)
            lefts, rights = [], []
            for p in range(SLOTS):
                m = left[r, c * SLOTS + p]
                lefts.append(a_all[jnp.where(m < S, g * S + m, zero)])
                rights.append(b_all[jnp.minimum(right[r, c * SLOTS + p], ROW * S - 1)])
            value = jnp.dot(
                jnp.concatenate(lefts, axis=1),
                jnp.concatenate(rights, axis=0),
                preferred_element_type=jnp.float32,
            )
            total = value if total is None else total + value
        return total

    if first:

        @pl.loop(0, R)
        def _(r):
            out[r] = one(r)
    else:
        per = R // (Y * CORE)
        for target, other in ((send, 1), (keep, 0)):

            @pl.loop(0, Y * per)
            def _(k, target=target, other=other):
                to = lax.rem(y + k // per, Y)
                mine = lax.rem(core + other, CORE)
                target[k] = one((to * CORE + mine) * per + lax.rem(k, per))


def call(groups, place, left, right, arrays, b_arrays, before=None):
    first = before is None
    smem = pl.BlockSpec(memory_space=pltpu.SMEM)
    vmem = pl.BlockSpec(memory_space=pltpu.VMEM)
    hbm = pl.BlockSpec(memory_space=pl.ANY)
    flat = [a for group in arrays for a in group]
    operands = [place, left, right, *flat, *b_arrays]
    specs = [smem] * 3 + [hbm] * (len(flat) + len(b_arrays))
    if not first:
        operands.append(before)
        specs.append(vmem)
    half = jax.ShapeDtypeStruct((R // 2, BS, BS), jnp.float32)
    return pl.pallas_call(
        functools.partial(products, groups, first),
        out_shape=jax.ShapeDtypeStruct((R, BS, BS), jnp.float32) if first else (half, half),
        in_specs=specs,
        out_specs=vmem if first else (vmem, vmem),
        scratch_shapes=[
            pltpu.VMEM((len(groups) * S + 1, BS, BS), jnp.bfloat16),
            pltpu.VMEM((ROW * S, BS, BS), jnp.bfloat16),
            pltpu.SemaphoreType.DMA((len(flat),)),
            pltpu.SemaphoreType.DMA((ROW,)),
        ],
        compiler_params=pltpu.CompilerParams(vmem_limit_bytes=24 * 1024 * 1024),
        cost_estimate=pl.CostEstimate(
            flops=R * len(groups) * SLOTS * 2 * BS**3, bytes_accessed=4 * 1024 * 1024, transcendentals=0
        ),
    )(*operands)


def on_device(tiles, pair_a, pair_b):
    own = tiles.reshape(S, BS, BS)
    left = pair_a.reshape(R, COLS * SLOTS)
    right = pair_b.reshape(R, COLS * SLOTS)
    place = jnp.stack([lax.axis_index(n) for n in ("x", "zh", "row", "core", "y")]).astype(jnp.int32)

    def over_x(value):
        return [value] + [lax.ppermute(value, "x", ring(X, -d)) for d in range(1, X)]

    z1 = lax.ppermute(own, "zh", ring(ZH, -1))
    z3 = lax.ppermute(own, "zh", ring(ZH, 1))
    x0 = over_x(own)

    routed = lax.all_to_all(own, ("y", "core"), split_axis=0, concat_axis=0, tiled=True)
    b_right, b_left = [], []
    value = routed
    for s in range(1, ROW):
        value = lax.ppermute(value, "row", [(p, p + 1) for p in range(s - 1, ROW - 1)])
        b_right.append(value)
    value = routed
    for s in range(1, ROW):
        value = lax.ppermute(value, "row", [(p, p - 1) for p in range(1, ROW - s + 1)])
        b_left.append(value)
    b_arrays = [routed, *b_right, *b_left]

    x1 = over_x(z1)
    x3 = over_x(z3)
    half = S // 2
    z2_low = lax.ppermute(z1[:half], "zh", ring(ZH, -1))
    z2_high = lax.ppermute(z3[half:], "zh", ring(ZH, 1))
    x2_low = over_x(z2_low)
    x2_high = over_x(z2_high)

    whole = ((0, S),)
    halves = ((0, half), (half, half))
    early = [(d, z, whole) for z in (0, 1, 3) for d in range(X)]
    late = [(d, 2, halves) for d in range(X)]
    acc = call(early, place, left, right, [[a] for a in x0 + x1 + x3], b_arrays)
    keep, send = call(late, place, left, right, [[a, b] for a, b in zip(x2_low, x2_high)], b_arrays, acc)

    got = lax.ppermute(send, "core", ring(CORE, 1))
    per = R // (Y * CORE)
    quarter = [keep[d * per : (d + 1) * per] + got[d * per : (d + 1) * per] for d in range(Y)]
    total = quarter[0]
    for d in range(1, Y):
        total = total + lax.ppermute(quarter[d], "y", ring(Y, d))
    return total[None, None]


def solution(mesh):
    fine = Mesh(mesh.devices.reshape(ROW, X, ZH, Y, CORE), ("row", "x", "zh", "y", "core"))
    spec = ("row", ("x", "zh"), ("y", "core"))
    return jax.shard_map(
        on_device,
        mesh=fine,
        in_specs=(P(*spec), P(*spec), P(*spec)),
        out_specs=P(*spec),
        check_vma=False,
    )
```

time: 509 us -> 249 us (0.49)
  waiting for transfers between devices: 357 us -> 27.3 us
  starting transfers between devices: 0.08 us -> 159 us
  local copies, waits for them, and re-layouts: 95.6 us -> 19.3 us
  matrix products: 16.9 us -> 0 us
  Pallas kernels: 0 us -> 15.4 us
  between operations: 13.1 us -> 0.66 us
    all_gather x2 -> x0, waiting for transfers between devices: 318 us -> none  [the longest x1 251 us: on_device(): panel = lax.all_gather(tiles, 'col', axis=1, tiled=True)]
    ppermute x0 -> x37, starting transfers between devices: none -> 159 us  [the longest x15 79.7 us: over_x(): lax.ppermute(value, 'x', ring(X, -d))]
    gather x32 -> x0, local copies, waits for them, and re-layouts: 84.7 us -> none  [the longest x16 47.1 us: one_result(): left_tiles = flat[indices[0]]]
    reduce_scatter x1 -> x0, waiting for transfers between devices: 37.7 us -> none  [on_device(): lax.psum_scatter(partial_value[None, None], 'layer', scatter_dimension=2,...]
    ppermute x0 -> x37, waiting for transfers between devices: none -> 27.3 us  [the longest x7 11.1 us: on_device(): lax.ppermute(value, 'row', [(p, p - 1) for p in range(1, ROW - s + 1)])]
    dot_general x16 -> x0, matrix products: 16.9 us -> none  [one_result(): jnp.einsum('pik,pkj->ij', left_tiles, right_tiles, preferred_element_type...]
    pallas_call x0 -> x2, Pallas kernels: none -> 15.4 us  [call(): pl.pallas_call(functools.partial(products, groups, first), out_shape=jax....]
    unnamed x2 -> x46, local copies, waits for them, and re-layouts: 1.6 us -> 16.2 us
  transfers between devices with their start and end apart: 3 -> 37, of which waited for: 3 -> 9; matrix products, arithmetic and copies ran while one was open for 1% -> 2% of each run, Pallas kernels for 0% -> 3%
where the time goes in v1:
time: 249 us; the launch traced here: 246 us
  starting transfers between devices  159 us (64%)
  waiting for transfers between devices  27.3 us (11%)
  blocking collectives  24.1 us (10%)
  local copies, waits for them, and re-layouts  19.3 us (8%)
  Pallas kernels  15.4 us (6%)
    ppermute x15, starting transfers between devices, over_x(): lax.ppermute(value, 'x', ring(X, -d))  79.7 us
    ppermute x1, starting transfers between devices, on_device(): got = lax.ppermute(send, 'core', ring(CORE, 1))  26.7 us
    all_to_all x1, blocking collectives, on_device(): lax.all_to_all(own, ('y', 'core'), split_axis=0, concat_axis=0, tiled=True)  24.1 us
    unnamed x46, local copies, waits for them, and re-layouts  16.2 us
    pallas_call x2, Pallas kernels, call(): pl.pallas_call(functools.partial(products, groups, first), out_shape=jax....  15.4 us
    ppermute x1, starting transfers between devices, on_device(): z1 = lax.ppermute(own, 'zh', ring(ZH, -1))  12 us
    ppermute x7, waiting for transfers between devices, on_device(): lax.ppermute(value, 'row', [(p, p - 1) for p in range(1, ROW - s + 1)])  11.1 us
    ppermute x1, starting transfers between devices, on_device(): z2_low = lax.ppermute(z1[:half], 'zh', ring(ZH, -1))  10.9 us
  transfers between devices with their start and end apart: 37, of which 9 were waited for; matrix products, arithmetic and copies ran while one was open for 2% of the time, Pallas kernels for 3%

profile of v1, /device:TPU:1, one launch (start us, length us, event | category | flops | bytes accessed | tf_op | source)
XLA Modules:
  0.0 246.5 jit_solution(11022698390385226550)
XLA Ops:
  0.0 24.1 %all_to_all.5.refs_12_.refs_8_ = bf16[8,128,128]{2,1,0:T(8,128)(2,1)S(1)} all-to-all(bf16[8,128,128]{2,1,0:T(8,128)(2,1)} %bitcast.10), channel_id=1, replica_groups=mesh['row'=8,'x'=4,'zh'=4,'y'=4,'core'=2] {'y','core'}, dimensions={0} | all-to-all | bytes 524288 | tf_op jit(solution)/shard_map/all_to_all | solution.py:143
  24.1 1.3 collective-permute-start.10
  25.4 1.3 collective-permute-start.17
  26.7 3.5 %collective-permute-done.10.refs_13_.refs_9_ = bf16[8,128,128]{2,1,0:T(8,128)(2,1)S(1)} collective-permute-done((bf16[8,128,128]{2,1,0:T(8,128)(2,1)S(1)}, bf16[8,128,128]{2,1,0:T(8,128)(2,1)S(1)}, u32[]{:S(2)}, u32[]{:S(2)}) %collective-permute-start.10) | collective-permute-done | bytes 262176 | tf_op jit(solution)/shard_map/ppermute | solution.py:147
  30.9 3.1 %collective-permute-done.17.refs_20_.refs_16_ = bf16[8,128,128]{2,1,0:T(8,128)(2,1)S(1)} collective-permute-done((bf16[8,128,128]{2,1,0:T(8,128)(2,1)S(1)}, bf16[8,128,128]{2,1,0:T(8,128)(2,1)S(1)}, u32[]{:S(2)}, u32[]{:S(2)}) %collective-permute-start.17) | collective-permute-done | bytes 262176 | tf_op jit(solution)/shard_map/ppermute | solution.py:151
  34.1 1.3 collective-permute-start.18
  35.4 0.7 collective-permute-start.12
  36.0 5.7 %collective-permute-done.18.refs_21_.refs_17_ = bf16[8,128,128]{2,1,0:T(8,128)(2,1)S(1)} collective-permute-done((bf16[8,128,128]{2,1,0:T(8,128)(2,1)S(1)}, bf16[8,128,128]{2,1,0:T(8,128)(2,1)S(1)}, u32[]{:S(2)}, u32[]{:S(2)}) %collective-permute-start.18) | collective-permute-done | bytes 262176 | tf_op jit(solution)/shard_map/ppermute | solution.py:151
  41.8 1.3 collective-permute-start.19
  43.1 12.0 %collective-permute-start = (bf16[8,128,128]{2,1,0:T(8,128)(2,1)S(1)}, bf16[8,128,128]{2,1,0:T(8,128)(2,1)S(1)}, u32[]{:S(2)}, u32[]{:S(2)}) collective-permute-start(bf16[8,128,128]{2,1,0:T(8,128)(2,1)S(1)} %bitcast.11), channel_id=1, source_target_pairs={{0,24},{8,0},{16,8},{24,16},{1,25},{9,1},{17,9},{25,17},{2,26},{10... | collective-permute-start | bytes 786440 | tf_op jit(solution)/shard_map/ppermute | solution.py:139
  55.1 2.0 collective-permute-start.2
  57.8 1.3 collective-permute-start.20
  59.1 4.3 %collective-permute-start.24 = (bf16[8,128,128]{2,1,0:T(8,128)(2,1)S(1)}, bf16[8,128,128]{2,1,0:T(8,128)(2,1)S(1)}, u32[]{:S(2)}, u32[]{:S(2)}) collective-permute-start(bf16[8,128,128]{2,1,0:T(8,128)(2,1)S(1)} %bitcast.13), channel_id=1, source_target_pairs={{0,96},{32,0},{64,32},{96,64},{1,97},{33,1},{65,33},{97,65},{2,98}... | collective-permute-start | bytes 786440 | tf_op jit(solution)/shard_map/ppermute | solution.py:137
  63.4 1.7 collective-permute-done.refs_4_
  65.1 38.3 %collective-permute-start.25 = (bf16[8,128,128]{2,1,0:T(8,128)(2,1)S(1)}, bf16[8,128,128]{2,1,0:T(8,128)(2,1)S(1)}, u32[]{:S(2)}, u32[]{:S(2)}) collective-permute-start(bf16[8,128,128]{2,1,0:T(8,128)(2,1)S(1)} %bitcast.14), channel_id=1, source_target_pairs={{0,64},{32,96},{64,0},{96,32},{1,65},{33,97},{65,1},{97,33},{2,66}... | collective-permute-start | bytes 786440 | tf_op jit(solution)/shard_map/ppermute | solution.py:137
  103.4 2.3 collective-permute-start.26
  106.4 2.2 collective-permute-done.20.refs_23_.refs_19_
  108.6 1.3 collective-permute-start.21
  109.9 0.9 slice.41
  111.5 10.9 %collective-permute-start.1 = (bf16[4,128,128]{2,1,0:T(8,128)(2,1)S(1)}, bf16[4,128,128]{2,1,0:T(8,128)(2,1)S(1)}, u32[]{:S(2)}, u32[]{:S(2)}) collective-permute-start(bf16[4,128,128]{2,1,0:T(8,128)(2,1)S(1)} %slice.40), channel_id=1, source_target_pairs={{0,24},{8,0},{16,8},{24,16},{1,25},{9,1},{17,9},{25,17},{2,26},{10... | collective-permute-start | bytes 393224 | tf_op jit(solution)/shard_map/ppermute | solution.py:158
  122.4 0.7 copy-done.6
  123.1 3.1 %collective-permute-start.3 = (bf16[4,128,128]{2,1,0:T(8,128)(2,1)S(1)}, bf16[4,128,128]{2,1,0:T(8,128)(2,1)S(1)}, u32[]{:S(2)}, u32[]{:S(2)}) collective-permute-start(bf16[4,128,128]{2,1,0:T(8,128)(2,1)S(1)} %slice.41), channel_id=1, source_target_pairs={{0,8},{8,16},{16,24},{24,0},{1,9},{9,17},{17,25},{25,1},{2,10},{10... | collective-permute-start | bytes 393224 | tf_op jit(solution)/shard_map/ppermute | solution.py:159
  126.2 0.7 copy-done.8
  126.9 3.0 %collective-permute-start.27 = (bf16[8,128,128]{2,1,0:T(8,128)(2,1)S(1)}, bf16[8,128,128]{2,1,0:T(8,128)(2,1)S(1)}, u32[]{:S(2)}, u32[]{:S(2)}) collective-permute-start(bf16[8,128,128]{2,1,0:T(8,128)(2,1)S(1)} %collective-permute-done.refs_4_), channel_id=1, source_target_pairs={{0,96},{32,0},{64,32},{96,64},{1,97},{33,1},{65,33},{97,65},{2,98}... | collective-permute-start | bytes 786440 | tf_op jit(solution)/shard_map/ppermute | solution.py:137
  130.0 1.9 collective-permute-start.28
  131.9 5.9 %collective-permute-done.3.refs_1_ = bf16[4,128,128]{2,1,0:T(8,128)(2,1)S(1)} collective-permute-done((bf16[4,128,128]{2,1,0:T(8,128)(2,1)S(1)}, bf16[4,128,128]{2,1,0:T(8,128)(2,1)S(1)}, u32[]{:S(2)}, u32[]{:S(2)}) %collective-permute-start.3) | collective-permute-done | bytes 131104 | tf_op jit(solution)/shard_map/ppermute | solution.py:159
  137.8 1.9 collective-permute-start.29
  139.7 0.7 collective-permute-start.15
  140.4 1.3 collective-permute-start.22
  141.7 0.7 copy-done.10
  142.4 4.6 %collective-permute-start.30 = (bf16[8,128,128]{2,1,0:T(8,128)(2,1)}, bf16[8,128,128]{2,1,0:T(8,128)(2,1)S(1)}, u32[]{:S(2)}, u32[]{:S(2)}) collective-permute-start(bf16[8,128,128]{2,1,0:T(8,128)(2,1)} %collective-permute-done.2.refs_8_), channel_id=1, source_target_pairs={{0,96},{32,0},{64,32},{96,64},{1,97},{33,1},{65,33},{97,65},{2,98}... | collective-permute-start | bytes 786440 | tf_op jit(solution)/shard_map/ppermute | solution.py:137
  147.0 0.7 copy-done.12
  147.7 2.7 %collective-permute-start.31 = (bf16[8,128,128]{2,1,0:T(8,128)(2,1)}, bf16[8,128,128]{2,1,0:T(8,128)(2,1)}, u32[]{:S(2)}, u32[]{:S(2)}) collective-permute-start(bf16[8,128,128]{2,1,0:T(8,128)(2,1)} %collective-permute-done.2.refs_8_), channel_id=1, source_target_pairs={{0,64},{32,96},{64,0},{96,32},{1,65},{33,97},{65,1},{97,33},{2,66}... | collective-permute-start | bytes 786440 | tf_op jit(solution)/shard_map/ppermute | solution.py:137
  150.5 0.7 copy-done.14
  151.2 2.7 %collective-permute-start.32 = (bf16[8,128,128]{2,1,0:T(8,128)(2,1)}, bf16[8,128,128]{2,1,0:T(8,128)(2,1)}, u32[]{:S(2)}, u32[]{:S(2)}) collective-permute-start(bf16[8,128,128]{2,1,0:T(8,128)(2,1)} %collective-permute-done.2.refs_8_), channel_id=1, source_target_pairs={{0,32},{32,64},{64,96},{96,0},{1,33},{33,65},{65,97},{97,1},{2,34}... | collective-permute-start | bytes 786440 | tf_op jit(solution)/shard_map/ppermute | solution.py:137
  154.0 1.4 collective-permute-start.16
  155.3 1.3 collective-permute-start.23
  157.3 3.7 %collective-permute-start.4 = (bf16[4,128,128]{2,1,0:T(8,128)(2,1)S(1)}, bf16[4,128,128]{2,1,0:T(8,128)(2,1)}, u32[]{:S(2)}, u32[]{:S(2)}) collective-permute-start(bf16[4,128,128]{2,1,0:T(8,128)(2,1)S(1)} %collective-permute-done.1.refs_0_), channel_id=1, source_target_pairs={{0,96},{32,0},{64,32},{96,64},{1,97},{33,1},{65,33},{97,65},{2,98}... | collective-permute-start | bytes 393224 | tf_op jit(solution)/shard_map/ppermute | solution.py:137
  161.8 0.8 copy.10.left
  162.5 1.4 copy.7
  163.9 0.8 copy.11.right
  165.4 2.8 %collective-permute-start.6 = (bf16[4,128,128]{2,1,0:T(8,128)(2,1)S(1)}, bf16[4,128,128]{2,1,0:T(8,128)(2,1)S(1)}, u32[]{:S(2)}, u32[]{:S(2)}) collective-permute-start(bf16[4,128,128]{2,1,0:T(8,128)(2,1)S(1)} %collective-permute-done.1.refs_0_), channel_id=1, source_target_pairs={{0,64},{32,96},{64,0},{96,32},{1,65},{33,97},{65,1},{97,33},{2,66}... | collective-permute-start | bytes 393224 | tf_op jit(solution)/shard_map/ppermute | solution.py:137
  168.2 3.0 %collective-permute-start.5 = (bf16[4,128,128]{2,1,0:T(8,128)(2,1)}, bf16[4,128,128]{2,1,0:T(8,128)(2,1)S(1)}, u32[]{:S(2)}, u32[]{:S(2)}) collective-permute-start(bf16[4,128,128]{2,1,0:T(8,128)(2,1)} %copy-done.18), channel_id=1, source_target_pairs={{0,96},{32,0},{64,32},{96,64},{1,97},{33,1},{65,33},{97,65},{2,98}... | collective-permute-start | bytes 393224 | tf_op jit(solution)/shard_map/ppermute | solution.py:137
  171.3 2.9 %collective-permute-start.7 = (bf16[4,128,128]{2,1,0:T(8,128)(2,1)}, bf16[4,128,128]{2,1,0:T(8,128)(2,1)S(1)}, u32[]{:S(2)}, u32[]{:S(2)}) collective-permute-start(bf16[4,128,128]{2,1,0:T(8,128)(2,1)} %copy-done.18), channel_id=1, source_target_pairs={{0,64},{32,96},{64,0},{96,32},{1,65},{33,97},{65,1},{97,33},{2,66}... | collective-permute-start | bytes 393224 | tf_op jit(solution)/shard_map/ppermute | solution.py:137
  174.1 2.8 %collective-permute-start.8 = (bf16[4,128,128]{2,1,0:T(8,128)(2,1)S(1)}, bf16[4,128,128]{2,1,0:T(8,128)(2,1)S(1)}, u32[]{:S(2)}, u32[]{:S(2)}) collective-permute-start(bf16[4,128,128]{2,1,0:T(8,128)(2,1)S(1)} %collective-permute-done.1.refs_0_), channel_id=1, source_target_pairs={{0,32},{32,64},{64,96},{96,0},{1,33},{33,65},{65,97},{97,1},{2,34}... | collective-permute-start | bytes 393224 | tf_op jit(solution)/shard_map/ppermute | solution.py:137
  176.9 2.8 %collective-permute-start.9 = (bf16[4,128,128]{2,1,0:T(8,128)(2,1)}, bf16[4,128,128]{2,1,0:T(8,128)(2,1)S(1)}, u32[]{:S(2)}, u32[]{:S(2)}) collective-permute-start(bf16[4,128,128]{2,1,0:T(8,128)(2,1)} %copy-done.18), channel_id=1, source_target_pairs={{0,32},{32,64},{64,96},{96,0},{1,33},{33,65},{65,97},{97,1},{2,34}... | collective-permute-start | bytes 393224 | tf_op jit(solution)/shard_map/ppermute | solution.py:137
  179.7 0.9 copy-done.1
  180.6 0.9 copy-done.3
  181.6 0.9 copy-done.5
  182.5 0.9 copy-done.7
  183.5 0.9 copy-done.9
  184.4 0.9 copy-done.11
  185.4 0.9 copy-done.13
  186.3 0.9 copy-done.15
  187.3 0.9 copy-done.17
  188.9 8.3 %shard_map.37.refs_23_ = f32[16,128,128]{2,1,0:T(8,128)S(1)} custom-call(s32[5]{0:T(128)S(1)} %copy-done.20, s32[16,32]{1,0:T(8,128)S(1)} %copy.10.left, s32[16,32]{1,0:T(8,128)S(1)} %copy.11.right, bf16[8,128,128]{2,1,0:T(8,128)(2,1)S(1)} %bitcast.16, bf16[8,128,128]{2,1,0:T(8,128)(2,1)S(1)} %copy-done.5, bf16[8,128,128]{2,1,0:T(8,128)(2,1)S(1)} %copy-done.7, ...), custom_call_target="tpu_custom_call" | custom-call | flops 1610612736 | bytes 4194304 | tf_op jit(solution)/shard_map/pallas_call | solution.py:112
  197.2 7.2 %shard_map.38 = (f32[8,128,128]{2,1,0:T(8,128)S(1)}, f32[8,128,128]{2,1,0:T(8,128)S(1)}) custom-call(s32[5]{0:T(128)S(1)} %copy-done.20, s32[16,32]{1,0:T(8,128)S(1)} %copy.10.left, s32[16,32]{1,0:T(8,128)S(1)} %copy.11.right, bf16[4,128,128]{2,1,0:T(8,128)(2,1)S(1)} %collective-permute-done.1.refs_0_, bf16[4,128,128]{2,1,0:T(8,128)(2,1)S(1)} %copy-done.19, ...), custom_call_target="tpu_custom_call" | custom-call | flops 536870912 | bytes 4194304 | tf_op jit(solution)/shard_map/pallas_call | solution.py:112
  204.4 26.7 %collective-permute-start.33 = (f32[8,128,128]{2,1,0:T(8,128)S(1)}, f32[8,128,128]{2,1,0:T(8,128)S(1)}, u32[]{:S(2)}, u32[]{:S(2)}) collective-permute-start(f32[8,128,128]{2,1,0:T(8,128)S(1)} %get-tuple-element.8), channel_id=1, source_target_pairs={{0,1},{1,0},{2,3},{3,2},{4,5},{5,4},{6,7},{7,6},{8,9},{9,8},{10,11... | collective-permute-start | bytes 1572872 | tf_op jit(solution)/shard_map/ppermute | solution.py:170
  231.1 1.5 collective-permute-done.33
  232.7 2.2 collective-permute-start.34
  234.9 3.7 %collective-permute-start.35 = (f32[2,128,128]{2,1,0:T(8,128)S(1)}, f32[2,128,128]{2,1,0:T(8,128)S(1)}, u32[]{:S(2)}, u32[]{:S(2)}) collective-permute-start(f32[2,128,128]{2,1,0:T(8,128)S(1)} %get-tuple-element.11), channel_id=1, source_target_pairs={{0,4},{2,6},{4,0},{6,2},{1,5},{3,7},{5,1},{7,3},{8,12},{10,14},{12... | collective-permute-start | bytes 393224 | tf_op jit(solution)/shard_map/ppermute | solution.py:175
  238.6 3.6 %collective-permute-start.36 = (f32[2,128,128]{2,1,0:T(8,128)S(1)}, f32[2,128,128]{2,1,0:T(8,128)S(1)}, u32[]{:S(2)}, u32[]{:S(2)}) collective-permute-start(f32[2,128,128]{2,1,0:T(8,128)S(1)} %get-tuple-element.10), channel_id=1, source_target_pairs={{0,6},{2,0},{4,2},{6,4},{1,7},{3,1},{5,3},{7,5},{8,14},{10,8},{12,... | collective-permute-start | bytes 393224 | tf_op jit(solution)/shard_map/ppermute | solution.py:175
  242.8 3.0 %collective-permute-done.36 = f32[2,128,128]{2,1,0:T(8,128)S(1)} collective-permute-done((f32[2,128,128]{2,1,0:T(8,128)S(1)}, f32[2,128,128]{2,1,0:T(8,128)S(1)}, u32[]{:S(2)}, u32[]{:S(2)}) %collective-permute-start.36) | collective-permute-done | bytes 131104 | tf_op jit(solution)/shard_map/ppermute | solution.py:175
  245.8 0.7 fusion.3
  (66 shorter events, 6.1 us)
Async XLA Ops:
  0.0 43.1 %copy-start = (bf16[1,1,1,8,1,128,128]{6,5,4,3,2,1,0:T(8,128)(2,1)S(1)}, bf16[1,1,1,8,1,128,128]{6,5,4,3,2,1,0:T(8,128)(2,1)}, u32[]{:S(2)}) copy-start(bf16[1,1,1,8,1,128,128]{6,5,4,3,2,1,0:T(8,128)(2,1)} %param.3) | copy-start | bytes 786436
  24.1 6.1 %collective-permute-start.10 = (bf16[8,128,128]{2,1,0:T(8,128)(2,1)S(1)}, bf16[8,128,128]{2,1,0:T(8,128)(2,1)S(1)}, u32[]{:S(2)}, u32[]{:S(2)}) collective-permute-start(bf16[8,128,128]{2,1,0:T(8,128)(2,1)S(1)} %all_to_all.5.refs_12_.refs_8_), channel_id=1, source_target_pairs={{0,128},{128,256},{256,384},{384,512},{512,640},{640,768},{768,896... | collective-permute-start | bytes 786440 | tf_op jit(solution)/shard_map/ppermute | solution.py:147
  25.4 8.7 %collective-permute-start.17 = (bf16[8,128,128]{2,1,0:T(8,128)(2,1)S(1)}, bf16[8,128,128]{2,1,0:T(8,128)(2,1)S(1)}, u32[]{:S(2)}, u32[]{:S(2)}) collective-permute-start(bf16[8,128,128]{2,1,0:T(8,128)(2,1)S(1)} %all_to_all.5.refs_12_.refs_8_), channel_id=1, source_target_pairs={{128,0},{256,128},{384,256},{512,384},{640,512},{768,640},{896,768... | collective-permute-start | bytes 786440 | tf_op jit(solution)/shard_map/ppermute | solution.py:151
  30.2 5.1 %collective-permute-start.11 = (bf16[8,128,128]{2,1,0:T(8,128)(2,1)S(1)}, bf16[8,128,128]{2,1,0:T(8,128)(2,1)S(1)}, u32[]{:S(2)}, u32[]{:S(2)}) collective-permute-start(bf16[8,128,128]{2,1,0:T(8,128)(2,1)S(1)} %collective-permute-done.10.refs_13_.refs_9_), channel_id=1, source_target_pairs={{128,256},{256,384},{384,512},{512,640},{640,768},{768,896},{129,2... | collective-permute-start | bytes 786440 | tf_op jit(solution)/shard_map/ppermute | solution.py:147
  34.1 7.7 %collective-permute-start.18 = (bf16[8,128,128]{2,1,0:T(8,128)(2,1)S(1)}, bf16[8,128,128]{2,1,0:T(8,128)(2,1)S(1)}, u32[]{:S(2)}, u32[]{:S(2)}) collective-permute-start(bf16[8,128,128]{2,1,0:T(8,128)(2,1)S(1)} %collective-permute-done.17.refs_20_.refs_16_), channel_id=1, source_target_pairs={{128,0},{256,128},{384,256},{512,384},{640,512},{768,640},{129,1},... | collective-permute-start | bytes 786440 | tf_op jit(solution)/shard_map/ppermute | solution.py:151
  35.4 21.7 %collective-permute-start.12 = (bf16[8,128,128]{2,1,0:T(8,128)(2,1)S(1)}, bf16[8,128,128]{2,1,0:T(8,128)(2,1)S(1)}, u32[]{:S(2)}, u32[]{:S(2)}) collective-permute-start(bf16[8,128,128]{2,1,0:T(8,128)(2,1)S(1)} %collective-permute-done.11.refs_14_.refs_10_), channel_id=1, source_target_pairs={{256,384},{384,512},{512,640},{640,768},{768,896},{257,385},{385,5... | collective-permute-start | bytes 786440 | tf_op jit(solution)/shard_map/ppermute | solution.py:147
  41.8 16.0 %collective-permute-start.19 = (bf16[8,128,128]{2,1,0:T(8,128)(2,1)S(1)}, bf16[8,128,128]{2,1,0:T(8,128)(2,1)S(1)}, u32[]{:S(2)}, u32[]{:S(2)}) collective-permute-start(bf16[8,128,128]{2,1,0:T(8,128)(2,1)S(1)} %collective-permute-done.18.refs_21_.refs_17_), channel_id=1, source_target_pairs={{128,0},{256,128},{384,256},{512,384},{640,512},{129,1},{257,129},... | collective-permute-start | bytes 786440 | tf_op jit(solution)/shard_map/ppermute | solution.py:151
  43.1 22.0 %collective-permute-start = (bf16[8,128,128]{2,1,0:T(8,128)(2,1)S(1)}, bf16[8,128,128]{2,1,0:T(8,128)(2,1)S(1)}, u32[]{:S(2)}, u32[]{:S(2)}) collective-permute-start(bf16[8,128,128]{2,1,0:T(8,128)(2,1)S(1)} %bitcast.11), channel_id=1, source_target_pairs={{0,24},{8,0},{16,8},{24,16},{1,25},{9,1},{17,9},{25,17},{2,26},{10... | collective-permute-start | bytes 786440 | tf_op jit(solution)/shard_map/ppermute | solution.py:139
  55.1 48.3 %collective-permute-start.2 = (bf16[8,128,128]{2,1,0:T(8,128)(2,1)S(1)}, bf16[8,128,128]{2,1,0:T(8,128)(2,1)}, u32[]{:S(2)}, u32[]{:S(2)}) collective-permute-start(bf16[8,128,128]{2,1,0:T(8,128)(2,1)S(1)} %bitcast.12), channel_id=1, source_target_pairs={{0,8},{8,16},{16,24},{24,0},{1,9},{9,17},{17,25},{25,1},{2,10},{10... | collective-permute-start | bytes 786440 | tf_op jit(solution)/shard_map/ppermute | solution.py:140
  57.1 48.6 %collective-permute-start.13 = (bf16[8,128,128]{2,1,0:T(8,128)(2,1)S(1)}, bf16[8,128,128]{2,1,0:T(8,128)(2,1)S(1)}, u32[]{:S(2)}, u32[]{:S(2)}) collective-permute-start(bf16[8,128,128]{2,1,0:T(8,128)(2,1)S(1)} %collective-permute-done.12.refs_15_.refs_11_), channel_id=1, source_target_pairs={{384,512},{512,640},{640,768},{768,896},{385,513},{513,641},{641,7... | collective-permute-start | bytes 786440 | tf_op jit(solution)/shard_map/ppermute | solution.py:147
  57.8 50.8 %collective-permute-start.20 = (bf16[8,128,128]{2,1,0:T(8,128)(2,1)S(1)}, bf16[8,128,128]{2,1,0:T(8,128)(2,1)S(1)}, u32[]{:S(2)}, u32[]{:S(2)}) collective-permute-start(bf16[8,128,128]{2,1,0:T(8,128)(2,1)S(1)} %collective-permute-done.19.refs_22_.refs_18_), channel_id=1, source_target_pairs={{128,0},{256,128},{384,256},{512,384},{129,1},{257,129},{385,257},... | collective-permute-start | bytes 786440 | tf_op jit(solution)/shard_map/ppermute | solution.py:151
  59.1 51.7 %collective-permute-start.24 = (bf16[8,128,128]{2,1,0:T(8,128)(2,1)S(1)}, bf16[8,128,128]{2,1,0:T(8,128)(2,1)S(1)}, u32[]{:S(2)}, u32[]{:S(2)}) collective-permute-start(bf16[8,128,128]{2,1,0:T(8,128)(2,1)S(1)} %bitcast.13), channel_id=1, source_target_pairs={{0,96},{32,0},{64,32},{96,64},{1,97},{33,1},{65,33},{97,65},{2,98}... | collective-permute-start | bytes 786440 | tf_op jit(solution)/shard_map/ppermute | solution.py:137
  65.1 90.3 %copy-start.2 = (bf16[8,128,128]{2,1,0:T(8,128)(2,1)}, bf16[8,128,128]{2,1,0:T(8,128)(2,1)S(1)}, u32[]{:S(2)}) copy-start(bf16[8,128,128]{2,1,0:T(8,128)(2,1)S(1)} %collective-permute-done.refs_4_) | copy-start | bytes 786436
  65.1 57.3 %collective-permute-start.25 = (bf16[8,128,128]{2,1,0:T(8,128)(2,1)S(1)}, bf16[8,128,128]{2,1,0:T(8,128)(2,1)S(1)}, u32[]{:S(2)}, u32[]{:S(2)}) collective-permute-start(bf16[8,128,128]{2,1,0:T(8,128)(2,1)S(1)} %bitcast.14), channel_id=1, source_target_pairs={{0,64},{32,96},{64,0},{96,32},{1,65},{33,97},{65,1},{97,33},{2,66}... | collective-permute-start | bytes 786440 | tf_op jit(solution)/shard_map/ppermute | solution.py:137
  103.4 22.8 %collective-permute-start.26 = (bf16[8,128,128]{2,1,0:T(8,128)(2,1)S(1)}, bf16[8,128,128]{2,1,0:T(8,128)(2,1)S(1)}, u32[]{:S(2)}, u32[]{:S(2)}) collective-permute-start(bf16[8,128,128]{2,1,0:T(8,128)(2,1)S(1)} %bitcast.15), channel_id=1, source_target_pairs={{0,32},{32,64},{64,96},{96,0},{1,33},{33,65},{65,97},{97,1},{2,34}... | collective-permute-start | bytes 786440 | tf_op jit(solution)/shard_map/ppermute | solution.py:137
  105.7 34.0 %collective-permute-start.14 = (bf16[8,128,128]{2,1,0:T(8,128)(2,1)S(1)}, bf16[8,128,128]{2,1,0:T(8,128)(2,1)S(1)}, u32[]{:S(2)}, u32[]{:S(2)}) collective-permute-start(bf16[8,128,128]{2,1,0:T(8,128)(2,1)S(1)} %collective-permute-done.13.refs_16_.refs_12_), channel_id=1, source_target_pairs={{512,640},{640,768},{768,896},{513,641},{641,769},{769,897},{514,6... | collective-permute-start | bytes 786440 | tf_op jit(solution)/shard_map/ppermute | solution.py:147
  108.6 31.8 %collective-permute-start.21 = (bf16[8,128,128]{2,1,0:T(8,128)(2,1)S(1)}, bf16[8,128,128]{2,1,0:T(8,128)(2,1)S(1)}, u32[]{:S(2)}, u32[]{:S(2)}) collective-permute-start(bf16[8,128,128]{2,1,0:T(8,128)(2,1)S(1)} %collective-permute-done.20.refs_23_.refs_19_), channel_id=1, source_target_pairs={{128,0},{256,128},{384,256},{129,1},{257,129},{385,257},{130,2},{2... | collective-permute-start | bytes 786440 | tf_op jit(solution)/shard_map/ppermute | solution.py:151
  110.8 50.3 %copy-start.21 = (s32[1,1,1,16,16,2]{4,5,3,2,1,0:T(2,128)S(1)}, s32[1,1,1,16,16,2]{4,5,3,2,1,0:T(2,128)}, u32[]{:S(2)}) copy-start(s32[1,1,1,16,16,2]{4,5,3,2,1,0:T(2,128)} %param.4) | copy-start | bytes 6148
  110.8 0.7 copy-start.4
  111.5 18.5 %collective-permute-start.1 = (bf16[4,128,128]{2,1,0:T(8,128)(2,1)S(1)}, bf16[4,128,128]{2,1,0:T(8,128)(2,1)S(1)}, u32[]{:S(2)}, u32[]{:S(2)}) collective-permute-start(bf16[4,128,128]{2,1,0:T(8,128)(2,1)S(1)} %slice.40), channel_id=1, source_target_pairs={{0,24},{8,0},{16,8},{24,16},{1,25},{9,1},{17,9},{25,17},{2,26},{10... | collective-permute-start | bytes 393224 | tf_op jit(solution)/shard_map/ppermute | solution.py:158
  122.4 0.7 copy-start.6
  123.1 14.7 %collective-permute-start.3 = (bf16[4,128,128]{2,1,0:T(8,128)(2,1)S(1)}, bf16[4,128,128]{2,1,0:T(8,128)(2,1)S(1)}, u32[]{:S(2)}, u32[]{:S(2)}) collective-permute-start(bf16[4,128,128]{2,1,0:T(8,128)(2,1)S(1)} %slice.41), channel_id=1, source_target_pairs={{0,8},{8,16},{16,24},{24,0},{1,9},{9,17},{17,25},{25,1},{2,10},{10... | collective-permute-start | bytes 393224 | tf_op jit(solution)/shard_map/ppermute | solution.py:159
  126.2 0.7 copy-start.8
  126.9 14.8 %collective-permute-start.27 = (bf16[8,128,128]{2,1,0:T(8,128)(2,1)S(1)}, bf16[8,128,128]{2,1,0:T(8,128)(2,1)S(1)}, u32[]{:S(2)}, u32[]{:S(2)}) collective-permute-start(bf16[8,128,128]{2,1,0:T(8,128)(2,1)S(1)} %collective-permute-done.refs_4_), channel_id=1, source_target_pairs={{0,96},{32,0},{64,32},{96,64},{1,97},{33,1},{65,33},{97,65},{2,98}... | collective-permute-start | bytes 786440 | tf_op jit(solution)/shard_map/ppermute | solution.py:137
  130.0 17.0 %collective-permute-start.28 = (bf16[8,128,128]{2,1,0:T(8,128)(2,1)S(1)}, bf16[8,128,128]{2,1,0:T(8,128)(2,1)S(1)}, u32[]{:S(2)}, u32[]{:S(2)}) collective-permute-start(bf16[8,128,128]{2,1,0:T(8,128)(2,1)S(1)} %collective-permute-done.refs_4_), channel_id=1, source_target_pairs={{0,64},{32,96},{64,0},{96,32},{1,65},{33,97},{65,1},{97,33},{2,66}... | collective-permute-start | bytes 786440 | tf_op jit(solution)/shard_map/ppermute | solution.py:137
  137.8 18.8 %copy-start.18 = (bf16[4,128,128]{2,1,0:T(8,128)(2,1)}, bf16[4,128,128]{2,1,0:T(8,128)(2,1)S(1)}, u32[]{:S(2)}) copy-start(bf16[4,128,128]{2,1,0:T(8,128)(2,1)S(1)} %collective-permute-done.3.refs_1_) | copy-start | bytes 393220
  137.8 12.7 %collective-permute-start.29 = (bf16[8,128,128]{2,1,0:T(8,128)(2,1)S(1)}, bf16[8,128,128]{2,1,0:T(8,128)(2,1)S(1)}, u32[]{:S(2)}, u32[]{:S(2)}) collective-permute-start(bf16[8,128,128]{2,1,0:T(8,128)(2,1)S(1)} %collective-permute-done.refs_4_), channel_id=1, source_target_pairs={{0,32},{32,64},{64,96},{96,0},{1,33},{33,65},{65,97},{97,1},{2,34}... | collective-permute-start | bytes 786440 | tf_op jit(solution)/shard_map/ppermute | solution.py:137
  139.7 14.2 %collective-permute-start.15 = (bf16[8,128,128]{2,1,0:T(8,128)(2,1)S(1)}, bf16[8,128,128]{2,1,0:T(8,128)(2,1)S(1)}, u32[]{:S(2)}, u32[]{:S(2)}) collective-permute-start(bf16[8,128,128]{2,1,0:T(8,128)(2,1)S(1)} %collective-permute-done.14.refs_17_.refs_13_), channel_id=1, source_target_pairs={{640,768},{768,896},{641,769},{769,897},{642,770},{770,898},{643,7... | collective-permute-start | bytes 786440 | tf_op jit(solution)/shard_map/ppermute | solution.py:147
  140.4 14.9 %collective-permute-start.22 = (bf16[8,128,128]{2,1,0:T(8,128)(2,1)S(1)}, bf16[8,128,128]{2,1,0:T(8,128)(2,1)S(1)}, u32[]{:S(2)}, u32[]{:S(2)}) collective-permute-start(bf16[8,128,128]{2,1,0:T(8,128)(2,1)S(1)} %collective-permute-done.21.refs_24_.refs_20_), channel_id=1, source_target_pairs={{128,0},{256,128},{129,1},{257,129},{130,2},{258,130},{131,3},{259... | collective-permute-start | bytes 786440 | tf_op jit(solution)/shard_map/ppermute | solution.py:151
  141.7 0.7 copy-start.10
  142.4 14.2 %collective-permute-start.30 = (bf16[8,128,128]{2,1,0:T(8,128)(2,1)}, bf16[8,128,128]{2,1,0:T(8,128)(2,1)S(1)}, u32[]{:S(2)}, u32[]{:S(2)}) collective-permute-start(bf16[8,128,128]{2,1,0:T(8,128)(2,1)} %collective-permute-done.2.refs_8_), channel_id=1, source_target_pairs={{0,96},{32,0},{64,32},{96,64},{1,97},{33,1},{65,33},{97,65},{2,98}... | collective-permute-start | bytes 786440 | tf_op jit(solution)/shard_map/ppermute | solution.py:137
  147.0 0.7 copy-start.12
  147.7 17.7 %collective-permute-start.31 = (bf16[8,128,128]{2,1,0:T(8,128)(2,1)}, bf16[8,128,128]{2,1,0:T(8,128)(2,1)}, u32[]{:S(2)}, u32[]{:S(2)}) collective-permute-start(bf16[8,128,128]{2,1,0:T(8,128)(2,1)} %collective-permute-done.2.refs_8_), channel_id=1, source_target_pairs={{0,64},{32,96},{64,0},{96,32},{1,65},{33,97},{65,1},{97,33},{2,66}... | collective-permute-start | bytes 786440 | tf_op jit(solution)/shard_map/ppermute | solution.py:137
  150.5 0.7 copy-start.14
  151.2 17.0 %collective-permute-start.32 = (bf16[8,128,128]{2,1,0:T(8,128)(2,1)}, bf16[8,128,128]{2,1,0:T(8,128)(2,1)}, u32[]{:S(2)}, u32[]{:S(2)}) collective-permute-start(bf16[8,128,128]{2,1,0:T(8,128)(2,1)} %collective-permute-done.2.refs_8_), channel_id=1, source_target_pairs={{0,32},{32,64},{64,96},{96,0},{1,33},{33,65},{65,97},{97,1},{2,34}... | collective-permute-start | bytes 786440 | tf_op jit(solution)/shard_map/ppermute | solution.py:137
  154.0 20.2 %collective-permute-start.16 = (bf16[8,128,128]{2,1,0:T(8,128)(2,1)S(1)}, bf16[8,128,128]{2,1,0:T(8,128)(2,1)}, u32[]{:S(2)}, u32[]{:S(2)}) collective-permute-start(bf16[8,128,128]{2,1,0:T(8,128)(2,1)S(1)} %collective-permute-done.15.refs_18_.refs_14_), channel_id=1, source_target_pairs={{768,896},{769,897},{770,898},{771,899},{772,900},{773,901},{774,9... | collective-permute-start | bytes 786440 | tf_op jit(solution)/shard_map/ppermute | solution.py:147
  155.3 21.6 %collective-permute-start.23 = (bf16[8,128,128]{2,1,0:T(8,128)(2,1)S(1)}, bf16[8,128,128]{2,1,0:T(8,128)(2,1)}, u32[]{:S(2)}, u32[]{:S(2)}) collective-permute-start(bf16[8,128,128]{2,1,0:T(8,128)(2,1)S(1)} %collective-permute-done.22.refs_25_.refs_21_), channel_id=1, source_target_pairs={{128,0},{129,1},{130,2},{131,3},{132,4},{133,5},{134,6},{135,7},{1... | collective-permute-start | bytes 786440 | tf_op jit(solution)/shard_map/ppermute | solution.py:151
  156.7 0.7 copy-start.16
  157.3 13.9 %collective-permute-start.4 = (bf16[4,128,128]{2,1,0:T(8,128)(2,1)S(1)}, bf16[4,128,128]{2,1,0:T(8,128)(2,1)}, u32[]{:S(2)}, u32[]{:S(2)}) collective-permute-start(bf16[4,128,128]{2,1,0:T(8,128)(2,1)S(1)} %collective-permute-done.1.refs_0_), channel_id=1, source_target_pairs={{0,96},{32,0},{64,32},{96,64},{1,97},{33,1},{65,33},{97,65},{2,98}... | collective-permute-start | bytes 393224 | tf_op jit(solution)/shard_map/ppermute | solution.py:137
  165.4 31.8 %collective-permute-start.6 = (bf16[4,128,128]{2,1,0:T(8,128)(2,1)S(1)}, bf16[4,128,128]{2,1,0:T(8,128)(2,1)S(1)}, u32[]{:S(2)}, u32[]{:S(2)}) collective-permute-start(bf16[4,128,128]{2,1,0:T(8,128)(2,1)S(1)} %collective-permute-done.1.refs_0_), channel_id=1, source_target_pairs={{0,64},{32,96},{64,0},{96,32},{1,65},{33,97},{65,1},{97,33},{2,66}... | collective-permute-start | bytes 393224 | tf_op jit(solution)/shard_map/ppermute | solution.py:137
  168.2 28.9 %collective-permute-start.5 = (bf16[4,128,128]{2,1,0:T(8,128)(2,1)}, bf16[4,128,128]{2,1,0:T(8,128)(2,1)S(1)}, u32[]{:S(2)}, u32[]{:S(2)}) collective-permute-start(bf16[4,128,128]{2,1,0:T(8,128)(2,1)} %copy-done.18), channel_id=1, source_target_pairs={{0,96},{32,0},{64,32},{96,64},{1,97},{33,1},{65,33},{97,65},{2,98}... | collective-permute-start | bytes 393224 | tf_op jit(solution)/shard_map/ppermute | solution.py:137
  171.3 25.9 %collective-permute-start.7 = (bf16[4,128,128]{2,1,0:T(8,128)(2,1)}, bf16[4,128,128]{2,1,0:T(8,128)(2,1)S(1)}, u32[]{:S(2)}, u32[]{:S(2)}) collective-permute-start(bf16[4,128,128]{2,1,0:T(8,128)(2,1)} %copy-done.18), channel_id=1, source_target_pairs={{0,64},{32,96},{64,0},{96,32},{1,65},{33,97},{65,1},{97,33},{2,66}... | collective-permute-start | bytes 393224 | tf_op jit(solution)/shard_map/ppermute | solution.py:137
  174.1 23.1 %collective-permute-start.8 = (bf16[4,128,128]{2,1,0:T(8,128)(2,1)S(1)}, bf16[4,128,128]{2,1,0:T(8,128)(2,1)S(1)}, u32[]{:S(2)}, u32[]{:S(2)}) collective-permute-start(bf16[4,128,128]{2,1,0:T(8,128)(2,1)S(1)} %collective-permute-done.1.refs_0_), channel_id=1, source_target_pairs={{0,32},{32,64},{64,96},{96,0},{1,33},{33,65},{65,97},{97,1},{2,34}... | collective-permute-start | bytes 393224 | tf_op jit(solution)/shard_map/ppermute | solution.py:137
  176.9 20.3 %collective-permute-start.9 = (bf16[4,128,128]{2,1,0:T(8,128)(2,1)}, bf16[4,128,128]{2,1,0:T(8,128)(2,1)S(1)}, u32[]{:S(2)}, u32[]{:S(2)}) collective-permute-start(bf16[4,128,128]{2,1,0:T(8,128)(2,1)} %copy-done.18), channel_id=1, source_target_pairs={{0,32},{32,64},{64,96},{96,0},{1,33},{33,65},{65,97},{97,1},{2,34}... | collective-permute-start | bytes 393224 | tf_op jit(solution)/shard_map/ppermute | solution.py:137
  179.7 1.0 copy-start.1
  180.6 0.9 copy-start.3
  181.6 0.9 copy-start.5
  182.5 0.9 copy-start.7
  183.5 0.9 copy-start.9
  184.4 0.9 copy-start.11
  185.4 0.9 copy-start.13
  186.3 0.9 copy-start.15
  187.3 0.9 copy-start.17
  188.2 0.7 copy-start.20
  188.9 8.3 %copy-start.19 = (bf16[4,128,128]{2,1,0:T(8,128)(2,1)S(1)}, bf16[4,128,128]{2,1,0:T(8,128)(2,1)}, u32[]{:S(2)}) copy-start(bf16[4,128,128]{2,1,0:T(8,128)(2,1)} %copy-done.18) | copy-start | bytes 393220
  204.4 28.2 %collective-permute-start.33 = (f32[8,128,128]{2,1,0:T(8,128)S(1)}, f32[8,128,128]{2,1,0:T(8,128)S(1)}, u32[]{:S(2)}, u32[]{:S(2)}) collective-permute-start(f32[8,128,128]{2,1,0:T(8,128)S(1)} %get-tuple-element.8), channel_id=1, source_target_pairs={{0,1},{1,0},{2,3},{3,2},{4,5},{5,4},{6,7},{7,6},{8,9},{9,8},{10,11... | collective-permute-start | bytes 1572872 | tf_op jit(solution)/shard_map/ppermute | solution.py:170
  232.7 9.5 %collective-permute-start.34 = (f32[2,128,128]{2,1,0:T(8,128)S(1)}, f32[2,128,128]{2,1,0:T(8,128)S(1)}, u32[]{:S(2)}, u32[]{:S(2)}) collective-permute-start(f32[2,128,128]{2,1,0:T(8,128)S(1)} %get-tuple-element.9), channel_id=1, source_target_pairs={{0,2},{2,4},{4,6},{6,0},{1,3},{3,5},{5,7},{7,1},{8,10},{10,12},{12... | collective-permute-start | bytes 393224 | tf_op jit(solution)/shard_map/ppermute | solution.py:175
  234.9 7.9 %collective-permute-start.35 = (f32[2,128,128]{2,1,0:T(8,128)S(1)}, f32[2,128,128]{2,1,0:T(8,128)S(1)}, u32[]{:S(2)}, u32[]{:S(2)}) collective-permute-start(f32[2,128,128]{2,1,0:T(8,128)S(1)} %get-tuple-element.11), channel_id=1, source_target_pairs={{0,4},{2,6},{4,0},{6,2},{1,5},{3,7},{5,1},{7,3},{8,12},{10,14},{12... | collective-permute-start | bytes 393224 | tf_op jit(solution)/shard_map/ppermute | solution.py:175
  238.6 7.2 %collective-permute-start.36 = (f32[2,128,128]{2,1,0:T(8,128)S(1)}, f32[2,128,128]{2,1,0:T(8,128)S(1)}, u32[]{:S(2)}, u32[]{:S(2)}) collective-permute-start(f32[2,128,128]{2,1,0:T(8,128)S(1)} %get-tuple-element.10), channel_id=1, source_target_pairs={{0,6},{2,0},{4,2},{6,4},{1,7},{3,1},{5,3},{7,5},{8,14},{10,8},{12,... | collective-permute-start | bytes 393224 | tf_op jit(solution)/shard_map/ppermute | solution.py:175

commit v2 on v0

v2 whole, which is shorter than its diff:
```python
import functools

import jax
import jax.numpy as jnp
from jax import lax
from jax.experimental import pallas as pl
from jax.experimental.pallas import tpu as pltpu
from jax.sharding import Mesh
from jax.sharding import PartitionSpec as P

X, ZH, Y, CORE, ROW = 4, 4, 4, 2, 8
S, SLOTS, R, BS = 8, 2, 16, 128
COLS = X * ZH
PER = R // (Y * CORE)


def ring(n, k):
    return [(i, (i + k) % n) for i in range(n)]


def products(groups, unroll, place, left, right, *refs):
    n = 1 + max(g[0] for g in groups)
    a, b, refs = refs[:n], refs[n], refs[n + 1 :]
    first = len(refs) == 1
    x, zh, core, y = (place[k] for k in range(4))

    def one(r):
        total = None if first else refs[0][r]
        for array, start, dx, dz in groups:
            c = lax.rem(x + dx, X) * ZH + lax.rem(zh + dz, ZH)
            lefts, rights = [], []
            for p in range(SLOTS):
                m = left[r, c * SLOTS + p]
                tile = a[array][start + jnp.minimum(m, S - 1)]
                lefts.append(jnp.where(m < S, tile, jnp.zeros_like(tile)))
                rights.append(b[jnp.minimum(right[r, c * SLOTS + p], ROW * S - 1)])
            value = jnp.dot(
                jnp.concatenate(lefts, axis=1),
                jnp.concatenate(rights, axis=0),
                preferred_element_type=jnp.float32,
            )
            total = value if total is None else total + value
        return total

    if first:

        @pl.loop(0, R, unroll=unroll)
        def _(r):
            refs[0][r] = one(r)
    else:
        _, keep, send = refs
        for target, other in ((send, 1), (keep, 0)):

            @pl.loop(0, Y * PER, unroll=unroll)
            def _(k, target=target, other=other):
                to = lax.rem(y + k // PER, Y)
                mine = lax.rem(core + other, CORE)
                target[k] = one((to * CORE + mine) * PER + lax.rem(k, PER))


def call(groups, unroll, lists, arrays, b, *before):
    smem = pl.BlockSpec(memory_space=pltpu.SMEM)
    vmem = pl.BlockSpec(memory_space=pltpu.VMEM)
    operands = [*lists, *arrays, b, *before]
    half = jax.ShapeDtypeStruct((R // 2, BS, BS), jnp.float32)
    return pl.pallas_call(
        functools.partial(products, groups, unroll),
        out_shape=(half, half) if before else jax.ShapeDtypeStruct((R, BS, BS), jnp.float32),
        in_specs=[smem] * len(lists) + [vmem] * (len(operands) - len(lists)),
        out_specs=(vmem, vmem) if before else vmem,
        compiler_params=pltpu.CompilerParams(vmem_limit_bytes=24 * 1024 * 1024),
        cost_estimate=pl.CostEstimate(
            flops=R * len(groups) * SLOTS * 2 * BS**3, bytes_accessed=4 * 1024 * 1024, transcendentals=0
        ),
    )(*operands)


def on_device(tiles, pair_a, pair_b):
    own = tiles.reshape(S, BS, BS)
    left = pair_a.reshape(R, COLS * SLOTS)
    right = pair_b.reshape(R, COLS * SLOTS)
    place = jnp.stack([lax.axis_index(n) for n in ("x", "zh", "core", "y")]).astype(jnp.int32)
    lists = (place, left, right)

    def over_x(value):
        return [value] + [lax.ppermute(value, "x", ring(X, -d)) for d in range(1, X)]

    z1 = lax.ppermute(own, "zh", ring(ZH, -1))
    z3 = lax.ppermute(own, "zh", ring(ZH, 1))

    routed = lax.all_to_all(own, ("y", "core"), split_axis=0, concat_axis=0, tiled=True)
    b = lax.all_gather(routed, "row", axis=0, tiled=True)

    half = S // 2
    z2_low = lax.ppermute(z1[:half], "zh", ring(ZH, -1))
    z2_high = lax.ppermute(z3[half:], "zh", ring(ZH, 1))
    early = over_x(jnp.concatenate([own, z1, z3]))
    late = over_x(jnp.concatenate([z2_low, z2_high]))

    early_groups = [(d, k * S, d, z) for k, z in enumerate((0, 1, 3)) for d in range(X)]
    late_groups = [(d, 0, d, 2) for d in range(X)]
    acc = call(early_groups, 4, lists, early, b)
    keep, send = call(late_groups, 8, lists, late, b, acc)

    got = lax.ppermute(send, "core", ring(CORE, 1))
    quarter = [keep[d * PER : (d + 1) * PER] + got[d * PER : (d + 1) * PER] for d in range(Y)]
    total = quarter[0]
    for d in range(1, Y):
        total = total + lax.ppermute(quarter[d], "y", ring(Y, d))
    return total[None, None]


def solution(mesh):
    fine = Mesh(mesh.devices.reshape(ROW, X, ZH, Y, CORE), ("row", "x", "zh", "y", "core"))
    spec = ("row", ("x", "zh"), ("y", "core"))
    return jax.shard_map(
        on_device,
        mesh=fine,
        in_specs=(P(*spec), P(*spec), P(*spec)),
        out_specs=P(*spec),
        check_vma=False,
    )
```

time: 509 us -> 206 us (0.40)
  the two profiles are of different devices: /device:TPU:1 before, /device:TPU:32 now
where the time goes in v2:
time: 206 us; the launch traced here: 205 us
  waiting for transfers between devices  92.8 us (45%)
  starting transfers between devices  73.3 us (36%)
  between operations  13.6 us (7%)
  blocking collectives  12.2 us (6%)
  Pallas kernels  7.94 us (4%)
  local copies, waits for them, and re-layouts  3.51 us (2%)
    ppermute x1, waiting for transfers between devices, on_device(): z1 = lax.ppermute(own, 'zh', ring(ZH, -1))  54.5 us
    ppermute x6, starting transfers between devices, over_x(): lax.ppermute(value, 'x', ring(X, -d))  23 us
    ppermute x1, starting transfers between devices, on_device(): z1 = lax.ppermute(own, 'zh', ring(ZH, -1))  22.1 us
    ppermute x1, waiting for transfers between devices, on_device(): z2_low = lax.ppermute(z1[:half], 'zh', ring(ZH, -1))  15.2 us
    all_to_all x1, blocking collectives, on_device(): lax.all_to_all(own, ('y', 'core'), split_axis=0, concat_axis=0, tiled=True)  12.2 us
    ppermute x3, starting transfers between devices, on_device(): total = total + lax.ppermute(quarter[d], 'y', ring(Y, d))  9.79 us
    ppermute x1, waiting for transfers between devices, on_device(): z3 = lax.ppermute(own, 'zh', ring(ZH, 1))  9.52 us
    ppermute x1, starting transfers between devices, on_device(): z2_high = lax.ppermute(z3[half:], 'zh', ring(ZH, 1))  8.16 us
  transfers between devices with their start and end apart: 15, of which 8 were waited for; matrix products, arithmetic and copies ran while one was open for 1% of the time, Pallas kernels for 3%

profile of v2, /device:TPU:32, one launch (start us, length us, event | category | flops | bytes accessed | tf_op | source)
XLA Modules:
  0.0 205.2 jit_solution(5936052971780238268)
XLA Ops:
  6.5 0.0 copy-start.2
  6.5 0.0 copy-start.3
  6.5 0.0 all-gather.2.cloned.1.call-start
  6.5 12.2 %all_to_all.5 = bf16[8,128,128]{2,1,0:T(8,128)(2,1)} all-to-all(bf16[8,128,128]{2,1,0:T(8,128)(2,1)} %bitcast.9), channel_id=1, replica_groups=mesh['row'=8,'x'=4,'zh'=4,'y'=4,'core'=2] {'y','core'}, dimensions={0} | all-to-all | bytes 524288 | tf_op jit(solution)/shard_map/all_to_all | solution.py:91
  18.8 0.0 all-gather.2.cloned.1.call-update
  18.8 22.1 %collective-permute-start = (bf16[8,128,128]{2,1,0:T(8,128)(2,1)}, bf16[8,128,128]{2,1,0:T(8,128)(2,1)S(1)}, u32[]{:S(2)}, u32[]{:S(2)}) collective-permute-start(bf16[8,128,128]{2,1,0:T(8,128)(2,1)} %bitcast.10), channel_id=1, source_target_pairs={{0,24},{8,0},{16,8},{24,16},{1,25},{9,1},{17,9},{25,17},{2,26},{10... | collective-permute-start | bytes 786440 | tf_op jit(solution)/shard_map/ppermute | solution.py:88
  40.9 1.9 collective-permute-start.2
  42.8 54.5 %collective-permute-done = bf16[8,128,128]{2,1,0:T(8,128)(2,1)S(1)} collective-permute-done((bf16[8,128,128]{2,1,0:T(8,128)(2,1)}, bf16[8,128,128]{2,1,0:T(8,128)(2,1)S(1)}, u32[]{:S(2)}, u32[]{:S(2)}) %collective-permute-start) | collective-permute-done | bytes 262176 | tf_op jit(solution)/shard_map/ppermute | solution.py:88
  97.3 9.5 %collective-permute-done.2 = bf16[8,128,128]{2,1,0:T(8,128)(2,1)S(1)} collective-permute-done((bf16[8,128,128]{2,1,0:T(8,128)(2,1)}, bf16[8,128,128]{2,1,0:T(8,128)(2,1)S(1)}, u32[]{:S(2)}, u32[]{:S(2)}) %collective-permute-start.2) | collective-permute-done | bytes 262176 | tf_op jit(solution)/shard_map/ppermute | solution.py:89
  106.8 1.0 pad_maximum_fusion.refs_0_
  107.9 6.9 %collective-permute-start.7 = (bf16[24,128,128]{2,1,0:T(8,128)(2,1)S(1)}, bf16[24,128,128]{2,1,0:T(8,128)(2,1)S(1)}, u32[]{:S(2)}, u32[]{:S(2)}) collective-permute-start(bf16[24,128,128]{2,1,0:T(8,128)(2,1)S(1)} %pad_maximum_fusion.refs_0_), channel_id=1, source_target_pairs={{0,96},{32,0},{64,32},{96,64},{1,97},{33,1},{65,33},{97,65},{2,98}... | collective-permute-start | bytes 2359304 | tf_op jit(solution)/shard_map/ppermute | solution.py:86
  114.8 2.7 %collective-permute-start.8 = (bf16[24,128,128]{2,1,0:T(8,128)(2,1)S(1)}, bf16[24,128,128]{2,1,0:T(8,128)(2,1)S(1)}, u32[]{:S(2)}, u32[]{:S(2)}) collective-permute-start(bf16[24,128,128]{2,1,0:T(8,128)(2,1)S(1)} %pad_maximum_fusion.refs_0_), channel_id=1, source_target_pairs={{0,64},{32,96},{64,0},{96,32},{1,65},{33,97},{65,1},{97,33},{2,66}... | collective-permute-start | bytes 2359304 | tf_op jit(solution)/shard_map/ppermute | solution.py:86
  117.5 2.8 %collective-permute-start.9 = (bf16[24,128,128]{2,1,0:T(8,128)(2,1)S(1)}, bf16[24,128,128]{2,1,0:T(8,128)(2,1)S(1)}, u32[]{:S(2)}, u32[]{:S(2)}) collective-permute-start(bf16[24,128,128]{2,1,0:T(8,128)(2,1)S(1)} %pad_maximum_fusion.refs_0_), channel_id=1, source_target_pairs={{0,32},{32,64},{64,96},{96,0},{1,33},{33,65},{65,97},{97,1},{2,34}... | collective-permute-start | bytes 2359304 | tf_op jit(solution)/shard_map/ppermute | solution.py:86
  120.3 6.4 %collective-permute-start.1 = (bf16[4,128,128]{2,1,0:T(8,128)(2,1)S(1)}, bf16[4,128,128]{2,1,0:T(8,128)(2,1)S(1)}, u32[]{:S(2)}, u32[]{:S(2)}) collective-permute-start(bf16[4,128,128]{2,1,0:T(8,128)(2,1)S(1)} %slice.40), channel_id=1, source_target_pairs={{0,24},{8,0},{16,8},{24,16},{1,25},{9,1},{17,9},{25,17},{2,26},{10... | collective-permute-start | bytes 393224 | tf_op jit(solution)/shard_map/ppermute | solution.py:95
  126.7 0.7 slice.41
  127.4 8.2 %collective-permute-start.3 = (bf16[4,128,128]{2,1,0:T(8,128)(2,1)}, bf16[4,128,128]{2,1,0:T(8,128)(2,1)}, u32[]{:S(2)}, u32[]{:S(2)}) collective-permute-start(bf16[4,128,128]{2,1,0:T(8,128)(2,1)} %slice.41), channel_id=1, source_target_pairs={{0,8},{8,16},{16,24},{24,0},{1,9},{9,17},{17,25},{25,1},{2,10},{10... | collective-permute-start | bytes 393224 | tf_op jit(solution)/shard_map/ppermute | solution.py:96
  135.6 0.0 copy-done.2
  135.6 0.1 copy.12
  135.7 0.1 copy.16.left
  135.7 0.0 copy-done.3
  135.7 0.1 copy.13
  135.8 0.1 copy.17.right
  135.9 15.2 %collective-permute-done.1 = bf16[4,128,128]{2,1,0:T(8,128)(2,1)S(1)} collective-permute-done((bf16[4,128,128]{2,1,0:T(8,128)(2,1)S(1)}, bf16[4,128,128]{2,1,0:T(8,128)(2,1)S(1)}, u32[]{:S(2)}, u32[]{:S(2)}) %collective-permute-start.1) | collective-permute-done | bytes 131104 | tf_op jit(solution)/shard_map/ppermute | solution.py:95
  151.1 6.7 %collective-permute-done.3 = bf16[4,128,128]{2,1,0:T(8,128)(2,1)} collective-permute-done((bf16[4,128,128]{2,1,0:T(8,128)(2,1)}, bf16[4,128,128]{2,1,0:T(8,128)(2,1)}, u32[]{:S(2)}, u32[]{:S(2)}) %collective-permute-start.3) | collective-permute-done | bytes 131104 | tf_op jit(solution)/shard_map/ppermute | solution.py:96
  157.8 0.9 constant_dynamic-update-slice_fusion.refs_0_
  158.8 4.7 %collective-permute-start.4 = (bf16[8,128,128]{2,1,0:T(8,128)(2,1)S(1)}, bf16[8,128,128]{2,1,0:T(8,128)(2,1)}, u32[]{:S(2)}, u32[]{:S(2)}) collective-permute-start(bf16[8,128,128]{2,1,0:T(8,128)(2,1)S(1)} %constant_dynamic-update-slice_fusion.refs_0_), channel_id=1, source_target_pairs={{0,96},{32,0},{64,32},{96,64},{1,97},{33,1},{65,33},{97,65},{2,98}... | collective-permute-start | bytes 786440 | tf_op jit(solution)/shard_map/ppermute | solution.py:86
  163.4 3.0 %collective-permute-start.5 = (bf16[8,128,128]{2,1,0:T(8,128)(2,1)S(1)}, bf16[8,128,128]{2,1,0:T(8,128)(2,1)}, u32[]{:S(2)}, u32[]{:S(2)}) collective-permute-start(bf16[8,128,128]{2,1,0:T(8,128)(2,1)S(1)} %constant_dynamic-update-slice_fusion.refs_0_), channel_id=1, source_target_pairs={{0,64},{32,96},{64,0},{96,32},{1,65},{33,97},{65,1},{97,33},{2,66}... | collective-permute-start | bytes 786440 | tf_op jit(solution)/shard_map/ppermute | solution.py:86
  166.4 0.0 collective-permute-done.7.refs_1_
  166.4 2.9 %collective-permute-start.6 = (bf16[8,128,128]{2,1,0:T(8,128)(2,1)S(1)}, bf16[8,128,128]{2,1,0:T(8,128)(2,1)}, u32[]{:S(2)}, u32[]{:S(2)}) collective-permute-start(bf16[8,128,128]{2,1,0:T(8,128)(2,1)S(1)} %constant_dynamic-update-slice_fusion.refs_0_), channel_id=1, source_target_pairs={{0,32},{32,64},{64,96},{96,0},{1,33},{33,65},{65,97},{97,1},{2,34}... | collective-permute-start | bytes 786440 | tf_op jit(solution)/shard_map/ppermute | solution.py:86
  169.3 0.1 pad_add_fusion.place
  169.4 0.0 collective-permute-done.8.refs_2_
  169.4 0.0 collective-permute-done.9.refs_3_
  169.4 0.0 all-gather.2.cloned.1.call-done.refs_4_
  169.5 0.0 copy-start
  169.5 1.6 copy-done
  171.0 0.0 copy-start.1
  171.0 5.3 %shard_map.37.refs_5_ = f32[16,128,128]{2,1,0:T(8,128)S(1)} custom-call(s32[4]{0:T(128)S(1)} %pad_add_fusion.place, s32[16,32]{1,0:T(8,128)S(1)} %copy.16.left, s32[16,32]{1,0:T(8,128)S(1)} %copy.17.right, bf16[24,128,128]{2,1,0:T(8,128)(2,1)S(1)} %pad_maximum_fusion.refs_0_, bf16[24,128,128]{2,1,0:T(8,128)(2,1)S(1)} %collective-permute-done.7.refs_1_, ...), custom_call_target="tpu_custom_call" | custom-call | flops 1610612736 | bytes 4194304 | tf_op jit(solution)/shard_map/pallas_call | solution.py:66
  176.4 0.0 collective-permute-done.4.refs_1_
  176.4 0.0 collective-permute-done.5.refs_2_
  176.4 0.8 collective-permute-done.6.refs_3_
  177.2 0.0 copy-done.1
  177.2 2.6 %shard_map.38 = (f32[8,128,128]{2,1,0:T(8,128)S(1)}, f32[8,128,128]{2,1,0:T(8,128)S(1)}) custom-call(s32[4]{0:T(128)S(1)} %pad_add_fusion.place, s32[16,32]{1,0:T(8,128)S(1)} %copy.16.left, s32[16,32]{1,0:T(8,128)S(1)} %copy.17.right, bf16[8,128,128]{2,1,0:T(8,128)(2,1)S(1)} %constant_dynamic-update-slice_fusion.refs_0_, ...), custom_call_target="tpu_custom_call" | custom-call | flops 536870912 | bytes 4194304 | tf_op jit(solution)/shard_map/pallas_call | solution.py:66
  179.9 1.9 collective-permute-start.10
  181.8 1.9 collective-permute-done.10
  183.7 3.3 %collective-permute-start.11 = (f32[2,128,128]{2,1,0:T(8,128)S(1)}, f32[2,128,128]{2,1,0:T(8,128)S(1)}, u32[]{:S(2)}, u32[]{:S(2)}) collective-permute-start(f32[2,128,128]{2,1,0:T(8,128)S(1)} %get-tuple-element.9), channel_id=1, source_target_pairs={{0,2},{2,4},{4,6},{6,0},{1,3},{3,5},{5,7},{7,1},{8,10},{10,12},{12... | collective-permute-start | bytes 393224 | tf_op jit(solution)/shard_map/ppermute | solution.py:109
  187.0 3.0 %collective-permute-start.12 = (f32[2,128,128]{2,1,0:T(8,128)S(1)}, f32[2,128,128]{2,1,0:T(8,128)S(1)}, u32[]{:S(2)}, u32[]{:S(2)}) collective-permute-start(f32[2,128,128]{2,1,0:T(8,128)S(1)} %get-tuple-element.11), channel_id=1, source_target_pairs={{0,4},{2,6},{4,0},{6,2},{1,5},{3,7},{5,1},{7,3},{8,12},{10,14},{12... | collective-permute-start | bytes 393224 | tf_op jit(solution)/shard_map/ppermute | solution.py:109
  190.0 3.6 %collective-permute-start.13 = (f32[2,128,128]{2,1,0:T(8,128)S(1)}, f32[2,128,128]{2,1,0:T(8,128)S(1)}, u32[]{:S(2)}, u32[]{:S(2)}) collective-permute-start(f32[2,128,128]{2,1,0:T(8,128)S(1)} %get-tuple-element.10), channel_id=1, source_target_pairs={{0,6},{2,0},{4,2},{6,4},{1,7},{3,1},{5,3},{7,5},{8,14},{10,8},{12,... | collective-permute-start | bytes 393224 | tf_op jit(solution)/shard_map/ppermute | solution.py:109
  193.5 0.0 collective-permute-done.11
  193.5 2.1 %collective-permute-done.12 = f32[2,128,128]{2,1,0:T(8,128)S(1)} collective-permute-done((f32[2,128,128]{2,1,0:T(8,128)S(1)}, f32[2,128,128]{2,1,0:T(8,128)S(1)}, u32[]{:S(2)}, u32[]{:S(2)}) %collective-permute-start.12) | collective-permute-done | bytes 131104 | tf_op jit(solution)/shard_map/ppermute | solution.py:109
  195.7 2.0 collective-permute-done.13
  197.7 0.7 fusion.3
  (3 shorter events, 0.1 us)
Async XLA Ops:
  6.5 129.0 %copy-start.2 = (s32[1,1,1,16,16,2]{4,5,3,2,1,0:T(2,128)S(1)}, s32[1,1,1,16,16,2]{4,5,3,2,1,0:T(2,128)}, u32[]{:S(2)}) copy-start(s32[1,1,1,16,16,2]{4,5,3,2,1,0:T(2,128)} %param.4) | copy-start | bytes 6148
  6.5 129.2 %copy-start.3 = (s32[1,1,1,16,16,2]{4,5,3,2,1,0:T(2,128)S(1)}, s32[1,1,1,16,16,2]{4,5,3,2,1,0:T(2,128)}, u32[]{:S(2)}) copy-start(s32[1,1,1,16,16,2]{4,5,3,2,1,0:T(2,128)} %param.5) | copy-start | bytes 6148
  6.5 162.9 %all-gather.2.cloned.1.call-start = ((), (), s32[]{:S(2)}) async-start(), calls=%async_computation.1 | async-start | bytes 2359296 | tf_op jit(solution)/shard_map/all_gather | solution.py:92
  18.8 78.5 %collective-permute-start = (bf16[8,128,128]{2,1,0:T(8,128)(2,1)}, bf16[8,128,128]{2,1,0:T(8,128)(2,1)S(1)}, u32[]{:S(2)}, u32[]{:S(2)}) collective-permute-start(bf16[8,128,128]{2,1,0:T(8,128)(2,1)} %bitcast.10), channel_id=1, source_target_pairs={{0,24},{8,0},{16,8},{24,16},{1,25},{9,1},{17,9},{25,17},{2,26},{10... | collective-permute-start | bytes 786440 | tf_op jit(solution)/shard_map/ppermute | solution.py:88
  40.9 65.9 %collective-permute-start.2 = (bf16[8,128,128]{2,1,0:T(8,128)(2,1)}, bf16[8,128,128]{2,1,0:T(8,128)(2,1)S(1)}, u32[]{:S(2)}, u32[]{:S(2)}) collective-permute-start(bf16[8,128,128]{2,1,0:T(8,128)(2,1)} %bitcast.11), channel_id=1, source_target_pairs={{0,8},{8,16},{16,24},{24,0},{1,9},{9,17},{17,25},{25,1},{2,10},{10... | collective-permute-start | bytes 786440 | tf_op jit(solution)/shard_map/ppermute | solution.py:89
  107.9 58.5 %collective-permute-start.7 = (bf16[24,128,128]{2,1,0:T(8,128)(2,1)S(1)}, bf16[24,128,128]{2,1,0:T(8,128)(2,1)S(1)}, u32[]{:S(2)}, u32[]{:S(2)}) collective-permute-start(bf16[24,128,128]{2,1,0:T(8,128)(2,1)S(1)} %pad_maximum_fusion.refs_0_), channel_id=1, source_target_pairs={{0,96},{32,0},{64,32},{96,64},{1,97},{33,1},{65,33},{97,65},{2,98}... | collective-permute-start | bytes 2359304 | tf_op jit(solution)/shard_map/ppermute | solution.py:86
  114.8 54.6 %collective-permute-start.8 = (bf16[24,128,128]{2,1,0:T(8,128)(2,1)S(1)}, bf16[24,128,128]{2,1,0:T(8,128)(2,1)S(1)}, u32[]{:S(2)}, u32[]{:S(2)}) collective-permute-start(bf16[24,128,128]{2,1,0:T(8,128)(2,1)S(1)} %pad_maximum_fusion.refs_0_), channel_id=1, source_target_pairs={{0,64},{32,96},{64,0},{96,32},{1,65},{33,97},{65,1},{97,33},{2,66}... | collective-permute-start | bytes 2359304 | tf_op jit(solution)/shard_map/ppermute | solution.py:86
  117.5 51.9 %collective-permute-start.9 = (bf16[24,128,128]{2,1,0:T(8,128)(2,1)S(1)}, bf16[24,128,128]{2,1,0:T(8,128)(2,1)S(1)}, u32[]{:S(2)}, u32[]{:S(2)}) collective-permute-start(bf16[24,128,128]{2,1,0:T(8,128)(2,1)S(1)} %pad_maximum_fusion.refs_0_), channel_id=1, source_target_pairs={{0,32},{32,64},{64,96},{96,0},{1,33},{33,65},{65,97},{97,1},{2,34}... | collective-permute-start | bytes 2359304 | tf_op jit(solution)/shard_map/ppermute | solution.py:86
  120.3 30.8 %collective-permute-start.1 = (bf16[4,128,128]{2,1,0:T(8,128)(2,1)S(1)}, bf16[4,128,128]{2,1,0:T(8,128)(2,1)S(1)}, u32[]{:S(2)}, u32[]{:S(2)}) collective-permute-start(bf16[4,128,128]{2,1,0:T(8,128)(2,1)S(1)} %slice.40), channel_id=1, source_target_pairs={{0,24},{8,0},{16,8},{24,16},{1,25},{9,1},{17,9},{25,17},{2,26},{10... | collective-permute-start | bytes 393224 | tf_op jit(solution)/shard_map/ppermute | solution.py:95
  127.4 30.4 %collective-permute-start.3 = (bf16[4,128,128]{2,1,0:T(8,128)(2,1)}, bf16[4,128,128]{2,1,0:T(8,128)(2,1)}, u32[]{:S(2)}, u32[]{:S(2)}) collective-permute-start(bf16[4,128,128]{2,1,0:T(8,128)(2,1)} %slice.41), channel_id=1, source_target_pairs={{0,8},{8,16},{16,24},{24,0},{1,9},{9,17},{17,25},{25,1},{2,10},{10... | collective-permute-start | bytes 393224 | tf_op jit(solution)/shard_map/ppermute | solution.py:96
  158.8 17.6 %collective-permute-start.4 = (bf16[8,128,128]{2,1,0:T(8,128)(2,1)S(1)}, bf16[8,128,128]{2,1,0:T(8,128)(2,1)}, u32[]{:S(2)}, u32[]{:S(2)}) collective-permute-start(bf16[8,128,128]{2,1,0:T(8,128)(2,1)S(1)} %constant_dynamic-update-slice_fusion.refs_0_), channel_id=1, source_target_pairs={{0,96},{32,0},{64,32},{96,64},{1,97},{33,1},{65,33},{97,65},{2,98}... | collective-permute-start | bytes 786440 | tf_op jit(solution)/shard_map/ppermute | solution.py:86
  163.4 13.0 %collective-permute-start.5 = (bf16[8,128,128]{2,1,0:T(8,128)(2,1)S(1)}, bf16[8,128,128]{2,1,0:T(8,128)(2,1)}, u32[]{:S(2)}, u32[]{:S(2)}) collective-permute-start(bf16[8,128,128]{2,1,0:T(8,128)(2,1)S(1)} %constant_dynamic-update-slice_fusion.refs_0_), channel_id=1, source_target_pairs={{0,64},{32,96},{64,0},{96,32},{1,65},{33,97},{65,1},{97,33},{2,66}... | collective-permute-start | bytes 786440 | tf_op jit(solution)/shard_map/ppermute | solution.py:86
  166.4 10.8 %collective-permute-start.6 = (bf16[8,128,128]{2,1,0:T(8,128)(2,1)S(1)}, bf16[8,128,128]{2,1,0:T(8,128)(2,1)}, u32[]{:S(2)}, u32[]{:S(2)}) collective-permute-start(bf16[8,128,128]{2,1,0:T(8,128)(2,1)S(1)} %constant_dynamic-update-slice_fusion.refs_0_), channel_id=1, source_target_pairs={{0,32},{32,64},{64,96},{96,0},{1,33},{33,65},{65,97},{97,1},{2,34}... | collective-permute-start | bytes 786440 | tf_op jit(solution)/shard_map/ppermute | solution.py:86
  169.5 1.6 copy-start
  171.0 6.2 %copy-start.1 = (bf16[64,128,128]{2,1,0:T(8,128)(2,1)S(1)}, bf16[64,128,128]{2,1,0:T(8,128)(2,1)}, u32[]{:S(2)}) copy-start(bf16[64,128,128]{2,1,0:T(8,128)(2,1)} %all-gather.2.cloned.1.call-done.refs_4_) | copy-start | bytes 6291460
  179.9 3.8 %collective-permute-start.10 = (f32[8,128,128]{2,1,0:T(8,128)S(1)}, f32[8,128,128]{2,1,0:T(8,128)S(1)}, u32[]{:S(2)}, u32[]{:S(2)}) collective-permute-start(f32[8,128,128]{2,1,0:T(8,128)S(1)} %get-tuple-element.8), channel_id=1, source_target_pairs={{0,1},{1,0},{2,3},{3,2},{4,5},{5,4},{6,7},{7,6},{8,9},{9,8},{10,11... | collective-permute-start | bytes 1572872 | tf_op jit(solution)/shard_map/ppermute | solution.py:105
  183.7 9.8 %collective-permute-start.11 = (f32[2,128,128]{2,1,0:T(8,128)S(1)}, f32[2,128,128]{2,1,0:T(8,128)S(1)}, u32[]{:S(2)}, u32[]{:S(2)}) collective-permute-start(f32[2,128,128]{2,1,0:T(8,128)S(1)} %get-tuple-element.9), channel_id=1, source_target_pairs={{0,2},{2,4},{4,6},{6,0},{1,3},{3,5},{5,7},{7,1},{8,10},{10,12},{12... | collective-permute-start | bytes 393224 | tf_op jit(solution)/shard_map/ppermute | solution.py:109
  187.0 8.7 %collective-permute-start.12 = (f32[2,128,128]{2,1,0:T(8,128)S(1)}, f32[2,128,128]{2,1,0:T(8,128)S(1)}, u32[]{:S(2)}, u32[]{:S(2)}) collective-permute-start(f32[2,128,128]{2,1,0:T(8,128)S(1)} %get-tuple-element.11), channel_id=1, source_target_pairs={{0,4},{2,6},{4,0},{6,2},{1,5},{3,7},{5,1},{7,3},{8,12},{10,14},{12... | collective-permute-start | bytes 393224 | tf_op jit(solution)/shard_map/ppermute | solution.py:109
  190.0 7.7 %collective-permute-start.13 = (f32[2,128,128]{2,1,0:T(8,128)S(1)}, f32[2,128,128]{2,1,0:T(8,128)S(1)}, u32[]{:S(2)}, u32[]{:S(2)}) collective-permute-start(f32[2,128,128]{2,1,0:T(8,128)S(1)} %get-tuple-element.10), channel_id=1, source_target_pairs={{0,6},{2,0},{4,2},{6,4},{1,7},{3,1},{5,3},{7,5},{8,14},{10,8},{12,... | collective-permute-start | bytes 393224 | tf_op jit(solution)/shard_map/ppermute | solution.py:109
Sparse Core Ops, SparseCore 0:
  18.9 132.2 all-gather.1

commit v3 on v2

v3 whole, which is shorter than its diff:
```python
import functools

import jax
import jax.numpy as jnp
from jax import lax
from jax.experimental import pallas as pl
from jax.experimental.pallas import tpu as pltpu
from jax.sharding import Mesh
from jax.sharding import PartitionSpec as P

X, ZH, Y, CORE, ROW = 4, 4, 4, 2, 8
S, SLOTS, R, BS = 8, 2, 16, 128
COLS = X * ZH
PER = R // (Y * CORE)
QUAD = ROW // 2


def ring(n, k):
    return [(i, (i + k) % n) for i in range(n)]


def products(groups, other, place, left, right, *refs):
    n = 1 + max(g[0] for g in groups)
    a, refs = refs[:n], refs[n:]
    x, zh, core, y, row = (place[k] for k in range(5))
    if other:
        own, right_way, left_way = refs[0], refs[1:QUAD], refs[QUAD : 2 * QUAD - 1]
        out, b, sems = refs[2 * QUAD - 1 :]
        at = lax.rem(row, QUAD)

        def copy(source, s):
            slot = lax.rem(at - s + QUAD, QUAD)
            return pltpu.make_async_copy(source, b.at[pl.ds(slot * 2 * S, 2 * S)], sems.at[s])

        copy(own, 0).start()
        for s in range(1, QUAD):

            @pl.when(at >= s)
            def _(s=s):
                copy(right_way[s - 1], s).start()

            @pl.when(at < s)
            def _(s=s):
                copy(left_way[QUAD - s - 1], s).start()

        for s in range(QUAD):
            copy(own, s).wait()
    else:
        b, out = refs

    def panel_tile(t):
        t = jnp.minimum(t, ROW * S - 1)
        row_of, tile = t // S, lax.rem(t, S)
        return lax.rem(row_of, QUAD) * 2 * S + tile * 2 + row_of // QUAD

    def one(r):
        total = None
        for array, start, dx, dz in groups:
            c = lax.rem(x + dx, X) * ZH + lax.rem(zh + dz, ZH)
            lefts, rights = [], []
            for p in range(SLOTS):
                m = left[r, c * SLOTS + p]
                tile = a[array][start + jnp.minimum(m, S - 1)]
                lefts.append(jnp.where(m < S, tile, jnp.zeros_like(tile)))
                rights.append(b[panel_tile(right[r, c * SLOTS + p])])
            value = jnp.dot(
                jnp.concatenate(lefts, axis=1),
                jnp.concatenate(rights, axis=0),
                preferred_element_type=jnp.float32,
            )
            total = value if total is None else total + value
        return total

    @pl.loop(0, Y * PER, unroll=4)
    def _(k):
        to = lax.rem(y + k // PER, Y)
        mine = lax.rem(core + other, CORE)
        out[k] = one((to * CORE + mine) * PER + lax.rem(k, PER))


def call(groups, other, lists, arrays, b):
    smem = pl.BlockSpec(memory_space=pltpu.SMEM)
    vmem = pl.BlockSpec(memory_space=pltpu.VMEM)
    operands = [*lists, *arrays, *b]
    half = jax.ShapeDtypeStruct((R // 2, BS, BS), jnp.float32)
    panel = jax.ShapeDtypeStruct((ROW * S, BS, BS), jnp.bfloat16)
    return pl.pallas_call(
        functools.partial(products, groups, other),
        out_shape=(half, panel) if other else half,
        in_specs=[smem] * len(lists) + [vmem] * (len(operands) - len(lists)),
        out_specs=(vmem, vmem) if other else vmem,
        scratch_shapes=[pltpu.SemaphoreType.DMA((ROW,))] if other else [],
        compiler_params=pltpu.CompilerParams(vmem_limit_bytes=24 * 1024 * 1024),
        cost_estimate=pl.CostEstimate(
            flops=R // 2 * len(groups) * SLOTS * 2 * BS**3, bytes_accessed=8 * 1024 * 1024, transcendentals=0
        ),
    )(*operands)


def on_device(tiles, pair_a, pair_b):
    own = tiles.reshape(S, BS, BS)
    left = pair_a.reshape(R, COLS * SLOTS)
    right = pair_b.reshape(R, COLS * SLOTS)
    place = jnp.stack([lax.axis_index(n) for n in ("x", "zh", "core", "y", "row")]).astype(jnp.int32)
    lists = (place, left, right)

    def over_x(value):
        return [value] + [lax.ppermute(value, "x", ring(X, -d)) for d in range(1, X)]

    def along_z(value, k):
        at = [row * ZH + zh for zh in range(ZH) for row in range(ROW)]
        return lax.ppermute(value, ("row", "zh"), [(at[p], at[q]) for p, q in ring(ZH * ROW, k)])

    below, above = along_z(own, QUAD), along_z(own, -QUAD)
    own_x = over_x(own)
    below, above, *own_x = lax.optimization_barrier((below, above, *own_x))

    z3, z1 = along_z(below, QUAD), along_z(above, -QUAD)
    upper = lax.axis_index("row") >= QUAD
    both = jnp.stack([jnp.where(upper, below, own), jnp.where(upper, own, above)], axis=1)
    routed = lax.all_to_all(both, ("y", "core"), split_axis=0, concat_axis=0, tiled=True)
    routed = routed.reshape(2 * S, BS, BS)
    z1, z3, routed = lax.optimization_barrier((z1, z3, routed))

    half = S // 2
    z2_low = lax.ppermute(z1[:half], "zh", ring(ZH, -1))
    z2_high = lax.ppermute(z3[half:], "zh", ring(ZH, 1))

    right_way, left_way = [], []
    up = down = routed
    for s in range(1, QUAD):
        up = lax.ppermute(up, "row", [(q + p, q + p + 1) for q in (0, QUAD) for p in range(s - 1, QUAD - 1)])
        down = lax.ppermute(down, "row", [(q + p, q + p - 1) for q in (0, QUAD) for p in range(1, QUAD - s + 1)])
        if s == 1:
            up, down, z2_low, z2_high = lax.optimization_barrier((up, down, z2_low, z2_high))
        right_way.append(up)
        left_way.append(down)

    rest_x = over_x(jnp.concatenate([z1, z3, z2_low, z2_high]))
    groups = [(d, 0, d, 0) for d in range(X)]
    groups += [(X + d, k * S, d, z) for k, z in enumerate((1, 3, 2)) for d in range(X)]

    send, b = call(groups, 1, lists, own_x + rest_x, [routed, *right_way, *left_way])
    got = lax.ppermute(send, "core", ring(CORE, 1))
    keep = call(groups, 0, lists, own_x + rest_x, [b])

    quarter = [keep[d * PER : (d + 1) * PER] + got[d * PER : (d + 1) * PER] for d in range(Y)]
    total = quarter[0]
    for d in range(1, Y):
        total = total + lax.ppermute(quarter[d], "y", ring(Y, d))
    return total[None, None]


def solution(mesh):
    fine = Mesh(mesh.devices.reshape(ROW, X, ZH, Y, CORE), ("row", "x", "zh", "y", "core"))
    spec = ("row", ("x", "zh"), ("y", "core"))
    return jax.shard_map(
        on_device,
        mesh=fine,
        in_specs=(P(*spec), P(*spec), P(*spec)),
        out_specs=P(*spec),
        check_vma=False,
    )
```

time: 206 us -> 225 us (1.092)
  the two profiles are of different devices: /device:TPU:32 before, /device:TPU:1 now
where the time goes in v3:
time: 225 us; the launch traced here: 224 us
  starting transfers between devices  101 us (45%)
  waiting for transfers between devices  100 us (44%)
  Pallas kernels  12.8 us (6%)
  local copies, waits for them, and re-layouts  8.12 us (4%)
    ppermute x4, waiting for transfers between devices, along_z(): lax.ppermute(value, ('row', 'zh'), [(at[p], at[q]) for p, q in ring(ZH *...  45.8 us
    ppermute x4, starting transfers between devices, along_z(): lax.ppermute(value, ('row', 'zh'), [(at[p], at[q]) for p, q in ring(ZH *...  36.8 us
    ppermute x6, waiting for transfers between devices, over_x(): lax.ppermute(value, 'x', ring(X, -d))  28.1 us
    ppermute x6, starting transfers between devices, over_x(): lax.ppermute(value, 'x', ring(X, -d))  21.4 us
    ppermute x1, waiting for transfers between devices, on_device(): z2_high = lax.ppermute(z3[half:], 'zh', ring(ZH, 1))  20.6 us
    pallas_call x2, Pallas kernels, call(): pl.pallas_call(functools.partial(products, groups, other), out_shape=(hal...  12.8 us
    ppermute x1, starting transfers between devices, on_device(): z2_low = lax.ppermute(z1[:half], 'zh', ring(ZH, -1))  12.1 us
    ppermute x3, starting transfers between devices, on_device(): total = total + lax.ppermute(quarter[d], 'y', ring(Y, d))  8.84 us
  transfers between devices with their start and end apart: 23, of which 9 were waited for; matrix products, arithmetic and copies ran while one was open for 0% of the time, Pallas kernels for 3%

profile of v3, /device:TPU:1, one launch (start us, length us, event | category | flops | bytes accessed | tf_op | source)
XLA Modules:
  0.0 223.8 jit_solution(13088023728911685210)
XLA Ops:
  0.0 3.9 %collective-permute-start.4 = (bf16[8,128,128]{2,1,0:T(8,128)(2,1)}, bf16[8,128,128]{2,1,0:T(8,128)(2,1)S(1)}, u32[]{:S(2)}, u32[]{:S(2)}) collective-permute-start(bf16[8,128,128]{2,1,0:T(8,128)(2,1)} %bitcast.17), channel_id=1, source_target_pairs={{0,32},{32,64},{64,96},{96,0},{1,33},{33,65},{65,97},{97,1},{2,34}... | collective-permute-start | bytes 786440 | tf_op jit(solution)/shard_map/ppermute | solution.py:108
  3.9 4.4 %collective-permute-start.3 = (bf16[8,128,128]{2,1,0:T(8,128)(2,1)}, bf16[8,128,128]{2,1,0:T(8,128)(2,1)S(1)}, u32[]{:S(2)}, u32[]{:S(2)}) collective-permute-start(bf16[8,128,128]{2,1,0:T(8,128)(2,1)} %bitcast.18), channel_id=1, source_target_pairs={{0,64},{32,96},{64,0},{96,32},{1,65},{33,97},{65,1},{97,33},{2,66}... | collective-permute-start | bytes 786440 | tf_op jit(solution)/shard_map/ppermute | solution.py:108
  8.3 3.1 %collective-permute-start.2 = (bf16[8,128,128]{2,1,0:T(8,128)(2,1)}, bf16[8,128,128]{2,1,0:T(8,128)(2,1)S(1)}, u32[]{:S(2)}, u32[]{:S(2)}) collective-permute-start(bf16[8,128,128]{2,1,0:T(8,128)(2,1)} %bitcast.19), channel_id=1, source_target_pairs={{0,96},{32,0},{64,32},{96,64},{1,97},{33,1},{65,33},{97,65},{2,98}... | collective-permute-start | bytes 786440 | tf_op jit(solution)/shard_map/ppermute | solution.py:108
  11.4 19.7 %collective-permute-start.1 = (bf16[8,128,128]{2,1,0:T(8,128)(2,1)}, bf16[8,128,128]{2,1,0:T(8,128)(2,1)S(1)}, u32[]{:S(2)}, u32[]{:S(2)}) collective-permute-start(bf16[8,128,128]{2,1,0:T(8,128)(2,1)} %bitcast.20), channel_id=1, source_target_pairs={{0,536},{128,664},{256,792},{384,920},{512,0},{640,128},{768,256},... | collective-permute-start | bytes 786440 | tf_op jit(solution)/shard_map/ppermute | solution.py:112
  31.1 1.9 collective-permute-start
  33.1 0.0 collective-permute-done.4.refs_3_
  33.1 0.0 collective-permute-done.3.refs_2_
  33.1 0.0 collective-permute-done.2.refs_1_
  33.1 20.7 %collective-permute-done.1 = bf16[8,128,128]{2,1,0:T(8,128)(2,1)S(1)} collective-permute-done((bf16[8,128,128]{2,1,0:T(8,128)(2,1)}, bf16[8,128,128]{2,1,0:T(8,128)(2,1)S(1)}, u32[]{:S(2)}, u32[]{:S(2)}) %collective-permute-start.1) | collective-permute-done | bytes 262176 | tf_op jit(solution)/shard_map/ppermute | solution.py:112
  53.9 0.0 collective-permute-done
  53.9 1.0 select_bitcast_fusion.1
  54.9 0.1 pad_maximum_fusion
  54.9 0.0 copy-start.13
  54.9 0.0 copy-start.14
  55.0 0.0 copy-start
  55.0 0.8 copy.15
  55.8 5.5 %all-to-all-start = ((bf16[8,2,128,128]{3,2,1,0:T(8,128)(2,1)}), bf16[8,2,128,128]{3,2,1,0:T(8,128)(2,1)S(1)}, u32[]{:S(2)}, u32[]{:S(2)}) async-start(bf16[8,2,128,128]{3,2,1,0:T(8,128)(2,1)} %copy.15), calls=%async_computation | async-start | bytes 1048576 | tf_op jit(solution)/shard_map/all_to_all | solution.py:121
  61.3 13.2 %collective-permute-start.5 = (bf16[8,128,128]{2,1,0:T(8,128)(2,1)S(1)}, bf16[8,128,128]{2,1,0:T(8,128)(2,1)S(1)}, u32[]{:S(2)}, u32[]{:S(2)}) collective-permute-start(bf16[8,128,128]{2,1,0:T(8,128)(2,1)S(1)} %collective-permute-done.1), channel_id=1, source_target_pairs={{0,536},{128,664},{256,792},{384,920},{512,0},{640,128},{768,256},... | collective-permute-start | bytes 786440 | tf_op jit(solution)/shard_map/ppermute | solution.py:112
  74.5 1.9 collective-permute-start.6
  76.4 15.5 %collective-permute-done.5 = bf16[8,128,128]{2,1,0:T(8,128)(2,1)S(1)} collective-permute-done((bf16[8,128,128]{2,1,0:T(8,128)(2,1)S(1)}, bf16[8,128,128]{2,1,0:T(8,128)(2,1)S(1)}, u32[]{:S(2)}, u32[]{:S(2)}) %collective-permute-start.5) | collective-permute-done | bytes 262176 | tf_op jit(solution)/shard_map/ppermute | solution.py:112
  91.9 9.6 %collective-permute-done.6 = bf16[8,128,128]{2,1,0:T(8,128)(2,1)S(1)} collective-permute-done((bf16[8,128,128]{2,1,0:T(8,128)(2,1)S(1)}, bf16[8,128,128]{2,1,0:T(8,128)(2,1)S(1)}, u32[]{:S(2)}, u32[]{:S(2)}) %collective-permute-start.6) | collective-permute-done | bytes 262176 | tf_op jit(solution)/shard_map/ppermute | solution.py:112
  101.5 0.0 all-to-all-done
  101.5 1.3 collective-permute-start.8
  102.7 4.0 %collective-permute-start.7 = (bf16[16,128,128]{2,1,0:T(8,128)(2,1)S(1)}, bf16[16,128,128]{2,1,0:T(8,128)(2,1)S(1)}, u32[]{:S(2)}, u32[]{:S(2)}) collective-permute-start(bf16[16,128,128]{2,1,0:T(8,128)(2,1)S(1)} %bitcast.25), channel_id=1, source_target_pairs={{0,128},{128,256},{256,384},{512,640},{640,768},{768,896},{1,129},... | collective-permute-start | bytes 1572872 | tf_op jit(solution)/shard_map/ppermute | solution.py:132
  106.8 1.9 collective-permute-start.10
  108.7 12.1 %collective-permute-start.9 = (bf16[4,128,128]{2,1,0:T(8,128)(2,1)S(1)}, bf16[4,128,128]{2,1,0:T(8,128)(2,1)S(1)}, u32[]{:S(2)}, u32[]{:S(2)}) collective-permute-start(bf16[4,128,128]{2,1,0:T(8,128)(2,1)S(1)} %slice.30), channel_id=1, source_target_pairs={{0,24},{8,0},{16,8},{24,16},{1,25},{9,1},{17,9},{25,17},{2,26},{10... | collective-permute-start | bytes 393224 | tf_op jit(solution)/shard_map/ppermute | solution.py:126
  120.9 20.6 %collective-permute-done.10 = bf16[4,128,128]{2,1,0:T(8,128)(2,1)S(1)} collective-permute-done((bf16[4,128,128]{2,1,0:T(8,128)(2,1)S(1)}, bf16[4,128,128]{2,1,0:T(8,128)(2,1)S(1)}, u32[]{:S(2)}, u32[]{:S(2)}) %collective-permute-start.10) | collective-permute-done | bytes 131104 | tf_op jit(solution)/shard_map/ppermute | solution.py:127
  141.4 0.0 collective-permute-done.9
  141.4 0.0 collective-permute-done.8.refs_12_
  141.4 0.0 collective-permute-done.7.refs_9_
  141.5 1.5 collective-permute-start.14
  142.9 0.8 copy-done.11
  143.7 1.3 collective-permute-start.16
  145.1 2.2 collective-permute-start.13
  147.3 5.9 %collective-permute-start.12 = (bf16[24,128,128]{2,1,0:T(8,128)(2,1)S(1)}, bf16[24,128,128]{2,1,0:T(8,128)(2,1)S(1)}, u32[]{:S(2)}, u32[]{:S(2)}) collective-permute-start(bf16[24,128,128]{2,1,0:T(8,128)(2,1)S(1)} %constant_dynamic-update-slice_fusion.refs_4_), channel_id=1, source_target_pairs={{0,64},{32,96},{64,0},{96,32},{1,65},{33,97},{65,1},{97,33},{2,66}... | collective-permute-start | bytes 2359304 | tf_op jit(solution)/shard_map/ppermute | solution.py:108
  153.2 1.9 collective-permute-start.11
  155.1 0.0 collective-permute-done.14.refs_10_
  155.1 1.5 collective-permute-start.15
  156.6 1.3 collective-permute-start.17
  157.9 0.1 copy.13
  158.0 0.1 copy.18.left
  158.1 0.1 copy.14
  158.2 0.1 copy.19.right
  158.3 0.1 stack.32.place
  158.3 4.4 %collective-permute-done.13.refs_7_ = bf16[24,128,128]{2,1,0:T(8,128)(2,1)S(1)} collective-permute-done((bf16[24,128,128]{2,1,0:T(8,128)(2,1)S(1)}, bf16[24,128,128]{2,1,0:T(8,128)(2,1)S(1)}, u32[]{:S(2)}, u32[]{:S(2)}) %collective-permute-start.13) | collective-permute-done | bytes 786464 | tf_op jit(solution)/shard_map/ppermute | solution.py:108
  162.7 20.7 %collective-permute-done.12.refs_6_ = bf16[24,128,128]{2,1,0:T(8,128)(2,1)S(1)} collective-permute-done((bf16[24,128,128]{2,1,0:T(8,128)(2,1)S(1)}, bf16[24,128,128]{2,1,0:T(8,128)(2,1)S(1)}, u32[]{:S(2)}, u32[]{:S(2)}) %collective-permute-start.12) | collective-permute-done | bytes 786464 | tf_op jit(solution)/shard_map/ppermute | solution.py:108
  183.4 3.0 %collective-permute-done.11.refs_5_ = bf16[24,128,128]{2,1,0:T(8,128)(2,1)S(1)} collective-permute-done((bf16[24,128,128]{2,1,0:T(8,128)(2,1)S(1)}, bf16[24,128,128]{2,1,0:T(8,128)(2,1)S(1)}, u32[]{:S(2)}, u32[]{:S(2)}) %collective-permute-start.11) | collective-permute-done | bytes 786464 | tf_op jit(solution)/shard_map/ppermute | solution.py:108
  186.4 0.0 collective-permute-done.15.refs_11_
  186.4 1.0 copy-done.2
  187.5 0.9 copy-done.4
  188.4 0.9 copy-done.6
  189.4 0.9 copy-done.8
  190.3 1.0 copy-done.10
  191.4 1.0 copy-done.12
  192.4 6.9 %shard_map.37 = (f32[8,128,128]{2,1,0:T(8,128)S(1)}, bf16[64,128,128]{2,1,0:T(8,128)(2,1)S(1)}) custom-call(s32[5]{0:T(128)S(1)} %stack.32.place, s32[16,32]{1,0:T(8,128)S(1)} %copy.18.left, s32[16,32]{1,0:T(8,128)S(1)} %copy.19.right, bf16[8,128,128]{2,1,0:T(8,128)(2,1)S(1)} %bitcast.22, bf16[8,128,128]{2,1,0:T(8,128)(2,1)S(1)} %copy-done.8, ...), custom_call_target="tpu_custom_call" | custom-call | flops 1073741824 | bytes 8388608 | tf_op jit(solution)/shard_map/pallas_call | solution.py:87
  199.3 3.5 %collective-permute-start.18 = (f32[8,128,128]{2,1,0:T(8,128)S(1)}, f32[8,128,128]{2,1,0:T(8,128)S(1)}, u32[]{:S(2)}, u32[]{:S(2)}) collective-permute-start(f32[8,128,128]{2,1,0:T(8,128)S(1)} %get-tuple-element.34), channel_id=1, source_target_pairs={{0,1},{1,0},{2,3},{3,2},{4,5},{5,4},{6,7},{7,6},{8,9},{9,8},{10,11... | collective-permute-start | bytes 1572872 | tf_op jit(solution)/shard_map/ppermute | solution.py:144
  202.8 6.0 %shard_map.38 = f32[8,128,128]{2,1,0:T(8,128)S(1)} custom-call(s32[5]{0:T(128)S(1)} %stack.32.place, s32[16,32]{1,0:T(8,128)S(1)} %copy.18.left, s32[16,32]{1,0:T(8,128)S(1)} %copy.19.right, bf16[8,128,128]{2,1,0:T(8,128)(2,1)S(1)} %bitcast.23, bf16[8,128,128]{2,1,0:T(8,128)(2,1)S(1)} %copy-done.8, bf16[8,128,128]{2,1,0:T(8,128)(2,1)S(1)} %copy-done.6, ...), custom_call_target="tpu_custom_call" | custom-call | flops 1073741824 | bytes 8388608 | tf_op jit(solution)/shard_map/pallas_call | solution.py:87
  208.8 2.1 collective-permute-start.19
  210.9 4.4 %collective-permute-start.21 = (f32[2,128,128]{2,1,0:T(8,128)S(1)}, f32[2,128,128]{2,1,0:T(8,128)S(1)}, u32[]{:S(2)}, u32[]{:S(2)}) collective-permute-start(f32[2,128,128]{2,1,0:T(8,128)S(1)} %get-tuple-element.36), channel_id=1, source_target_pairs={{0,6},{2,0},{4,2},{6,4},{1,7},{3,1},{5,3},{7,5},{8,14},{10,8},{12,... | collective-permute-start | bytes 393224 | tf_op jit(solution)/shard_map/ppermute | solution.py:150
  215.3 2.3 %collective-permute-start.20 = (f32[2,128,128]{2,1,0:T(8,128)S(1)}, f32[2,128,128]{2,1,0:T(8,128)S(1)}, u32[]{:S(2)}, u32[]{:S(2)}) collective-permute-start(f32[2,128,128]{2,1,0:T(8,128)S(1)} %get-tuple-element.37), channel_id=1, source_target_pairs={{0,4},{2,6},{4,0},{6,2},{1,5},{3,7},{5,1},{7,3},{8,12},{10,14},{12... | collective-permute-start | bytes 393224 | tf_op jit(solution)/shard_map/ppermute | solution.py:150
  217.6 0.0 collective-permute-done.19
  217.6 0.2 collective-permute-done.21
  217.9 5.3 %collective-permute-done.20 = f32[2,128,128]{2,1,0:T(8,128)S(1)} collective-permute-done((f32[2,128,128]{2,1,0:T(8,128)S(1)}, f32[2,128,128]{2,1,0:T(8,128)S(1)}, u32[]{:S(2)}, u32[]{:S(2)}) %collective-permute-start.20) | collective-permute-done | bytes 131104 | tf_op jit(solution)/shard_map/ppermute | solution.py:150
  223.2 0.7 fusion.3
  (30 shorter events, 0.2 us)
Async XLA Ops:
  0.0 33.1 %collective-permute-start.4 = (bf16[8,128,128]{2,1,0:T(8,128)(2,1)}, bf16[8,128,128]{2,1,0:T(8,128)(2,1)S(1)}, u32[]{:S(2)}, u32[]{:S(2)}) collective-permute-start(bf16[8,128,128]{2,1,0:T(8,128)(2,1)} %bitcast.17), channel_id=1, source_target_pairs={{0,32},{32,64},{64,96},{96,0},{1,33},{33,65},{65,97},{97,1},{2,34}... | collective-permute-start | bytes 786440 | tf_op jit(solution)/shard_map/ppermute | solution.py:108
  3.9 29.1 %collective-permute-start.3 = (bf16[8,128,128]{2,1,0:T(8,128)(2,1)}, bf16[8,128,128]{2,1,0:T(8,128)(2,1)S(1)}, u32[]{:S(2)}, u32[]{:S(2)}) collective-permute-start(bf16[8,128,128]{2,1,0:T(8,128)(2,1)} %bitcast.18), channel_id=1, source_target_pairs={{0,64},{32,96},{64,0},{96,32},{1,65},{33,97},{65,1},{97,33},{2,66}... | collective-permute-start | bytes 786440 | tf_op jit(solution)/shard_map/ppermute | solution.py:108
  8.3 24.8 %collective-permute-start.2 = (bf16[8,128,128]{2,1,0:T(8,128)(2,1)}, bf16[8,128,128]{2,1,0:T(8,128)(2,1)S(1)}, u32[]{:S(2)}, u32[]{:S(2)}) collective-permute-start(bf16[8,128,128]{2,1,0:T(8,128)(2,1)} %bitcast.19), channel_id=1, source_target_pairs={{0,96},{32,0},{64,32},{96,64},{1,97},{33,1},{65,33},{97,65},{2,98}... | collective-permute-start | bytes 786440 | tf_op jit(solution)/shard_map/ppermute | solution.py:108
  11.4 42.5 %collective-permute-start.1 = (bf16[8,128,128]{2,1,0:T(8,128)(2,1)}, bf16[8,128,128]{2,1,0:T(8,128)(2,1)S(1)}, u32[]{:S(2)}, u32[]{:S(2)}) collective-permute-start(bf16[8,128,128]{2,1,0:T(8,128)(2,1)} %bitcast.20), channel_id=1, source_target_pairs={{0,536},{128,664},{256,792},{384,920},{512,0},{640,128},{768,256},... | collective-permute-start | bytes 786440 | tf_op jit(solution)/shard_map/ppermute | solution.py:112
  31.1 22.7 %collective-permute-start = (bf16[8,128,128]{2,1,0:T(8,128)(2,1)}, bf16[8,128,128]{2,1,0:T(8,128)(2,1)S(1)}, u32[]{:S(2)}, u32[]{:S(2)}) collective-permute-start(bf16[8,128,128]{2,1,0:T(8,128)(2,1)} %bitcast.21), channel_id=1, source_target_pairs={{0,512},{128,640},{256,768},{384,896},{512,8},{640,136},{768,264},... | collective-permute-start | bytes 786440 | tf_op jit(solution)/shard_map/ppermute | solution.py:112
  33.1 22.7 %copy-start.3 = (bf16[8,128,128]{2,1,0:T(8,128)(2,1)}, bf16[8,128,128]{2,1,0:T(8,128)(2,1)S(1)}, u32[]{:S(2)}) copy-start(bf16[8,128,128]{2,1,0:T(8,128)(2,1)S(1)} %collective-permute-done.4.refs_3_) | copy-start | bytes 786436
  33.1 22.7 %copy-start.5 = (bf16[8,128,128]{2,1,0:T(8,128)(2,1)}, bf16[8,128,128]{2,1,0:T(8,128)(2,1)S(1)}, u32[]{:S(2)}) copy-start(bf16[8,128,128]{2,1,0:T(8,128)(2,1)S(1)} %collective-permute-done.3.refs_2_) | copy-start | bytes 786436
  33.1 22.7 %copy-start.7 = (bf16[8,128,128]{2,1,0:T(8,128)(2,1)}, bf16[8,128,128]{2,1,0:T(8,128)(2,1)S(1)}, u32[]{:S(2)}) copy-start(bf16[8,128,128]{2,1,0:T(8,128)(2,1)S(1)} %collective-permute-done.2.refs_1_) | copy-start | bytes 786436
  54.9 103.0 %copy-start.13 = (s32[1,1,1,16,16,2]{4,5,3,2,1,0:T(2,128)S(1)}, s32[1,1,1,16,16,2]{4,5,3,2,1,0:T(2,128)}, u32[]{:S(2)}) copy-start(s32[1,1,1,16,16,2]{4,5,3,2,1,0:T(2,128)} %param.4) | copy-start | bytes 6148
  54.9 103.2 %copy-start.14 = (s32[1,1,1,16,16,2]{4,5,3,2,1,0:T(2,128)S(1)}, s32[1,1,1,16,16,2]{4,5,3,2,1,0:T(2,128)}, u32[]{:S(2)}) copy-start(s32[1,1,1,16,16,2]{4,5,3,2,1,0:T(2,128)} %param.5) | copy-start | bytes 6148
  55.0 131.5 %copy-start = (bf16[1,1,1,8,1,128,128]{6,5,4,3,2,1,0:T(8,128)(2,1)S(1)}, bf16[1,1,1,8,1,128,128]{6,5,4,3,2,1,0:T(8,128)(2,1)}, u32[]{:S(2)}) copy-start(bf16[1,1,1,8,1,128,128]{6,5,4,3,2,1,0:T(8,128)(2,1)} %param.3) | copy-start | bytes 786436
  55.8 45.7 %all-to-all-start = ((bf16[8,2,128,128]{3,2,1,0:T(8,128)(2,1)}), bf16[8,2,128,128]{3,2,1,0:T(8,128)(2,1)S(1)}, u32[]{:S(2)}, u32[]{:S(2)}) async-start(bf16[8,2,128,128]{3,2,1,0:T(8,128)(2,1)} %copy.15), calls=%async_computation | async-start | bytes 1048576 | tf_op jit(solution)/shard_map/all_to_all | solution.py:121
  61.3 30.6 %collective-permute-start.5 = (bf16[8,128,128]{2,1,0:T(8,128)(2,1)S(1)}, bf16[8,128,128]{2,1,0:T(8,128)(2,1)S(1)}, u32[]{:S(2)}, u32[]{:S(2)}) collective-permute-start(bf16[8,128,128]{2,1,0:T(8,128)(2,1)S(1)} %collective-permute-done.1), channel_id=1, source_target_pairs={{0,536},{128,664},{256,792},{384,920},{512,0},{640,128},{768,256},... | collective-permute-start | bytes 786440 | tf_op jit(solution)/shard_map/ppermute | solution.py:112
  74.5 27.0 %collective-permute-start.6 = (bf16[8,128,128]{2,1,0:T(8,128)(2,1)S(1)}, bf16[8,128,128]{2,1,0:T(8,128)(2,1)S(1)}, u32[]{:S(2)}, u32[]{:S(2)}) collective-permute-start(bf16[8,128,128]{2,1,0:T(8,128)(2,1)S(1)} %collective-permute-done), channel_id=1, source_target_pairs={{0,512},{128,640},{256,768},{384,896},{512,8},{640,136},{768,264},... | collective-permute-start | bytes 786440 | tf_op jit(solution)/shard_map/ppermute | solution.py:112
  101.5 43.6 %copy-start.1 = (bf16[8,2,128,128]{3,2,1,0:T(8,128)(2,1)}, bf16[8,2,128,128]{3,2,1,0:T(8,128)(2,1)S(1)}, u32[]{:S(2)}) copy-start(bf16[8,2,128,128]{3,2,1,0:T(8,128)(2,1)S(1)} %all-to-all-done) | copy-start | bytes 1572868
  101.5 40.0 %collective-permute-start.8 = (bf16[16,128,128]{2,1,0:T(8,128)(2,1)S(1)}, bf16[16,128,128]{2,1,0:T(8,128)(2,1)S(1)}, u32[]{:S(2)}, u32[]{:S(2)}) collective-permute-start(bf16[16,128,128]{2,1,0:T(8,128)(2,1)S(1)} %bitcast.24), channel_id=1, source_target_pairs={{128,0},{256,128},{384,256},{640,512},{768,640},{896,768},{129,1},... | collective-permute-start | bytes 1572872 | tf_op jit(solution)/shard_map/ppermute | solution.py:133
  102.7 38.7 %collective-permute-start.7 = (bf16[16,128,128]{2,1,0:T(8,128)(2,1)S(1)}, bf16[16,128,128]{2,1,0:T(8,128)(2,1)S(1)}, u32[]{:S(2)}, u32[]{:S(2)}) collective-permute-start(bf16[16,128,128]{2,1,0:T(8,128)(2,1)S(1)} %bitcast.25), channel_id=1, source_target_pairs={{0,128},{128,256},{256,384},{512,640},{640,768},{768,896},{1,129},... | collective-permute-start | bytes 1572872 | tf_op jit(solution)/shard_map/ppermute | solution.py:132
  106.8 34.6 %collective-permute-start.10 = (bf16[4,128,128]{2,1,0:T(8,128)(2,1)S(1)}, bf16[4,128,128]{2,1,0:T(8,128)(2,1)S(1)}, u32[]{:S(2)}, u32[]{:S(2)}) collective-permute-start(bf16[4,128,128]{2,1,0:T(8,128)(2,1)S(1)} %slice.31), channel_id=1, source_target_pairs={{0,8},{8,16},{16,24},{24,0},{1,9},{9,17},{17,25},{25,1},{2,10},{10... | collective-permute-start | bytes 393224 | tf_op jit(solution)/shard_map/ppermute | solution.py:127
  108.7 32.7 %collective-permute-start.9 = (bf16[4,128,128]{2,1,0:T(8,128)(2,1)S(1)}, bf16[4,128,128]{2,1,0:T(8,128)(2,1)S(1)}, u32[]{:S(2)}, u32[]{:S(2)}) collective-permute-start(bf16[4,128,128]{2,1,0:T(8,128)(2,1)S(1)} %slice.30), channel_id=1, source_target_pairs={{0,24},{8,0},{16,8},{24,16},{1,25},{9,1},{17,9},{25,17},{2,26},{10... | collective-permute-start | bytes 393224 | tf_op jit(solution)/shard_map/ppermute | solution.py:126
  141.4 5.9 %copy-start.9 = (bf16[16,128,128]{2,1,0:T(8,128)(2,1)}, bf16[16,128,128]{2,1,0:T(8,128)(2,1)S(1)}, u32[]{:S(2)}) copy-start(bf16[16,128,128]{2,1,0:T(8,128)(2,1)S(1)} %collective-permute-done.8.refs_12_) | copy-start | bytes 1572868
  141.5 13.7 %collective-permute-start.14 = (bf16[16,128,128]{2,1,0:T(8,128)(2,1)S(1)}, bf16[16,128,128]{2,1,0:T(8,128)(2,1)}, u32[]{:S(2)}, u32[]{:S(2)}) collective-permute-start(bf16[16,128,128]{2,1,0:T(8,128)(2,1)S(1)} %collective-permute-done.7.refs_9_), channel_id=1, source_target_pairs={{128,256},{256,384},{640,768},{768,896},{129,257},{257,385},{641,7... | collective-permute-start | bytes 1572872 | tf_op jit(solution)/shard_map/ppermute | solution.py:132
  142.9 0.8 copy-start.11
  143.7 12.9 %collective-permute-start.16 = (bf16[16,128,128]{2,1,0:T(8,128)(2,1)S(1)}, bf16[16,128,128]{2,1,0:T(8,128)(2,1)}, u32[]{:S(2)}, u32[]{:S(2)}) collective-permute-start(bf16[16,128,128]{2,1,0:T(8,128)(2,1)S(1)} %collective-permute-done.8.refs_12_), channel_id=1, source_target_pairs={{128,0},{256,128},{640,512},{768,640},{129,1},{257,129},{641,513},... | collective-permute-start | bytes 1572872 | tf_op jit(solution)/shard_map/ppermute | solution.py:133
  145.1 17.6 %collective-permute-start.13 = (bf16[24,128,128]{2,1,0:T(8,128)(2,1)S(1)}, bf16[24,128,128]{2,1,0:T(8,128)(2,1)S(1)}, u32[]{:S(2)}, u32[]{:S(2)}) collective-permute-start(bf16[24,128,128]{2,1,0:T(8,128)(2,1)S(1)} %constant_dynamic-update-slice_fusion.refs_4_), channel_id=1, source_target_pairs={{0,32},{32,64},{64,96},{96,0},{1,33},{33,65},{65,97},{97,1},{2,34}... | collective-permute-start | bytes 2359304 | tf_op jit(solution)/shard_map/ppermute | solution.py:108
  147.3 36.1 %collective-permute-start.12 = (bf16[24,128,128]{2,1,0:T(8,128)(2,1)S(1)}, bf16[24,128,128]{2,1,0:T(8,128)(2,1)S(1)}, u32[]{:S(2)}, u32[]{:S(2)}) collective-permute-start(bf16[24,128,128]{2,1,0:T(8,128)(2,1)S(1)} %constant_dynamic-update-slice_fusion.refs_4_), channel_id=1, source_target_pairs={{0,64},{32,96},{64,0},{96,32},{1,65},{33,97},{65,1},{97,33},{2,66}... | collective-permute-start | bytes 2359304 | tf_op jit(solution)/shard_map/ppermute | solution.py:108
  153.2 33.2 %collective-permute-start.11 = (bf16[24,128,128]{2,1,0:T(8,128)(2,1)S(1)}, bf16[24,128,128]{2,1,0:T(8,128)(2,1)S(1)}, u32[]{:S(2)}, u32[]{:S(2)}) collective-permute-start(bf16[24,128,128]{2,1,0:T(8,128)(2,1)S(1)} %constant_dynamic-update-slice_fusion.refs_4_), channel_id=1, source_target_pairs={{0,96},{32,0},{64,32},{96,64},{1,97},{33,1},{65,33},{97,65},{2,98}... | collective-permute-start | bytes 2359304 | tf_op jit(solution)/shard_map/ppermute | solution.py:108
  155.1 31.3 %collective-permute-start.15 = (bf16[16,128,128]{2,1,0:T(8,128)(2,1)}, bf16[16,128,128]{2,1,0:T(8,128)(2,1)}, u32[]{:S(2)}, u32[]{:S(2)}) collective-permute-start(bf16[16,128,128]{2,1,0:T(8,128)(2,1)} %collective-permute-done.14.refs_10_), channel_id=1, source_target_pairs={{256,384},{768,896},{257,385},{769,897},{258,386},{770,898},{259,3... | collective-permute-start | bytes 1572872 | tf_op jit(solution)/shard_map/ppermute | solution.py:132
  156.6 29.8 %collective-permute-start.17 = (bf16[16,128,128]{2,1,0:T(8,128)(2,1)}, bf16[16,128,128]{2,1,0:T(8,128)(2,1)}, u32[]{:S(2)}, u32[]{:S(2)}) collective-permute-start(bf16[16,128,128]{2,1,0:T(8,128)(2,1)} %collective-permute-done.16.refs_13_), channel_id=1, source_target_pairs={{128,0},{640,512},{129,1},{641,513},{130,2},{642,514},{131,3},{643... | collective-permute-start | bytes 1572872 | tf_op jit(solution)/shard_map/ppermute | solution.py:133
  186.4 1.0 copy-start.2
  187.5 0.9 copy-start.4
  188.4 0.9 copy-start.6
  189.4 0.9 copy-start.8
  190.3 1.0 copy-start.10
  191.4 1.0 copy-start.12
  199.3 9.4 %collective-permute-start.18 = (f32[8,128,128]{2,1,0:T(8,128)S(1)}, f32[8,128,128]{2,1,0:T(8,128)S(1)}, u32[]{:S(2)}, u32[]{:S(2)}) collective-permute-start(f32[8,128,128]{2,1,0:T(8,128)S(1)} %get-tuple-element.34), channel_id=1, source_target_pairs={{0,1},{1,0},{2,3},{3,2},{4,5},{5,4},{6,7},{7,6},{8,9},{9,8},{10,11... | collective-permute-start | bytes 1572872 | tf_op jit(solution)/shard_map/ppermute | solution.py:144
  208.8 8.9 %collective-permute-start.19 = (f32[2,128,128]{2,1,0:T(8,128)S(1)}, f32[2,128,128]{2,1,0:T(8,128)S(1)}, u32[]{:S(2)}, u32[]{:S(2)}) collective-permute-start(f32[2,128,128]{2,1,0:T(8,128)S(1)} %get-tuple-element.35), channel_id=1, source_target_pairs={{0,2},{2,4},{4,6},{6,0},{1,3},{3,5},{5,7},{7,1},{8,10},{10,12},{12... | collective-permute-start | bytes 393224 | tf_op jit(solution)/shard_map/ppermute | solution.py:150
  210.9 6.9 %collective-permute-start.21 = (f32[2,128,128]{2,1,0:T(8,128)S(1)}, f32[2,128,128]{2,1,0:T(8,128)S(1)}, u32[]{:S(2)}, u32[]{:S(2)}) collective-permute-start(f32[2,128,128]{2,1,0:T(8,128)S(1)} %get-tuple-element.36), channel_id=1, source_target_pairs={{0,6},{2,0},{4,2},{6,4},{1,7},{3,1},{5,3},{7,5},{8,14},{10,8},{12,... | collective-permute-start | bytes 393224 | tf_op jit(solution)/shard_map/ppermute | solution.py:150
  215.3 7.9 %collective-permute-start.20 = (f32[2,128,128]{2,1,0:T(8,128)S(1)}, f32[2,128,128]{2,1,0:T(8,128)S(1)}, u32[]{:S(2)}, u32[]{:S(2)}) collective-permute-start(f32[2,128,128]{2,1,0:T(8,128)S(1)} %get-tuple-element.37), channel_id=1, source_target_pairs={{0,4},{2,6},{4,0},{6,2},{1,5},{3,7},{5,1},{7,3},{8,12},{10,14},{12... | collective-permute-start | bytes 393224 | tf_op jit(solution)/shard_map/ppermute | solution.py:150

commit v4 on v2

v4 whole, which is shorter than its diff:
```python
import functools

import jax
import jax.numpy as jnp
from jax import lax
from jax.experimental import pallas as pl
from jax.experimental.pallas import tpu as pltpu
from jax.sharding import Mesh
from jax.sharding import PartitionSpec as P

X, ZH, Y, CORE, ROW = 4, 4, 4, 2, 8
S, SLOTS, R, BS = 8, 2, 16, 128
COLS = X * ZH
WEIGHT = 7 * 10**9
PER = R // (Y * CORE)


def ring(n, k):
    return [(i, (i + k) % n) for i in range(n)]


def products(groups, other, place, left, right, *refs):
    n = 1 + max(g[0] for g in groups)
    a, refs = refs[:n], refs[n:]
    b, out = refs
    x, zh, core, y = (place[k] for k in range(4))

    def one(r):
        total = None
        for array, start, dx, dz in groups:
            c = lax.rem(x + dx, X) * ZH + lax.rem(zh + dz, ZH)
            lefts, rights = [], []
            for p in range(SLOTS):
                m = left[r, c * SLOTS + p]
                tile = a[array][start + jnp.minimum(m, S - 1)]
                lefts.append(jnp.where(m < S, tile, jnp.zeros_like(tile)))
                rights.append(b[jnp.minimum(right[r, c * SLOTS + p], ROW * S - 1)])
            value = jnp.dot(
                jnp.concatenate(lefts, axis=1),
                jnp.concatenate(rights, axis=0),
                preferred_element_type=jnp.float32,
            )
            total = value if total is None else total + value
        return total

    @pl.loop(0, Y * PER, unroll=8)
    def _(k):
        to = lax.rem(y + k // PER, Y)
        mine = lax.rem(core + other, CORE)
        out[k] = one((to * CORE + mine) * PER + lax.rem(k, PER))


def call(groups, other, lists, arrays, b):
    smem = pl.BlockSpec(memory_space=pltpu.SMEM)
    vmem = pl.BlockSpec(memory_space=pltpu.VMEM)
    operands = [*lists, *arrays, b]
    return pl.pallas_call(
        functools.partial(products, groups, other),
        out_shape=jax.ShapeDtypeStruct((R // 2, BS, BS), jnp.float32),
        in_specs=[smem] * len(lists) + [vmem] * (len(operands) - len(lists)),
        out_specs=vmem,
        compiler_params=pltpu.CompilerParams(vmem_limit_bytes=24 * 1024 * 1024),
        cost_estimate=pl.CostEstimate(
            flops=R // 2 * len(groups) * SLOTS * 2 * BS**3, bytes_accessed=8 * 1024 * 1024, transcendentals=0
        ),
    )(*operands)


def passing(place, weight, *after):
    def body(place_ref, out_ref):
        for k in range(place.shape[0]):
            out_ref[k] = place_ref[k]

    place, *after = lax.optimization_barrier((place, *after))
    smem = pl.BlockSpec(memory_space=pltpu.SMEM)
    place = pl.pallas_call(
        body,
        out_shape=jax.ShapeDtypeStruct(place.shape, place.dtype),
        in_specs=[smem],
        out_specs=smem,
        cost_estimate=pl.CostEstimate(flops=weight, bytes_accessed=1024, transcendentals=0),
    )(place)
    return place, after


def on_device(tiles, pair_a, pair_b):
    own = tiles.reshape(S, BS, BS)
    left = pair_a.reshape(R, COLS * SLOTS)
    right = pair_b.reshape(R, COLS * SLOTS)
    place = jnp.stack([lax.axis_index(n) for n in ("x", "zh", "core", "y")]).astype(jnp.int32)

    def over_x(value, after_first=False):
        got = {0: value}
        for d in (1, 3, 2):
            got[d] = lax.ppermute(value, "x", ring(X, -d))
            if after_first and d == 1:
                value, got[d] = lax.optimization_barrier((value, got[d]))
        return [got[d] for d in range(X)]

    z1 = lax.ppermute(own, "zh", ring(ZH, -1))
    z3 = lax.ppermute(own, "zh", ring(ZH, 1))
    own_x = over_x(own)
    routed = lax.all_to_all(own, ("y", "core"), split_axis=0, concat_axis=0, tiled=True)
    b = lax.all_gather(routed, "row", axis=0, tiled=True)
    z1, z3, _, *own_x = lax.optimization_barrier((z1, z3, routed, *own_x))

    half = S // 2
    z2_low = lax.ppermute(z1[:half], "zh", ring(ZH, -1))
    z2_high = lax.ppermute(z3[half:], "zh", ring(ZH, 1))
    near_x = over_x(jnp.concatenate([z1, z3]))
    far_x = over_x(jnp.concatenate([z2_low, z2_high]))
    place, arrays = passing(place, WEIGHT, *own_x, *near_x, *far_x)
    lists = (place, left, right)

    groups = [(d, 0, d, 0) for d in range(X)]
    groups += [(X + d, k * S, d, z) for k, z in enumerate((1, 3)) for d in range(X)]
    groups += [(2 * X + d, 0, d, 2) for d in range(X)]

    send = call(groups, 1, lists, arrays, b)
    keep = call(groups, 0, lists, arrays, b)
    got = lax.ppermute(send, "core", ring(CORE, 1))

    quarter = [keep[d * PER : (d + 1) * PER] + got[d * PER : (d + 1) * PER] for d in range(Y)]
    total = quarter[0]
    for d in range(1, Y):
        total = total + lax.ppermute(quarter[d], "y", ring(Y, d))
    return total[None, None]


def solution(mesh):
    fine = Mesh(mesh.devices.reshape(ROW, X, ZH, Y, CORE), ("row", "x", "zh", "y", "core"))
    spec = ("row", ("x", "zh"), ("y", "core"))
    return jax.shard_map(
        on_device,
        mesh=fine,
        in_specs=(P(*spec), P(*spec), P(*spec)),
        out_specs=P(*spec),
        check_vma=False,
    )
```

time: 206 us -> 237 us (1.15)
  the two profiles are of different devices: /device:TPU:32 before, /device:TPU:192 now
where the time goes in v4:
time: 237 us; the launch traced here: 236 us
  waiting for transfers between devices  119 us (50%)
  starting transfers between devices  76.6 us (32%)
  between operations  13.7 us (6%)
  blocking collectives  12.2 us (5%)
  Pallas kernels  8.67 us (4%)
  local copies, waits for them, and re-layouts  4.31 us (2%)
    ppermute x1, waiting for transfers between devices, on_device(): z3 = lax.ppermute(own, 'zh', ring(ZH, 1))  53.1 us
    ppermute x9, starting transfers between devices, over_x(): got[d] = lax.ppermute(value, 'x', ring(X, -d))  32.2 us
    ppermute x9, waiting for transfers between devices, over_x(): got[d] = lax.ppermute(value, 'x', ring(X, -d))  22.3 us
    ppermute x1, waiting for transfers between devices, on_device(): z2_low = lax.ppermute(z1[:half], 'zh', ring(ZH, -1))  17.8 us
    ppermute x1, starting transfers between devices, on_device(): z3 = lax.ppermute(own, 'zh', ring(ZH, 1))  15.7 us
    ppermute x1, waiting for transfers between devices, on_device(): z1 = lax.ppermute(own, 'zh', ring(ZH, -1))  12.5 us
    all_to_all x1, blocking collectives, on_device(): lax.all_to_all(own, ('y', 'core'), split_axis=0, concat_axis=0, tiled=True)  12.2 us
    ppermute x3, starting transfers between devices, on_device(): total = total + lax.ppermute(quarter[d], 'y', ring(Y, d))  8.97 us
  transfers between devices with their start and end apart: 18, of which 8 were waited for; matrix products, arithmetic and copies ran while one was open for 0% of the time, Pallas kernels for 2%

profile of v4, /device:TPU:192, one launch (start us, length us, event | category | flops | bytes accessed | tf_op | source)
XLA Modules:
  0.0 236.1 jit_solution(16297649539389530226)
XLA Ops:
  6.5 0.0 copy-start.5
  6.5 0.0 copy-start.6
  6.5 0.0 all-gather.2.cloned.1.call-start
  6.5 12.2 %all_to_all.5 = bf16[8,128,128]{2,1,0:T(8,128)(2,1)} all-to-all(bf16[8,128,128]{2,1,0:T(8,128)(2,1)} %bitcast.9), channel_id=1, replica_groups=mesh['row'=8,'x'=4,'zh'=4,'y'=4,'core'=2] {'y','core'}, dimensions={0} | all-to-all | bytes 524288 | tf_op jit(solution)/shard_map/all_to_all | solution.py:103
  18.8 0.0 all-gather.2.cloned.1.call-update
  18.8 3.4 %collective-permute-start.4 = (bf16[8,128,128]{2,1,0:T(8,128)(2,1)}, bf16[8,128,128]{2,1,0:T(8,128)(2,1)S(1)}, u32[]{:S(2)}, u32[]{:S(2)}) collective-permute-start(bf16[8,128,128]{2,1,0:T(8,128)(2,1)} %bitcast.10), channel_id=1, source_target_pairs={{0,32},{32,64},{64,96},{96,0},{1,33},{33,65},{65,97},{97,1},{2,34}... | collective-permute-start | bytes 786440 | tf_op jit(solution)/shard_map/ppermute | solution.py:95
  22.2 4.6 %collective-permute-start.3 = (bf16[8,128,128]{2,1,0:T(8,128)(2,1)}, bf16[8,128,128]{2,1,0:T(8,128)(2,1)S(1)}, u32[]{:S(2)}, u32[]{:S(2)}) collective-permute-start(bf16[8,128,128]{2,1,0:T(8,128)(2,1)} %bitcast.11), channel_id=1, source_target_pairs={{0,64},{32,96},{64,0},{96,32},{1,65},{33,97},{65,1},{97,33},{2,66}... | collective-permute-start | bytes 786440 | tf_op jit(solution)/shard_map/ppermute | solution.py:95
  26.9 3.3 %collective-permute-start.2 = (bf16[8,128,128]{2,1,0:T(8,128)(2,1)}, bf16[8,128,128]{2,1,0:T(8,128)(2,1)S(1)}, u32[]{:S(2)}, u32[]{:S(2)}) collective-permute-start(bf16[8,128,128]{2,1,0:T(8,128)(2,1)} %bitcast.12), channel_id=1, source_target_pairs={{0,96},{32,0},{64,32},{96,64},{1,97},{33,1},{65,33},{97,65},{2,98}... | collective-permute-start | bytes 786440 | tf_op jit(solution)/shard_map/ppermute | solution.py:95
  30.2 15.7 %collective-permute-start.1 = (bf16[8,128,128]{2,1,0:T(8,128)(2,1)}, bf16[8,128,128]{2,1,0:T(8,128)(2,1)S(1)}, u32[]{:S(2)}, u32[]{:S(2)}) collective-permute-start(bf16[8,128,128]{2,1,0:T(8,128)(2,1)} %bitcast.13), channel_id=1, source_target_pairs={{0,8},{8,16},{16,24},{24,0},{1,9},{9,17},{17,25},{25,1},{2,10},{10... | collective-permute-start | bytes 786440 | tf_op jit(solution)/shard_map/ppermute | solution.py:101
  46.0 2.6 %collective-permute-start = (bf16[8,128,128]{2,1,0:T(8,128)(2,1)}, bf16[8,128,128]{2,1,0:T(8,128)(2,1)S(1)}, u32[]{:S(2)}, u32[]{:S(2)}) collective-permute-start(bf16[8,128,128]{2,1,0:T(8,128)(2,1)} %bitcast.14), channel_id=1, source_target_pairs={{0,24},{8,0},{16,8},{24,16},{1,25},{9,1},{17,9},{25,17},{2,26},{10... | collective-permute-start | bytes 786440 | tf_op jit(solution)/shard_map/ppermute | solution.py:100
  48.6 0.0 collective-permute-done.4.refs_3_
  48.6 0.0 collective-permute-done.3.refs_2_
  48.6 0.0 collective-permute-done.2.refs_1_
  48.6 53.1 %collective-permute-done.1 = bf16[8,128,128]{2,1,0:T(8,128)(2,1)S(1)} collective-permute-done((bf16[8,128,128]{2,1,0:T(8,128)(2,1)}, bf16[8,128,128]{2,1,0:T(8,128)(2,1)S(1)}, u32[]{:S(2)}, u32[]{:S(2)}) %collective-permute-start.1) | collective-permute-done | bytes 262176 | tf_op jit(solution)/shard_map/ppermute | solution.py:101
  101.7 12.5 %collective-permute-done = bf16[8,128,128]{2,1,0:T(8,128)(2,1)S(1)} collective-permute-done((bf16[8,128,128]{2,1,0:T(8,128)(2,1)}, bf16[8,128,128]{2,1,0:T(8,128)(2,1)S(1)}, u32[]{:S(2)}, u32[]{:S(2)}) %collective-permute-start) | collective-permute-done | bytes 262176 | tf_op jit(solution)/shard_map/ppermute | solution.py:100
  114.2 6.7 %collective-permute-start.8 = (bf16[4,128,128]{2,1,0:T(8,128)(2,1)S(1)}, bf16[4,128,128]{2,1,0:T(8,128)(2,1)S(1)}, u32[]{:S(2)}, u32[]{:S(2)}) collective-permute-start(bf16[4,128,128]{2,1,0:T(8,128)(2,1)S(1)} %slice.30), channel_id=1, source_target_pairs={{0,24},{8,0},{16,8},{24,16},{1,25},{9,1},{17,9},{25,17},{2,26},{10... | collective-permute-start | bytes 393224 | tf_op jit(solution)/shard_map/ppermute | solution.py:108
  120.9 8.5 %collective-permute-start.9 = (bf16[4,128,128]{2,1,0:T(8,128)(2,1)S(1)}, bf16[4,128,128]{2,1,0:T(8,128)(2,1)S(1)}, u32[]{:S(2)}, u32[]{:S(2)}) collective-permute-start(bf16[4,128,128]{2,1,0:T(8,128)(2,1)S(1)} %slice.31), channel_id=1, source_target_pairs={{0,8},{8,16},{16,24},{24,0},{1,9},{9,17},{17,25},{25,1},{2,10},{10... | collective-permute-start | bytes 393224 | tf_op jit(solution)/shard_map/ppermute | solution.py:109
  129.5 17.8 %collective-permute-done.8 = bf16[4,128,128]{2,1,0:T(8,128)(2,1)S(1)} collective-permute-done((bf16[4,128,128]{2,1,0:T(8,128)(2,1)S(1)}, bf16[4,128,128]{2,1,0:T(8,128)(2,1)S(1)}, u32[]{:S(2)}, u32[]{:S(2)}) %collective-permute-start.8) | collective-permute-done | bytes 131104 | tf_op jit(solution)/shard_map/ppermute | solution.py:108
  147.3 6.6 %collective-permute-done.9 = bf16[4,128,128]{2,1,0:T(8,128)(2,1)S(1)} collective-permute-done((bf16[4,128,128]{2,1,0:T(8,128)(2,1)S(1)}, bf16[4,128,128]{2,1,0:T(8,128)(2,1)S(1)}, u32[]{:S(2)}, u32[]{:S(2)}) %collective-permute-start.9) | collective-permute-done | bytes 131104 | tf_op jit(solution)/shard_map/ppermute | solution.py:109
  153.9 3.5 %collective-permute-start.12 = (bf16[8,128,128]{2,1,0:T(8,128)(2,1)S(1)}, bf16[8,128,128]{2,1,0:T(8,128)(2,1)S(1)}, u32[]{:S(2)}, u32[]{:S(2)}) collective-permute-start(bf16[8,128,128]{2,1,0:T(8,128)(2,1)S(1)} %constant_dynamic-update-slice_fusion.2.refs_8_), channel_id=1, source_target_pairs={{0,32},{32,64},{64,96},{96,0},{1,33},{33,65},{65,97},{97,1},{2,34}... | collective-permute-start | bytes 786440 | tf_op jit(solution)/shard_map/ppermute | solution.py:95
  157.4 1.9 collective-permute-start.7
  159.3 5.0 %collective-permute-start.6 = (bf16[16,128,128]{2,1,0:T(8,128)(2,1)S(1)}, bf16[16,128,128]{2,1,0:T(8,128)(2,1)S(1)}, u32[]{:S(2)}, u32[]{:S(2)}) collective-permute-start(bf16[16,128,128]{2,1,0:T(8,128)(2,1)S(1)} %constant_dynamic-update-slice_fusion.refs_4_), channel_id=1, source_target_pairs={{0,64},{32,96},{64,0},{96,32},{1,65},{33,97},{65,1},{97,33},{2,66}... | collective-permute-start | bytes 1572872 | tf_op jit(solution)/shard_map/ppermute | solution.py:95
  164.3 2.2 collective-permute-start.5
  166.6 4.6 %collective-permute-start.11 = (bf16[8,128,128]{2,1,0:T(8,128)(2,1)S(1)}, bf16[8,128,128]{2,1,0:T(8,128)(2,1)}, u32[]{:S(2)}, u32[]{:S(2)}) collective-permute-start(bf16[8,128,128]{2,1,0:T(8,128)(2,1)S(1)} %constant_dynamic-update-slice_fusion.2.refs_8_), channel_id=1, source_target_pairs={{0,64},{32,96},{64,0},{96,32},{1,65},{33,97},{65,1},{97,33},{2,66}... | collective-permute-start | bytes 786440 | tf_op jit(solution)/shard_map/ppermute | solution.py:95
  171.2 0.0 collective-permute-done.12.refs_11_
  171.2 0.0 copy-start.2
  171.2 0.7 copy-done.2
  171.9 3.6 %collective-permute-start.10 = (bf16[8,128,128]{2,1,0:T(8,128)(2,1)S(1)}, bf16[8,128,128]{2,1,0:T(8,128)(2,1)}, u32[]{:S(2)}, u32[]{:S(2)}) collective-permute-start(bf16[8,128,128]{2,1,0:T(8,128)(2,1)S(1)} %constant_dynamic-update-slice_fusion.2.refs_8_), channel_id=1, source_target_pairs={{0,96},{32,0},{64,32},{96,64},{1,97},{33,1},{65,33},{97,65},{2,98}... | collective-permute-start | bytes 786440 | tf_op jit(solution)/shard_map/ppermute | solution.py:95
  175.5 0.0 copy-done.5
  175.5 0.1 copy.12
  175.6 0.1 copy.14.left
  175.7 0.0 copy-done.6
  175.7 0.1 copy.13
  175.8 0.1 copy.15.right
  175.8 0.7 pad_add_fusion.place_ref
  176.5 0.0 copy-start.1
  176.5 15.4 %collective-permute-done.11.refs_10_ = bf16[8,128,128]{2,1,0:T(8,128)(2,1)} collective-permute-done((bf16[8,128,128]{2,1,0:T(8,128)(2,1)S(1)}, bf16[8,128,128]{2,1,0:T(8,128)(2,1)}, u32[]{:S(2)}, u32[]{:S(2)}) %collective-permute-start.11) | collective-permute-done | bytes 262176 | tf_op jit(solution)/shard_map/ppermute | solution.py:95
  191.9 6.9 %collective-permute-done.10.refs_9_ = bf16[8,128,128]{2,1,0:T(8,128)(2,1)} collective-permute-done((bf16[8,128,128]{2,1,0:T(8,128)(2,1)S(1)}, bf16[8,128,128]{2,1,0:T(8,128)(2,1)}, u32[]{:S(2)}, u32[]{:S(2)}) %collective-permute-start.10) | collective-permute-done | bytes 262176 | tf_op jit(solution)/shard_map/ppermute | solution.py:95
  198.8 0.0 collective-permute-done.7.refs_7_
  198.8 0.0 collective-permute-done.6.refs_6_
  198.8 0.0 collective-permute-done.5.refs_5_
  198.8 1.2 shard_map.37.place
  200.0 0.0 all-gather.2.cloned.1.call-done.refs_12_
  200.0 0.0 copy-done.1
  200.0 0.0 copy-start
  200.0 1.6 copy-done
  201.6 0.0 copy-start.3
  201.6 0.9 copy-done.3
  202.6 0.0 copy-start.4
  202.6 0.7 copy-done.4
  203.2 3.7 %shard_map.39 = f32[8,128,128]{2,1,0:T(8,128)S(1)} custom-call(s32[4]{0:T(128)S(1)} %copy-done.4, s32[16,32]{1,0:T(8,128)S(1)} %copy.14.left, s32[16,32]{1,0:T(8,128)S(1)} %copy.15.right, bf16[8,128,128]{2,1,0:T(8,128)(2,1)S(1)} %bitcast.15, bf16[8,128,128]{2,1,0:T(8,128)(2,1)S(1)} %collective-permute-done.2.refs_1_, ...), custom_call_target="tpu_custom_call" | custom-call | flops 1073741824 | bytes 8388608 | tf_op jit(solution)/shard_map/pallas_call | solution.py:57
  207.0 1.9 collective-permute-start.13
  208.9 3.8 %shard_map.38 = f32[8,128,128]{2,1,0:T(8,128)S(1)} custom-call(s32[4]{0:T(128)S(1)} %copy-done.4, s32[16,32]{1,0:T(8,128)S(1)} %copy.14.left, s32[16,32]{1,0:T(8,128)S(1)} %copy.15.right, bf16[8,128,128]{2,1,0:T(8,128)(2,1)S(1)} %bitcast.16, bf16[8,128,128]{2,1,0:T(8,128)(2,1)S(1)} %collective-permute-done.2.refs_1_, ...), custom_call_target="tpu_custom_call" | custom-call | flops 1073741824 | bytes 8388608 | tf_op jit(solution)/shard_map/pallas_call | solution.py:57
  212.7 0.0 collective-permute-done.13
  212.7 2.2 collective-permute-start.14
  214.9 4.9 %collective-permute-start.16 = (f32[2,128,128]{2,1,0:T(8,128)S(1)}, f32[2,128,128]{2,1,0:T(8,128)S(1)}, u32[]{:S(2)}, u32[]{:S(2)}) collective-permute-start(f32[2,128,128]{2,1,0:T(8,128)S(1)} %get-tuple-element.44), channel_id=1, source_target_pairs={{0,6},{2,0},{4,2},{6,4},{1,7},{3,1},{5,3},{7,5},{8,14},{10,8},{12,... | collective-permute-start | bytes 393224 | tf_op jit(solution)/shard_map/ppermute | solution.py:126
  219.8 1.9 collective-permute-start.15
  221.7 0.0 collective-permute-done.14
  221.7 4.0 %collective-permute-done.16 = f32[2,128,128]{2,1,0:T(8,128)S(1)} collective-permute-done((f32[2,128,128]{2,1,0:T(8,128)S(1)}, f32[2,128,128]{2,1,0:T(8,128)S(1)}, u32[]{:S(2)}, u32[]{:S(2)}) %collective-permute-start.16) | collective-permute-done | bytes 131104 | tf_op jit(solution)/shard_map/ppermute | solution.py:126
  225.7 2.8 %collective-permute-done.15 = f32[2,128,128]{2,1,0:T(8,128)S(1)} collective-permute-done((f32[2,128,128]{2,1,0:T(8,128)S(1)}, f32[2,128,128]{2,1,0:T(8,128)S(1)}, u32[]{:S(2)}, u32[]{:S(2)}) %collective-permute-start.15) | collective-permute-done | bytes 131104 | tf_op jit(solution)/shard_map/ppermute | solution.py:126
  228.5 0.7 fusion.3
  (7 shorter events, 0.1 us)
Async XLA Ops:
  6.5 169.0 %copy-start.5 = (s32[1,1,1,16,16,2]{4,5,3,2,1,0:T(2,128)S(1)}, s32[1,1,1,16,16,2]{4,5,3,2,1,0:T(2,128)}, u32[]{:S(2)}) copy-start(s32[1,1,1,16,16,2]{4,5,3,2,1,0:T(2,128)} %param.4) | copy-start | bytes 6148
  6.5 169.1 %copy-start.6 = (s32[1,1,1,16,16,2]{4,5,3,2,1,0:T(2,128)S(1)}, s32[1,1,1,16,16,2]{4,5,3,2,1,0:T(2,128)}, u32[]{:S(2)}) copy-start(s32[1,1,1,16,16,2]{4,5,3,2,1,0:T(2,128)} %param.5) | copy-start | bytes 6148
  6.5 193.5 %all-gather.2.cloned.1.call-start = ((), (), s32[]{:S(2)}) async-start(), calls=%async_computation.1 | async-start | bytes 2359296 | tf_op jit(solution)/shard_map/all_gather | solution.py:104
  18.8 29.7 %collective-permute-start.4 = (bf16[8,128,128]{2,1,0:T(8,128)(2,1)}, bf16[8,128,128]{2,1,0:T(8,128)(2,1)S(1)}, u32[]{:S(2)}, u32[]{:S(2)}) collective-permute-start(bf16[8,128,128]{2,1,0:T(8,128)(2,1)} %bitcast.10), channel_id=1, source_target_pairs={{0,32},{32,64},{64,96},{96,0},{1,33},{33,65},{65,97},{97,1},{2,34}... | collective-permute-start | bytes 786440 | tf_op jit(solution)/shard_map/ppermute | solution.py:95
  22.2 26.3 %collective-permute-start.3 = (bf16[8,128,128]{2,1,0:T(8,128)(2,1)}, bf16[8,128,128]{2,1,0:T(8,128)(2,1)S(1)}, u32[]{:S(2)}, u32[]{:S(2)}) collective-permute-start(bf16[8,128,128]{2,1,0:T(8,128)(2,1)} %bitcast.11), channel_id=1, source_target_pairs={{0,64},{32,96},{64,0},{96,32},{1,65},{33,97},{65,1},{97,33},{2,66}... | collective-permute-start | bytes 786440 | tf_op jit(solution)/shard_map/ppermute | solution.py:95
  26.9 21.7 %collective-permute-start.2 = (bf16[8,128,128]{2,1,0:T(8,128)(2,1)}, bf16[8,128,128]{2,1,0:T(8,128)(2,1)S(1)}, u32[]{:S(2)}, u32[]{:S(2)}) collective-permute-start(bf16[8,128,128]{2,1,0:T(8,128)(2,1)} %bitcast.12), channel_id=1, source_target_pairs={{0,96},{32,0},{64,32},{96,64},{1,97},{33,1},{65,33},{97,65},{2,98}... | collective-permute-start | bytes 786440 | tf_op jit(solution)/shard_map/ppermute | solution.py:95
  30.2 71.5 %collective-permute-start.1 = (bf16[8,128,128]{2,1,0:T(8,128)(2,1)}, bf16[8,128,128]{2,1,0:T(8,128)(2,1)S(1)}, u32[]{:S(2)}, u32[]{:S(2)}) collective-permute-start(bf16[8,128,128]{2,1,0:T(8,128)(2,1)} %bitcast.13), channel_id=1, source_target_pairs={{0,8},{8,16},{16,24},{24,0},{1,9},{9,17},{17,25},{25,1},{2,10},{10... | collective-permute-start | bytes 786440 | tf_op jit(solution)/shard_map/ppermute | solution.py:101
  46.0 68.2 %collective-permute-start = (bf16[8,128,128]{2,1,0:T(8,128)(2,1)}, bf16[8,128,128]{2,1,0:T(8,128)(2,1)S(1)}, u32[]{:S(2)}, u32[]{:S(2)}) collective-permute-start(bf16[8,128,128]{2,1,0:T(8,128)(2,1)} %bitcast.14), channel_id=1, source_target_pairs={{0,24},{8,0},{16,8},{24,16},{1,25},{9,1},{17,9},{25,17},{2,26},{10... | collective-permute-start | bytes 786440 | tf_op jit(solution)/shard_map/ppermute | solution.py:100
  114.2 33.0 %collective-permute-start.8 = (bf16[4,128,128]{2,1,0:T(8,128)(2,1)S(1)}, bf16[4,128,128]{2,1,0:T(8,128)(2,1)S(1)}, u32[]{:S(2)}, u32[]{:S(2)}) collective-permute-start(bf16[4,128,128]{2,1,0:T(8,128)(2,1)S(1)} %slice.30), channel_id=1, source_target_pairs={{0,24},{8,0},{16,8},{24,16},{1,25},{9,1},{17,9},{25,17},{2,26},{10... | collective-permute-start | bytes 393224 | tf_op jit(solution)/shard_map/ppermute | solution.py:108
  120.9 32.9 %collective-permute-start.9 = (bf16[4,128,128]{2,1,0:T(8,128)(2,1)S(1)}, bf16[4,128,128]{2,1,0:T(8,128)(2,1)S(1)}, u32[]{:S(2)}, u32[]{:S(2)}) collective-permute-start(bf16[4,128,128]{2,1,0:T(8,128)(2,1)S(1)} %slice.31), channel_id=1, source_target_pairs={{0,8},{8,16},{16,24},{24,0},{1,9},{9,17},{17,25},{25,1},{2,10},{10... | collective-permute-start | bytes 393224 | tf_op jit(solution)/shard_map/ppermute | solution.py:109
  153.9 17.4 %collective-permute-start.12 = (bf16[8,128,128]{2,1,0:T(8,128)(2,1)S(1)}, bf16[8,128,128]{2,1,0:T(8,128)(2,1)S(1)}, u32[]{:S(2)}, u32[]{:S(2)}) collective-permute-start(bf16[8,128,128]{2,1,0:T(8,128)(2,1)S(1)} %constant_dynamic-update-slice_fusion.2.refs_8_), channel_id=1, source_target_pairs={{0,32},{32,64},{64,96},{96,0},{1,33},{33,65},{65,97},{97,1},{2,34}... | collective-permute-start | bytes 786440 | tf_op jit(solution)/shard_map/ppermute | solution.py:95
  157.4 41.4 %collective-permute-start.7 = (bf16[16,128,128]{2,1,0:T(8,128)(2,1)S(1)}, bf16[16,128,128]{2,1,0:T(8,128)(2,1)S(1)}, u32[]{:S(2)}, u32[]{:S(2)}) collective-permute-start(bf16[16,128,128]{2,1,0:T(8,128)(2,1)S(1)} %constant_dynamic-update-slice_fusion.refs_4_), channel_id=1, source_target_pairs={{0,32},{32,64},{64,96},{96,0},{1,33},{33,65},{65,97},{97,1},{2,34}... | collective-permute-start | bytes 1572872 | tf_op jit(solution)/shard_map/ppermute | solution.py:95
  159.3 39.5 %collective-permute-start.6 = (bf16[16,128,128]{2,1,0:T(8,128)(2,1)S(1)}, bf16[16,128,128]{2,1,0:T(8,128)(2,1)S(1)}, u32[]{:S(2)}, u32[]{:S(2)}) collective-permute-start(bf16[16,128,128]{2,1,0:T(8,128)(2,1)S(1)} %constant_dynamic-update-slice_fusion.refs_4_), channel_id=1, source_target_pairs={{0,64},{32,96},{64,0},{96,32},{1,65},{33,97},{65,1},{97,33},{2,66}... | collective-permute-start | bytes 1572872 | tf_op jit(solution)/shard_map/ppermute | solution.py:95
  164.3 34.4 %collective-permute-start.5 = (bf16[16,128,128]{2,1,0:T(8,128)(2,1)S(1)}, bf16[16,128,128]{2,1,0:T(8,128)(2,1)S(1)}, u32[]{:S(2)}, u32[]{:S(2)}) collective-permute-start(bf16[16,128,128]{2,1,0:T(8,128)(2,1)S(1)} %constant_dynamic-update-slice_fusion.refs_4_), channel_id=1, source_target_pairs={{0,96},{32,0},{64,32},{96,64},{1,97},{33,1},{65,33},{97,65},{2,98}... | collective-permute-start | bytes 1572872 | tf_op jit(solution)/shard_map/ppermute | solution.py:95
  166.6 25.3 %collective-permute-start.11 = (bf16[8,128,128]{2,1,0:T(8,128)(2,1)S(1)}, bf16[8,128,128]{2,1,0:T(8,128)(2,1)}, u32[]{:S(2)}, u32[]{:S(2)}) collective-permute-start(bf16[8,128,128]{2,1,0:T(8,128)(2,1)S(1)} %constant_dynamic-update-slice_fusion.2.refs_8_), channel_id=1, source_target_pairs={{0,64},{32,96},{64,0},{96,32},{1,65},{33,97},{65,1},{97,33},{2,66}... | collective-permute-start | bytes 786440 | tf_op jit(solution)/shard_map/ppermute | solution.py:95
  171.2 0.7 copy-start.2
  171.9 26.8 %collective-permute-start.10 = (bf16[8,128,128]{2,1,0:T(8,128)(2,1)S(1)}, bf16[8,128,128]{2,1,0:T(8,128)(2,1)}, u32[]{:S(2)}, u32[]{:S(2)}) collective-permute-start(bf16[8,128,128]{2,1,0:T(8,128)(2,1)S(1)} %constant_dynamic-update-slice_fusion.2.refs_8_), channel_id=1, source_target_pairs={{0,96},{32,0},{64,32},{96,64},{1,97},{33,1},{65,33},{97,65},{2,98}... | collective-permute-start | bytes 786440 | tf_op jit(solution)/shard_map/ppermute | solution.py:95
  176.5 23.5 %copy-start.1 = (bf16[1,1,1,8,1,128,128]{6,5,4,3,2,1,0:T(8,128)(2,1)S(1)}, bf16[1,1,1,8,1,128,128]{6,5,4,3,2,1,0:T(8,128)(2,1)}, u32[]{:S(2)}) copy-start(bf16[1,1,1,8,1,128,128]{6,5,4,3,2,1,0:T(8,128)(2,1)} %param.3) | copy-start | bytes 786436
  200.0 1.6 copy-start
  201.6 0.9 copy-start.3
  202.6 0.7 copy-start.4
  207.0 5.7 %collective-permute-start.13 = (f32[8,128,128]{2,1,0:T(8,128)S(1)}, f32[8,128,128]{2,1,0:T(8,128)S(1)}, u32[]{:S(2)}, u32[]{:S(2)}) collective-permute-start(f32[8,128,128]{2,1,0:T(8,128)S(1)} %shard_map.39), channel_id=1, source_target_pairs={{0,1},{1,0},{2,3},{3,2},{4,5},{5,4},{6,7},{7,6},{8,9},{9,8},{10,11... | collective-permute-start | bytes 1572872 | tf_op jit(solution)/shard_map/ppermute | solution.py:121
  212.7 9.0 %collective-permute-start.14 = (f32[2,128,128]{2,1,0:T(8,128)S(1)}, f32[2,128,128]{2,1,0:T(8,128)S(1)}, u32[]{:S(2)}, u32[]{:S(2)}) collective-permute-start(f32[2,128,128]{2,1,0:T(8,128)S(1)} %get-tuple-element.43), channel_id=1, source_target_pairs={{0,2},{2,4},{4,6},{6,0},{1,3},{3,5},{5,7},{7,1},{8,10},{10,12},{12... | collective-permute-start | bytes 393224 | tf_op jit(solution)/shard_map/ppermute | solution.py:126
  214.9 10.8 %collective-permute-start.16 = (f32[2,128,128]{2,1,0:T(8,128)S(1)}, f32[2,128,128]{2,1,0:T(8,128)S(1)}, u32[]{:S(2)}, u32[]{:S(2)}) collective-permute-start(f32[2,128,128]{2,1,0:T(8,128)S(1)} %get-tuple-element.44), channel_id=1, source_target_pairs={{0,6},{2,0},{4,2},{6,4},{1,7},{3,1},{5,3},{7,5},{8,14},{10,8},{12,... | collective-permute-start | bytes 393224 | tf_op jit(solution)/shard_map/ppermute | solution.py:126
  219.8 8.7 %collective-permute-start.15 = (f32[2,128,128]{2,1,0:T(8,128)S(1)}, f32[2,128,128]{2,1,0:T(8,128)S(1)}, u32[]{:S(2)}, u32[]{:S(2)}) collective-permute-start(f32[2,128,128]{2,1,0:T(8,128)S(1)} %get-tuple-element.45), channel_id=1, source_target_pairs={{0,4},{2,6},{4,0},{6,2},{1,5},{3,7},{5,1},{7,3},{8,12},{10,14},{12... | collective-permute-start | bytes 393224 | tf_op jit(solution)/shard_map/ppermute | solution.py:126
Sparse Core Ops, SparseCore 0:
  18.9 140.7 all-gather.1

commit v5 on v4

--- a/solution.py
+++ b/solution.py
@@ -11,8 +11,8 @@
 X, ZH, Y, CORE, ROW = 4, 4, 4, 2, 8
 S, SLOTS, R, BS = 8, 2, 16, 128
 COLS = X * ZH
-WEIGHT = 7 * 10**9
 PER = R // (Y * CORE)
+WEIGHT = 32 * 10**9
 
 
 def ring(n, k):
@@ -45,7 +45,8 @@
 
     @pl.loop(0, Y * PER, unroll=8)
     def _(k):
-        to = lax.rem(y + k // PER, Y)
+        d = k // PER
+        to = y ^ d ^ (d >> 1)
         mine = lax.rem(core + other, CORE)
         out[k] = one((to * CORE + mine) * PER + lax.rem(k, PER))
 
@@ -53,17 +54,16 @@
 def call(groups, other, lists, arrays, b):
     smem = pl.BlockSpec(memory_space=pltpu.SMEM)
     vmem = pl.BlockSpec(memory_space=pltpu.VMEM)
-    operands = [*lists, *arrays, b]
     return pl.pallas_call(
         functools.partial(products, groups, other),
         out_shape=jax.ShapeDtypeStruct((R // 2, BS, BS), jnp.float32),
-        in_specs=[smem] * len(lists) + [vmem] * (len(operands) - len(lists)),
+        in_specs=[smem] * len(lists) + [vmem] * (len(arrays) + 1),
         out_specs=vmem,
         compiler_params=pltpu.CompilerParams(vmem_limit_bytes=24 * 1024 * 1024),
         cost_estimate=pl.CostEstimate(
             flops=R // 2 * len(groups) * SLOTS * 2 * BS**3, bytes_accessed=8 * 1024 * 1024, transcendentals=0
         ),
-    )(*operands)
+    )(*lists, *arrays, b)
 
 
 def passing(place, weight, *after):
@@ -89,41 +89,46 @@
     right = pair_b.reshape(R, COLS * SLOTS)
     place = jnp.stack([lax.axis_index(n) for n in ("x", "zh", "core", "y")]).astype(jnp.int32)
 
-    def over_x(value, after_first=False):
-        got = {0: value}
-        for d in (1, 3, 2):
-            got[d] = lax.ppermute(value, "x", ring(X, -d))
-            if after_first and d == 1:
-                value, got[d] = lax.optimization_barrier((value, got[d]))
-        return [got[d] for d in range(X)]
+    def over_x(value):
+        return [value] + [lax.ppermute(value, "x", ring(X, -d)) for d in range(1, X)]
+
+    def fenced(function, *args):
+        always = lax.optimization_barrier(jnp.bool_(True))
+        shapes = jax.eval_shape(function, *args)
+        never = lambda *args: jax.tree.map(lambda t: jnp.zeros(t.shape, t.dtype), shapes)
+        return lax.cond(always, function, never, *args)
+
+    def together(*values):
+        flat, tree = jax.tree.flatten(values)
+        return jax.tree.unflatten(tree, lax.optimization_barrier(tuple(flat)))
 
     z1 = lax.ppermute(own, "zh", ring(ZH, -1))
     z3 = lax.ppermute(own, "zh", ring(ZH, 1))
-    own_x = over_x(own)
     routed = lax.all_to_all(own, ("y", "core"), split_axis=0, concat_axis=0, tiled=True)
     b = lax.all_gather(routed, "row", axis=0, tiled=True)
-    z1, z3, _, *own_x = lax.optimization_barrier((z1, z3, routed, *own_x))
+    own_x = fenced(over_x, own)
+    z1, z3, own_x, _ = together(z1, z3, own_x, routed)
 
     half = S // 2
     z2_low = lax.ppermute(z1[:half], "zh", ring(ZH, -1))
     z2_high = lax.ppermute(z3[half:], "zh", ring(ZH, 1))
-    near_x = over_x(jnp.concatenate([z1, z3]))
-    far_x = over_x(jnp.concatenate([z2_low, z2_high]))
-    place, arrays = passing(place, WEIGHT, *own_x, *near_x, *far_x)
+    near = fenced(over_x, jnp.concatenate([z1, z3]))
+    z2_low, z2_high, near = together(z2_low, z2_high, near)
+    far = over_x(jnp.concatenate([z2_low, z2_high]))
+
+    place, arrays = passing(place, WEIGHT, *own_x, *near, *far)
     lists = (place, left, right)
-
     groups = [(d, 0, d, 0) for d in range(X)]
     groups += [(X + d, k * S, d, z) for k, z in enumerate((1, 3)) for d in range(X)]
     groups += [(2 * X + d, 0, d, 2) for d in range(X)]
+    send = call(groups, 1, lists, arrays, b)
+    got = lax.ppermute(send, "core", ring(CORE, 1))
+    keep = call(groups, 0, lists, arrays, b)
 
-    send = call(groups, 1, lists, arrays, b)
-    keep = call(groups, 0, lists, arrays, b)
-    got = lax.ppermute(send, "core", ring(CORE, 1))
-
-    quarter = [keep[d * PER : (d + 1) * PER] + got[d * PER : (d + 1) * PER] for d in range(Y)]
-    total = quarter[0]
-    for d in range(1, Y):
-        total = total + lax.ppermute(quarter[d], "y", ring(Y, d))
+    half = R // 4
+    mine, others = keep[:half] + got[:half], keep[half:] + got[half:]
+    mine = mine + lax.ppermute(others, "y", [(k, k ^ 3) for k in range(Y)])
+    total = mine[:PER] + lax.ppermute(mine[PER:], "y", [(k, k ^ 1) for k in range(Y)])
     return total[None, None]
 
 

time: 237 us -> 201 us (0.85)
  the two profiles are of different devices: /device:TPU:192 before, /device:TPU:96 now
where the time goes in v5:
time: 201 us; the launch traced here: 200 us
  waiting for transfers between devices  93 us (46%)
  starting transfers between devices  78.3 us (39%)
  between operations  13.6 us (7%)
  Pallas kernels  9.41 us (5%)
  local copies, waits for them, and re-layouts  4.3 us (2%)
    ppermute x9, waiting for transfers between devices, over_x(): lax.ppermute(value, 'x', ring(X, -d))  40.1 us
    ppermute x9, starting transfers between devices, over_x(): lax.ppermute(value, 'x', ring(X, -d))  28.5 us
    ppermute x1, waiting for transfers between devices, on_device(): z1 = lax.ppermute(own, 'zh', ring(ZH, -1))  24.7 us
    ppermute x1, starting transfers between devices, on_device(): z1 = lax.ppermute(own, 'zh', ring(ZH, -1))  20.3 us
    ppermute x1, waiting for transfers between devices, on_device(): z3 = lax.ppermute(own, 'zh', ring(ZH, 1))  15.9 us
    ppermute x1, starting transfers between devices, on_device(): z2_low = lax.ppermute(z1[:half], 'zh', ring(ZH, -1))  8.86 us
    pallas_call x2, Pallas kernels, call(): pl.pallas_call(functools.partial(products, groups, other), out_shape=jax....  8.23 us
    ppermute x1, waiting for transfers between devices, on_device(): mine = mine + lax.ppermute(others, 'y', [(k, k ^ 3) for k in range(Y)])  7.35 us
  transfers between devices with their start and end apart: 18, of which 12 were waited for; matrix products, arithmetic and copies ran while one was open for 1% of the time, Pallas kernels for 3%

profile of v5, /device:TPU:96, one launch (start us, length us, event | category | flops | bytes accessed | tf_op | source)
XLA Modules:
  0.0 200.1 jit_solution(6015895920026156247)
XLA Ops:
  6.5 4.5 %all-to-all-start = ((bf16[8,128,128]{2,1,0:T(8,128)(2,1)}), bf16[8,128,128]{2,1,0:T(8,128)(2,1)S(1)}, u32[]{:S(2)}, u32[]{:S(2)}) async-start(bf16[8,128,128]{2,1,0:T(8,128)(2,1)} %bitcast.9), calls=%async_computation | async-start | bytes 524288 | tf_op jit(solution)/shard_map/all_to_all | solution.py:107
  11.0 0.0 all-gather.2.cloned.1.call-start
  11.0 20.3 %collective-permute-start.6 = (bf16[8,128,128]{2,1,0:T(8,128)(2,1)}, bf16[8,128,128]{2,1,0:T(8,128)(2,1)S(1)}, u32[]{:S(2)}, u32[]{:S(2)}) collective-permute-start(bf16[8,128,128]{2,1,0:T(8,128)(2,1)} %bitcast.10), channel_id=1, source_target_pairs={{0,24},{8,0},{16,8},{24,16},{1,25},{9,1},{17,9},{25,17},{2,26},{10... | collective-permute-start | bytes 786440 | tf_op jit(solution)/shard_map/ppermute | solution.py:105
  31.4 1.9 collective-permute-start.7
  33.3 0.0 all-to-all-done
  33.3 0.0 copy-start.2
  33.3 0.7 copy-done.2
  34.0 0.0 all-gather.2.cloned.1.call-update
  34.0 22.1 %conditional.2 = (bf16[8,128,128]{2,1,0:T(8,128)(2,1)S(1)}, bf16[8,128,128]{2,1,0:T(8,128)(2,1)}, bf16[8,128,128]{2,1,0:T(8,128)(2,1)}, bf16[8,128,128]{2,1,0:T(8,128)(2,1)}) conditional(s32[]{:T(128)} %convert_element_type.4, () %tuple.24, bf16[8,128,128]{2,1,0:T(8,128)(2,1)} %bitcast.12), branch_computations={%region_0.0_spmd, %region_1.0_spmd} | conditional | bytes 3670168 | solution.py:99
  34.0 4.7 %collective-permute-start = (bf16[8,128,128]{2,1,0:T(8,128)(2,1)}, bf16[8,128,128]{2,1,0:T(8,128)(2,1)}, u32[]{:S(2)}, u32[]{:S(2)}) collective-permute-start(bf16[8,128,128]{2,1,0:T(8,128)(2,1)} %param.1), channel_id=1, source_target_pairs={{0,96},{32,0},{64,32},{96,64},{1,97},{33,1},{65,33},{97,65},{2,98}... | collective-permute-start | bytes 786440 | tf_op jit(solution)/shard_map/cond/branch_1_fun/ppermute | solution.py:93
  38.7 2.7 %collective-permute-start.1 = (bf16[8,128,128]{2,1,0:T(8,128)(2,1)}, bf16[8,128,128]{2,1,0:T(8,128)(2,1)}, u32[]{:S(2)}, u32[]{:S(2)}) collective-permute-start(bf16[8,128,128]{2,1,0:T(8,128)(2,1)} %param.1), channel_id=1, source_target_pairs={{0,64},{32,96},{64,0},{96,32},{1,65},{33,97},{65,1},{97,33},{2,66}... | collective-permute-start | bytes 786440 | tf_op jit(solution)/shard_map/cond/branch_1_fun/ppermute | solution.py:93
  41.4 2.8 %collective-permute-start.2 = (bf16[8,128,128]{2,1,0:T(8,128)(2,1)}, bf16[8,128,128]{2,1,0:T(8,128)(2,1)}, u32[]{:S(2)}, u32[]{:S(2)}) collective-permute-start(bf16[8,128,128]{2,1,0:T(8,128)(2,1)} %param.1), channel_id=1, source_target_pairs={{0,32},{32,64},{64,96},{96,0},{1,33},{33,65},{65,97},{97,1},{2,34}... | collective-permute-start | bytes 786440 | tf_op jit(solution)/shard_map/cond/branch_1_fun/ppermute | solution.py:93
  44.2 1.0 copy.22
  45.2 5.4 %collective-permute-done = bf16[8,128,128]{2,1,0:T(8,128)(2,1)} collective-permute-done((bf16[8,128,128]{2,1,0:T(8,128)(2,1)}, bf16[8,128,128]{2,1,0:T(8,128)(2,1)}, u32[]{:S(2)}, u32[]{:S(2)}) %collective-permute-start) | collective-permute-done | bytes 262176 | tf_op jit(solution)/shard_map/cond/branch_1_fun/ppermute | solution.py:93
  50.5 1.1 collective-permute-done.1
  51.7 4.5 %collective-permute-done.2 = bf16[8,128,128]{2,1,0:T(8,128)(2,1)} collective-permute-done((bf16[8,128,128]{2,1,0:T(8,128)(2,1)}, bf16[8,128,128]{2,1,0:T(8,128)(2,1)}, u32[]{:S(2)}, u32[]{:S(2)}) %collective-permute-start.2) | collective-permute-done | bytes 262176 | tf_op jit(solution)/shard_map/cond/branch_1_fun/ppermute | solution.py:93
  56.1 24.7 %collective-permute-done.6 = bf16[8,128,128]{2,1,0:T(8,128)(2,1)S(1)} collective-permute-done((bf16[8,128,128]{2,1,0:T(8,128)(2,1)}, bf16[8,128,128]{2,1,0:T(8,128)(2,1)S(1)}, u32[]{:S(2)}, u32[]{:S(2)}) %collective-permute-start.6) | collective-permute-done | bytes 262176 | tf_op jit(solution)/shard_map/ppermute | solution.py:105
  80.8 15.9 %collective-permute-done.7 = bf16[8,128,128]{2,1,0:T(8,128)(2,1)S(1)} collective-permute-done((bf16[8,128,128]{2,1,0:T(8,128)(2,1)}, bf16[8,128,128]{2,1,0:T(8,128)(2,1)S(1)}, u32[]{:S(2)}, u32[]{:S(2)}) %collective-permute-start.7) | collective-permute-done | bytes 262176 | tf_op jit(solution)/shard_map/ppermute | solution.py:106
  96.8 8.9 %collective-permute-start.8 = (bf16[4,128,128]{2,1,0:T(8,128)(2,1)S(1)}, bf16[4,128,128]{2,1,0:T(8,128)(2,1)S(1)}, u32[]{:S(2)}, u32[]{:S(2)}) collective-permute-start(bf16[4,128,128]{2,1,0:T(8,128)(2,1)S(1)} %slice.24), channel_id=1, source_target_pairs={{0,24},{8,0},{16,8},{24,16},{1,25},{9,1},{17,9},{25,17},{2,26},{10... | collective-permute-start | bytes 393224 | tf_op jit(solution)/shard_map/ppermute | solution.py:113
  105.7 5.7 %collective-permute-start.9 = (bf16[4,128,128]{2,1,0:T(8,128)(2,1)S(1)}, bf16[4,128,128]{2,1,0:T(8,128)(2,1)S(1)}, u32[]{:S(2)}, u32[]{:S(2)}) collective-permute-start(bf16[4,128,128]{2,1,0:T(8,128)(2,1)S(1)} %slice.25), channel_id=1, source_target_pairs={{0,8},{8,16},{16,24},{24,0},{1,9},{9,17},{17,25},{25,1},{2,10},{10... | collective-permute-start | bytes 393224 | tf_op jit(solution)/shard_map/ppermute | solution.py:114
  111.4 0.0 copy-start.3
  111.4 0.0 copy-start.4
  111.4 29.7 %conditional.3 = (bf16[16,128,128]{2,1,0:T(8,128)(2,1)S(1)}, bf16[16,128,128]{2,1,0:T(8,128)(2,1)}, bf16[16,128,128]{2,1,0:T(8,128)(2,1)}, bf16[16,128,128]{2,1,0:T(8,128)(2,1)}) conditional(s32[]{:T(128)} %convert_element_type.4, () %tuple.26, bf16[16,128,128]{2,1,0:T(8,128)(2,1)S(1)} %pad_maximum_fusion), branch_computations={%region_2.0_spmd, %region_3.0_spmd} | conditional | bytes 7340184 | solution.py:99
  111.5 4.9 %collective-permute-start.3 = (bf16[16,128,128]{2,1,0:T(8,128)(2,1)S(1)}, bf16[16,128,128]{2,1,0:T(8,128)(2,1)}, u32[]{:S(2)}, u32[]{:S(2)}) collective-permute-start(bf16[16,128,128]{2,1,0:T(8,128)(2,1)S(1)} %param.3), channel_id=1, source_target_pairs={{0,96},{32,0},{64,32},{96,64},{1,97},{33,1},{65,33},{97,65},{2,98}... | collective-permute-start | bytes 1572872 | tf_op jit(solution)/shard_map/cond/branch_1_fun/ppermute | solution.py:93
  116.4 2.7 %collective-permute-start.4 = (bf16[16,128,128]{2,1,0:T(8,128)(2,1)S(1)}, bf16[16,128,128]{2,1,0:T(8,128)(2,1)}, u32[]{:S(2)}, u32[]{:S(2)}) collective-permute-start(bf16[16,128,128]{2,1,0:T(8,128)(2,1)S(1)} %param.3), channel_id=1, source_target_pairs={{0,64},{32,96},{64,0},{96,32},{1,65},{33,97},{65,1},{97,33},{2,66}... | collective-permute-start | bytes 1572872 | tf_op jit(solution)/shard_map/cond/branch_1_fun/ppermute | solution.py:93
  119.0 2.8 %collective-permute-start.5 = (bf16[16,128,128]{2,1,0:T(8,128)(2,1)S(1)}, bf16[16,128,128]{2,1,0:T(8,128)(2,1)}, u32[]{:S(2)}, u32[]{:S(2)}) collective-permute-start(bf16[16,128,128]{2,1,0:T(8,128)(2,1)S(1)} %param.3), channel_id=1, source_target_pairs={{0,32},{32,64},{64,96},{96,0},{1,33},{33,65},{65,97},{97,1},{2,34}... | collective-permute-start | bytes 1572872 | tf_op jit(solution)/shard_map/cond/branch_1_fun/ppermute | solution.py:93
  121.9 13.5 %collective-permute-done.3 = bf16[16,128,128]{2,1,0:T(8,128)(2,1)} collective-permute-done((bf16[16,128,128]{2,1,0:T(8,128)(2,1)S(1)}, bf16[16,128,128]{2,1,0:T(8,128)(2,1)}, u32[]{:S(2)}, u32[]{:S(2)}) %collective-permute-start.3) | collective-permute-done | bytes 524320 | tf_op jit(solution)/shard_map/cond/branch_1_fun/ppermute | solution.py:93
  135.4 0.0 collective-permute-done.4
  135.4 5.7 %collective-permute-done.5 = bf16[16,128,128]{2,1,0:T(8,128)(2,1)} collective-permute-done((bf16[16,128,128]{2,1,0:T(8,128)(2,1)S(1)}, bf16[16,128,128]{2,1,0:T(8,128)(2,1)}, u32[]{:S(2)}, u32[]{:S(2)}) %collective-permute-start.5) | collective-permute-done | bytes 524320 | tf_op jit(solution)/shard_map/cond/branch_1_fun/ppermute | solution.py:93
  141.1 0.0 collective-permute-done.8
  141.1 0.0 collective-permute-done.9
  141.2 2.5 %collective-permute-start.10 = (bf16[8,128,128]{2,1,0:T(8,128)(2,1)S(1)}, bf16[8,128,128]{2,1,0:T(8,128)(2,1)S(1)}, u32[]{:S(2)}, u32[]{:S(2)}) collective-permute-start(bf16[8,128,128]{2,1,0:T(8,128)(2,1)S(1)} %constant_dynamic-update-slice_fusion.refs_8_), channel_id=1, source_target_pairs={{0,96},{32,0},{64,32},{96,64},{1,97},{33,1},{65,33},{97,65},{2,98}... | collective-permute-start | bytes 786440 | tf_op jit(solution)/shard_map/ppermute | solution.py:93
  143.7 2.7 %collective-permute-start.11 = (bf16[8,128,128]{2,1,0:T(8,128)(2,1)S(1)}, bf16[8,128,128]{2,1,0:T(8,128)(2,1)S(1)}, u32[]{:S(2)}, u32[]{:S(2)}) collective-permute-start(bf16[8,128,128]{2,1,0:T(8,128)(2,1)S(1)} %constant_dynamic-update-slice_fusion.refs_8_), channel_id=1, source_target_pairs={{0,64},{32,96},{64,0},{96,32},{1,65},{33,97},{65,1},{97,33},{2,66}... | collective-permute-start | bytes 786440 | tf_op jit(solution)/shard_map/ppermute | solution.py:93
  146.4 2.7 %collective-permute-start.12 = (bf16[8,128,128]{2,1,0:T(8,128)(2,1)S(1)}, bf16[8,128,128]{2,1,0:T(8,128)(2,1)S(1)}, u32[]{:S(2)}, u32[]{:S(2)}) collective-permute-start(bf16[8,128,128]{2,1,0:T(8,128)(2,1)S(1)} %constant_dynamic-update-slice_fusion.refs_8_), channel_id=1, source_target_pairs={{0,32},{32,64},{64,96},{96,0},{1,33},{33,65},{65,97},{97,1},{2,34}... | collective-permute-start | bytes 786440 | tf_op jit(solution)/shard_map/ppermute | solution.py:93
  149.1 0.0 copy-done.3
  149.1 0.1 copy.12
  149.2 0.1 copy.14.left
  149.3 0.0 copy-done.4
  149.3 0.1 copy.13
  149.4 0.1 copy.15.right
  149.4 0.6 pad_add_fusion.place_ref
  150.1 2.2 %collective-permute-done.10.refs_9_ = bf16[8,128,128]{2,1,0:T(8,128)(2,1)S(1)} collective-permute-done((bf16[8,128,128]{2,1,0:T(8,128)(2,1)S(1)}, bf16[8,128,128]{2,1,0:T(8,128)(2,1)S(1)}, u32[]{:S(2)}, u32[]{:S(2)}) %collective-permute-start.10) | collective-permute-done | bytes 262176 | tf_op jit(solution)/shard_map/ppermute | solution.py:93
  152.3 3.7 %collective-permute-done.11.refs_10_ = bf16[8,128,128]{2,1,0:T(8,128)(2,1)S(1)} collective-permute-done((bf16[8,128,128]{2,1,0:T(8,128)(2,1)S(1)}, bf16[8,128,128]{2,1,0:T(8,128)(2,1)S(1)}, u32[]{:S(2)}, u32[]{:S(2)}) %collective-permute-start.11) | collective-permute-done | bytes 262176 | tf_op jit(solution)/shard_map/ppermute | solution.py:93
  156.0 4.0 %collective-permute-done.12.refs_11_ = bf16[8,128,128]{2,1,0:T(8,128)(2,1)S(1)} collective-permute-done((bf16[8,128,128]{2,1,0:T(8,128)(2,1)S(1)}, bf16[8,128,128]{2,1,0:T(8,128)(2,1)S(1)}, u32[]{:S(2)}, u32[]{:S(2)}) %collective-permute-start.12) | collective-permute-done | bytes 262176 | tf_op jit(solution)/shard_map/ppermute | solution.py:93
  160.0 1.2 shard_map.37.place
  161.2 0.0 all-gather.2.cloned.1.call-done.refs_12_
  161.2 0.0 copy-start
  161.3 1.6 copy-done
  162.8 0.0 copy-start.1
  162.8 0.7 copy-done.1
  163.5 4.1 %shard_map.39 = f32[8,128,128]{2,1,0:T(8,128)S(1)} custom-call(s32[4]{0:T(128)S(1)} %copy-done.1, s32[16,32]{1,0:T(8,128)S(1)} %copy.14.left, s32[16,32]{1,0:T(8,128)S(1)} %copy.15.right, bf16[8,128,128]{2,1,0:T(8,128)(2,1)S(1)} %get-tuple-element.61.refs_0_, bf16[8,128,128]{2,1,0:T(8,128)(2,1)} %get-tuple-element.62.refs_1_, ...), custom_call_target="tpu_custom_call" | custom-call | flops 1073741824 | bytes 8388608 | tf_op jit(solution)/shard_map/pallas_call | solution.py:57
  167.6 1.9 collective-permute-start.13
  169.5 4.1 %shard_map.38 = f32[8,128,128]{2,1,0:T(8,128)S(1)} custom-call(s32[4]{0:T(128)S(1)} %copy-done.1, s32[16,32]{1,0:T(8,128)S(1)} %copy.14.left, s32[16,32]{1,0:T(8,128)S(1)} %copy.15.right, bf16[8,128,128]{2,1,0:T(8,128)(2,1)S(1)} %get-tuple-element.61.refs_0_, bf16[8,128,128]{2,1,0:T(8,128)(2,1)} %get-tuple-element.62.refs_1_, ...), custom_call_target="tpu_custom_call" | custom-call | flops 1073741824 | bytes 8388608 | tf_op jit(solution)/shard_map/pallas_call | solution.py:57
  173.7 0.0 collective-permute-done.13
  173.7 4.5 %collective-permute-start.14 = (f32[4,128,128]{2,1,0:T(8,128)S(1)}, f32[4,128,128]{2,1,0:T(8,128)S(1)}, u32[]{:S(2)}, u32[]{:S(2)}) collective-permute-start(f32[4,128,128]{2,1,0:T(8,128)S(1)} %slice_add_fusion), channel_id=1, source_target_pairs={{0,6},{2,4},{4,2},{6,0},{1,7},{3,5},{5,3},{7,1},{8,14},{10,12},{12... | collective-permute-start | bytes 786440 | tf_op jit(solution)/shard_map/ppermute | solution.py:130
  178.2 7.3 %collective-permute-done.14 = f32[4,128,128]{2,1,0:T(8,128)S(1)} collective-permute-done((f32[4,128,128]{2,1,0:T(8,128)S(1)}, f32[4,128,128]{2,1,0:T(8,128)S(1)}, u32[]{:S(2)}, u32[]{:S(2)}) %collective-permute-start.14) | collective-permute-done | bytes 262176 | tf_op jit(solution)/shard_map/ppermute | solution.py:130
  185.5 0.1 fusion
  185.6 2.1 %collective-permute-start.15 = (f32[2,128,128]{2,1,0:T(8,128)S(1)}, f32[2,128,128]{2,1,0:T(8,128)S(1)}, u32[]{:S(2)}, u32[]{:S(2)}) collective-permute-start(f32[2,128,128]{2,1,0:T(8,128)S(1)} %slice.37), channel_id=1, source_target_pairs={{0,2},{2,0},{4,6},{6,4},{1,3},{3,1},{5,7},{7,5},{8,10},{10,8},{12,... | collective-permute-start | bytes 393224 | tf_op jit(solution)/shard_map/ppermute | solution.py:131
  187.7 4.9 %collective-permute-done.15 = f32[2,128,128]{2,1,0:T(8,128)S(1)} collective-permute-done((f32[2,128,128]{2,1,0:T(8,128)S(1)}, f32[2,128,128]{2,1,0:T(8,128)S(1)}, u32[]{:S(2)}, u32[]{:S(2)}) %collective-permute-start.15) | collective-permute-done | bytes 131104 | tf_op jit(solution)/shard_map/ppermute | solution.py:131
  192.6 0.7 fusion.1
  (8 shorter events, 0.2 us)
Async XLA Ops:
  6.5 26.8 %all-to-all-start = ((bf16[8,128,128]{2,1,0:T(8,128)(2,1)}), bf16[8,128,128]{2,1,0:T(8,128)(2,1)S(1)}, u32[]{:S(2)}, u32[]{:S(2)}) async-start(bf16[8,128,128]{2,1,0:T(8,128)(2,1)} %bitcast.9), calls=%async_computation | async-start | bytes 524288 | tf_op jit(solution)/shard_map/all_to_all | solution.py:107
  11.0 150.2 %all-gather.2.cloned.1.call-start = ((), (), s32[]{:S(2)}) async-start(), calls=%async_computation.1 | async-start | bytes 2359296 | tf_op jit(solution)/shard_map/all_gather | solution.py:108
  11.0 69.8 %collective-permute-start.6 = (bf16[8,128,128]{2,1,0:T(8,128)(2,1)}, bf16[8,128,128]{2,1,0:T(8,128)(2,1)S(1)}, u32[]{:S(2)}, u32[]{:S(2)}) collective-permute-start(bf16[8,128,128]{2,1,0:T(8,128)(2,1)} %bitcast.10), channel_id=1, source_target_pairs={{0,24},{8,0},{16,8},{24,16},{1,25},{9,1},{17,9},{25,17},{2,26},{10... | collective-permute-start | bytes 786440 | tf_op jit(solution)/shard_map/ppermute | solution.py:105
  31.4 65.4 %collective-permute-start.7 = (bf16[8,128,128]{2,1,0:T(8,128)(2,1)}, bf16[8,128,128]{2,1,0:T(8,128)(2,1)S(1)}, u32[]{:S(2)}, u32[]{:S(2)}) collective-permute-start(bf16[8,128,128]{2,1,0:T(8,128)(2,1)} %bitcast.11), channel_id=1, source_target_pairs={{0,8},{8,16},{16,24},{24,0},{1,9},{9,17},{17,25},{25,1},{2,10},{10... | collective-permute-start | bytes 786440 | tf_op jit(solution)/shard_map/ppermute | solution.py:106
  33.3 0.7 copy-start.2
  34.0 16.5 %collective-permute-start = (bf16[8,128,128]{2,1,0:T(8,128)(2,1)}, bf16[8,128,128]{2,1,0:T(8,128)(2,1)}, u32[]{:S(2)}, u32[]{:S(2)}) collective-permute-start(bf16[8,128,128]{2,1,0:T(8,128)(2,1)} %param.1), channel_id=1, source_target_pairs={{0,96},{32,0},{64,32},{96,64},{1,97},{33,1},{65,33},{97,65},{2,98}... | collective-permute-start | bytes 786440 | tf_op jit(solution)/shard_map/cond/branch_1_fun/ppermute | solution.py:93
  38.7 12.9 %collective-permute-start.1 = (bf16[8,128,128]{2,1,0:T(8,128)(2,1)}, bf16[8,128,128]{2,1,0:T(8,128)(2,1)}, u32[]{:S(2)}, u32[]{:S(2)}) collective-permute-start(bf16[8,128,128]{2,1,0:T(8,128)(2,1)} %param.1), channel_id=1, source_target_pairs={{0,64},{32,96},{64,0},{96,32},{1,65},{33,97},{65,1},{97,33},{2,66}... | collective-permute-start | bytes 786440 | tf_op jit(solution)/shard_map/cond/branch_1_fun/ppermute | solution.py:93
  41.4 14.7 %collective-permute-start.2 = (bf16[8,128,128]{2,1,0:T(8,128)(2,1)}, bf16[8,128,128]{2,1,0:T(8,128)(2,1)}, u32[]{:S(2)}, u32[]{:S(2)}) collective-permute-start(bf16[8,128,128]{2,1,0:T(8,128)(2,1)} %param.1), channel_id=1, source_target_pairs={{0,32},{32,64},{64,96},{96,0},{1,33},{33,65},{65,97},{97,1},{2,34}... | collective-permute-start | bytes 786440 | tf_op jit(solution)/shard_map/cond/branch_1_fun/ppermute | solution.py:93
  96.8 44.4 %collective-permute-start.8 = (bf16[4,128,128]{2,1,0:T(8,128)(2,1)S(1)}, bf16[4,128,128]{2,1,0:T(8,128)(2,1)S(1)}, u32[]{:S(2)}, u32[]{:S(2)}) collective-permute-start(bf16[4,128,128]{2,1,0:T(8,128)(2,1)S(1)} %slice.24), channel_id=1, source_target_pairs={{0,24},{8,0},{16,8},{24,16},{1,25},{9,1},{17,9},{25,17},{2,26},{10... | collective-permute-start | bytes 393224 | tf_op jit(solution)/shard_map/ppermute | solution.py:113
  105.7 35.5 %collective-permute-start.9 = (bf16[4,128,128]{2,1,0:T(8,128)(2,1)S(1)}, bf16[4,128,128]{2,1,0:T(8,128)(2,1)S(1)}, u32[]{:S(2)}, u32[]{:S(2)}) collective-permute-start(bf16[4,128,128]{2,1,0:T(8,128)(2,1)S(1)} %slice.25), channel_id=1, source_target_pairs={{0,8},{8,16},{16,24},{24,0},{1,9},{9,17},{17,25},{25,1},{2,10},{10... | collective-permute-start | bytes 393224 | tf_op jit(solution)/shard_map/ppermute | solution.py:114
  111.4 37.7 %copy-start.3 = (s32[1,1,1,16,16,2]{4,5,3,2,1,0:T(2,128)S(1)}, s32[1,1,1,16,16,2]{4,5,3,2,1,0:T(2,128)}, u32[]{:S(2)}) copy-start(s32[1,1,1,16,16,2]{4,5,3,2,1,0:T(2,128)} %param.8) | copy-start | bytes 6148
  111.4 37.8 %copy-start.4 = (s32[1,1,1,16,16,2]{4,5,3,2,1,0:T(2,128)S(1)}, s32[1,1,1,16,16,2]{4,5,3,2,1,0:T(2,128)}, u32[]{:S(2)}) copy-start(s32[1,1,1,16,16,2]{4,5,3,2,1,0:T(2,128)} %param.9) | copy-start | bytes 6148
  111.5 24.0 %collective-permute-start.3 = (bf16[16,128,128]{2,1,0:T(8,128)(2,1)S(1)}, bf16[16,128,128]{2,1,0:T(8,128)(2,1)}, u32[]{:S(2)}, u32[]{:S(2)}) collective-permute-start(bf16[16,128,128]{2,1,0:T(8,128)(2,1)S(1)} %param.3), channel_id=1, source_target_pairs={{0,96},{32,0},{64,32},{96,64},{1,97},{33,1},{65,33},{97,65},{2,98}... | collective-permute-start | bytes 1572872 | tf_op jit(solution)/shard_map/cond/branch_1_fun/ppermute | solution.py:93
  116.4 19.0 %collective-permute-start.4 = (bf16[16,128,128]{2,1,0:T(8,128)(2,1)S(1)}, bf16[16,128,128]{2,1,0:T(8,128)(2,1)}, u32[]{:S(2)}, u32[]{:S(2)}) collective-permute-start(bf16[16,128,128]{2,1,0:T(8,128)(2,1)S(1)} %param.3), channel_id=1, source_target_pairs={{0,64},{32,96},{64,0},{96,32},{1,65},{33,97},{65,1},{97,33},{2,66}... | collective-permute-start | bytes 1572872 | tf_op jit(solution)/shard_map/cond/branch_1_fun/ppermute | solution.py:93
  119.0 22.1 %collective-permute-start.5 = (bf16[16,128,128]{2,1,0:T(8,128)(2,1)S(1)}, bf16[16,128,128]{2,1,0:T(8,128)(2,1)}, u32[]{:S(2)}, u32[]{:S(2)}) collective-permute-start(bf16[16,128,128]{2,1,0:T(8,128)(2,1)S(1)} %param.3), channel_id=1, source_target_pairs={{0,32},{32,64},{64,96},{96,0},{1,33},{33,65},{65,97},{97,1},{2,34}... | collective-permute-start | bytes 1572872 | tf_op jit(solution)/shard_map/cond/branch_1_fun/ppermute | solution.py:93
  141.2 11.1 %collective-permute-start.10 = (bf16[8,128,128]{2,1,0:T(8,128)(2,1)S(1)}, bf16[8,128,128]{2,1,0:T(8,128)(2,1)S(1)}, u32[]{:S(2)}, u32[]{:S(2)}) collective-permute-start(bf16[8,128,128]{2,1,0:T(8,128)(2,1)S(1)} %constant_dynamic-update-slice_fusion.refs_8_), channel_id=1, source_target_pairs={{0,96},{32,0},{64,32},{96,64},{1,97},{33,1},{65,33},{97,65},{2,98}... | collective-permute-start | bytes 786440 | tf_op jit(solution)/shard_map/ppermute | solution.py:93
  143.7 12.3 %collective-permute-start.11 = (bf16[8,128,128]{2,1,0:T(8,128)(2,1)S(1)}, bf16[8,128,128]{2,1,0:T(8,128)(2,1)S(1)}, u32[]{:S(2)}, u32[]{:S(2)}) collective-permute-start(bf16[8,128,128]{2,1,0:T(8,128)(2,1)S(1)} %constant_dynamic-update-slice_fusion.refs_8_), channel_id=1, source_target_pairs={{0,64},{32,96},{64,0},{96,32},{1,65},{33,97},{65,1},{97,33},{2,66}... | collective-permute-start | bytes 786440 | tf_op jit(solution)/shard_map/ppermute | solution.py:93
  146.4 13.6 %collective-permute-start.12 = (bf16[8,128,128]{2,1,0:T(8,128)(2,1)S(1)}, bf16[8,128,128]{2,1,0:T(8,128)(2,1)S(1)}, u32[]{:S(2)}, u32[]{:S(2)}) collective-permute-start(bf16[8,128,128]{2,1,0:T(8,128)(2,1)S(1)} %constant_dynamic-update-slice_fusion.refs_8_), channel_id=1, source_target_pairs={{0,32},{32,64},{64,96},{96,0},{1,33},{33,65},{65,97},{97,1},{2,34}... | collective-permute-start | bytes 786440 | tf_op jit(solution)/shard_map/ppermute | solution.py:93
  161.2 1.6 copy-start
  162.8 0.7 copy-start.1
  167.6 6.1 %collective-permute-start.13 = (f32[8,128,128]{2,1,0:T(8,128)S(1)}, f32[8,128,128]{2,1,0:T(8,128)S(1)}, u32[]{:S(2)}, u32[]{:S(2)}) collective-permute-start(f32[8,128,128]{2,1,0:T(8,128)S(1)} %shard_map.39), channel_id=1, source_target_pairs={{0,1},{1,0},{2,3},{3,2},{4,5},{5,4},{6,7},{7,6},{8,9},{9,8},{10,11... | collective-permute-start | bytes 1572872 | tf_op jit(solution)/shard_map/ppermute | solution.py:125
  173.7 11.8 %collective-permute-start.14 = (f32[4,128,128]{2,1,0:T(8,128)S(1)}, f32[4,128,128]{2,1,0:T(8,128)S(1)}, u32[]{:S(2)}, u32[]{:S(2)}) collective-permute-start(f32[4,128,128]{2,1,0:T(8,128)S(1)} %slice_add_fusion), channel_id=1, source_target_pairs={{0,6},{2,4},{4,2},{6,0},{1,7},{3,5},{5,3},{7,1},{8,14},{10,12},{12... | collective-permute-start | bytes 786440 | tf_op jit(solution)/shard_map/ppermute | solution.py:130
  185.6 7.0 %collective-permute-start.15 = (f32[2,128,128]{2,1,0:T(8,128)S(1)}, f32[2,128,128]{2,1,0:T(8,128)S(1)}, u32[]{:S(2)}, u32[]{:S(2)}) collective-permute-start(f32[2,128,128]{2,1,0:T(8,128)S(1)} %slice.37), channel_id=1, source_target_pairs={{0,2},{2,0},{4,6},{6,4},{1,3},{3,1},{5,7},{7,5},{8,10},{10,8},{12,... | collective-permute-start | bytes 393224 | tf_op jit(solution)/shard_map/ppermute | solution.py:131
Sparse Core Ops, SparseCore 0:
  34.1 110.4 all-gather.1

commit v6 on v5

--- a/solution.py
+++ b/solution.py
@@ -12,7 +12,7 @@
 S, SLOTS, R, BS = 8, 2, 16, 128
 COLS = X * ZH
 PER = R // (Y * CORE)
-WEIGHT = 32 * 10**9
+WEIGHT = 36 * 10**9
 
 
 def ring(n, k):
@@ -45,8 +45,7 @@
 
     @pl.loop(0, Y * PER, unroll=8)
     def _(k):
-        d = k // PER
-        to = y ^ d ^ (d >> 1)
+        to = lax.rem(y + k // PER, Y)
         mine = lax.rem(core + other, CORE)
         out[k] = one((to * CORE + mine) * PER + lax.rem(k, PER))
 
@@ -105,18 +104,20 @@
     z1 = lax.ppermute(own, "zh", ring(ZH, -1))
     z3 = lax.ppermute(own, "zh", ring(ZH, 1))
     routed = lax.all_to_all(own, ("y", "core"), split_axis=0, concat_axis=0, tiled=True)
+    own_x = fenced(over_x, own)
+    own_x, routed = together(own_x, routed)
     b = lax.all_gather(routed, "row", axis=0, tiled=True)
-    own_x = fenced(over_x, own)
-    z1, z3, own_x, _ = together(z1, z3, own_x, routed)
+    z1, z3, own_x, routed = together(z1, z3, own_x, routed)
 
     half = S // 2
     z2_low = lax.ppermute(z1[:half], "zh", ring(ZH, -1))
     z2_high = lax.ppermute(z3[half:], "zh", ring(ZH, 1))
     near = fenced(over_x, jnp.concatenate([z1, z3]))
-    z2_low, z2_high, near = together(z2_low, z2_high, near)
+    place, _ = passing(place, WEIGHT, z1, z3)
+    z2_low, z2_high, near, place = together(z2_low, z2_high, near, place)
     far = over_x(jnp.concatenate([z2_low, z2_high]))
 
-    place, arrays = passing(place, WEIGHT, *own_x, *near, *far)
+    arrays = own_x + near + far
     lists = (place, left, right)
     groups = [(d, 0, d, 0) for d in range(X)]
     groups += [(X + d, k * S, d, z) for k, z in enumerate((1, 3)) for d in range(X)]
@@ -125,10 +126,10 @@
     got = lax.ppermute(send, "core", ring(CORE, 1))
     keep = call(groups, 0, lists, arrays, b)
 
-    half = R // 4
-    mine, others = keep[:half] + got[:half], keep[half:] + got[half:]
-    mine = mine + lax.ppermute(others, "y", [(k, k ^ 3) for k in range(Y)])
-    total = mine[:PER] + lax.ppermute(mine[PER:], "y", [(k, k ^ 1) for k in range(Y)])
+    quarter = [keep[d * PER : (d + 1) * PER] + got[d * PER : (d + 1) * PER] for d in range(Y)]
+    total = quarter[0]
+    for d in range(1, Y):
+        total = total + lax.ppermute(quarter[d], "y", ring(Y, d))
     return total[None, None]
 
 

time: 201 us -> 192 us (0.955)
  the two profiles are of different devices: /device:TPU:96 before, /device:TPU:1 now
where the time goes in v6:
time: 192 us; the launch traced here: 191 us
  starting transfers between devices  94.2 us (49%)
  waiting for transfers between devices  68.3 us (36%)
  between operations  13.6 us (7%)
  Pallas kernels  9.47 us (5%)
  local copies, waits for them, and re-layouts  3.64 us (2%)
    ppermute x9, waiting for transfers between devices, over_x(): lax.ppermute(value, 'x', ring(X, -d))  37.7 us
    ppermute x9, starting transfers between devices, over_x(): lax.ppermute(value, 'x', ring(X, -d))  24.7 us
    ppermute x1, starting transfers between devices, on_device(): z1 = lax.ppermute(own, 'zh', ring(ZH, -1))  23.5 us
    ppermute x1, starting transfers between devices, on_device(): z2_low = lax.ppermute(z1[:half], 'zh', ring(ZH, -1))  18.8 us
    all_gather x1, waiting for transfers between devices, on_device(): b = lax.all_gather(routed, 'row', axis=0, tiled=True)  18.5 us
    ppermute x3, starting transfers between devices, on_device(): total = total + lax.ppermute(quarter[d], 'y', ring(Y, d))  12.1 us
    ppermute x1, waiting for transfers between devices, on_device(): z1 = lax.ppermute(own, 'zh', ring(ZH, -1))  8.67 us
    pallas_call x2, Pallas kernels, call(): pl.pallas_call(functools.partial(products, groups, other), out_shape=jax....  8.28 us
  transfers between devices with their start and end apart: 19, of which 12 were waited for; matrix products, arithmetic and copies ran while one was open for 1% of the time, Pallas kernels for 3%

profile of v6, /device:TPU:1, one launch (start us, length us, event | category | flops | bytes accessed | tf_op | source)
XLA Modules:
  0.0 190.7 jit_solution(13584957662709735359)
XLA Ops:
  6.5 23.5 %collective-permute-start.6 = (bf16[8,128,128]{2,1,0:T(8,128)(2,1)}, bf16[8,128,128]{2,1,0:T(8,128)(2,1)S(1)}, u32[]{:S(2)}, u32[]{:S(2)}) collective-permute-start(bf16[8,128,128]{2,1,0:T(8,128)(2,1)} %bitcast.9), channel_id=1, source_target_pairs={{0,24},{8,0},{16,8},{24,16},{1,25},{9,1},{17,9},{25,17},{2,26},{10... | collective-permute-start | bytes 786440 | tf_op jit(solution)/shard_map/ppermute | solution.py:104
  30.1 1.9 %collective-permute-start.7 = (bf16[8,128,128]{2,1,0:T(8,128)(2,1)}, bf16[8,128,128]{2,1,0:T(8,128)(2,1)S(1)}, u32[]{:S(2)}, u32[]{:S(2)}) collective-permute-start(bf16[8,128,128]{2,1,0:T(8,128)(2,1)} %bitcast.10), channel_id=1, source_target_pairs={{0,8},{8,16},{16,24},{24,0},{1,9},{9,17},{17,25},{25,1},{2,10},{10... | collective-permute-start | bytes 786440 | tf_op jit(solution)/shard_map/ppermute | solution.py:105
  32.0 6.6 %all-to-all-start = ((bf16[8,128,128]{2,1,0:T(8,128)(2,1)}), bf16[8,128,128]{2,1,0:T(8,128)(2,1)S(1)}, u32[]{:S(2)}, u32[]{:S(2)}) async-start(bf16[8,128,128]{2,1,0:T(8,128)(2,1)} %bitcast.11), calls=%async_computation | async-start | bytes 524288 | tf_op jit(solution)/shard_map/all_to_all | solution.py:106
  38.6 0.0 all-gather.2.cloned.1.call-start
  38.6 20.8 %conditional.2 = (bf16[8,128,128]{2,1,0:T(8,128)(2,1)S(1)}, bf16[8,128,128]{2,1,0:T(8,128)(2,1)}, bf16[8,128,128]{2,1,0:T(8,128)(2,1)}, bf16[8,128,128]{2,1,0:T(8,128)(2,1)}) conditional(s32[]{:T(128)} %convert_element_type.4, () %tuple.25, bf16[8,128,128]{2,1,0:T(8,128)(2,1)} %bitcast.12), branch_computations={%region_0.0_spmd, %region_1.0_spmd} | conditional | bytes 3670168 | solution.py:98
  38.6 3.2 %collective-permute-start = (bf16[8,128,128]{2,1,0:T(8,128)(2,1)}, bf16[8,128,128]{2,1,0:T(8,128)(2,1)}, u32[]{:S(2)}, u32[]{:S(2)}) collective-permute-start(bf16[8,128,128]{2,1,0:T(8,128)(2,1)} %param.1), channel_id=1, source_target_pairs={{0,96},{32,0},{64,32},{96,64},{1,97},{33,1},{65,33},{97,65},{2,98}... | collective-permute-start | bytes 786440 | tf_op jit(solution)/shard_map/cond/branch_1_fun/ppermute | solution.py:92
  41.8 2.4 %collective-permute-start.1 = (bf16[8,128,128]{2,1,0:T(8,128)(2,1)}, bf16[8,128,128]{2,1,0:T(8,128)(2,1)}, u32[]{:S(2)}, u32[]{:S(2)}) collective-permute-start(bf16[8,128,128]{2,1,0:T(8,128)(2,1)} %param.1), channel_id=1, source_target_pairs={{0,64},{32,96},{64,0},{96,32},{1,65},{33,97},{65,1},{97,33},{2,66}... | collective-permute-start | bytes 786440 | tf_op jit(solution)/shard_map/cond/branch_1_fun/ppermute | solution.py:92
  44.3 2.5 %collective-permute-start.2 = (bf16[8,128,128]{2,1,0:T(8,128)(2,1)}, bf16[8,128,128]{2,1,0:T(8,128)(2,1)}, u32[]{:S(2)}, u32[]{:S(2)}) collective-permute-start(bf16[8,128,128]{2,1,0:T(8,128)(2,1)} %param.1), channel_id=1, source_target_pairs={{0,32},{32,64},{64,96},{96,0},{1,33},{33,65},{65,97},{97,1},{2,34}... | collective-permute-start | bytes 786440 | tf_op jit(solution)/shard_map/cond/branch_1_fun/ppermute | solution.py:92
  46.8 1.0 copy.22
  47.8 0.8 collective-permute-done
  48.5 4.6 %collective-permute-done.1 = bf16[8,128,128]{2,1,0:T(8,128)(2,1)} collective-permute-done((bf16[8,128,128]{2,1,0:T(8,128)(2,1)}, bf16[8,128,128]{2,1,0:T(8,128)(2,1)}, u32[]{:S(2)}, u32[]{:S(2)}) %collective-permute-start.1) | collective-permute-done | bytes 262176 | tf_op jit(solution)/shard_map/cond/branch_1_fun/ppermute | solution.py:92
  53.1 6.3 %collective-permute-done.2 = bf16[8,128,128]{2,1,0:T(8,128)(2,1)} collective-permute-done((bf16[8,128,128]{2,1,0:T(8,128)(2,1)}, bf16[8,128,128]{2,1,0:T(8,128)(2,1)}, u32[]{:S(2)}, u32[]{:S(2)}) %collective-permute-start.2) | collective-permute-done | bytes 262176 | tf_op jit(solution)/shard_map/cond/branch_1_fun/ppermute | solution.py:92
  59.4 0.6 pad_add_fusion.place_ref
  60.0 0.0 all-to-all-done
  60.0 0.0 copy-start.2
  60.0 0.7 copy-done.2
  60.7 0.0 all-gather.2.cloned.1.call-update
  60.7 8.7 %collective-permute-done.6 = bf16[8,128,128]{2,1,0:T(8,128)(2,1)S(1)} collective-permute-done((bf16[8,128,128]{2,1,0:T(8,128)(2,1)}, bf16[8,128,128]{2,1,0:T(8,128)(2,1)S(1)}, u32[]{:S(2)}, u32[]{:S(2)}) %collective-permute-start.6) | collective-permute-done | bytes 262176 | tf_op jit(solution)/shard_map/ppermute | solution.py:104
  69.4 0.0 collective-permute-done.7
  69.4 18.8 %collective-permute-start.8 = (bf16[4,128,128]{2,1,0:T(8,128)(2,1)S(1)}, bf16[4,128,128]{2,1,0:T(8,128)(2,1)S(1)}, u32[]{:S(2)}, u32[]{:S(2)}) collective-permute-start(bf16[4,128,128]{2,1,0:T(8,128)(2,1)S(1)} %slice.30), channel_id=1, source_target_pairs={{0,24},{8,0},{16,8},{24,16},{1,25},{9,1},{17,9},{25,17},{2,26},{10... | collective-permute-start | bytes 393224 | tf_op jit(solution)/shard_map/ppermute | solution.py:113
  88.2 1.9 %collective-permute-start.9 = (bf16[4,128,128]{2,1,0:T(8,128)(2,1)S(1)}, bf16[4,128,128]{2,1,0:T(8,128)(2,1)S(1)}, u32[]{:S(2)}, u32[]{:S(2)}) collective-permute-start(bf16[4,128,128]{2,1,0:T(8,128)(2,1)S(1)} %slice.31), channel_id=1, source_target_pairs={{0,8},{8,16},{16,24},{24,0},{1,9},{9,17},{17,25},{25,1},{2,10},{10... | collective-permute-start | bytes 393224 | tf_op jit(solution)/shard_map/ppermute | solution.py:114
  90.2 1.2 shard_map.37.place
  91.4 0.0 copy-start.3
  91.4 0.0 copy-start.4
  91.4 0.0 copy-start.1
  91.4 29.2 %conditional.3 = (bf16[16,128,128]{2,1,0:T(8,128)(2,1)S(1)}, bf16[16,128,128]{2,1,0:T(8,128)(2,1)}, bf16[16,128,128]{2,1,0:T(8,128)(2,1)}, bf16[16,128,128]{2,1,0:T(8,128)(2,1)}) conditional(s32[]{:T(128)} %convert_element_type.4, () %tuple.28, bf16[16,128,128]{2,1,0:T(8,128)(2,1)S(1)} %pad_maximum_fusion), branch_computations={%region_2.0_spmd, %region_3.0_spmd} | conditional | bytes 7340184 | solution.py:98
  91.4 4.4 %collective-permute-start.3 = (bf16[16,128,128]{2,1,0:T(8,128)(2,1)S(1)}, bf16[16,128,128]{2,1,0:T(8,128)(2,1)}, u32[]{:S(2)}, u32[]{:S(2)}) collective-permute-start(bf16[16,128,128]{2,1,0:T(8,128)(2,1)S(1)} %param.3), channel_id=1, source_target_pairs={{0,96},{32,0},{64,32},{96,64},{1,97},{33,1},{65,33},{97,65},{2,98}... | collective-permute-start | bytes 1572872 | tf_op jit(solution)/shard_map/cond/branch_1_fun/ppermute | solution.py:92
  95.8 2.4 %collective-permute-start.4 = (bf16[16,128,128]{2,1,0:T(8,128)(2,1)S(1)}, bf16[16,128,128]{2,1,0:T(8,128)(2,1)}, u32[]{:S(2)}, u32[]{:S(2)}) collective-permute-start(bf16[16,128,128]{2,1,0:T(8,128)(2,1)S(1)} %param.3), channel_id=1, source_target_pairs={{0,64},{32,96},{64,0},{96,32},{1,65},{33,97},{65,1},{97,33},{2,66}... | collective-permute-start | bytes 1572872 | tf_op jit(solution)/shard_map/cond/branch_1_fun/ppermute | solution.py:92
  98.3 2.5 %collective-permute-start.5 = (bf16[16,128,128]{2,1,0:T(8,128)(2,1)S(1)}, bf16[16,128,128]{2,1,0:T(8,128)(2,1)}, u32[]{:S(2)}, u32[]{:S(2)}) collective-permute-start(bf16[16,128,128]{2,1,0:T(8,128)(2,1)S(1)} %param.3), channel_id=1, source_target_pairs={{0,32},{32,64},{64,96},{96,0},{1,33},{33,65},{65,97},{97,1},{2,34}... | collective-permute-start | bytes 1572872 | tf_op jit(solution)/shard_map/cond/branch_1_fun/ppermute | solution.py:92
  100.8 4.2 %collective-permute-done.3 = bf16[16,128,128]{2,1,0:T(8,128)(2,1)} collective-permute-done((bf16[16,128,128]{2,1,0:T(8,128)(2,1)S(1)}, bf16[16,128,128]{2,1,0:T(8,128)(2,1)}, u32[]{:S(2)}, u32[]{:S(2)}) %collective-permute-start.3) | collective-permute-done | bytes 524320 | tf_op jit(solution)/shard_map/cond/branch_1_fun/ppermute | solution.py:92
  105.1 2.7 %collective-permute-done.4 = bf16[16,128,128]{2,1,0:T(8,128)(2,1)} collective-permute-done((bf16[16,128,128]{2,1,0:T(8,128)(2,1)S(1)}, bf16[16,128,128]{2,1,0:T(8,128)(2,1)}, u32[]{:S(2)}, u32[]{:S(2)}) %collective-permute-start.4) | collective-permute-done | bytes 524320 | tf_op jit(solution)/shard_map/cond/branch_1_fun/ppermute | solution.py:92
  107.7 13.0 %collective-permute-done.5 = bf16[16,128,128]{2,1,0:T(8,128)(2,1)} collective-permute-done((bf16[16,128,128]{2,1,0:T(8,128)(2,1)S(1)}, bf16[16,128,128]{2,1,0:T(8,128)(2,1)}, u32[]{:S(2)}, u32[]{:S(2)}) %collective-permute-start.5) | collective-permute-done | bytes 524320 | tf_op jit(solution)/shard_map/cond/branch_1_fun/ppermute | solution.py:92
  120.7 0.0 collective-permute-done.8
  120.7 0.0 collective-permute-done.9
  120.7 1.9 %collective-permute-start.10 = (bf16[8,128,128]{2,1,0:T(8,128)(2,1)S(1)}, bf16[8,128,128]{2,1,0:T(8,128)(2,1)S(1)}, u32[]{:S(2)}, u32[]{:S(2)}) collective-permute-start(bf16[8,128,128]{2,1,0:T(8,128)(2,1)S(1)} %constant_dynamic-update-slice_fusion.refs_8_), channel_id=1, source_target_pairs={{0,96},{32,0},{64,32},{96,64},{1,97},{33,1},{65,33},{97,65},{2,98}... | collective-permute-start | bytes 786440 | tf_op jit(solution)/shard_map/ppermute | solution.py:92
  122.7 2.5 %collective-permute-start.11 = (bf16[8,128,128]{2,1,0:T(8,128)(2,1)S(1)}, bf16[8,128,128]{2,1,0:T(8,128)(2,1)S(1)}, u32[]{:S(2)}, u32[]{:S(2)}) collective-permute-start(bf16[8,128,128]{2,1,0:T(8,128)(2,1)S(1)} %constant_dynamic-update-slice_fusion.refs_8_), channel_id=1, source_target_pairs={{0,64},{32,96},{64,0},{96,32},{1,65},{33,97},{65,1},{97,33},{2,66}... | collective-permute-start | bytes 786440 | tf_op jit(solution)/shard_map/ppermute | solution.py:92
  125.2 2.8 %collective-permute-start.12 = (bf16[8,128,128]{2,1,0:T(8,128)(2,1)S(1)}, bf16[8,128,128]{2,1,0:T(8,128)(2,1)S(1)}, u32[]{:S(2)}, u32[]{:S(2)}) collective-permute-start(bf16[8,128,128]{2,1,0:T(8,128)(2,1)S(1)} %constant_dynamic-update-slice_fusion.refs_8_), channel_id=1, source_target_pairs={{0,32},{32,64},{64,96},{96,0},{1,33},{33,65},{65,97},{97,1},{2,34}... | collective-permute-start | bytes 786440 | tf_op jit(solution)/shard_map/ppermute | solution.py:92
  128.0 0.0 copy-done.3
  128.0 0.1 copy.12
  128.1 0.1 copy.14.left
  128.1 0.0 copy-done.4
  128.1 0.1 copy.13
  128.2 0.1 copy.15.right
  128.3 0.0 collective-permute-done.10.refs_9_
  128.3 3.4 %collective-permute-done.11.refs_10_ = bf16[8,128,128]{2,1,0:T(8,128)(2,1)S(1)} collective-permute-done((bf16[8,128,128]{2,1,0:T(8,128)(2,1)S(1)}, bf16[8,128,128]{2,1,0:T(8,128)(2,1)S(1)}, u32[]{:S(2)}, u32[]{:S(2)}) %collective-permute-start.11) | collective-permute-done | bytes 262176 | tf_op jit(solution)/shard_map/ppermute | solution.py:92
  131.7 2.8 %collective-permute-done.12.refs_11_ = bf16[8,128,128]{2,1,0:T(8,128)(2,1)S(1)} collective-permute-done((bf16[8,128,128]{2,1,0:T(8,128)(2,1)S(1)}, bf16[8,128,128]{2,1,0:T(8,128)(2,1)S(1)}, u32[]{:S(2)}, u32[]{:S(2)}) %collective-permute-start.12) | collective-permute-done | bytes 262176 | tf_op jit(solution)/shard_map/ppermute | solution.py:92
  134.5 18.5 %all-gather.2.cloned.1.call-done.refs_12_ = bf16[64,128,128]{2,1,0:T(8,128)(2,1)} async-done(((bf16[8,128,128]{2,1,0:T(8,128)(2,1)}), bf16[64,128,128]{2,1,0:T(8,128)(2,1)}) %all-gather.2.cloned.1.call-update) | async-done | bytes 2097168 | tf_op jit(solution)/shard_map/all_gather | solution.py:109
  153.0 0.0 copy-done.1
  153.0 0.0 copy-start
  153.0 1.6 copy-done
  154.6 4.2 %shard_map.39 = f32[8,128,128]{2,1,0:T(8,128)S(1)} custom-call(s32[4]{0:T(128)S(1)} %copy-done.1, s32[16,32]{1,0:T(8,128)S(1)} %copy.14.left, s32[16,32]{1,0:T(8,128)S(1)} %copy.15.right, bf16[8,128,128]{2,1,0:T(8,128)(2,1)S(1)} %get-tuple-element.51.refs_0_, bf16[8,128,128]{2,1,0:T(8,128)(2,1)} %get-tuple-element.52.refs_1_, ...), custom_call_target="tpu_custom_call" | custom-call | flops 1073741824 | bytes 8388608 | tf_op jit(solution)/shard_map/pallas_call | solution.py:56
  158.7 4.6 %collective-permute-start.13 = (f32[8,128,128]{2,1,0:T(8,128)S(1)}, f32[8,128,128]{2,1,0:T(8,128)S(1)}, u32[]{:S(2)}, u32[]{:S(2)}) collective-permute-start(f32[8,128,128]{2,1,0:T(8,128)S(1)} %shard_map.39), channel_id=1, source_target_pairs={{0,1},{1,0},{2,3},{3,2},{4,5},{5,4},{6,7},{7,6},{8,9},{9,8},{10,11... | collective-permute-start | bytes 1572872 | tf_op jit(solution)/shard_map/ppermute | solution.py:126
  163.4 4.1 %shard_map.38 = f32[8,128,128]{2,1,0:T(8,128)S(1)} custom-call(s32[4]{0:T(128)S(1)} %copy-done.1, s32[16,32]{1,0:T(8,128)S(1)} %copy.14.left, s32[16,32]{1,0:T(8,128)S(1)} %copy.15.right, bf16[8,128,128]{2,1,0:T(8,128)(2,1)S(1)} %get-tuple-element.51.refs_0_, bf16[8,128,128]{2,1,0:T(8,128)(2,1)} %get-tuple-element.52.refs_1_, ...), custom_call_target="tpu_custom_call" | custom-call | flops 1073741824 | bytes 8388608 | tf_op jit(solution)/shard_map/pallas_call | solution.py:56
  167.5 0.0 collective-permute-done.13
  167.6 4.6 %collective-permute-start.14 = (f32[2,128,128]{2,1,0:T(8,128)S(1)}, f32[2,128,128]{2,1,0:T(8,128)S(1)}, u32[]{:S(2)}, u32[]{:S(2)}) collective-permute-start(f32[2,128,128]{2,1,0:T(8,128)S(1)} %get-tuple-element.61), channel_id=1, source_target_pairs={{0,2},{2,4},{4,6},{6,0},{1,3},{3,5},{5,7},{7,1},{8,10},{10,12},{12... | collective-permute-start | bytes 393224 | tf_op jit(solution)/shard_map/ppermute | solution.py:132
  172.2 4.6 %collective-permute-start.15 = (f32[2,128,128]{2,1,0:T(8,128)S(1)}, f32[2,128,128]{2,1,0:T(8,128)S(1)}, u32[]{:S(2)}, u32[]{:S(2)}) collective-permute-start(f32[2,128,128]{2,1,0:T(8,128)S(1)} %get-tuple-element.63), channel_id=1, source_target_pairs={{0,4},{2,6},{4,0},{6,2},{1,5},{3,7},{5,1},{7,3},{8,12},{10,14},{12... | collective-permute-start | bytes 393224 | tf_op jit(solution)/shard_map/ppermute | solution.py:132
  176.8 2.9 %collective-permute-start.16 = (f32[2,128,128]{2,1,0:T(8,128)S(1)}, f32[2,128,128]{2,1,0:T(8,128)S(1)}, u32[]{:S(2)}, u32[]{:S(2)}) collective-permute-start(f32[2,128,128]{2,1,0:T(8,128)S(1)} %get-tuple-element.62), channel_id=1, source_target_pairs={{0,6},{2,0},{4,2},{6,4},{1,7},{3,1},{5,3},{7,5},{8,14},{10,8},{12,... | collective-permute-start | bytes 393224 | tf_op jit(solution)/shard_map/ppermute | solution.py:132
  179.7 0.0 collective-permute-done.14
  179.7 1.6 collective-permute-done.15
  181.3 1.9 collective-permute-done.16
  183.2 0.7 fusion.3
  (7 shorter events, 0.2 us)
Async XLA Ops:
  6.5 62.8 %collective-permute-start.6 = (bf16[8,128,128]{2,1,0:T(8,128)(2,1)}, bf16[8,128,128]{2,1,0:T(8,128)(2,1)S(1)}, u32[]{:S(2)}, u32[]{:S(2)}) collective-permute-start(bf16[8,128,128]{2,1,0:T(8,128)(2,1)} %bitcast.9), channel_id=1, source_target_pairs={{0,24},{8,0},{16,8},{24,16},{1,25},{9,1},{17,9},{25,17},{2,26},{10... | collective-permute-start | bytes 786440 | tf_op jit(solution)/shard_map/ppermute | solution.py:104
  30.1 39.3 %collective-permute-start.7 = (bf16[8,128,128]{2,1,0:T(8,128)(2,1)}, bf16[8,128,128]{2,1,0:T(8,128)(2,1)S(1)}, u32[]{:S(2)}, u32[]{:S(2)}) collective-permute-start(bf16[8,128,128]{2,1,0:T(8,128)(2,1)} %bitcast.10), channel_id=1, source_target_pairs={{0,8},{8,16},{16,24},{24,0},{1,9},{9,17},{17,25},{25,1},{2,10},{10... | collective-permute-start | bytes 786440 | tf_op jit(solution)/shard_map/ppermute | solution.py:105
  32.0 28.0 %all-to-all-start = ((bf16[8,128,128]{2,1,0:T(8,128)(2,1)}), bf16[8,128,128]{2,1,0:T(8,128)(2,1)S(1)}, u32[]{:S(2)}, u32[]{:S(2)}) async-start(bf16[8,128,128]{2,1,0:T(8,128)(2,1)} %bitcast.11), calls=%async_computation | async-start | bytes 524288 | tf_op jit(solution)/shard_map/all_to_all | solution.py:106
  38.6 114.4 %all-gather.2.cloned.1.call-start = ((), (), s32[]{:S(2)}) async-start(), calls=%async_computation.1 | async-start | bytes 2359296 | tf_op jit(solution)/shard_map/all_gather | solution.py:109
  38.6 9.9 %collective-permute-start = (bf16[8,128,128]{2,1,0:T(8,128)(2,1)}, bf16[8,128,128]{2,1,0:T(8,128)(2,1)}, u32[]{:S(2)}, u32[]{:S(2)}) collective-permute-start(bf16[8,128,128]{2,1,0:T(8,128)(2,1)} %param.1), channel_id=1, source_target_pairs={{0,96},{32,0},{64,32},{96,64},{1,97},{33,1},{65,33},{97,65},{2,98}... | collective-permute-start | bytes 786440 | tf_op jit(solution)/shard_map/cond/branch_1_fun/ppermute | solution.py:92
  41.8 11.3 %collective-permute-start.1 = (bf16[8,128,128]{2,1,0:T(8,128)(2,1)}, bf16[8,128,128]{2,1,0:T(8,128)(2,1)}, u32[]{:S(2)}, u32[]{:S(2)}) collective-permute-start(bf16[8,128,128]{2,1,0:T(8,128)(2,1)} %param.1), channel_id=1, source_target_pairs={{0,64},{32,96},{64,0},{96,32},{1,65},{33,97},{65,1},{97,33},{2,66}... | collective-permute-start | bytes 786440 | tf_op jit(solution)/shard_map/cond/branch_1_fun/ppermute | solution.py:92
  44.3 15.1 %collective-permute-start.2 = (bf16[8,128,128]{2,1,0:T(8,128)(2,1)}, bf16[8,128,128]{2,1,0:T(8,128)(2,1)}, u32[]{:S(2)}, u32[]{:S(2)}) collective-permute-start(bf16[8,128,128]{2,1,0:T(8,128)(2,1)} %param.1), channel_id=1, source_target_pairs={{0,32},{32,64},{64,96},{96,0},{1,33},{33,65},{65,97},{97,1},{2,34}... | collective-permute-start | bytes 786440 | tf_op jit(solution)/shard_map/cond/branch_1_fun/ppermute | solution.py:92
  60.0 0.7 copy-start.2
  69.4 51.3 %collective-permute-start.8 = (bf16[4,128,128]{2,1,0:T(8,128)(2,1)S(1)}, bf16[4,128,128]{2,1,0:T(8,128)(2,1)S(1)}, u32[]{:S(2)}, u32[]{:S(2)}) collective-permute-start(bf16[4,128,128]{2,1,0:T(8,128)(2,1)S(1)} %slice.30), channel_id=1, source_target_pairs={{0,24},{8,0},{16,8},{24,16},{1,25},{9,1},{17,9},{25,17},{2,26},{10... | collective-permute-start | bytes 393224 | tf_op jit(solution)/shard_map/ppermute | solution.py:113
  88.2 32.5 %collective-permute-start.9 = (bf16[4,128,128]{2,1,0:T(8,128)(2,1)S(1)}, bf16[4,128,128]{2,1,0:T(8,128)(2,1)S(1)}, u32[]{:S(2)}, u32[]{:S(2)}) collective-permute-start(bf16[4,128,128]{2,1,0:T(8,128)(2,1)S(1)} %slice.31), channel_id=1, source_target_pairs={{0,8},{8,16},{16,24},{24,0},{1,9},{9,17},{17,25},{25,1},{2,10},{10... | collective-permute-start | bytes 393224 | tf_op jit(solution)/shard_map/ppermute | solution.py:114
  91.4 36.6 %copy-start.3 = (s32[1,1,1,16,16,2]{4,5,3,2,1,0:T(2,128)S(1)}, s32[1,1,1,16,16,2]{4,5,3,2,1,0:T(2,128)}, u32[]{:S(2)}) copy-start(s32[1,1,1,16,16,2]{4,5,3,2,1,0:T(2,128)} %param.8) | copy-start | bytes 6148
  91.4 36.7 %copy-start.4 = (s32[1,1,1,16,16,2]{4,5,3,2,1,0:T(2,128)S(1)}, s32[1,1,1,16,16,2]{4,5,3,2,1,0:T(2,128)}, u32[]{:S(2)}) copy-start(s32[1,1,1,16,16,2]{4,5,3,2,1,0:T(2,128)} %param.9) | copy-start | bytes 6148
  91.4 61.6 %copy-start.1 = (s32[4]{0:T(128)S(1)}, s32[4]{0:T(128)}, u32[]{:S(2)}) copy-start(s32[4]{0:T(128)} %shard_map.37.place) | copy-start | bytes 52
  91.4 13.6 %collective-permute-start.3 = (bf16[16,128,128]{2,1,0:T(8,128)(2,1)S(1)}, bf16[16,128,128]{2,1,0:T(8,128)(2,1)}, u32[]{:S(2)}, u32[]{:S(2)}) collective-permute-start(bf16[16,128,128]{2,1,0:T(8,128)(2,1)S(1)} %param.3), channel_id=1, source_target_pairs={{0,96},{32,0},{64,32},{96,64},{1,97},{33,1},{65,33},{97,65},{2,98}... | collective-permute-start | bytes 1572872 | tf_op jit(solution)/shard_map/cond/branch_1_fun/ppermute | solution.py:92
  95.8 11.9 %collective-permute-start.4 = (bf16[16,128,128]{2,1,0:T(8,128)(2,1)S(1)}, bf16[16,128,128]{2,1,0:T(8,128)(2,1)}, u32[]{:S(2)}, u32[]{:S(2)}) collective-permute-start(bf16[16,128,128]{2,1,0:T(8,128)(2,1)S(1)} %param.3), channel_id=1, source_target_pairs={{0,64},{32,96},{64,0},{96,32},{1,65},{33,97},{65,1},{97,33},{2,66}... | collective-permute-start | bytes 1572872 | tf_op jit(solution)/shard_map/cond/branch_1_fun/ppermute | solution.py:92
  98.3 22.4 %collective-permute-start.5 = (bf16[16,128,128]{2,1,0:T(8,128)(2,1)S(1)}, bf16[16,128,128]{2,1,0:T(8,128)(2,1)}, u32[]{:S(2)}, u32[]{:S(2)}) collective-permute-start(bf16[16,128,128]{2,1,0:T(8,128)(2,1)S(1)} %param.3), channel_id=1, source_target_pairs={{0,32},{32,64},{64,96},{96,0},{1,33},{33,65},{65,97},{97,1},{2,34}... | collective-permute-start | bytes 1572872 | tf_op jit(solution)/shard_map/cond/branch_1_fun/ppermute | solution.py:92
  120.7 7.5 %collective-permute-start.10 = (bf16[8,128,128]{2,1,0:T(8,128)(2,1)S(1)}, bf16[8,128,128]{2,1,0:T(8,128)(2,1)S(1)}, u32[]{:S(2)}, u32[]{:S(2)}) collective-permute-start(bf16[8,128,128]{2,1,0:T(8,128)(2,1)S(1)} %constant_dynamic-update-slice_fusion.refs_8_), channel_id=1, source_target_pairs={{0,96},{32,0},{64,32},{96,64},{1,97},{33,1},{65,33},{97,65},{2,98}... | collective-permute-start | bytes 786440 | tf_op jit(solution)/shard_map/ppermute | solution.py:92
  122.7 9.0 %collective-permute-start.11 = (bf16[8,128,128]{2,1,0:T(8,128)(2,1)S(1)}, bf16[8,128,128]{2,1,0:T(8,128)(2,1)S(1)}, u32[]{:S(2)}, u32[]{:S(2)}) collective-permute-start(bf16[8,128,128]{2,1,0:T(8,128)(2,1)S(1)} %constant_dynamic-update-slice_fusion.refs_8_), channel_id=1, source_target_pairs={{0,64},{32,96},{64,0},{96,32},{1,65},{33,97},{65,1},{97,33},{2,66}... | collective-permute-start | bytes 786440 | tf_op jit(solution)/shard_map/ppermute | solution.py:92
  125.2 9.3 %collective-permute-start.12 = (bf16[8,128,128]{2,1,0:T(8,128)(2,1)S(1)}, bf16[8,128,128]{2,1,0:T(8,128)(2,1)S(1)}, u32[]{:S(2)}, u32[]{:S(2)}) collective-permute-start(bf16[8,128,128]{2,1,0:T(8,128)(2,1)S(1)} %constant_dynamic-update-slice_fusion.refs_8_), channel_id=1, source_target_pairs={{0,32},{32,64},{64,96},{96,0},{1,33},{33,65},{65,97},{97,1},{2,34}... | collective-permute-start | bytes 786440 | tf_op jit(solution)/shard_map/ppermute | solution.py:92
  153.0 1.6 copy-start
  158.7 8.8 %collective-permute-start.13 = (f32[8,128,128]{2,1,0:T(8,128)S(1)}, f32[8,128,128]{2,1,0:T(8,128)S(1)}, u32[]{:S(2)}, u32[]{:S(2)}) collective-permute-start(f32[8,128,128]{2,1,0:T(8,128)S(1)} %shard_map.39), channel_id=1, source_target_pairs={{0,1},{1,0},{2,3},{3,2},{4,5},{5,4},{6,7},{7,6},{8,9},{9,8},{10,11... | collective-permute-start | bytes 1572872 | tf_op jit(solution)/shard_map/ppermute | solution.py:126
  167.6 12.1 %collective-permute-start.14 = (f32[2,128,128]{2,1,0:T(8,128)S(1)}, f32[2,128,128]{2,1,0:T(8,128)S(1)}, u32[]{:S(2)}, u32[]{:S(2)}) collective-permute-start(f32[2,128,128]{2,1,0:T(8,128)S(1)} %get-tuple-element.61), channel_id=1, source_target_pairs={{0,2},{2,4},{4,6},{6,0},{1,3},{3,5},{5,7},{7,1},{8,10},{10,12},{12... | collective-permute-start | bytes 393224 | tf_op jit(solution)/shard_map/ppermute | solution.py:132
  172.2 9.1 %collective-permute-start.15 = (f32[2,128,128]{2,1,0:T(8,128)S(1)}, f32[2,128,128]{2,1,0:T(8,128)S(1)}, u32[]{:S(2)}, u32[]{:S(2)}) collective-permute-start(f32[2,128,128]{2,1,0:T(8,128)S(1)} %get-tuple-element.63), channel_id=1, source_target_pairs={{0,4},{2,6},{4,0},{6,2},{1,5},{3,7},{5,1},{7,3},{8,12},{10,14},{12... | collective-permute-start | bytes 393224 | tf_op jit(solution)/shard_map/ppermute | solution.py:132
  176.8 6.4 %collective-permute-start.16 = (f32[2,128,128]{2,1,0:T(8,128)S(1)}, f32[2,128,128]{2,1,0:T(8,128)S(1)}, u32[]{:S(2)}, u32[]{:S(2)}) collective-permute-start(f32[2,128,128]{2,1,0:T(8,128)S(1)} %get-tuple-element.62), channel_id=1, source_target_pairs={{0,6},{2,0},{4,2},{6,4},{1,7},{3,1},{5,3},{7,5},{8,14},{10,8},{12,... | collective-permute-start | bytes 393224 | tf_op jit(solution)/shard_map/ppermute | solution.py:132
Sparse Core Ops, SparseCore 0:
  60.8 92.1 all-gather.1

commit v7 on v6

v7 whole, which is shorter than its diff:
```python
import functools

import jax
import jax.numpy as jnp
from jax import lax
from jax.experimental import pallas as pl
from jax.experimental.pallas import tpu as pltpu
from jax.sharding import Mesh
from jax.sharding import PartitionSpec as P

X, ZH, Y, CORE, ROW = 4, 4, 4, 2, 8
S, SLOTS, R, BS = 8, 2, 16, 128
COLS = X * ZH
PER = R // (Y * CORE)
STEPS = ((1, 2, 3), (4, 5, 6, 7))
ORDER = (2, 1, 3, 0)


def ring(n, k):
    return [(i, (i + k) % n) for i in range(n)]


def products(groups, far, place, left, right, *refs):
    n = 1 + max(g[0] for g in groups)
    a, refs = refs[:n], refs[n:]
    x, zh, core, y, row = (place[k] for k in range(5))
    if far == ORDER[0]:
        own, right_way, left_way = refs[0], refs[1:ROW], refs[ROW : 2 * ROW - 1]
        out, b, sems = refs[2 * ROW - 1 :]

        def copy(source, s):
            slot = lax.rem(row - s + ROW, ROW)
            return pltpu.make_async_copy(source, b.at[pl.ds(slot * S, S)], sems.at[s])

        copy(own, 0).start()
        for s in range(1, ROW):

            @pl.when(row >= s)
            def _(s=s):
                copy(right_way[s - 1], s).start()

            @pl.when(row < s)
            def _(s=s):
                copy(left_way[ROW - s - 1], s).start()

        for s in range(ROW):
            copy(own, s).wait()
    else:
        b, out = refs

    def one(r):
        total = None
        for array, start, dx, dz in groups:
            c = lax.rem(x + dx, X) * ZH + lax.rem(zh + dz, ZH)
            lefts, rights = [], []
            for p in range(SLOTS):
                m = left[r, c * SLOTS + p]
                tile = a[array][start + jnp.minimum(m, S - 1)]
                lefts.append(jnp.where(m < S, tile, jnp.zeros_like(tile)))
                rights.append(b[jnp.minimum(right[r, c * SLOTS + p], ROW * S - 1)])
            value = jnp.dot(
                jnp.concatenate(lefts, axis=1),
                jnp.concatenate(rights, axis=0),
                preferred_element_type=jnp.float32,
            )
            total = value if total is None else total + value
        return total

    to = lax.rem(y + far, Y)

    @pl.loop(0, CORE * PER, unroll=4)
    def _(k):
        on = lax.rem(core + k // PER, CORE)
        out[k] = one((to * CORE + on) * PER + lax.rem(k, PER))


def call(groups, far, lists, arrays, b):
    first = far == ORDER[0]
    smem = pl.BlockSpec(memory_space=pltpu.SMEM)
    vmem = pl.BlockSpec(memory_space=pltpu.VMEM)
    anywhere = pl.BlockSpec(memory_space=pl.ANY)
    part = jax.ShapeDtypeStruct((CORE * PER, BS, BS), jnp.float32)
    panel = jax.ShapeDtypeStruct((ROW * S, BS, BS), jnp.bfloat16)
    return pl.pallas_call(
        functools.partial(products, groups, far),
        out_shape=(part, panel) if first else part,
        in_specs=[smem] * len(lists) + [vmem] * len(arrays) + [anywhere if first else vmem] * len(b),
        out_specs=(vmem, vmem) if first else vmem,
        scratch_shapes=[pltpu.SemaphoreType.DMA((ROW,))] if first else [],
        compiler_params=pltpu.CompilerParams(vmem_limit_bytes=24 * 1024 * 1024),
        cost_estimate=pl.CostEstimate(
            flops=CORE * PER * len(groups) * SLOTS * 2 * BS**3, bytes_accessed=1024 * 1024, transcendentals=0
        ),
    )(*lists, *arrays, *b)


def on_device(tiles, pair_a, pair_b):
    own = tiles.reshape(S, BS, BS)
    left = pair_a.reshape(R, COLS * SLOTS)
    right = pair_b.reshape(R, COLS * SLOTS)
    place = jnp.stack([lax.axis_index(n) for n in ("x", "zh", "core", "y", "row")]).astype(jnp.int32)
    lists = (place, left, right)

    def over_x(value):
        return [lax.ppermute(value, "x", ring(X, -d)) for d in range(1, X)]

    def fenced(function, *args):
        always = lax.optimization_barrier(jnp.bool_(True))
        shapes = jax.eval_shape(function, *args)
        never = lambda *args: jax.tree.map(lambda t: jnp.zeros(t.shape, t.dtype), shapes)
        return lax.cond(always, function, never, *args)

    def chain(steps, up, down):
        ups, downs = [], []
        for s in steps:
            up = lax.ppermute(up, "row", [(p, p + 1) for p in range(s - 1, ROW - 1)])
            down = lax.ppermute(down, "row", [(p, p - 1) for p in range(1, ROW - s + 1)])
            ups.append(up)
            downs.append(down)
        return ups, downs

    def together(*values):
        flat, tree = jax.tree.flatten(values)
        return jax.tree.unflatten(tree, lax.optimization_barrier(tuple(flat)))

    z1 = lax.ppermute(own, "zh", ring(ZH, -1))
    z3 = lax.ppermute(own, "zh", ring(ZH, 1))
    routed = lax.all_to_all(own, ("y", "core"), split_axis=0, concat_axis=0, tiled=True)
    own_x = fenced(over_x, own)
    own_x, routed = together(own_x, routed)
    ups, downs = fenced(functools.partial(chain, STEPS[0]), routed, routed)
    z1, z3, ups, downs = together(z1, z3, ups, downs)

    half = S // 2
    z2_low = lax.ppermute(z1[:half], "zh", ring(ZH, -1))
    z2_high = lax.ppermute(z3[half:], "zh", ring(ZH, 1))
    pair = jnp.concatenate([z1, z3])
    near = fenced(over_x, pair)
    z2_low, z2_high, near, ups, downs = together(z2_low, z2_high, near, ups, downs)

    antipode = jnp.concatenate([z2_low, z2_high])
    far = over_x(antipode)
    last_ups, last_downs = fenced(functools.partial(chain, STEPS[1]), ups[-1], downs[-1])
    b = [routed, *ups, *last_ups, *downs, *last_downs]

    arrays = [own, *own_x, pair, *near, antipode, *far]
    groups = [(d, 0, d, 0) for d in range(X)]
    groups += [(X + d, k * S, d, z) for k, z in enumerate((1, 3)) for d in range(X)]
    groups += [(2 * X + d, 0, d, 2) for d in range(X)]
    parts = []
    for d in ORDER:
        if d == 0:
            place, parts[0] = together(place, parts[0])
            lists = (place, left, right)
        part = call(groups, d, lists, arrays, b)
        if d == ORDER[0]:
            part, b = part[0], [part[1]]
        parts.append(lax.ppermute(part, "y", ring(Y, d)) if d else part)
    total = sum(parts[1:], parts[0])
    return (total[:PER] + lax.ppermute(total[PER:], "core", ring(CORE, 1)))[None, None]


def solution(mesh):
    fine = Mesh(mesh.devices.reshape(ROW, X, ZH, Y, CORE), ("row", "x", "zh", "y", "core"))
    spec = ("row", ("x", "zh"), ("y", "core"))
    return jax.shard_map(
        on_device,
        mesh=fine,
        in_specs=(P(*spec), P(*spec), P(*spec)),
        out_specs=P(*spec),
        check_vma=False,
    )
```

time: 192 us -> 231 us (1.20)
  starting transfers between devices: 94.2 us -> 124 us
  waiting for transfers between devices: 68.3 us -> 90.5 us
  between operations: 13.6 us -> 0.25 us
  Pallas kernels: 9.47 us -> 13.4 us
  local copies, waits for them, and re-layouts: 3.64 us -> 0.52 us
    ppermute x13 -> x27, waiting for transfers between devices: 41.1 us -> 90.5 us  [the longest x7 60.1 us: chain(): lax.ppermute(down, 'row', [(p, p - 1) for p in range(1, ROW - s + 1)])]
    ppermute x13 -> x27, starting transfers between devices: 41.5 us -> 76.8 us  [the longest x9 31.7 us: over_x(): return [lax.ppermute(value, 'x', ring(X, -d)) for d in range(1, X)]]
    all_gather x1 -> x0, waiting for transfers between devices: 18.5 us -> none  [on_device(): b = lax.all_gather(routed, 'row', axis=0, tiled=True)]
    ppermute x1, starting transfers between devices: 18.8 us -> 3.36 us  [on_device(): z2_low = lax.ppermute(z1[:half], 'zh', ring(ZH, -1))]
    ppermute x1, starting transfers between devices: 1.92 us -> 16.3 us  [on_device(): z3 = lax.ppermute(own, 'zh', ring(ZH, 1))]
    ppermute x1, starting transfers between devices: 23.5 us -> 9.2 us  [on_device(): z1 = lax.ppermute(own, 'zh', ring(ZH, -1))]
    ppermute x1, starting transfers between devices: 1.92 us -> 11.8 us  [on_device(): z2_high = lax.ppermute(z3[half:], 'zh', ring(ZH, 1))]
    ppermute x1, waiting for transfers between devices: 8.67 us -> 0.01 us  [on_device(): z1 = lax.ppermute(own, 'zh', ring(ZH, -1))]
  transfers between devices with their start and end apart: 19 -> 32, of which waited for: 12 -> 15; matrix products, arithmetic and copies ran while one was open for 1% -> 0% of each run, Pallas kernels for 3% -> 4%
where the time goes in v7:
time: 231 us; the launch traced here: 230 us
  starting transfers between devices  124 us (54%)
  waiting for transfers between devices  90.5 us (39%)
  Pallas kernels  13.4 us (6%)
    ppermute x7, waiting for transfers between devices, chain(): lax.ppermute(down, 'row', [(p, p - 1) for p in range(1, ROW - s + 1)])  60.1 us
    ppermute x9, starting transfers between devices, over_x(): return [lax.ppermute(value, 'x', ring(X, -d)) for d in range(1, X)]  31.7 us
    ppermute x9, waiting for transfers between devices, over_x(): return [lax.ppermute(value, 'x', ring(X, -d)) for d in range(1, X)]  28.5 us
    ppermute x1, starting transfers between devices, on_device(): z3 = lax.ppermute(own, 'zh', ring(ZH, 1))  16.3 us
    pallas_call x4, Pallas kernels, call(): pl.pallas_call(functools.partial(products, groups, far), out_shape=(part,...  13.4 us
    ppermute x7, starting transfers between devices, chain(): up = lax.ppermute(up, 'row', [(p, p + 1) for p in range(s - 1, ROW - 1)])  13 us
    ppermute x1, starting transfers between devices, on_device(): z2_high = lax.ppermute(z3[half:], 'zh', ring(ZH, 1))  11.8 us
    ppermute x1, starting transfers between devices, on_device(): lax.ppermute(total[PER:], 'core', ring(CORE, 1))  11.7 us
  transfers between devices with their start and end apart: 32, of which 15 were waited for; matrix products, arithmetic and copies ran while one was open for 0% of the time, Pallas kernels for 4%

profile of v7, /device:TPU:1, one launch (start us, length us, event | category | flops | bytes accessed | tf_op | source)
XLA Modules:
  0.0 229.6 jit_solution(14433941179675586306)
XLA Ops:
  0.0 16.3 %collective-permute-start.21 = (bf16[8,128,128]{2,1,0:T(8,128)(2,1)}, bf16[8,128,128]{2,1,0:T(8,128)(2,1)S(1)}, u32[]{:S(2)}, u32[]{:S(2)}) collective-permute-start(bf16[8,128,128]{2,1,0:T(8,128)(2,1)} %bitcast.10), channel_id=1, source_target_pairs={{0,8},{8,16},{16,24},{24,0},{1,9},{9,17},{17,25},{25,1},{2,10},{10... | collective-permute-start | bytes 786440 | tf_op jit(solution)/shard_map/ppermute | solution.py:127
  16.3 9.2 %collective-permute-start.20 = (bf16[8,128,128]{2,1,0:T(8,128)(2,1)}, bf16[8,128,128]{2,1,0:T(8,128)(2,1)S(1)}, u32[]{:S(2)}, u32[]{:S(2)}) collective-permute-start(bf16[8,128,128]{2,1,0:T(8,128)(2,1)} %bitcast.11), channel_id=1, source_target_pairs={{0,24},{8,0},{16,8},{24,16},{1,25},{9,1},{17,9},{25,17},{2,26},{10... | collective-permute-start | bytes 786440 | tf_op jit(solution)/shard_map/ppermute | solution.py:126
  25.5 6.6 %all-to-all-start = ((bf16[8,128,128]{2,1,0:T(8,128)(2,1)}), bf16[8,128,128]{2,1,0:T(8,128)(2,1)S(1)}, u32[]{:S(2)}, u32[]{:S(2)}) async-start(bf16[8,128,128]{2,1,0:T(8,128)(2,1)} %bitcast.12), calls=%async_computation | async-start | bytes 524288 | tf_op jit(solution)/shard_map/all_to_all | solution.py:128
  32.0 19.0 %conditional.4 = (bf16[8,128,128]{2,1,0:T(8,128)(2,1)}, bf16[8,128,128]{2,1,0:T(8,128)(2,1)}, bf16[8,128,128]{2,1,0:T(8,128)(2,1)}) conditional(s32[]{:T(128)} %convert_element_type.2, () %tuple.41, bf16[8,128,128]{2,1,0:T(8,128)(2,1)} %bitcast.13), branch_computations={%region_0.0_spmd, %region_1.0_spmd} | conditional | bytes 3145872 | solution.py:111
  32.0 2.0 collective-permute-start.2
  34.0 4.4 %collective-permute-start.1 = (bf16[8,128,128]{2,1,0:T(8,128)(2,1)}, bf16[8,128,128]{2,1,0:T(8,128)(2,1)}, u32[]{:S(2)}, u32[]{:S(2)}) collective-permute-start(bf16[8,128,128]{2,1,0:T(8,128)(2,1)} %param.1), channel_id=1, source_target_pairs={{0,64},{32,96},{64,0},{96,32},{1,65},{33,97},{65,1},{97,33},{2,66}... | collective-permute-start | bytes 786440 | tf_op jit(solution)/shard_map/cond/branch_1_fun/ppermute | solution.py:105
  38.4 3.1 %collective-permute-start = (bf16[8,128,128]{2,1,0:T(8,128)(2,1)}, bf16[8,128,128]{2,1,0:T(8,128)(2,1)}, u32[]{:S(2)}, u32[]{:S(2)}) collective-permute-start(bf16[8,128,128]{2,1,0:T(8,128)(2,1)} %param.1), channel_id=1, source_target_pairs={{0,96},{32,0},{64,32},{96,64},{1,97},{33,1},{65,33},{97,65},{2,98}... | collective-permute-start | bytes 786440 | tf_op jit(solution)/shard_map/cond/branch_1_fun/ppermute | solution.py:105
  41.5 1.8 collective-permute-done.2
  43.2 5.7 %collective-permute-done.1 = bf16[8,128,128]{2,1,0:T(8,128)(2,1)} collective-permute-done((bf16[8,128,128]{2,1,0:T(8,128)(2,1)}, bf16[8,128,128]{2,1,0:T(8,128)(2,1)}, u32[]{:S(2)}, u32[]{:S(2)}) %collective-permute-start.1) | collective-permute-done | bytes 262176 | tf_op jit(solution)/shard_map/cond/branch_1_fun/ppermute | solution.py:105
  48.9 2.2 collective-permute-done
  51.1 42.2 %conditional.5 = (bf16[8,128,128]{2,1,0:T(8,128)(2,1)}, bf16[8,128,128]{2,1,0:T(8,128)(2,1)}, bf16[8,128,128]{2,1,0:T(8,128)(2,1)}, bf16[8,128,128]{2,1,0:T(8,12...) conditional(s32[]{:T(128)} %convert_element_type.2, () %tuple.43, ...), branch_computations={%region_2.0_spmd, %region_3.0_spmd} | conditional | bytes 6291744 | solution.py:111
  51.1 1.3 collective-permute-start.6
  52.4 4.7 %collective-permute-start.3 = (bf16[8,128,128]{2,1,0:T(8,128)(2,1)S(1)}, bf16[8,128,128]{2,1,0:T(8,128)(2,1)}, u32[]{:S(2)}, u32[]{:S(2)}) collective-permute-start(bf16[8,128,128]{2,1,0:T(8,128)(2,1)S(1)} %param.3), channel_id=1, source_target_pairs={{0,128},{128,256},{256,384},{384,512},{512,640},{640,768},{768,896... | collective-permute-start | bytes 786440 | tf_op jit(solution)/shard_map/cond/branch_1_fun/ppermute | solution.py:116
  57.1 17.9 %collective-permute-done.6 = bf16[8,128,128]{2,1,0:T(8,128)(2,1)} collective-permute-done((bf16[8,128,128]{2,1,0:T(8,128)(2,1)S(1)}, bf16[8,128,128]{2,1,0:T(8,128)(2,1)}, u32[]{:S(2)}, u32[]{:S(2)}) %collective-permute-start.6) | collective-permute-done | bytes 262176 | tf_op jit(solution)/shard_map/cond/branch_1_fun/ppermute | solution.py:117
  74.9 1.3 collective-permute-start.7
  76.2 0.0 collective-permute-done.3
  76.2 1.4 collective-permute-start.4
  77.6 4.7 %collective-permute-done.7 = bf16[8,128,128]{2,1,0:T(8,128)(2,1)} collective-permute-done((bf16[8,128,128]{2,1,0:T(8,128)(2,1)}, bf16[8,128,128]{2,1,0:T(8,128)(2,1)}, u32[]{:S(2)}, u32[]{:S(2)}) %collective-permute-start.7) | collective-permute-done | bytes 262176 | tf_op jit(solution)/shard_map/cond/branch_1_fun/ppermute | solution.py:117
  82.4 1.3 collective-permute-start.8
  83.7 1.4 collective-permute-start.5
  85.0 8.2 %collective-permute-done.8 = bf16[8,128,128]{2,1,0:T(8,128)(2,1)} collective-permute-done((bf16[8,128,128]{2,1,0:T(8,128)(2,1)}, bf16[8,128,128]{2,1,0:T(8,128)(2,1)}, u32[]{:S(2)}, u32[]{:S(2)}) %collective-permute-start.8) | collective-permute-done | bytes 262176 | tf_op jit(solution)/shard_map/cond/branch_1_fun/ppermute | solution.py:117
  93.3 11.8 %collective-permute-start.23 = (bf16[4,128,128]{2,1,0:T(8,128)(2,1)S(1)}, bf16[4,128,128]{2,1,0:T(8,128)(2,1)S(1)}, u32[]{:S(2)}, u32[]{:S(2)}) collective-permute-start(bf16[4,128,128]{2,1,0:T(8,128)(2,1)S(1)} %slice.13), channel_id=1, source_target_pairs={{0,8},{8,16},{16,24},{24,0},{1,9},{9,17},{17,25},{25,1},{2,10},{10... | collective-permute-start | bytes 393224 | tf_op jit(solution)/shard_map/ppermute | solution.py:136
  105.2 3.4 %collective-permute-start.22 = (bf16[4,128,128]{2,1,0:T(8,128)(2,1)S(1)}, bf16[4,128,128]{2,1,0:T(8,128)(2,1)S(1)}, u32[]{:S(2)}, u32[]{:S(2)}) collective-permute-start(bf16[4,128,128]{2,1,0:T(8,128)(2,1)S(1)} %slice.12), channel_id=1, source_target_pairs={{0,24},{8,0},{16,8},{24,16},{1,25},{9,1},{17,9},{25,17},{2,26},{10... | collective-permute-start | bytes 393224 | tf_op jit(solution)/shard_map/ppermute | solution.py:135
  108.6 0.0 copy-start
  108.6 29.6 %conditional.6 = (bf16[16,128,128]{2,1,0:T(8,128)(2,1)}, bf16[16,128,128]{2,1,0:T(8,128)(2,1)}, bf16[16,128,128]{2,1,0:T(8,128)(2,1)}) conditional(s32[]{:T(128)} %convert_element_type.2, () %tuple.45, bf16[16,128,128]{2,1,0:T(8,128)(2,1)S(1)} %constant_dynamic-update-slice_fusion.refs_4_), branch_computations={%region_4.0_spmd, %region_5.0_spmd} | conditional | bytes 6291600 | solution.py:111
  108.6 3.3 %collective-permute-start.11 = (bf16[16,128,128]{2,1,0:T(8,128)(2,1)S(1)}, bf16[16,128,128]{2,1,0:T(8,128)(2,1)}, u32[]{:S(2)}, u32[]{:S(2)}) collective-permute-start(bf16[16,128,128]{2,1,0:T(8,128)(2,1)S(1)} %param.5), channel_id=1, source_target_pairs={{0,32},{32,64},{64,96},{96,0},{1,33},{33,65},{65,97},{97,1},{2,34}... | collective-permute-start | bytes 1572872 | tf_op jit(solution)/shard_map/cond/branch_1_fun/ppermute | solution.py:105
  111.9 4.4 %collective-permute-start.10 = (bf16[16,128,128]{2,1,0:T(8,128)(2,1)S(1)}, bf16[16,128,128]{2,1,0:T(8,128)(2,1)}, u32[]{:S(2)}, u32[]{:S(2)}) collective-permute-start(bf16[16,128,128]{2,1,0:T(8,128)(2,1)S(1)} %param.5), channel_id=1, source_target_pairs={{0,64},{32,96},{64,0},{96,32},{1,65},{33,97},{65,1},{97,33},{2,66}... | collective-permute-start | bytes 1572872 | tf_op jit(solution)/shard_map/cond/branch_1_fun/ppermute | solution.py:105
  116.2 3.1 %collective-permute-start.9 = (bf16[16,128,128]{2,1,0:T(8,128)(2,1)S(1)}, bf16[16,128,128]{2,1,0:T(8,128)(2,1)}, u32[]{:S(2)}, u32[]{:S(2)}) collective-permute-start(bf16[16,128,128]{2,1,0:T(8,128)(2,1)S(1)} %param.5), channel_id=1, source_target_pairs={{0,96},{32,0},{64,32},{96,64},{1,97},{33,1},{65,33},{97,65},{2,98}... | collective-permute-start | bytes 1572872 | tf_op jit(solution)/shard_map/cond/branch_1_fun/ppermute | solution.py:105
  119.3 2.9 %collective-permute-done.11 = bf16[16,128,128]{2,1,0:T(8,128)(2,1)} collective-permute-done((bf16[16,128,128]{2,1,0:T(8,128)(2,1)S(1)}, bf16[16,128,128]{2,1,0:T(8,128)(2,1)}, u32[]{:S(2)}, u32[]{:S(2)}) %collective-permute-start.11) | collective-permute-done | bytes 524320 | tf_op jit(solution)/shard_map/cond/branch_1_fun/ppermute | solution.py:105
  122.3 12.2 %collective-permute-done.10 = bf16[16,128,128]{2,1,0:T(8,128)(2,1)} collective-permute-done((bf16[16,128,128]{2,1,0:T(8,128)(2,1)S(1)}, bf16[16,128,128]{2,1,0:T(8,128)(2,1)}, u32[]{:S(2)}, u32[]{:S(2)}) %collective-permute-start.10) | collective-permute-done | bytes 524320 | tf_op jit(solution)/shard_map/cond/branch_1_fun/ppermute | solution.py:105
  134.5 3.7 %collective-permute-done.9 = bf16[16,128,128]{2,1,0:T(8,128)(2,1)} collective-permute-done((bf16[16,128,128]{2,1,0:T(8,128)(2,1)S(1)}, bf16[16,128,128]{2,1,0:T(8,128)(2,1)}, u32[]{:S(2)}, u32[]{:S(2)}) %collective-permute-start.9) | collective-permute-done | bytes 524320 | tf_op jit(solution)/shard_map/cond/branch_1_fun/ppermute | solution.py:105
  138.2 5.4 %collective-permute-start.26 = (bf16[8,128,128]{2,1,0:T(8,128)(2,1)S(1)}, bf16[8,128,128]{2,1,0:T(8,128)(2,1)S(1)}, u32[]{:S(2)}, u32[]{:S(2)}) collective-permute-start(bf16[8,128,128]{2,1,0:T(8,128)(2,1)S(1)} %constant_dynamic-update-slice_fusion.2.refs_8_), channel_id=1, source_target_pairs={{0,32},{32,64},{64,96},{96,0},{1,33},{33,65},{65,97},{97,1},{2,34}... | collective-permute-start | bytes 786440 | tf_op jit(solution)/shard_map/ppermute | solution.py:105
  143.6 3.1 %collective-permute-start.25 = (bf16[8,128,128]{2,1,0:T(8,128)(2,1)S(1)}, bf16[8,128,128]{2,1,0:T(8,128)(2,1)S(1)}, u32[]{:S(2)}, u32[]{:S(2)}) collective-permute-start(bf16[8,128,128]{2,1,0:T(8,128)(2,1)S(1)} %constant_dynamic-update-slice_fusion.2.refs_8_), channel_id=1, source_target_pairs={{0,64},{32,96},{64,0},{96,32},{1,65},{33,97},{65,1},{97,33},{2,66}... | collective-permute-start | bytes 786440 | tf_op jit(solution)/shard_map/ppermute | solution.py:105
  146.8 3.1 %collective-permute-start.24 = (bf16[8,128,128]{2,1,0:T(8,128)(2,1)S(1)}, bf16[8,128,128]{2,1,0:T(8,128)(2,1)S(1)}, u32[]{:S(2)}, u32[]{:S(2)}) collective-permute-start(bf16[8,128,128]{2,1,0:T(8,128)(2,1)S(1)} %constant_dynamic-update-slice_fusion.2.refs_8_), channel_id=1, source_target_pairs={{0,96},{32,0},{64,32},{96,64},{1,97},{33,1},{65,33},{97,65},{2,98}... | collective-permute-start | bytes 786440 | tf_op jit(solution)/shard_map/ppermute | solution.py:105
  149.9 0.1 copy.6
  150.0 0.1 copy.8.left
  150.0 0.1 copy.7
  150.1 0.1 copy.9.right
  150.2 0.1 stack.23.place
  150.3 40.0 %conditional.7 = (bf16[8,128,128]{2,1,0:T(8,128)(2,1)}, bf16[8,128,128]{2,1,0:T(8,128)(2,1)}, bf16[8,128,128]{2,1,0:T(8,128)(2,1)}, bf16[8,128,128]{2,1,0:T(8,12...) conditional(s32[]{:T(128)} %convert_element_type.2, () %tuple.47, ...), branch_computations={%region_6.0_spmd, %region_7.0_spmd} | conditional | bytes 8388992 | solution.py:111
  150.3 1.4 collective-permute-start.12
  151.7 1.3 collective-permute-start.16
  153.0 1.4 collective-permute-start.13
  154.3 5.7 %collective-permute-done.16 = bf16[8,128,128]{2,1,0:T(8,128)(2,1)} collective-permute-done((bf16[8,128,128]{2,1,0:T(8,128)(2,1)}, bf16[8,128,128]{2,1,0:T(8,128)(2,1)}, u32[]{:S(2)}, u32[]{:S(2)}) %collective-permute-start.16) | collective-permute-done | bytes 262176 | tf_op jit(solution)/shard_map/cond/branch_1_fun/ppermute | solution.py:117
  160.0 1.3 collective-permute-start.17
  161.3 1.4 collective-permute-start.14
  162.7 6.6 %collective-permute-done.17 = bf16[8,128,128]{2,1,0:T(8,128)(2,1)} collective-permute-done((bf16[8,128,128]{2,1,0:T(8,128)(2,1)}, bf16[8,128,128]{2,1,0:T(8,128)(2,1)}, u32[]{:S(2)}, u32[]{:S(2)}) %collective-permute-start.17) | collective-permute-done | bytes 262176 | tf_op jit(solution)/shard_map/cond/branch_1_fun/ppermute | solution.py:117
  169.3 1.3 collective-permute-start.18
  170.6 1.4 collective-permute-start.15
  172.0 8.0 %collective-permute-done.18 = bf16[8,128,128]{2,1,0:T(8,128)(2,1)} collective-permute-done((bf16[8,128,128]{2,1,0:T(8,128)(2,1)}, bf16[8,128,128]{2,1,0:T(8,128)(2,1)}, u32[]{:S(2)}, u32[]{:S(2)}) %collective-permute-start.18) | collective-permute-done | bytes 262176 | tf_op jit(solution)/shard_map/cond/branch_1_fun/ppermute | solution.py:117
  180.0 1.3 collective-permute-start.19
  181.3 8.9 %collective-permute-done.19 = bf16[8,128,128]{2,1,0:T(8,128)(2,1)} collective-permute-done((bf16[8,128,128]{2,1,0:T(8,128)(2,1)}, bf16[8,128,128]{2,1,0:T(8,128)(2,1)}, u32[]{:S(2)}, u32[]{:S(2)}) %collective-permute-start.19) | collective-permute-done | bytes 262176 | tf_op jit(solution)/shard_map/cond/branch_1_fun/ppermute | solution.py:117
  190.3 4.5 %shard_map.37 = (f32[4,128,128]{2,1,0:T(8,128)S(1)}, bf16[64,128,128]{2,1,0:T(8,128)(2,1)S(1)}) custom-call(s32[5]{0:T(128)S(1)} %stack.23.place, s32[16,32]{1,0:T(8,128)S(1)} %copy.8.left, s32[16,32]{1,0:T(8,128)S(1)} %copy.9.right, bf16[8,128,128]{2,1,0:T(8,128)(2,1)S(1)} %bitcast.14, bf16[8,128,128]{2,1,0:T(8,128)(2,1)} %get-tuple-element.64.refs_1_, ...), custom_call_target="tpu_custom_call" | custom-call | flops 536870912 | bytes 1048576 | tf_op jit(solution)/shard_map/pallas_call | solution.py:84
  194.8 5.0 %collective-permute-start.27 = (f32[4,128,128]{2,1,0:T(8,128)S(1)}, f32[4,128,128]{2,1,0:T(8,128)S(1)}, u32[]{:S(2)}, u32[]{:S(2)}) collective-permute-start(f32[4,128,128]{2,1,0:T(8,128)S(1)} %get-tuple-element.104), channel_id=1, source_target_pairs={{0,4},{2,6},{4,0},{6,2},{1,5},{3,7},{5,1},{7,3},{8,12},{10,14},{12... | collective-permute-start | bytes 786440 | tf_op jit(solution)/shard_map/ppermute | solution.py:158
  199.8 3.0 %shard_map.38 = f32[4,128,128]{2,1,0:T(8,128)S(1)} custom-call(s32[5]{0:T(128)S(1)} %stack.23.place, s32[16,32]{1,0:T(8,128)S(1)} %copy.8.left, s32[16,32]{1,0:T(8,128)S(1)} %copy.9.right, bf16[8,128,128]{2,1,0:T(8,128)(2,1)S(1)} %bitcast.15, bf16[8,128,128]{2,1,0:T(8,128)(2,1)} %get-tuple-element.64.refs_1_, ...), custom_call_target="tpu_custom_call" | custom-call | flops 536870912 | bytes 1048576 | tf_op jit(solution)/shard_map/pallas_call | solution.py:84
  202.8 2.3 %collective-permute-start.28 = (f32[4,128,128]{2,1,0:T(8,128)S(1)}, f32[4,128,128]{2,1,0:T(8,128)S(1)}, u32[]{:S(2)}, u32[]{:S(2)}) collective-permute-start(f32[4,128,128]{2,1,0:T(8,128)S(1)} %shard_map.38), channel_id=1, source_target_pairs={{0,2},{2,4},{4,6},{6,0},{1,3},{3,5},{5,7},{7,1},{8,10},{10,12},{12... | collective-permute-start | bytes 786440 | tf_op jit(solution)/shard_map/ppermute | solution.py:158
  205.1 3.0 %shard_map.39 = f32[4,128,128]{2,1,0:T(8,128)S(1)} custom-call(s32[5]{0:T(128)S(1)} %stack.23.place, s32[16,32]{1,0:T(8,128)S(1)} %copy.8.left, s32[16,32]{1,0:T(8,128)S(1)} %copy.9.right, bf16[8,128,128]{2,1,0:T(8,128)(2,1)S(1)} %bitcast.16, bf16[8,128,128]{2,1,0:T(8,128)(2,1)} %get-tuple-element.64.refs_1_, ...), custom_call_target="tpu_custom_call" | custom-call | flops 536870912 | bytes 1048576 | tf_op jit(solution)/shard_map/pallas_call | solution.py:84
  208.1 4.2 %collective-permute-start.29 = (f32[4,128,128]{2,1,0:T(8,128)S(1)}, f32[4,128,128]{2,1,0:T(8,128)S(1)}, u32[]{:S(2)}, u32[]{:S(2)}) collective-permute-start(f32[4,128,128]{2,1,0:T(8,128)S(1)} %shard_map.39), channel_id=1, source_target_pairs={{0,6},{2,0},{4,2},{6,4},{1,7},{3,1},{5,3},{7,5},{8,14},{10,8},{12,... | collective-permute-start | bytes 786440 | tf_op jit(solution)/shard_map/ppermute | solution.py:158
  212.3 3.0 %shard_map.40 = f32[4,128,128]{2,1,0:T(8,128)S(1)} custom-call(s32[5]{0:T(128)S(1)} %stack.23.place, s32[16,32]{1,0:T(8,128)S(1)} %copy.8.left, s32[16,32]{1,0:T(8,128)S(1)} %copy.9.right, bf16[8,128,128]{2,1,0:T(8,128)(2,1)S(1)} %bitcast.17, bf16[8,128,128]{2,1,0:T(8,128)(2,1)} %get-tuple-element.64.refs_1_, ...), custom_call_target="tpu_custom_call" | custom-call | flops 536870912 | bytes 1048576 | tf_op jit(solution)/shard_map/pallas_call | solution.py:84
  215.3 0.9 collective-permute-done.29
  216.2 0.1 add_add_fusion
  216.3 11.7 %collective-permute-start.30 = (f32[2,128,128]{2,1,0:T(8,128)S(1)}, f32[2,128,128]{2,1,0:T(8,128)S(1)}, u32[]{:S(2)}, u32[]{:S(2)}) collective-permute-start(f32[2,128,128]{2,1,0:T(8,128)S(1)} %slice.17), channel_id=1, source_target_pairs={{0,1},{1,0},{2,3},{3,2},{4,5},{5,4},{6,7},{7,6},{8,9},{9,8},{10,11... | collective-permute-start | bytes 393224 | tf_op jit(solution)/shard_map/ppermute | solution.py:160
  227.9 1.0 collective-permute-done.30
  228.9 0.7 fusion
  (28 shorter events, 0.2 us)
Async XLA Ops:
  0.0 93.2 %collective-permute-start.21 = (bf16[8,128,128]{2,1,0:T(8,128)(2,1)}, bf16[8,128,128]{2,1,0:T(8,128)(2,1)S(1)}, u32[]{:S(2)}, u32[]{:S(2)}) collective-permute-start(bf16[8,128,128]{2,1,0:T(8,128)(2,1)} %bitcast.10), channel_id=1, source_target_pairs={{0,8},{8,16},{16,24},{24,0},{1,9},{9,17},{17,25},{25,1},{2,10},{10... | collective-permute-start | bytes 786440 | tf_op jit(solution)/shard_map/ppermute | solution.py:127
  16.3 77.0 %collective-permute-start.20 = (bf16[8,128,128]{2,1,0:T(8,128)(2,1)}, bf16[8,128,128]{2,1,0:T(8,128)(2,1)S(1)}, u32[]{:S(2)}, u32[]{:S(2)}) collective-permute-start(bf16[8,128,128]{2,1,0:T(8,128)(2,1)} %bitcast.11), channel_id=1, source_target_pairs={{0,24},{8,0},{16,8},{24,16},{1,25},{9,1},{17,9},{25,17},{2,26},{10... | collective-permute-start | bytes 786440 | tf_op jit(solution)/shard_map/ppermute | solution.py:126
  25.5 25.6 %all-to-all-start = ((bf16[8,128,128]{2,1,0:T(8,128)(2,1)}), bf16[8,128,128]{2,1,0:T(8,128)(2,1)S(1)}, u32[]{:S(2)}, u32[]{:S(2)}) async-start(bf16[8,128,128]{2,1,0:T(8,128)(2,1)} %bitcast.12), calls=%async_computation | async-start | bytes 524288 | tf_op jit(solution)/shard_map/all_to_all | solution.py:128
  32.0 11.2 %collective-permute-start.2 = (bf16[8,128,128]{2,1,0:T(8,128)(2,1)}, bf16[8,128,128]{2,1,0:T(8,128)(2,1)}, u32[]{:S(2)}, u32[]{:S(2)}) collective-permute-start(bf16[8,128,128]{2,1,0:T(8,128)(2,1)} %param.1), channel_id=1, source_target_pairs={{0,32},{32,64},{64,96},{96,0},{1,33},{33,65},{65,97},{97,1},{2,34}... | collective-permute-start | bytes 786440 | tf_op jit(solution)/shard_map/cond/branch_1_fun/ppermute | solution.py:105
  34.0 14.9 %collective-permute-start.1 = (bf16[8,128,128]{2,1,0:T(8,128)(2,1)}, bf16[8,128,128]{2,1,0:T(8,128)(2,1)}, u32[]{:S(2)}, u32[]{:S(2)}) collective-permute-start(bf16[8,128,128]{2,1,0:T(8,128)(2,1)} %param.1), channel_id=1, source_target_pairs={{0,64},{32,96},{64,0},{96,32},{1,65},{33,97},{65,1},{97,33},{2,66}... | collective-permute-start | bytes 786440 | tf_op jit(solution)/shard_map/cond/branch_1_fun/ppermute | solution.py:105
  38.4 12.7 %collective-permute-start = (bf16[8,128,128]{2,1,0:T(8,128)(2,1)}, bf16[8,128,128]{2,1,0:T(8,128)(2,1)}, u32[]{:S(2)}, u32[]{:S(2)}) collective-permute-start(bf16[8,128,128]{2,1,0:T(8,128)(2,1)} %param.1), channel_id=1, source_target_pairs={{0,96},{32,0},{64,32},{96,64},{1,97},{33,1},{65,33},{97,65},{2,98}... | collective-permute-start | bytes 786440 | tf_op jit(solution)/shard_map/cond/branch_1_fun/ppermute | solution.py:105
  51.1 23.9 %collective-permute-start.6 = (bf16[8,128,128]{2,1,0:T(8,128)(2,1)S(1)}, bf16[8,128,128]{2,1,0:T(8,128)(2,1)}, u32[]{:S(2)}, u32[]{:S(2)}) collective-permute-start(bf16[8,128,128]{2,1,0:T(8,128)(2,1)S(1)} %param.3), channel_id=1, source_target_pairs={{128,0},{256,128},{384,256},{512,384},{640,512},{768,640},{896,768... | collective-permute-start | bytes 786440 | tf_op jit(solution)/shard_map/cond/branch_1_fun/ppermute | solution.py:117
  52.4 23.9 %collective-permute-start.3 = (bf16[8,128,128]{2,1,0:T(8,128)(2,1)S(1)}, bf16[8,128,128]{2,1,0:T(8,128)(2,1)}, u32[]{:S(2)}, u32[]{:S(2)}) collective-permute-start(bf16[8,128,128]{2,1,0:T(8,128)(2,1)S(1)} %param.3), channel_id=1, source_target_pairs={{0,128},{128,256},{256,384},{384,512},{512,640},{640,768},{768,896... | collective-permute-start | bytes 786440 | tf_op jit(solution)/shard_map/cond/branch_1_fun/ppermute | solution.py:116
  74.9 7.4 %collective-permute-start.7 = (bf16[8,128,128]{2,1,0:T(8,128)(2,1)}, bf16[8,128,128]{2,1,0:T(8,128)(2,1)}, u32[]{:S(2)}, u32[]{:S(2)}) collective-permute-start(bf16[8,128,128]{2,1,0:T(8,128)(2,1)} %collective-permute-done.6), channel_id=1, source_target_pairs={{128,0},{256,128},{384,256},{512,384},{640,512},{768,640},{129,1},... | collective-permute-start | bytes 786440 | tf_op jit(solution)/shard_map/cond/branch_1_fun/ppermute | solution.py:117
  76.2 7.4 %collective-permute-start.4 = (bf16[8,128,128]{2,1,0:T(8,128)(2,1)}, bf16[8,128,128]{2,1,0:T(8,128)(2,1)}, u32[]{:S(2)}, u32[]{:S(2)}) collective-permute-start(bf16[8,128,128]{2,1,0:T(8,128)(2,1)} %collective-permute-done.3), channel_id=1, source_target_pairs={{128,256},{256,384},{384,512},{512,640},{640,768},{768,896},{129,2... | collective-permute-start | bytes 786440 | tf_op jit(solution)/shard_map/cond/branch_1_fun/ppermute | solution.py:116
  82.4 10.9 %collective-permute-start.8 = (bf16[8,128,128]{2,1,0:T(8,128)(2,1)}, bf16[8,128,128]{2,1,0:T(8,128)(2,1)}, u32[]{:S(2)}, u32[]{:S(2)}) collective-permute-start(bf16[8,128,128]{2,1,0:T(8,128)(2,1)} %collective-permute-done.7), channel_id=1, source_target_pairs={{128,0},{256,128},{384,256},{512,384},{640,512},{129,1},{257,129},... | collective-permute-start | bytes 786440 | tf_op jit(solution)/shard_map/cond/branch_1_fun/ppermute | solution.py:117
  83.7 9.6 %collective-permute-start.5 = (bf16[8,128,128]{2,1,0:T(8,128)(2,1)}, bf16[8,128,128]{2,1,0:T(8,128)(2,1)}, u32[]{:S(2)}, u32[]{:S(2)}) collective-permute-start(bf16[8,128,128]{2,1,0:T(8,128)(2,1)} %collective-permute-done.4), channel_id=1, source_target_pairs={{256,384},{384,512},{512,640},{640,768},{768,896},{257,385},{385,5... | collective-permute-start | bytes 786440 | tf_op jit(solution)/shard_map/cond/branch_1_fun/ppermute | solution.py:116
  93.2 56.7 %copy-start.1 = (s32[1,1,1,16,16,2]{4,5,3,2,1,0:T(2,128)S(1)}, s32[1,1,1,16,16,2]{4,5,3,2,1,0:T(2,128)}, u32[]{:S(2)}) copy-start(s32[1,1,1,16,16,2]{4,5,3,2,1,0:T(2,128)} %param.12) | copy-start | bytes 6148
  93.2 56.8 %copy-start.2 = (s32[1,1,1,16,16,2]{4,5,3,2,1,0:T(2,128)S(1)}, s32[1,1,1,16,16,2]{4,5,3,2,1,0:T(2,128)}, u32[]{:S(2)}) copy-start(s32[1,1,1,16,16,2]{4,5,3,2,1,0:T(2,128)} %param.13) | copy-start | bytes 6148
  93.3 44.9 %collective-permute-start.23 = (bf16[4,128,128]{2,1,0:T(8,128)(2,1)S(1)}, bf16[4,128,128]{2,1,0:T(8,128)(2,1)S(1)}, u32[]{:S(2)}, u32[]{:S(2)}) collective-permute-start(bf16[4,128,128]{2,1,0:T(8,128)(2,1)S(1)} %slice.13), channel_id=1, source_target_pairs={{0,8},{8,16},{16,24},{24,0},{1,9},{9,17},{17,25},{25,1},{2,10},{10... | collective-permute-start | bytes 393224 | tf_op jit(solution)/shard_map/ppermute | solution.py:136
  105.2 33.0 %collective-permute-start.22 = (bf16[4,128,128]{2,1,0:T(8,128)(2,1)S(1)}, bf16[4,128,128]{2,1,0:T(8,128)(2,1)S(1)}, u32[]{:S(2)}, u32[]{:S(2)}) collective-permute-start(bf16[4,128,128]{2,1,0:T(8,128)(2,1)S(1)} %slice.12), channel_id=1, source_target_pairs={{0,24},{8,0},{16,8},{24,16},{1,25},{9,1},{17,9},{25,17},{2,26},{10... | collective-permute-start | bytes 393224 | tf_op jit(solution)/shard_map/ppermute | solution.py:135
  108.6 81.7 %copy-start = (bf16[1,1,1,8,1,128,128]{6,5,4,3,2,1,0:T(8,128)(2,1)S(1)}, bf16[1,1,1,8,1,128,128]{6,5,4,3,2,1,0:T(8,128)(2,1)}, u32[]{:S(2)}) copy-start(bf16[1,1,1,8,1,128,128]{6,5,4,3,2,1,0:T(8,128)(2,1)} %param.11) | copy-start | bytes 786436
  108.6 13.6 %collective-permute-start.11 = (bf16[16,128,128]{2,1,0:T(8,128)(2,1)S(1)}, bf16[16,128,128]{2,1,0:T(8,128)(2,1)}, u32[]{:S(2)}, u32[]{:S(2)}) collective-permute-start(bf16[16,128,128]{2,1,0:T(8,128)(2,1)S(1)} %param.5), channel_id=1, source_target_pairs={{0,32},{32,64},{64,96},{96,0},{1,33},{33,65},{65,97},{97,1},{2,34}... | collective-permute-start | bytes 1572872 | tf_op jit(solution)/shard_map/cond/branch_1_fun/ppermute | solution.py:105
  111.9 22.6 %collective-permute-start.10 = (bf16[16,128,128]{2,1,0:T(8,128)(2,1)S(1)}, bf16[16,128,128]{2,1,0:T(8,128)(2,1)}, u32[]{:S(2)}, u32[]{:S(2)}) collective-permute-start(bf16[16,128,128]{2,1,0:T(8,128)(2,1)S(1)} %param.5), channel_id=1, source_target_pairs={{0,64},{32,96},{64,0},{96,32},{1,65},{33,97},{65,1},{97,33},{2,66}... | collective-permute-start | bytes 1572872 | tf_op jit(solution)/shard_map/cond/branch_1_fun/ppermute | solution.py:105
  116.2 21.9 %collective-permute-start.9 = (bf16[16,128,128]{2,1,0:T(8,128)(2,1)S(1)}, bf16[16,128,128]{2,1,0:T(8,128)(2,1)}, u32[]{:S(2)}, u32[]{:S(2)}) collective-permute-start(bf16[16,128,128]{2,1,0:T(8,128)(2,1)S(1)} %param.5), channel_id=1, source_target_pairs={{0,96},{32,0},{64,32},{96,64},{1,97},{33,1},{65,33},{97,65},{2,98}... | collective-permute-start | bytes 1572872 | tf_op jit(solution)/shard_map/cond/branch_1_fun/ppermute | solution.py:105
  138.2 52.1 %collective-permute-start.26 = (bf16[8,128,128]{2,1,0:T(8,128)(2,1)S(1)}, bf16[8,128,128]{2,1,0:T(8,128)(2,1)S(1)}, u32[]{:S(2)}, u32[]{:S(2)}) collective-permute-start(bf16[8,128,128]{2,1,0:T(8,128)(2,1)S(1)} %constant_dynamic-update-slice_fusion.2.refs_8_), channel_id=1, source_target_pairs={{0,32},{32,64},{64,96},{96,0},{1,33},{33,65},{65,97},{97,1},{2,34}... | collective-permute-start | bytes 786440 | tf_op jit(solution)/shard_map/ppermute | solution.py:105
  143.6 46.7 %collective-permute-start.25 = (bf16[8,128,128]{2,1,0:T(8,128)(2,1)S(1)}, bf16[8,128,128]{2,1,0:T(8,128)(2,1)S(1)}, u32[]{:S(2)}, u32[]{:S(2)}) collective-permute-start(bf16[8,128,128]{2,1,0:T(8,128)(2,1)S(1)} %constant_dynamic-update-slice_fusion.2.refs_8_), channel_id=1, source_target_pairs={{0,64},{32,96},{64,0},{96,32},{1,65},{33,97},{65,1},{97,33},{2,66}... | collective-permute-start | bytes 786440 | tf_op jit(solution)/shard_map/ppermute | solution.py:105
  146.8 43.5 %collective-permute-start.24 = (bf16[8,128,128]{2,1,0:T(8,128)(2,1)S(1)}, bf16[8,128,128]{2,1,0:T(8,128)(2,1)S(1)}, u32[]{:S(2)}, u32[]{:S(2)}) collective-permute-start(bf16[8,128,128]{2,1,0:T(8,128)(2,1)S(1)} %constant_dynamic-update-slice_fusion.2.refs_8_), channel_id=1, source_target_pairs={{0,96},{32,0},{64,32},{96,64},{1,97},{33,1},{65,33},{97,65},{2,98}... | collective-permute-start | bytes 786440 | tf_op jit(solution)/shard_map/ppermute | solution.py:105
  150.3 2.7 %collective-permute-start.12 = (bf16[8,128,128]{2,1,0:T(8,128)(2,1)}, bf16[8,128,128]{2,1,0:T(8,128)(2,1)}, u32[]{:S(2)}, u32[]{:S(2)}) collective-permute-start(bf16[8,128,128]{2,1,0:T(8,128)(2,1)} %get-tuple-element.12), channel_id=1, source_target_pairs={{384,512},{512,640},{640,768},{768,896},{385,513},{513,641},{641,7... | collective-permute-start | bytes 786440 | tf_op jit(solution)/shard_map/cond/branch_1_fun/ppermute | solution.py:116
  151.7 8.3 %collective-permute-start.16 = (bf16[8,128,128]{2,1,0:T(8,128)(2,1)}, bf16[8,128,128]{2,1,0:T(8,128)(2,1)}, u32[]{:S(2)}, u32[]{:S(2)}) collective-permute-start(bf16[8,128,128]{2,1,0:T(8,128)(2,1)} %get-tuple-element.13), channel_id=1, source_target_pairs={{128,0},{256,128},{384,256},{512,384},{129,1},{257,129},{385,257},... | collective-permute-start | bytes 786440 | tf_op jit(solution)/shard_map/cond/branch_1_fun/ppermute | solution.py:117
  153.0 8.3 %collective-permute-start.13 = (bf16[8,128,128]{2,1,0:T(8,128)(2,1)}, bf16[8,128,128]{2,1,0:T(8,128)(2,1)}, u32[]{:S(2)}, u32[]{:S(2)}) collective-permute-start(bf16[8,128,128]{2,1,0:T(8,128)(2,1)} %collective-permute-done.12), channel_id=1, source_target_pairs={{512,640},{640,768},{768,896},{513,641},{641,769},{769,897},{514,6... | collective-permute-start | bytes 786440 | tf_op jit(solution)/shard_map/cond/branch_1_fun/ppermute | solution.py:116
  160.0 9.3 %collective-permute-start.17 = (bf16[8,128,128]{2,1,0:T(8,128)(2,1)}, bf16[8,128,128]{2,1,0:T(8,128)(2,1)}, u32[]{:S(2)}, u32[]{:S(2)}) collective-permute-start(bf16[8,128,128]{2,1,0:T(8,128)(2,1)} %collective-permute-done.16), channel_id=1, source_target_pairs={{128,0},{256,128},{384,256},{129,1},{257,129},{385,257},{130,2},{2... | collective-permute-start | bytes 786440 | tf_op jit(solution)/shard_map/cond/branch_1_fun/ppermute | solution.py:117
  161.3 9.3 %collective-permute-start.14 = (bf16[8,128,128]{2,1,0:T(8,128)(2,1)}, bf16[8,128,128]{2,1,0:T(8,128)(2,1)}, u32[]{:S(2)}, u32[]{:S(2)}) collective-permute-start(bf16[8,128,128]{2,1,0:T(8,128)(2,1)} %collective-permute-done.13), channel_id=1, source_target_pairs={{640,768},{768,896},{641,769},{769,897},{642,770},{770,898},{643,7... | collective-permute-start | bytes 786440 | tf_op jit(solution)/shard_map/cond/branch_1_fun/ppermute | solution.py:116
  169.3 10.7 %collective-permute-start.18 = (bf16[8,128,128]{2,1,0:T(8,128)(2,1)}, bf16[8,128,128]{2,1,0:T(8,128)(2,1)}, u32[]{:S(2)}, u32[]{:S(2)}) collective-permute-start(bf16[8,128,128]{2,1,0:T(8,128)(2,1)} %collective-permute-done.17), channel_id=1, source_target_pairs={{128,0},{256,128},{129,1},{257,129},{130,2},{258,130},{131,3},{259... | collective-permute-start | bytes 786440 | tf_op jit(solution)/shard_map/cond/branch_1_fun/ppermute | solution.py:117
  170.6 10.7 %collective-permute-start.15 = (bf16[8,128,128]{2,1,0:T(8,128)(2,1)}, bf16[8,128,128]{2,1,0:T(8,128)(2,1)}, u32[]{:S(2)}, u32[]{:S(2)}) collective-permute-start(bf16[8,128,128]{2,1,0:T(8,128)(2,1)} %collective-permute-done.14), channel_id=1, source_target_pairs={{768,896},{769,897},{770,898},{771,899},{772,900},{773,901},{774,9... | collective-permute-start | bytes 786440 | tf_op jit(solution)/shard_map/cond/branch_1_fun/ppermute | solution.py:116
  180.0 10.2 %collective-permute-start.19 = (bf16[8,128,128]{2,1,0:T(8,128)(2,1)}, bf16[8,128,128]{2,1,0:T(8,128)(2,1)}, u32[]{:S(2)}, u32[]{:S(2)}) collective-permute-start(bf16[8,128,128]{2,1,0:T(8,128)(2,1)} %collective-permute-done.18), channel_id=1, source_target_pairs={{128,0},{129,1},{130,2},{131,3},{132,4},{133,5},{134,6},{135,7},{1... | collective-permute-start | bytes 786440 | tf_op jit(solution)/shard_map/cond/branch_1_fun/ppermute | solution.py:117
  194.8 17.5 %collective-permute-start.27 = (f32[4,128,128]{2,1,0:T(8,128)S(1)}, f32[4,128,128]{2,1,0:T(8,128)S(1)}, u32[]{:S(2)}, u32[]{:S(2)}) collective-permute-start(f32[4,128,128]{2,1,0:T(8,128)S(1)} %get-tuple-element.104), channel_id=1, source_target_pairs={{0,4},{2,6},{4,0},{6,2},{1,5},{3,7},{5,1},{7,3},{8,12},{10,14},{12... | collective-permute-start | bytes 786440 | tf_op jit(solution)/shard_map/ppermute | solution.py:158
  202.8 12.5 %collective-permute-start.28 = (f32[4,128,128]{2,1,0:T(8,128)S(1)}, f32[4,128,128]{2,1,0:T(8,128)S(1)}, u32[]{:S(2)}, u32[]{:S(2)}) collective-permute-start(f32[4,128,128]{2,1,0:T(8,128)S(1)} %shard_map.38), channel_id=1, source_target_pairs={{0,2},{2,4},{4,6},{6,0},{1,3},{3,5},{5,7},{7,1},{8,10},{10,12},{12... | collective-permute-start | bytes 786440 | tf_op jit(solution)/shard_map/ppermute | solution.py:158
  208.1 8.1 %collective-permute-start.29 = (f32[4,128,128]{2,1,0:T(8,128)S(1)}, f32[4,128,128]{2,1,0:T(8,128)S(1)}, u32[]{:S(2)}, u32[]{:S(2)}) collective-permute-start(f32[4,128,128]{2,1,0:T(8,128)S(1)} %shard_map.39), channel_id=1, source_target_pairs={{0,6},{2,0},{4,2},{6,4},{1,7},{3,1},{5,3},{7,5},{8,14},{10,8},{12,... | collective-permute-start | bytes 786440 | tf_op jit(solution)/shard_map/ppermute | solution.py:158
  216.3 12.6 %collective-permute-start.30 = (f32[2,128,128]{2,1,0:T(8,128)S(1)}, f32[2,128,128]{2,1,0:T(8,128)S(1)}, u32[]{:S(2)}, u32[]{:S(2)}) collective-permute-start(f32[2,128,128]{2,1,0:T(8,128)S(1)} %slice.17), channel_id=1, source_target_pairs={{0,1},{1,0},{2,3},{3,2},{4,5},{5,4},{6,7},{7,6},{8,9},{9,8},{10,11... | collective-permute-start | bytes 393224 | tf_op jit(solution)/shard_map/ppermute | solution.py:160

commit v8 on v6

--- a/solution.py
+++ b/solution.py
@@ -20,19 +20,26 @@
 
 
 def products(groups, other, place, left, right, *refs):
-    n = 1 + max(g[0] for g in groups)
+    n = 1 + max(array for group in groups for array, _ in group[2])
     a, refs = refs[:n], refs[n:]
     b, out = refs
     x, zh, core, y = (place[k] for k in range(4))
 
     def one(r):
         total = None
-        for array, start, dx, dz in groups:
+        for dx, dz, ((low, low_at), (high, high_at)) in groups:
             c = lax.rem(x + dx, X) * ZH + lax.rem(zh + dz, ZH)
             lefts, rights = [], []
             for p in range(SLOTS):
                 m = left[r, c * SLOTS + p]
-                tile = a[array][start + jnp.minimum(m, S - 1)]
+                if low == high and high_at == low_at + S // 2:
+                    tile = a[low][low_at + jnp.minimum(m, S - 1)]
+                else:
+                    tile = jnp.where(
+                        m < S // 2,
+                        a[low][low_at + jnp.minimum(m, S // 2 - 1)],
+                        a[high][high_at + jnp.clip(m - S // 2, 0, S // 2 - 1)],
+                    )
                 lefts.append(jnp.where(m < S, tile, jnp.zeros_like(tile)))
                 rights.append(b[jnp.minimum(right[r, c * SLOTS + p], ROW * S - 1)])
             value = jnp.dot(
@@ -45,7 +52,7 @@
 
     @pl.loop(0, Y * PER, unroll=8)
     def _(k):
-        to = lax.rem(y + k // PER, Y)
+        to = k // PER
         mine = lax.rem(core + other, CORE)
         out[k] = one((to * CORE + mine) * PER + lax.rem(k, PER))
 
@@ -88,8 +95,13 @@
     right = pair_b.reshape(R, COLS * SLOTS)
     place = jnp.stack([lax.axis_index(n) for n in ("x", "zh", "core", "y")]).astype(jnp.int32)
 
-    def over_x(value):
-        return [value] + [lax.ppermute(value, "x", ring(X, -d)) for d in range(1, X)]
+    def over_x(value, in_turn=False):
+        got = {}
+        for d in (2, 1, 3):
+            got[d] = lax.ppermute(value, "x", ring(X, -d))
+            if in_turn:
+                value, got[d] = lax.optimization_barrier((value, got[d]))
+        return [got[d] for d in range(1, X)]
 
     def fenced(function, *args):
         always = lax.optimization_barrier(jnp.bool_(True))
@@ -101,36 +113,42 @@
         flat, tree = jax.tree.flatten(values)
         return jax.tree.unflatten(tree, lax.optimization_barrier(tuple(flat)))
 
-    z1 = lax.ppermute(own, "zh", ring(ZH, -1))
-    z3 = lax.ppermute(own, "zh", ring(ZH, 1))
+    half = S // 2
+    z1_low = lax.ppermute(own[:half], "zh", ring(ZH, -1))
+    z3_high = lax.ppermute(own[half:], "zh", ring(ZH, 1))
     routed = lax.all_to_all(own, ("y", "core"), split_axis=0, concat_axis=0, tiled=True)
     own_x = fenced(over_x, own)
-    own_x, routed = together(own_x, routed)
+    own_x, routed, rest = together(own_x, routed, own)
     b = lax.all_gather(routed, "row", axis=0, tiled=True)
-    z1, z3, own_x, routed = together(z1, z3, own_x, routed)
+    z1_low, z3_high, own_x, rest = together(z1_low, z3_high, own_x, rest)
 
-    half = S // 2
-    z2_low = lax.ppermute(z1[:half], "zh", ring(ZH, -1))
-    z2_high = lax.ppermute(z3[half:], "zh", ring(ZH, 1))
-    near = fenced(over_x, jnp.concatenate([z1, z3]))
-    place, _ = passing(place, WEIGHT, z1, z3)
-    z2_low, z2_high, near, place = together(z2_low, z2_high, near, place)
-    far = over_x(jnp.concatenate([z2_low, z2_high]))
+    z2_low = lax.ppermute(z1_low, "zh", ring(ZH, -1))
+    z2_high = lax.ppermute(z3_high, "zh", ring(ZH, 1))
+    z1_high = lax.ppermute(rest[half:], "zh", ring(ZH, -1))
+    z3_low = lax.ppermute(rest[:half], "zh", ring(ZH, 1))
+    first = jnp.concatenate([z1_low, z3_high])
+    first_x = fenced(functools.partial(over_x, in_turn=True), first)
+    place, _ = passing(place, WEIGHT, z1_low, z3_high)
+    z2_low, z2_high, z1_high, z3_low, first_x, place = together(z2_low, z2_high, z1_high, z3_low, first_x, place)
+    last = jnp.concatenate([z2_low, z2_high, z1_high, z3_low])
+    last_x = over_x(last)
 
-    arrays = own_x + near + far
+    arrays = [own, *own_x, first, *first_x, last, *last_x]
     lists = (place, left, right)
-    groups = [(d, 0, d, 0) for d in range(X)]
-    groups += [(X + d, k * S, d, z) for k, z in enumerate((1, 3)) for d in range(X)]
-    groups += [(2 * X + d, 0, d, 2) for d in range(X)]
+    groups = []
+    for d in range(X):
+        at_own, at_first, at_last = d, X + d, 2 * X + d
+        groups.append((d, 0, ((at_own, 0), (at_own, half))))
+        groups.append((d, 1, ((at_first, 0), (at_last, 2 * half))))
+        groups.append((d, 3, ((at_last, 3 * half), (at_first, half))))
+        groups.append((d, 2, ((at_last, 0), (at_last, half))))
     send = call(groups, 1, lists, arrays, b)
     got = lax.ppermute(send, "core", ring(CORE, 1))
     keep = call(groups, 0, lists, arrays, b)
 
-    quarter = [keep[d * PER : (d + 1) * PER] + got[d * PER : (d + 1) * PER] for d in range(Y)]
-    total = quarter[0]
-    for d in range(1, Y):
-        total = total + lax.ppermute(quarter[d], "y", ring(Y, d))
-    return total[None, None]
+    parts = (keep + got).reshape(Y, PER, BS, BS)
+    parts = lax.all_to_all(parts, "y", split_axis=0, concat_axis=0, tiled=True)
+    return jnp.sum(parts, axis=0)[None, None]
 
 
 def solution(mesh):

time: 192 us -> 207 us (1.078)
  blocking collectives: 0 us -> 13.6 us
  starting transfers between devices: 94.2 us -> 103 us
  waiting for transfers between devices: 68.3 us -> 61.1 us
    all_to_all x0 -> x1, blocking collectives: none -> 13.6 us  [on_device(): parts = lax.all_to_all(parts, 'y', split_axis=0, concat_axis=0, tiled=True)]
    all_to_all x1, starting transfers between devices: 6.57 us -> 17.5 us  [on_device(): lax.all_to_all(own, ('y', 'core'), split_axis=0, concat_axis=0, tiled=True)]
    all_gather x1, waiting for transfers between devices: 18.5 us -> 9.9 us  [on_device(): b = lax.all_gather(routed, 'row', axis=0, tiled=True)]
    ppermute x16 -> x15, starting transfers between devices: 83 us -> 81.2 us  [the longest x9 39.2 us: over_x(): got[d] = lax.ppermute(value, 'x', ring(X, -d))]
    ppermute x16 -> x15, waiting for transfers between devices: 49.8 us -> 51.2 us  [the longest x9 41.6 us: over_x(): got[d] = lax.ppermute(value, 'x', ring(X, -d))]
  transfers between devices with their start and end apart: 19 -> 18, of which waited for: 12 -> 11; matrix products, arithmetic and copies ran while one was open for 1% -> 1% of each run, Pallas kernels for 3% -> 3%
where the time goes in v8:
time: 207 us; the launch traced here: 206 us
  starting transfers between devices  103 us (50%)
  waiting for transfers between devices  61.1 us (30%)
  blocking collectives  13.6 us (7%)
  between operations  13.6 us (7%)
  Pallas kernels  9.57 us (5%)
  local copies, waits for them, and re-layouts  4 us (2%)
    ppermute x9, waiting for transfers between devices, over_x(): got[d] = lax.ppermute(value, 'x', ring(X, -d))  41.6 us
    ppermute x9, starting transfers between devices, over_x(): got[d] = lax.ppermute(value, 'x', ring(X, -d))  39.2 us
    all_to_all x1, starting transfers between devices, on_device(): lax.all_to_all(own, ('y', 'core'), split_axis=0, concat_axis=0, tiled=True)  17.5 us
    all_to_all x1, blocking collectives, on_device(): parts = lax.all_to_all(parts, 'y', split_axis=0, concat_axis=0, tiled=True)  13.6 us
    ppermute x1, starting transfers between devices, on_device(): z3_low = lax.ppermute(rest[:half], 'zh', ring(ZH, 1))  12 us
    ppermute x1, starting transfers between devices, on_device(): z1_low = lax.ppermute(own[:half], 'zh', ring(ZH, -1))  10.1 us
    all_gather x1, waiting for transfers between devices, on_device(): b = lax.all_gather(routed, 'row', axis=0, tiled=True)  9.9 us
    ppermute x1, waiting for transfers between devices, on_device(): z1_low = lax.ppermute(own[:half], 'zh', ring(ZH, -1))  9.52 us
  transfers between devices with their start and end apart: 18, of which 11 were waited for; matrix products, arithmetic and copies ran while one was open for 1% of the time, Pallas kernels for 3%

profile of v8, /device:TPU:1, one launch (start us, length us, event | category | flops | bytes accessed | tf_op | source)
XLA Modules:
  0.0 206.5 jit_solution(12198771566256443742)
XLA Ops:
  6.5 17.5 %all-to-all-start = ((bf16[8,128,128]{2,1,0:T(8,128)(2,1)}), bf16[8,128,128]{2,1,0:T(8,128)(2,1)S(1)}, u32[]{:S(2)}, u32[]{:S(2)}) async-start(bf16[8,128,128]{2,1,0:T(8,128)(2,1)} %bitcast.14), calls=%async_computation | async-start | bytes 524288 | tf_op jit(solution)/shard_map/all_to_all | solution.py:119
  24.0 0.0 all-gather.2.cloned.1.call-start
  24.0 1.0 slice_bitcast_fusion
  25.0 3.9 %collective-permute-start.7 = (bf16[4,128,128]{2,1,0:T(8,128)(2,1)S(1)}, bf16[4,128,128]{2,1,0:T(8,128)(2,1)S(1)}, u32[]{:S(2)}, u32[]{:S(2)}) collective-permute-start(bf16[4,128,128]{2,1,0:T(8,128)(2,1)S(1)} %get-tuple-element.66), channel_id=1, source_target_pairs={{0,8},{8,16},{16,24},{24,0},{1,9},{9,17},{17,25},{25,1},{2,10},{10... | collective-permute-start | bytes 393224 | tf_op jit(solution)/shard_map/ppermute | solution.py:118
  29.0 10.1 %collective-permute-start.6 = (bf16[4,128,128]{2,1,0:T(8,128)(2,1)S(1)}, bf16[4,128,128]{2,1,0:T(8,128)(2,1)S(1)}, u32[]{:S(2)}, u32[]{:S(2)}) collective-permute-start(bf16[4,128,128]{2,1,0:T(8,128)(2,1)S(1)} %get-tuple-element.67), channel_id=1, source_target_pairs={{0,24},{8,0},{16,8},{24,16},{1,25},{9,1},{17,9},{25,17},{2,26},{10... | collective-permute-start | bytes 393224 | tf_op jit(solution)/shard_map/ppermute | solution.py:117
  39.0 18.8 %conditional.2 = (bf16[8,128,128]{2,1,0:T(8,128)(2,1)}, bf16[8,128,128]{2,1,0:T(8,128)(2,1)}, bf16[8,128,128]{2,1,0:T(8,128)(2,1)}) conditional(s32[]{:T(128)} %convert_element_type.4, () %tuple.28, bf16[8,128,128]{2,1,0:T(8,128)(2,1)} %bitcast.16), branch_computations={%region_0.0_spmd, %region_1.0_spmd} | conditional | bytes 3145872 | solution.py:110
  39.0 2.3 %collective-permute-start.2 = (bf16[8,128,128]{2,1,0:T(8,128)(2,1)}, bf16[8,128,128]{2,1,0:T(8,128)(2,1)}, u32[]{:S(2)}, u32[]{:S(2)}) collective-permute-start(bf16[8,128,128]{2,1,0:T(8,128)(2,1)} %param.1), channel_id=1, source_target_pairs={{0,32},{32,64},{64,96},{96,0},{1,33},{33,65},{65,97},{97,1},{2,34}... | collective-permute-start | bytes 786440 | tf_op jit(solution)/shard_map/cond/branch_1_fun/ppermute | solution.py:101
  41.3 4.4 %collective-permute-start.1 = (bf16[8,128,128]{2,1,0:T(8,128)(2,1)}, bf16[8,128,128]{2,1,0:T(8,128)(2,1)}, u32[]{:S(2)}, u32[]{:S(2)}) collective-permute-start(bf16[8,128,128]{2,1,0:T(8,128)(2,1)} %param.1), channel_id=1, source_target_pairs={{0,64},{32,96},{64,0},{96,32},{1,65},{33,97},{65,1},{97,33},{2,66}... | collective-permute-start | bytes 786440 | tf_op jit(solution)/shard_map/cond/branch_1_fun/ppermute | solution.py:101
  45.7 3.1 %collective-permute-start = (bf16[8,128,128]{2,1,0:T(8,128)(2,1)}, bf16[8,128,128]{2,1,0:T(8,128)(2,1)}, u32[]{:S(2)}, u32[]{:S(2)}) collective-permute-start(bf16[8,128,128]{2,1,0:T(8,128)(2,1)} %param.1), channel_id=1, source_target_pairs={{0,96},{32,0},{64,32},{96,64},{1,97},{33,1},{65,33},{97,65},{2,98}... | collective-permute-start | bytes 786440 | tf_op jit(solution)/shard_map/cond/branch_1_fun/ppermute | solution.py:101
  48.7 0.8 collective-permute-done.2
  49.6 6.2 %collective-permute-done.1 = bf16[8,128,128]{2,1,0:T(8,128)(2,1)} collective-permute-done((bf16[8,128,128]{2,1,0:T(8,128)(2,1)}, bf16[8,128,128]{2,1,0:T(8,128)(2,1)}, u32[]{:S(2)}, u32[]{:S(2)}) %collective-permute-start.1) | collective-permute-done | bytes 262176 | tf_op jit(solution)/shard_map/cond/branch_1_fun/ppermute | solution.py:101
  55.8 2.0 collective-permute-done
  57.8 0.6 pad_add_fusion.place_ref
  58.4 0.0 all-to-all-done
  58.4 0.0 copy-start.3
  58.4 0.0 collective-permute-done.7
  58.4 9.5 %collective-permute-done.6 = bf16[4,128,128]{2,1,0:T(8,128)(2,1)S(1)} collective-permute-done((bf16[4,128,128]{2,1,0:T(8,128)(2,1)S(1)}, bf16[4,128,128]{2,1,0:T(8,128)(2,1)S(1)}, u32[]{:S(2)}, u32[]{:S(2)}) %collective-permute-start.6) | collective-permute-done | bytes 131104 | tf_op jit(solution)/shard_map/ppermute | solution.py:117
  67.9 6.4 %collective-permute-start.8 = (bf16[4,128,128]{2,1,0:T(8,128)(2,1)S(1)}, bf16[4,128,128]{2,1,0:T(8,128)(2,1)S(1)}, u32[]{:S(2)}, u32[]{:S(2)}) collective-permute-start(bf16[4,128,128]{2,1,0:T(8,128)(2,1)S(1)} %collective-permute-done.6), channel_id=1, source_target_pairs={{0,24},{8,0},{16,8},{24,16},{1,25},{9,1},{17,9},{25,17},{2,26},{10... | collective-permute-start | bytes 393224 | tf_op jit(solution)/shard_map/ppermute | solution.py:125
  74.3 7.5 %collective-permute-start.9 = (bf16[4,128,128]{2,1,0:T(8,128)(2,1)S(1)}, bf16[4,128,128]{2,1,0:T(8,128)(2,1)S(1)}, u32[]{:S(2)}, u32[]{:S(2)}) collective-permute-start(bf16[4,128,128]{2,1,0:T(8,128)(2,1)S(1)} %collective-permute-done.7), channel_id=1, source_target_pairs={{0,8},{8,16},{16,24},{24,0},{1,9},{9,17},{17,25},{25,1},{2,10},{10... | collective-permute-start | bytes 393224 | tf_op jit(solution)/shard_map/ppermute | solution.py:126
  81.9 0.0 copy-done.3
  81.9 0.0 all-gather.2.cloned.1.call-update
  81.9 1.0 fusion
  82.9 12.0 %collective-permute-start.11 = (bf16[4,128,128]{2,1,0:T(8,128)(2,1)S(1)}, bf16[4,128,128]{2,1,0:T(8,128)(2,1)S(1)}, u32[]{:S(2)}, u32[]{:S(2)}) collective-permute-start(bf16[4,128,128]{2,1,0:T(8,128)(2,1)S(1)} %get-tuple-element.64), channel_id=1, source_target_pairs={{0,8},{8,16},{16,24},{24,0},{1,9},{9,17},{17,25},{25,1},{2,10},{10... | collective-permute-start | bytes 393224 | tf_op jit(solution)/shard_map/ppermute | solution.py:128
  94.9 2.0 collective-permute-start.10
  96.9 1.2 shard_map.37.place
  98.1 0.0 copy-start.4
  98.1 0.0 copy-start.5
  98.1 0.0 copy-start.1
  98.2 0.0 copy-start.2
  98.2 26.5 %conditional.3 = (bf16[8,128,128]{2,1,0:T(8,128)(2,1)}, bf16[8,128,128]{2,1,0:T(8,128)(2,1)}, bf16[8,128,128]{2,1,0:T(8,128)(2,1)}) conditional(s32[]{:T(128)} %convert_element_type.4, () %tuple.31, bf16[8,128,128]{2,1,0:T(8,128)(2,1)S(1)} %constant_dynamic-update-slice_fusion.refs_4_), branch_computations={%region_2.0_spmd, %region_3.0_spmd} | conditional | bytes 3145872 | solution.py:110
  98.2 4.8 %collective-permute-start.3 = (bf16[8,128,128]{2,1,0:T(8,128)(2,1)S(1)}, bf16[8,128,128]{2,1,0:T(8,128)(2,1)}, u32[]{:S(2)}, u32[]{:S(2)}) collective-permute-start(bf16[8,128,128]{2,1,0:T(8,128)(2,1)S(1)} %param.3), channel_id=1, source_target_pairs={{0,64},{32,96},{64,0},{96,32},{1,65},{33,97},{65,1},{97,33},{2,66}... | collective-permute-start | bytes 786440 | tf_op jit(solution)/shard_map/cond/branch_1_fun/ppermute | solution.py:101
  103.0 4.7 %collective-permute-done.3 = bf16[8,128,128]{2,1,0:T(8,128)(2,1)} collective-permute-done((bf16[8,128,128]{2,1,0:T(8,128)(2,1)S(1)}, bf16[8,128,128]{2,1,0:T(8,128)(2,1)}, u32[]{:S(2)}, u32[]{:S(2)}) %collective-permute-start.3) | collective-permute-done | bytes 262176 | tf_op jit(solution)/shard_map/cond/branch_1_fun/ppermute | solution.py:101
  107.7 4.4 %collective-permute-start.4 = (bf16[8,128,128]{2,1,0:T(8,128)(2,1)S(1)}, bf16[8,128,128]{2,1,0:T(8,128)(2,1)}, u32[]{:S(2)}, u32[]{:S(2)}) collective-permute-start(bf16[8,128,128]{2,1,0:T(8,128)(2,1)S(1)} %param.3), channel_id=1, source_target_pairs={{0,96},{32,0},{64,32},{96,64},{1,97},{33,1},{65,33},{97,65},{2,98}... | collective-permute-start | bytes 786440 | tf_op jit(solution)/shard_map/cond/branch_1_fun/ppermute | solution.py:101
  112.1 3.3 %collective-permute-done.4 = bf16[8,128,128]{2,1,0:T(8,128)(2,1)} collective-permute-done((bf16[8,128,128]{2,1,0:T(8,128)(2,1)S(1)}, bf16[8,128,128]{2,1,0:T(8,128)(2,1)}, u32[]{:S(2)}, u32[]{:S(2)}) %collective-permute-start.4) | collective-permute-done | bytes 262176 | tf_op jit(solution)/shard_map/cond/branch_1_fun/ppermute | solution.py:101
  115.4 2.9 %collective-permute-start.5 = (bf16[8,128,128]{2,1,0:T(8,128)(2,1)S(1)}, bf16[8,128,128]{2,1,0:T(8,128)(2,1)}, u32[]{:S(2)}, u32[]{:S(2)}) collective-permute-start(bf16[8,128,128]{2,1,0:T(8,128)(2,1)S(1)} %param.3), channel_id=1, source_target_pairs={{0,32},{32,64},{64,96},{96,0},{1,33},{33,65},{65,97},{97,1},{2,34}... | collective-permute-start | bytes 786440 | tf_op jit(solution)/shard_map/cond/branch_1_fun/ppermute | solution.py:101
  118.3 6.3 %collective-permute-done.5 = bf16[8,128,128]{2,1,0:T(8,128)(2,1)} collective-permute-done((bf16[8,128,128]{2,1,0:T(8,128)(2,1)S(1)}, bf16[8,128,128]{2,1,0:T(8,128)(2,1)}, u32[]{:S(2)}, u32[]{:S(2)}) %collective-permute-start.5) | collective-permute-done | bytes 262176 | tf_op jit(solution)/shard_map/cond/branch_1_fun/ppermute | solution.py:101
  124.7 0.0 collective-permute-done.8
  124.7 0.0 collective-permute-done.9
  124.7 0.0 collective-permute-done.11
  124.7 0.0 collective-permute-done.10
  124.8 11.2 %collective-permute-start.14 = (bf16[16,128,128]{2,1,0:T(8,128)(2,1)S(1)}, bf16[16,128,128]{2,1,0:T(8,128)(2,1)S(1)}, u32[]{:S(2)}, u32[]{:S(2)}) collective-permute-start(bf16[16,128,128]{2,1,0:T(8,128)(2,1)S(1)} %constant_dynamic-update-slice_fusion.2.refs_8_), channel_id=1, source_target_pairs={{0,32},{32,64},{64,96},{96,0},{1,33},{33,65},{65,97},{97,1},{2,34}... | collective-permute-start | bytes 1572872 | tf_op jit(solution)/shard_map/ppermute | solution.py:101
  136.0 1.9 collective-permute-start.13
  138.0 4.3 %collective-permute-start.12 = (bf16[16,128,128]{2,1,0:T(8,128)(2,1)S(1)}, bf16[16,128,128]{2,1,0:T(8,128)(2,1)S(1)}, u32[]{:S(2)}, u32[]{:S(2)}) collective-permute-start(bf16[16,128,128]{2,1,0:T(8,128)(2,1)S(1)} %constant_dynamic-update-slice_fusion.2.refs_8_), channel_id=1, source_target_pairs={{0,96},{32,0},{64,32},{96,64},{1,97},{33,1},{65,33},{97,65},{2,98}... | collective-permute-start | bytes 1572872 | tf_op jit(solution)/shard_map/ppermute | solution.py:101
  142.3 0.0 copy-done.4
  142.3 0.1 copy.18
  142.4 0.1 copy.20.left
  142.4 0.0 copy-done.5
  142.4 0.1 copy.19
  142.5 0.1 copy.21.right
  142.6 3.9 %collective-permute-done.14.refs_11_ = bf16[16,128,128]{2,1,0:T(8,128)(2,1)S(1)} collective-permute-done((bf16[16,128,128]{2,1,0:T(8,128)(2,1)S(1)}, bf16[16,128,128]{2,1,0:T(8,128)(2,1)S(1)}, u32[]{:S(2)}, u32[]{:S(2)}) %collective-permute-start.14) | collective-permute-done | bytes 524320 | tf_op jit(solution)/shard_map/ppermute | solution.py:101
  146.5 11.2 %collective-permute-done.13.refs_10_ = bf16[16,128,128]{2,1,0:T(8,128)(2,1)S(1)} collective-permute-done((bf16[16,128,128]{2,1,0:T(8,128)(2,1)S(1)}, bf16[16,128,128]{2,1,0:T(8,128)(2,1)S(1)}, u32[]{:S(2)}, u32[]{:S(2)}) %collective-permute-start.13) | collective-permute-done | bytes 524320 | tf_op jit(solution)/shard_map/ppermute | solution.py:101
  157.7 3.1 %collective-permute-done.12.refs_9_ = bf16[16,128,128]{2,1,0:T(8,128)(2,1)S(1)} collective-permute-done((bf16[16,128,128]{2,1,0:T(8,128)(2,1)S(1)}, bf16[16,128,128]{2,1,0:T(8,128)(2,1)S(1)}, u32[]{:S(2)}, u32[]{:S(2)}) %collective-permute-start.12) | collective-permute-done | bytes 524320 | tf_op jit(solution)/shard_map/ppermute | solution.py:101
  160.9 9.9 %all-gather.2.cloned.1.call-done.refs_12_ = bf16[64,128,128]{2,1,0:T(8,128)(2,1)} async-done(((bf16[8,128,128]{2,1,0:T(8,128)(2,1)}), bf16[64,128,128]{2,1,0:T(8,128)(2,1)}) %all-gather.2.cloned.1.call-update) | async-done | bytes 2097168 | tf_op jit(solution)/shard_map/all_gather | solution.py:122
  170.8 0.0 copy-done.1
  170.8 0.0 copy-done.2
  170.8 0.0 copy-start
  170.8 1.6 copy-done
  172.4 4.2 %shard_map.39 = f32[8,128,128]{2,1,0:T(8,128)S(1)} custom-call(s32[4]{0:T(128)S(1)} %copy-done.1, s32[16,32]{1,0:T(8,128)S(1)} %copy.20.left, s32[16,32]{1,0:T(8,128)S(1)} %copy.21.right, bf16[8,128,128]{2,1,0:T(8,128)(2,1)S(1)} %bitcast.18, bf16[8,128,128]{2,1,0:T(8,128)(2,1)} %get-tuple-element.53.refs_1_, bf16[8,128,128]{2,1,0:T(8,128)(2,1)} %get-tuple-element.54.refs_2_, ...), custom_call_target="tpu_custom_call" | custom-call | flops 1073741824 | bytes 8388608 | tf_op jit(solution)/shard_map/pallas_call | solution.py:63
  176.6 4.5 %collective-permute-start.15 = (f32[8,128,128]{2,1,0:T(8,128)S(1)}, f32[8,128,128]{2,1,0:T(8,128)S(1)}, u32[]{:S(2)}, u32[]{:S(2)}) collective-permute-start(f32[8,128,128]{2,1,0:T(8,128)S(1)} %shard_map.39), channel_id=1, source_target_pairs={{0,1},{1,0},{2,3},{3,2},{4,5},{5,4},{6,7},{7,6},{8,9},{9,8},{10,11... | collective-permute-start | bytes 1572872 | tf_op jit(solution)/shard_map/ppermute | solution.py:146
  181.1 4.2 %shard_map.38 = f32[8,128,128]{2,1,0:T(8,128)S(1)} custom-call(s32[4]{0:T(128)S(1)} %copy-done.1, s32[16,32]{1,0:T(8,128)S(1)} %copy.20.left, s32[16,32]{1,0:T(8,128)S(1)} %copy.21.right, bf16[8,128,128]{2,1,0:T(8,128)(2,1)S(1)} %bitcast.19, bf16[8,128,128]{2,1,0:T(8,128)(2,1)} %get-tuple-element.53.refs_1_, bf16[8,128,128]{2,1,0:T(8,128)(2,1)} %get-tuple-element.54.refs_2_, ...), custom_call_target="tpu_custom_call" | custom-call | flops 1073741824 | bytes 8388608 | tf_op jit(solution)/shard_map/pallas_call | solution.py:63
  185.3 0.0 collective-permute-done.15
  185.3 0.1 add.3
  185.4 13.6 %all_to_all.10 = f32[4,2,128,128]{3,2,1,0:T(8,128)S(1)} all-to-all(f32[4,2,128,128]{3,2,1,0:T(8,128)S(1)} %bitcast.20), channel_id=1, replica_groups=mesh['row'=8,'x'=4,'zh'=4,'y'=4,'core'=2] {'y'}, dimensions={0} | all-to-all | bytes 1048576 | tf_op jit(solution)/shard_map/all_to_all | solution.py:150
  199.0 0.7 reduce_sum.9
  (6 shorter events, 0.1 us)
Async XLA Ops:
  6.5 51.8 %all-to-all-start = ((bf16[8,128,128]{2,1,0:T(8,128)(2,1)}), bf16[8,128,128]{2,1,0:T(8,128)(2,1)S(1)}, u32[]{:S(2)}, u32[]{:S(2)}) async-start(bf16[8,128,128]{2,1,0:T(8,128)(2,1)} %bitcast.14), calls=%async_computation | async-start | bytes 524288 | tf_op jit(solution)/shard_map/all_to_all | solution.py:119
  24.0 146.8 %all-gather.2.cloned.1.call-start = ((), (), s32[]{:S(2)}) async-start(), calls=%async_computation.2 | async-start | bytes 2359296 | tf_op jit(solution)/shard_map/all_gather | solution.py:122
  25.0 33.4 %collective-permute-start.7 = (bf16[4,128,128]{2,1,0:T(8,128)(2,1)S(1)}, bf16[4,128,128]{2,1,0:T(8,128)(2,1)S(1)}, u32[]{:S(2)}, u32[]{:S(2)}) collective-permute-start(bf16[4,128,128]{2,1,0:T(8,128)(2,1)S(1)} %get-tuple-element.66), channel_id=1, source_target_pairs={{0,8},{8,16},{16,24},{24,0},{1,9},{9,17},{17,25},{25,1},{2,10},{10... | collective-permute-start | bytes 393224 | tf_op jit(solution)/shard_map/ppermute | solution.py:118
  29.0 38.9 %collective-permute-start.6 = (bf16[4,128,128]{2,1,0:T(8,128)(2,1)S(1)}, bf16[4,128,128]{2,1,0:T(8,128)(2,1)S(1)}, u32[]{:S(2)}, u32[]{:S(2)}) collective-permute-start(bf16[4,128,128]{2,1,0:T(8,128)(2,1)S(1)} %get-tuple-element.67), channel_id=1, source_target_pairs={{0,24},{8,0},{16,8},{24,16},{1,25},{9,1},{17,9},{25,17},{2,26},{10... | collective-permute-start | bytes 393224 | tf_op jit(solution)/shard_map/ppermute | solution.py:117
  39.0 10.5 %collective-permute-start.2 = (bf16[8,128,128]{2,1,0:T(8,128)(2,1)}, bf16[8,128,128]{2,1,0:T(8,128)(2,1)}, u32[]{:S(2)}, u32[]{:S(2)}) collective-permute-start(bf16[8,128,128]{2,1,0:T(8,128)(2,1)} %param.1), channel_id=1, source_target_pairs={{0,32},{32,64},{64,96},{96,0},{1,33},{33,65},{65,97},{97,1},{2,34}... | collective-permute-start | bytes 786440 | tf_op jit(solution)/shard_map/cond/branch_1_fun/ppermute | solution.py:101
  41.3 14.5 %collective-permute-start.1 = (bf16[8,128,128]{2,1,0:T(8,128)(2,1)}, bf16[8,128,128]{2,1,0:T(8,128)(2,1)}, u32[]{:S(2)}, u32[]{:S(2)}) collective-permute-start(bf16[8,128,128]{2,1,0:T(8,128)(2,1)} %param.1), channel_id=1, source_target_pairs={{0,64},{32,96},{64,0},{96,32},{1,65},{33,97},{65,1},{97,33},{2,66}... | collective-permute-start | bytes 786440 | tf_op jit(solution)/shard_map/cond/branch_1_fun/ppermute | solution.py:101
  45.7 12.1 %collective-permute-start = (bf16[8,128,128]{2,1,0:T(8,128)(2,1)}, bf16[8,128,128]{2,1,0:T(8,128)(2,1)}, u32[]{:S(2)}, u32[]{:S(2)}) collective-permute-start(bf16[8,128,128]{2,1,0:T(8,128)(2,1)} %param.1), channel_id=1, source_target_pairs={{0,96},{32,0},{64,32},{96,64},{1,97},{33,1},{65,33},{97,65},{2,98}... | collective-permute-start | bytes 786440 | tf_op jit(solution)/shard_map/cond/branch_1_fun/ppermute | solution.py:101
  58.4 23.5 %copy-start.3 = (bf16[8,128,128]{2,1,0:T(8,128)(2,1)}, bf16[8,128,128]{2,1,0:T(8,128)(2,1)S(1)}, u32[]{:S(2)}) copy-start(bf16[8,128,128]{2,1,0:T(8,128)(2,1)S(1)} %all-to-all-done) | copy-start | bytes 786436
  67.9 56.8 %collective-permute-start.8 = (bf16[4,128,128]{2,1,0:T(8,128)(2,1)S(1)}, bf16[4,128,128]{2,1,0:T(8,128)(2,1)S(1)}, u32[]{:S(2)}, u32[]{:S(2)}) collective-permute-start(bf16[4,128,128]{2,1,0:T(8,128)(2,1)S(1)} %collective-permute-done.6), channel_id=1, source_target_pairs={{0,24},{8,0},{16,8},{24,16},{1,25},{9,1},{17,9},{25,17},{2,26},{10... | collective-permute-start | bytes 393224 | tf_op jit(solution)/shard_map/ppermute | solution.py:125
  74.3 50.3 %collective-permute-start.9 = (bf16[4,128,128]{2,1,0:T(8,128)(2,1)S(1)}, bf16[4,128,128]{2,1,0:T(8,128)(2,1)S(1)}, u32[]{:S(2)}, u32[]{:S(2)}) collective-permute-start(bf16[4,128,128]{2,1,0:T(8,128)(2,1)S(1)} %collective-permute-done.7), channel_id=1, source_target_pairs={{0,8},{8,16},{16,24},{24,0},{1,9},{9,17},{17,25},{25,1},{2,10},{10... | collective-permute-start | bytes 393224 | tf_op jit(solution)/shard_map/ppermute | solution.py:126
  82.9 41.8 %collective-permute-start.11 = (bf16[4,128,128]{2,1,0:T(8,128)(2,1)S(1)}, bf16[4,128,128]{2,1,0:T(8,128)(2,1)S(1)}, u32[]{:S(2)}, u32[]{:S(2)}) collective-permute-start(bf16[4,128,128]{2,1,0:T(8,128)(2,1)S(1)} %get-tuple-element.64), channel_id=1, source_target_pairs={{0,8},{8,16},{16,24},{24,0},{1,9},{9,17},{17,25},{25,1},{2,10},{10... | collective-permute-start | bytes 393224 | tf_op jit(solution)/shard_map/ppermute | solution.py:128
  94.9 29.8 %collective-permute-start.10 = (bf16[4,128,128]{2,1,0:T(8,128)(2,1)S(1)}, bf16[4,128,128]{2,1,0:T(8,128)(2,1)S(1)}, u32[]{:S(2)}, u32[]{:S(2)}) collective-permute-start(bf16[4,128,128]{2,1,0:T(8,128)(2,1)S(1)} %get-tuple-element.65), channel_id=1, source_target_pairs={{0,24},{8,0},{16,8},{24,16},{1,25},{9,1},{17,9},{25,17},{2,26},{10... | collective-permute-start | bytes 393224 | tf_op jit(solution)/shard_map/ppermute | solution.py:127
  98.1 44.2 %copy-start.4 = (s32[1,1,1,16,16,2]{4,5,3,2,1,0:T(2,128)S(1)}, s32[1,1,1,16,16,2]{4,5,3,2,1,0:T(2,128)}, u32[]{:S(2)}) copy-start(s32[1,1,1,16,16,2]{4,5,3,2,1,0:T(2,128)} %param.8) | copy-start | bytes 6148
  98.1 44.3 %copy-start.5 = (s32[1,1,1,16,16,2]{4,5,3,2,1,0:T(2,128)S(1)}, s32[1,1,1,16,16,2]{4,5,3,2,1,0:T(2,128)}, u32[]{:S(2)}) copy-start(s32[1,1,1,16,16,2]{4,5,3,2,1,0:T(2,128)} %param.9) | copy-start | bytes 6148
  98.1 72.6 %copy-start.1 = (s32[4]{0:T(128)S(1)}, s32[4]{0:T(128)}, u32[]{:S(2)}) copy-start(s32[4]{0:T(128)} %shard_map.37.place) | copy-start | bytes 52
  98.2 72.6 %copy-start.2 = (bf16[1,1,1,8,1,128,128]{6,5,4,3,2,1,0:T(8,128)(2,1)S(1)}, bf16[1,1,1,8,1,128,128]{6,5,4,3,2,1,0:T(8,128)(2,1)}, u32[]{:S(2)}) copy-start(bf16[1,1,1,8,1,128,128]{6,5,4,3,2,1,0:T(8,128)(2,1)} %param.7) | copy-start | bytes 786436
  98.2 9.5 %collective-permute-start.3 = (bf16[8,128,128]{2,1,0:T(8,128)(2,1)S(1)}, bf16[8,128,128]{2,1,0:T(8,128)(2,1)}, u32[]{:S(2)}, u32[]{:S(2)}) collective-permute-start(bf16[8,128,128]{2,1,0:T(8,128)(2,1)S(1)} %param.3), channel_id=1, source_target_pairs={{0,64},{32,96},{64,0},{96,32},{1,65},{33,97},{65,1},{97,33},{2,66}... | collective-permute-start | bytes 786440 | tf_op jit(solution)/shard_map/cond/branch_1_fun/ppermute | solution.py:101
  107.7 7.7 %collective-permute-start.4 = (bf16[8,128,128]{2,1,0:T(8,128)(2,1)S(1)}, bf16[8,128,128]{2,1,0:T(8,128)(2,1)}, u32[]{:S(2)}, u32[]{:S(2)}) collective-permute-start(bf16[8,128,128]{2,1,0:T(8,128)(2,1)S(1)} %param.3), channel_id=1, source_target_pairs={{0,96},{32,0},{64,32},{96,64},{1,97},{33,1},{65,33},{97,65},{2,98}... | collective-permute-start | bytes 786440 | tf_op jit(solution)/shard_map/cond/branch_1_fun/ppermute | solution.py:101
  115.4 9.3 %collective-permute-start.5 = (bf16[8,128,128]{2,1,0:T(8,128)(2,1)S(1)}, bf16[8,128,128]{2,1,0:T(8,128)(2,1)}, u32[]{:S(2)}, u32[]{:S(2)}) collective-permute-start(bf16[8,128,128]{2,1,0:T(8,128)(2,1)S(1)} %param.3), channel_id=1, source_target_pairs={{0,32},{32,64},{64,96},{96,0},{1,33},{33,65},{65,97},{97,1},{2,34}... | collective-permute-start | bytes 786440 | tf_op jit(solution)/shard_map/cond/branch_1_fun/ppermute | solution.py:101
  124.8 21.7 %collective-permute-start.14 = (bf16[16,128,128]{2,1,0:T(8,128)(2,1)S(1)}, bf16[16,128,128]{2,1,0:T(8,128)(2,1)S(1)}, u32[]{:S(2)}, u32[]{:S(2)}) collective-permute-start(bf16[16,128,128]{2,1,0:T(8,128)(2,1)S(1)} %constant_dynamic-update-slice_fusion.2.refs_8_), channel_id=1, source_target_pairs={{0,32},{32,64},{64,96},{96,0},{1,33},{33,65},{65,97},{97,1},{2,34}... | collective-permute-start | bytes 1572872 | tf_op jit(solution)/shard_map/ppermute | solution.py:101
  136.0 21.7 %collective-permute-start.13 = (bf16[16,128,128]{2,1,0:T(8,128)(2,1)S(1)}, bf16[16,128,128]{2,1,0:T(8,128)(2,1)S(1)}, u32[]{:S(2)}, u32[]{:S(2)}) collective-permute-start(bf16[16,128,128]{2,1,0:T(8,128)(2,1)S(1)} %constant_dynamic-update-slice_fusion.2.refs_8_), channel_id=1, source_target_pairs={{0,64},{32,96},{64,0},{96,32},{1,65},{33,97},{65,1},{97,33},{2,66}... | collective-permute-start | bytes 1572872 | tf_op jit(solution)/shard_map/ppermute | solution.py:101
  138.0 22.9 %collective-permute-start.12 = (bf16[16,128,128]{2,1,0:T(8,128)(2,1)S(1)}, bf16[16,128,128]{2,1,0:T(8,128)(2,1)S(1)}, u32[]{:S(2)}, u32[]{:S(2)}) collective-permute-start(bf16[16,128,128]{2,1,0:T(8,128)(2,1)S(1)} %constant_dynamic-update-slice_fusion.2.refs_8_), channel_id=1, source_target_pairs={{0,96},{32,0},{64,32},{96,64},{1,97},{33,1},{65,33},{97,65},{2,98}... | collective-permute-start | bytes 1572872 | tf_op jit(solution)/shard_map/ppermute | solution.py:101
  170.8 1.6 copy-start
  176.6 8.7 %collective-permute-start.15 = (f32[8,128,128]{2,1,0:T(8,128)S(1)}, f32[8,128,128]{2,1,0:T(8,128)S(1)}, u32[]{:S(2)}, u32[]{:S(2)}) collective-permute-start(f32[8,128,128]{2,1,0:T(8,128)S(1)} %shard_map.39), channel_id=1, source_target_pairs={{0,1},{1,0},{2,3},{3,2},{4,5},{5,4},{6,7},{7,6},{8,9},{9,8},{10,11... | collective-permute-start | bytes 1572872 | tf_op jit(solution)/shard_map/ppermute | solution.py:146
Sparse Core Ops, SparseCore 0:
  82.0 88.6 all-gather.1

commit v9 on v6

--- a/solution.py
+++ b/solution.py
@@ -24,11 +24,12 @@
     a, refs = refs[:n], refs[n:]
     b, out = refs
     x, zh, core, y = (place[k] for k in range(4))
+    to_zh = (0, 1 + 2 * core, 3 - 2 * core, 2)
 
     def one(r):
         total = None
         for array, start, dx, dz in groups:
-            c = lax.rem(x + dx, X) * ZH + lax.rem(zh + dz, ZH)
+            c = lax.rem(x + dx, X) * ZH + lax.rem(zh + to_zh[dz], ZH)
             lefts, rights = [], []
             for p in range(SLOTS):
                 m = left[r, c * SLOTS + p]
@@ -45,7 +46,7 @@
 
     @pl.loop(0, Y * PER, unroll=8)
     def _(k):
-        to = lax.rem(y + k // PER, Y)
+        to = k // PER
         mine = lax.rem(core + other, CORE)
         out[k] = one((to * CORE + mine) * PER + lax.rem(k, PER))
 
@@ -89,7 +90,8 @@
     place = jnp.stack([lax.axis_index(n) for n in ("x", "zh", "core", "y")]).astype(jnp.int32)
 
     def over_x(value):
-        return [value] + [lax.ppermute(value, "x", ring(X, -d)) for d in range(1, X)]
+        two, one, three = (lax.ppermute(value, "x", ring(X, -d)) for d in (2, 1, 3))
+        return [one, two, three]
 
     def fenced(function, *args):
         always = lax.optimization_barrier(jnp.bool_(True))
@@ -101,36 +103,37 @@
         flat, tree = jax.tree.flatten(values)
         return jax.tree.unflatten(tree, lax.optimization_barrier(tuple(flat)))
 
-    z1 = lax.ppermute(own, "zh", ring(ZH, -1))
-    z3 = lax.ppermute(own, "zh", ring(ZH, 1))
+    def along_z(value, step):
+        pairs = [((z + (step if k else -step)) % ZH, z, k) for z in range(ZH) for k in range(CORE)]
+        return lax.ppermute(value, ("zh", "core"), [(z * CORE + k, to * CORE + k) for to, z, k in pairs])
+
+    n1 = along_z(own, 1)
+    n2 = along_z(own, -1)
     routed = lax.all_to_all(own, ("y", "core"), split_axis=0, concat_axis=0, tiled=True)
     own_x = fenced(over_x, own)
     own_x, routed = together(own_x, routed)
     b = lax.all_gather(routed, "row", axis=0, tiled=True)
-    z1, z3, own_x, routed = together(z1, z3, own_x, routed)
+    n1, n2, own_x, routed = together(n1, n2, own_x, routed)
 
-    half = S // 2
-    z2_low = lax.ppermute(z1[:half], "zh", ring(ZH, -1))
-    z2_high = lax.ppermute(z3[half:], "zh", ring(ZH, 1))
-    near = fenced(over_x, jnp.concatenate([z1, z3]))
-    place, _ = passing(place, WEIGHT, z1, z3)
-    z2_low, z2_high, near, place = together(z2_low, z2_high, near, place)
-    far = over_x(jnp.concatenate([z2_low, z2_high]))
+    opposite = along_z(n1, 1)
+    both = jnp.concatenate([n1, n2])
+    near = fenced(over_x, both)
+    place, _ = passing(place, WEIGHT, n1, n2)
+    opposite, near, place = together(opposite, near, place)
+    far = over_x(opposite)
 
-    arrays = own_x + near + far
+    arrays = [own, *own_x, both, *near, opposite, *far]
     lists = (place, left, right)
     groups = [(d, 0, d, 0) for d in range(X)]
-    groups += [(X + d, k * S, d, z) for k, z in enumerate((1, 3)) for d in range(X)]
-    groups += [(2 * X + d, 0, d, 2) for d in range(X)]
+    groups += [(X + d, k * S, d, z) for k, z in enumerate((1, 2)) for d in range(X)]
+    groups += [(2 * X + d, 0, d, 3) for d in range(X)]
     send = call(groups, 1, lists, arrays, b)
     got = lax.ppermute(send, "core", ring(CORE, 1))
     keep = call(groups, 0, lists, arrays, b)
 
-    quarter = [keep[d * PER : (d + 1) * PER] + got[d * PER : (d + 1) * PER] for d in range(Y)]
-    total = quarter[0]
-    for d in range(1, Y):
-        total = total + lax.ppermute(quarter[d], "y", ring(Y, d))
-    return total[None, None]
+    parts = (keep + got).reshape(Y, PER, BS, BS)
+    parts = lax.all_to_all(parts, "y", split_axis=0, concat_axis=0, tiled=True)
+    return jnp.sum(parts, axis=0)[None, None]
 
 
 def solution(mesh):

time: 192 us -> 185 us (0.964)
  waiting for transfers between devices: 68.3 us -> 42.2 us
  blocking collectives: 0 us -> 13.4 us
  starting transfers between devices: 94.2 us -> 102 us
    ppermute x16 -> x12, waiting for transfers between devices: 49.8 us -> 35.9 us  [the longest x9 25.7 us: over_x(): two, one, three = (lax.ppermute(value, 'x', ring(X, -d)) for d in (2, 1, 3))]
    all_to_all x0 -> x1, blocking collectives: none -> 13.4 us  [on_device(): parts = lax.all_to_all(parts, 'y', split_axis=0, concat_axis=0, tiled=True)]
    all_gather x1, waiting for transfers between devices: 18.5 us -> 6.25 us  [on_device(): b = lax.all_gather(routed, 'row', axis=0, tiled=True)]
    ppermute x16 -> x12, starting transfers between devices: 83 us -> 90.6 us  [the longest x3 59.2 us: along_z(): lax.ppermute(value, ('zh', 'core'), [(z * CORE + k, to * CORE + k) for to...]
  transfers between devices with their start and end apart: 19 -> 15, of which waited for: 12 -> 10; matrix products, arithmetic and copies ran while one was open for 1% -> 1% of each run, Pallas kernels for 3% -> 3%
where the time goes in v9:
time: 185 us; the launch traced here: 184 us
  starting transfers between devices  102 us (55%)
  waiting for transfers between devices  42.2 us (23%)
  between operations  13.5 us (7%)
  blocking collectives  13.4 us (7%)
  Pallas kernels  9.44 us (5%)
  local copies, waits for them, and re-layouts  2.66 us (1%)
    ppermute x3, starting transfers between devices, along_z(): lax.ppermute(value, ('zh', 'core'), [(z * CORE + k, to * CORE + k) for to...  59.2 us
    ppermute x9, starting transfers between devices, over_x(): two, one, three = (lax.ppermute(value, 'x', ring(X, -d)) for d in (2, 1, 3))  31.4 us
    ppermute x9, waiting for transfers between devices, over_x(): two, one, three = (lax.ppermute(value, 'x', ring(X, -d)) for d in (2, 1, 3))  25.7 us
    all_to_all x1, blocking collectives, on_device(): parts = lax.all_to_all(parts, 'y', split_axis=0, concat_axis=0, tiled=True)  13.4 us
    ppermute x3, waiting for transfers between devices, along_z(): lax.ppermute(value, ('zh', 'core'), [(z * CORE + k, to * CORE + k) for to...  10.2 us
    pallas_call x2, Pallas kernels, call(): pl.pallas_call(functools.partial(products, groups, other), out_shape=jax....  8.26 us
    all_to_all x1, starting transfers between devices, on_device(): lax.all_to_all(own, ('y', 'core'), split_axis=0, concat_axis=0, tiled=True)  6.57 us
    all_gather x1, waiting for transfers between devices, on_device(): b = lax.all_gather(routed, 'row', axis=0, tiled=True)  6.25 us
  transfers between devices with their start and end apart: 15, of which 10 were waited for; matrix products, arithmetic and copies ran while one was open for 1% of the time, Pallas kernels for 3%

profile of v9, /device:TPU:1, one launch (start us, length us, event | category | flops | bytes accessed | tf_op | source)
XLA Modules:
  0.0 184.3 jit_solution(3620379457486310997)
XLA Ops:
  6.5 23.5 %collective-permute-start.7 = (bf16[8,128,128]{2,1,0:T(8,128)(2,1)}, bf16[8,128,128]{2,1,0:T(8,128)(2,1)S(1)}, u32[]{:S(2)}, u32[]{:S(2)}) collective-permute-start(bf16[8,128,128]{2,1,0:T(8,128)(2,1)} %bitcast.9), channel_id=1, source_target_pairs={{0,8},{1,25},{8,16},{9,1},{16,24},{17,9},{24,0},{25,17},{2,10},{3,... | collective-permute-start | bytes 786440 | tf_op jit(solution)/shard_map/ppermute | solution.py:108
  30.1 1.9 %collective-permute-start.6 = (bf16[8,128,128]{2,1,0:T(8,128)(2,1)}, bf16[8,128,128]{2,1,0:T(8,128)(2,1)S(1)}, u32[]{:S(2)}, u32[]{:S(2)}) collective-permute-start(bf16[8,128,128]{2,1,0:T(8,128)(2,1)} %bitcast.10), channel_id=1, source_target_pairs={{0,24},{1,9},{8,0},{9,17},{16,8},{17,25},{24,16},{25,1},{2,26},{3,... | collective-permute-start | bytes 786440 | tf_op jit(solution)/shard_map/ppermute | solution.py:108
  32.0 6.6 %all-to-all-start = ((bf16[8,128,128]{2,1,0:T(8,128)(2,1)}), bf16[8,128,128]{2,1,0:T(8,128)(2,1)S(1)}, u32[]{:S(2)}, u32[]{:S(2)}) async-start(bf16[8,128,128]{2,1,0:T(8,128)(2,1)} %bitcast.11), calls=%async_computation | async-start | bytes 524288 | tf_op jit(solution)/shard_map/all_to_all | solution.py:112
  38.6 0.0 all-gather.2.cloned.1.call-start
  38.6 19.0 %conditional.2 = (bf16[8,128,128]{2,1,0:T(8,128)(2,1)}, bf16[8,128,128]{2,1,0:T(8,128)(2,1)}, bf16[8,128,128]{2,1,0:T(8,128)(2,1)}) conditional(s32[]{:T(128)} %convert_element_type.4, () %tuple.25, bf16[8,128,128]{2,1,0:T(8,128)(2,1)} %bitcast.12), branch_computations={%region_0.0_spmd, %region_1.0_spmd} | conditional | bytes 3145872 | solution.py:100
  38.6 2.0 %collective-permute-start.2 = (bf16[8,128,128]{2,1,0:T(8,128)(2,1)}, bf16[8,128,128]{2,1,0:T(8,128)(2,1)}, u32[]{:S(2)}, u32[]{:S(2)}) collective-permute-start(bf16[8,128,128]{2,1,0:T(8,128)(2,1)} %param.1), channel_id=1, source_target_pairs={{0,32},{32,64},{64,96},{96,0},{1,33},{33,65},{65,97},{97,1},{2,34}... | collective-permute-start | bytes 786440 | tf_op jit(solution)/shard_map/cond/branch_1_fun/ppermute | solution.py:93
  40.6 4.4 %collective-permute-start.1 = (bf16[8,128,128]{2,1,0:T(8,128)(2,1)}, bf16[8,128,128]{2,1,0:T(8,128)(2,1)}, u32[]{:S(2)}, u32[]{:S(2)}) collective-permute-start(bf16[8,128,128]{2,1,0:T(8,128)(2,1)} %param.1), channel_id=1, source_target_pairs={{0,64},{32,96},{64,0},{96,32},{1,65},{33,97},{65,1},{97,33},{2,66}... | collective-permute-start | bytes 786440 | tf_op jit(solution)/shard_map/cond/branch_1_fun/ppermute | solution.py:93
  44.9 3.1 %collective-permute-start = (bf16[8,128,128]{2,1,0:T(8,128)(2,1)}, bf16[8,128,128]{2,1,0:T(8,128)(2,1)}, u32[]{:S(2)}, u32[]{:S(2)}) collective-permute-start(bf16[8,128,128]{2,1,0:T(8,128)(2,1)} %param.1), channel_id=1, source_target_pairs={{0,96},{32,0},{64,32},{96,64},{1,97},{33,1},{65,33},{97,65},{2,98}... | collective-permute-start | bytes 786440 | tf_op jit(solution)/shard_map/cond/branch_1_fun/ppermute | solution.py:93
  48.0 1.7 collective-permute-done.2
  49.8 5.6 %collective-permute-done.1 = bf16[8,128,128]{2,1,0:T(8,128)(2,1)} collective-permute-done((bf16[8,128,128]{2,1,0:T(8,128)(2,1)}, bf16[8,128,128]{2,1,0:T(8,128)(2,1)}, u32[]{:S(2)}, u32[]{:S(2)}) %collective-permute-start.1) | collective-permute-done | bytes 262176 | tf_op jit(solution)/shard_map/cond/branch_1_fun/ppermute | solution.py:93
  55.4 2.2 %collective-permute-done = bf16[8,128,128]{2,1,0:T(8,128)(2,1)} collective-permute-done((bf16[8,128,128]{2,1,0:T(8,128)(2,1)}, bf16[8,128,128]{2,1,0:T(8,128)(2,1)}, u32[]{:S(2)}, u32[]{:S(2)}) %collective-permute-start) | collective-permute-done | bytes 262176 | tf_op jit(solution)/shard_map/cond/branch_1_fun/ppermute | solution.py:93
  57.6 0.6 pad_add_fusion.place_ref
  58.2 0.0 all-to-all-done
  58.2 0.0 copy-start.3
  58.2 0.7 copy-done.3
  58.9 0.0 all-gather.2.cloned.1.call-update
  58.9 10.2 %collective-permute-done.7 = bf16[8,128,128]{2,1,0:T(8,128)(2,1)S(1)} collective-permute-done((bf16[8,128,128]{2,1,0:T(8,128)(2,1)}, bf16[8,128,128]{2,1,0:T(8,128)(2,1)S(1)}, u32[]{:S(2)}, u32[]{:S(2)}) %collective-permute-start.7) | collective-permute-done | bytes 262176 | tf_op jit(solution)/shard_map/ppermute | solution.py:108
  69.2 0.0 collective-permute-done.6
  69.2 33.8 %collective-permute-start.8 = (bf16[8,128,128]{2,1,0:T(8,128)(2,1)S(1)}, bf16[8,128,128]{2,1,0:T(8,128)(2,1)S(1)}, u32[]{:S(2)}, u32[]{:S(2)}) collective-permute-start(bf16[8,128,128]{2,1,0:T(8,128)(2,1)S(1)} %collective-permute-done.6), channel_id=1, source_target_pairs={{0,24},{1,9},{8,0},{9,17},{16,8},{17,25},{24,16},{25,1},{2,26},{3,... | collective-permute-start | bytes 786440 | tf_op jit(solution)/shard_map/ppermute | solution.py:108
  102.9 1.2 shard_map.37.place
  104.1 0.0 copy-start.4
  104.2 0.0 copy-start.5
  104.2 0.0 copy-start.1
  104.2 0.0 copy-start.2
  104.3 22.9 %conditional.3 = (bf16[16,128,128]{2,1,0:T(8,128)(2,1)}, bf16[16,128,128]{2,1,0:T(8,128)(2,1)}, bf16[16,128,128]{2,1,0:T(8,128)(2,1)}) conditional(s32[]{:T(128)} %convert_element_type.4, () %tuple.28, bf16[16,128,128]{2,1,0:T(8,128)(2,1)S(1)} %constant_dynamic-update-slice_fusion.refs_4_), branch_computations={%region_2.0_spmd, %region_3.0_spmd} | conditional | bytes 6291600 | solution.py:100
  104.3 3.0 %collective-permute-start.5 = (bf16[16,128,128]{2,1,0:T(8,128)(2,1)S(1)}, bf16[16,128,128]{2,1,0:T(8,128)(2,1)}, u32[]{:S(2)}, u32[]{:S(2)}) collective-permute-start(bf16[16,128,128]{2,1,0:T(8,128)(2,1)S(1)} %param.3), channel_id=1, source_target_pairs={{0,32},{32,64},{64,96},{96,0},{1,33},{33,65},{65,97},{97,1},{2,34}... | collective-permute-start | bytes 1572872 | tf_op jit(solution)/shard_map/cond/branch_1_fun/ppermute | solution.py:93
  107.3 4.2 %collective-permute-start.4 = (bf16[16,128,128]{2,1,0:T(8,128)(2,1)S(1)}, bf16[16,128,128]{2,1,0:T(8,128)(2,1)}, u32[]{:S(2)}, u32[]{:S(2)}) collective-permute-start(bf16[16,128,128]{2,1,0:T(8,128)(2,1)S(1)} %param.3), channel_id=1, source_target_pairs={{0,64},{32,96},{64,0},{96,32},{1,65},{33,97},{65,1},{97,33},{2,66}... | collective-permute-start | bytes 1572872 | tf_op jit(solution)/shard_map/cond/branch_1_fun/ppermute | solution.py:93
  111.5 3.1 %collective-permute-start.3 = (bf16[16,128,128]{2,1,0:T(8,128)(2,1)S(1)}, bf16[16,128,128]{2,1,0:T(8,128)(2,1)}, u32[]{:S(2)}, u32[]{:S(2)}) collective-permute-start(bf16[16,128,128]{2,1,0:T(8,128)(2,1)S(1)} %param.3), channel_id=1, source_target_pairs={{0,96},{32,0},{64,32},{96,64},{1,97},{33,1},{65,33},{97,65},{2,98}... | collective-permute-start | bytes 1572872 | tf_op jit(solution)/shard_map/cond/branch_1_fun/ppermute | solution.py:93
  114.6 1.2 collective-permute-done.5
  115.8 9.7 %collective-permute-done.4 = bf16[16,128,128]{2,1,0:T(8,128)(2,1)} collective-permute-done((bf16[16,128,128]{2,1,0:T(8,128)(2,1)S(1)}, bf16[16,128,128]{2,1,0:T(8,128)(2,1)}, u32[]{:S(2)}, u32[]{:S(2)}) %collective-permute-start.4) | collective-permute-done | bytes 524320 | tf_op jit(solution)/shard_map/cond/branch_1_fun/ppermute | solution.py:93
  125.5 1.7 collective-permute-done.3
  127.2 0.0 collective-permute-done.8.refs_8_
  127.2 5.5 %collective-permute-start.11 = (bf16[8,128,128]{2,1,0:T(8,128)(2,1)S(1)}, bf16[8,128,128]{2,1,0:T(8,128)(2,1)S(1)}, u32[]{:S(2)}, u32[]{:S(2)}) collective-permute-start(bf16[8,128,128]{2,1,0:T(8,128)(2,1)S(1)} %collective-permute-done.8.refs_8_), channel_id=1, source_target_pairs={{0,32},{32,64},{64,96},{96,0},{1,33},{33,65},{65,97},{97,1},{2,34}... | collective-permute-start | bytes 786440 | tf_op jit(solution)/shard_map/ppermute | solution.py:93
  132.7 2.6 %collective-permute-start.10 = (bf16[8,128,128]{2,1,0:T(8,128)(2,1)S(1)}, bf16[8,128,128]{2,1,0:T(8,128)(2,1)S(1)}, u32[]{:S(2)}, u32[]{:S(2)}) collective-permute-start(bf16[8,128,128]{2,1,0:T(8,128)(2,1)S(1)} %collective-permute-done.8.refs_8_), channel_id=1, source_target_pairs={{0,64},{32,96},{64,0},{96,32},{1,65},{33,97},{65,1},{97,33},{2,66}... | collective-permute-start | bytes 786440 | tf_op jit(solution)/shard_map/ppermute | solution.py:93
  135.2 3.7 %collective-permute-start.9 = (bf16[8,128,128]{2,1,0:T(8,128)(2,1)S(1)}, bf16[8,128,128]{2,1,0:T(8,128)(2,1)S(1)}, u32[]{:S(2)}, u32[]{:S(2)}) collective-permute-start(bf16[8,128,128]{2,1,0:T(8,128)(2,1)S(1)} %collective-permute-done.8.refs_8_), channel_id=1, source_target_pairs={{0,96},{32,0},{64,32},{96,64},{1,97},{33,1},{65,33},{97,65},{2,98}... | collective-permute-start | bytes 786440 | tf_op jit(solution)/shard_map/ppermute | solution.py:93
  138.9 0.0 copy-done.4
  138.9 0.1 copy.12
  139.0 0.1 copy.14.left
  139.1 0.0 copy-done.5
  139.1 0.1 copy.13
  139.1 0.1 copy.15.right
  139.2 0.0 collective-permute-done.11.refs_11_
  139.2 2.5 %collective-permute-done.10.refs_10_ = bf16[8,128,128]{2,1,0:T(8,128)(2,1)S(1)} collective-permute-done((bf16[8,128,128]{2,1,0:T(8,128)(2,1)S(1)}, bf16[8,128,128]{2,1,0:T(8,128)(2,1)S(1)}, u32[]{:S(2)}, u32[]{:S(2)}) %collective-permute-start.10) | collective-permute-done | bytes 262176 | tf_op jit(solution)/shard_map/ppermute | solution.py:93
  141.7 1.1 collective-permute-done.9.refs_9_
  142.7 6.2 %all-gather.2.cloned.1.call-done.refs_12_ = bf16[64,128,128]{2,1,0:T(8,128)(2,1)} async-done(((bf16[8,128,128]{2,1,0:T(8,128)(2,1)}), bf16[64,128,128]{2,1,0:T(8,128)(2,1)}) %all-gather.2.cloned.1.call-update) | async-done | bytes 2097168 | tf_op jit(solution)/shard_map/all_gather | solution.py:115
  149.0 0.0 copy-done.1
  149.0 0.0 copy-done.2
  149.0 0.0 copy-start
  149.0 1.6 copy-done
  150.6 4.1 %shard_map.39 = f32[8,128,128]{2,1,0:T(8,128)S(1)} custom-call(s32[4]{0:T(128)S(1)} %copy-done.1, s32[16,32]{1,0:T(8,128)S(1)} %copy.14.left, s32[16,32]{1,0:T(8,128)S(1)} %copy.15.right, bf16[8,128,128]{2,1,0:T(8,128)(2,1)S(1)} %bitcast.13, bf16[8,128,128]{2,1,0:T(8,128)(2,1)} %get-tuple-element.42.refs_1_, bf16[8,128,128]{2,1,0:T(8,128)(2,1)} %get-tuple-element.43.refs_2_, ...), custom_call_target="tpu_custom_call" | custom-call | flops 1073741824 | bytes 8388608 | tf_op jit(solution)/shard_map/pallas_call | solution.py:57
  154.7 4.5 %collective-permute-start.12 = (f32[8,128,128]{2,1,0:T(8,128)S(1)}, f32[8,128,128]{2,1,0:T(8,128)S(1)}, u32[]{:S(2)}, u32[]{:S(2)}) collective-permute-start(f32[8,128,128]{2,1,0:T(8,128)S(1)} %shard_map.39), channel_id=1, source_target_pairs={{0,1},{1,0},{2,3},{3,2},{4,5},{5,4},{6,7},{7,6},{8,9},{9,8},{10,11... | collective-permute-start | bytes 1572872 | tf_op jit(solution)/shard_map/ppermute | solution.py:131
  159.2 4.1 %shard_map.38 = f32[8,128,128]{2,1,0:T(8,128)S(1)} custom-call(s32[4]{0:T(128)S(1)} %copy-done.1, s32[16,32]{1,0:T(8,128)S(1)} %copy.14.left, s32[16,32]{1,0:T(8,128)S(1)} %copy.15.right, bf16[8,128,128]{2,1,0:T(8,128)(2,1)S(1)} %bitcast.14, bf16[8,128,128]{2,1,0:T(8,128)(2,1)} %get-tuple-element.42.refs_1_, bf16[8,128,128]{2,1,0:T(8,128)(2,1)} %get-tuple-element.43.refs_2_, ...), custom_call_target="tpu_custom_call" | custom-call | flops 1073741824 | bytes 8388608 | tf_op jit(solution)/shard_map/pallas_call | solution.py:57
  163.3 0.0 collective-permute-done.12
  163.3 0.1 add.3
  163.4 13.4 %all_to_all.10 = f32[4,2,128,128]{3,2,1,0:T(8,128)S(1)} all-to-all(f32[4,2,128,128]{3,2,1,0:T(8,128)S(1)} %bitcast.15), channel_id=1, replica_groups=mesh['row'=8,'x'=4,'zh'=4,'y'=4,'core'=2] {'y'}, dimensions={0} | all-to-all | bytes 1048576 | tf_op jit(solution)/shard_map/all_to_all | solution.py:135
  176.8 0.7 reduce_sum.9
  (2 shorter events, 0.1 us)
Async XLA Ops:
  6.5 62.6 %collective-permute-start.7 = (bf16[8,128,128]{2,1,0:T(8,128)(2,1)}, bf16[8,128,128]{2,1,0:T(8,128)(2,1)S(1)}, u32[]{:S(2)}, u32[]{:S(2)}) collective-permute-start(bf16[8,128,128]{2,1,0:T(8,128)(2,1)} %bitcast.9), channel_id=1, source_target_pairs={{0,8},{1,25},{8,16},{9,1},{16,24},{17,9},{24,0},{25,17},{2,10},{3,... | collective-permute-start | bytes 786440 | tf_op jit(solution)/shard_map/ppermute | solution.py:108
  30.1 39.1 %collective-permute-start.6 = (bf16[8,128,128]{2,1,0:T(8,128)(2,1)}, bf16[8,128,128]{2,1,0:T(8,128)(2,1)S(1)}, u32[]{:S(2)}, u32[]{:S(2)}) collective-permute-start(bf16[8,128,128]{2,1,0:T(8,128)(2,1)} %bitcast.10), channel_id=1, source_target_pairs={{0,24},{1,9},{8,0},{9,17},{16,8},{17,25},{24,16},{25,1},{2,26},{3,... | collective-permute-start | bytes 786440 | tf_op jit(solution)/shard_map/ppermute | solution.py:108
  32.0 26.2 %all-to-all-start = ((bf16[8,128,128]{2,1,0:T(8,128)(2,1)}), bf16[8,128,128]{2,1,0:T(8,128)(2,1)S(1)}, u32[]{:S(2)}, u32[]{:S(2)}) async-start(bf16[8,128,128]{2,1,0:T(8,128)(2,1)} %bitcast.11), calls=%async_computation | async-start | bytes 524288 | tf_op jit(solution)/shard_map/all_to_all | solution.py:112
  38.6 110.4 %all-gather.2.cloned.1.call-start = ((), (), s32[]{:S(2)}) async-start(), calls=%async_computation.2 | async-start | bytes 2359296 | tf_op jit(solution)/shard_map/all_gather | solution.py:115
  38.6 11.2 %collective-permute-start.2 = (bf16[8,128,128]{2,1,0:T(8,128)(2,1)}, bf16[8,128,128]{2,1,0:T(8,128)(2,1)}, u32[]{:S(2)}, u32[]{:S(2)}) collective-permute-start(bf16[8,128,128]{2,1,0:T(8,128)(2,1)} %param.1), channel_id=1, source_target_pairs={{0,32},{32,64},{64,96},{96,0},{1,33},{33,65},{65,97},{97,1},{2,34}... | collective-permute-start | bytes 786440 | tf_op jit(solution)/shard_map/cond/branch_1_fun/ppermute | solution.py:93
  40.6 14.8 %collective-permute-start.1 = (bf16[8,128,128]{2,1,0:T(8,128)(2,1)}, bf16[8,128,128]{2,1,0:T(8,128)(2,1)}, u32[]{:S(2)}, u32[]{:S(2)}) collective-permute-start(bf16[8,128,128]{2,1,0:T(8,128)(2,1)} %param.1), channel_id=1, source_target_pairs={{0,64},{32,96},{64,0},{96,32},{1,65},{33,97},{65,1},{97,33},{2,66}... | collective-permute-start | bytes 786440 | tf_op jit(solution)/shard_map/cond/branch_1_fun/ppermute | solution.py:93
  44.9 12.6 %collective-permute-start = (bf16[8,128,128]{2,1,0:T(8,128)(2,1)}, bf16[8,128,128]{2,1,0:T(8,128)(2,1)}, u32[]{:S(2)}, u32[]{:S(2)}) collective-permute-start(bf16[8,128,128]{2,1,0:T(8,128)(2,1)} %param.1), channel_id=1, source_target_pairs={{0,96},{32,0},{64,32},{96,64},{1,97},{33,1},{65,33},{97,65},{2,98}... | collective-permute-start | bytes 786440 | tf_op jit(solution)/shard_map/cond/branch_1_fun/ppermute | solution.py:93
  58.2 0.7 copy-start.3
  69.2 58.0 %collective-permute-start.8 = (bf16[8,128,128]{2,1,0:T(8,128)(2,1)S(1)}, bf16[8,128,128]{2,1,0:T(8,128)(2,1)S(1)}, u32[]{:S(2)}, u32[]{:S(2)}) collective-permute-start(bf16[8,128,128]{2,1,0:T(8,128)(2,1)S(1)} %collective-permute-done.6), channel_id=1, source_target_pairs={{0,24},{1,9},{8,0},{9,17},{16,8},{17,25},{24,16},{25,1},{2,26},{3,... | collective-permute-start | bytes 786440 | tf_op jit(solution)/shard_map/ppermute | solution.py:108
  104.1 34.8 %copy-start.4 = (s32[1,1,1,16,16,2]{4,5,3,2,1,0:T(2,128)S(1)}, s32[1,1,1,16,16,2]{4,5,3,2,1,0:T(2,128)}, u32[]{:S(2)}) copy-start(s32[1,1,1,16,16,2]{4,5,3,2,1,0:T(2,128)} %param.8) | copy-start | bytes 6148
  104.2 34.9 %copy-start.5 = (s32[1,1,1,16,16,2]{4,5,3,2,1,0:T(2,128)S(1)}, s32[1,1,1,16,16,2]{4,5,3,2,1,0:T(2,128)}, u32[]{:S(2)}) copy-start(s32[1,1,1,16,16,2]{4,5,3,2,1,0:T(2,128)} %param.9) | copy-start | bytes 6148
  104.2 44.8 %copy-start.1 = (s32[4]{0:T(128)S(1)}, s32[4]{0:T(128)}, u32[]{:S(2)}) copy-start(s32[4]{0:T(128)} %shard_map.37.place) | copy-start | bytes 52
  104.2 44.8 %copy-start.2 = (bf16[1,1,1,8,1,128,128]{6,5,4,3,2,1,0:T(8,128)(2,1)S(1)}, bf16[1,1,1,8,1,128,128]{6,5,4,3,2,1,0:T(8,128)(2,1)}, u32[]{:S(2)}) copy-start(bf16[1,1,1,8,1,128,128]{6,5,4,3,2,1,0:T(8,128)(2,1)} %param.7) | copy-start | bytes 786436
  104.3 11.5 %collective-permute-start.5 = (bf16[16,128,128]{2,1,0:T(8,128)(2,1)S(1)}, bf16[16,128,128]{2,1,0:T(8,128)(2,1)}, u32[]{:S(2)}, u32[]{:S(2)}) collective-permute-start(bf16[16,128,128]{2,1,0:T(8,128)(2,1)S(1)} %param.3), channel_id=1, source_target_pairs={{0,32},{32,64},{64,96},{96,0},{1,33},{33,65},{65,97},{97,1},{2,34}... | collective-permute-start | bytes 1572872 | tf_op jit(solution)/shard_map/cond/branch_1_fun/ppermute | solution.py:93
  107.3 18.2 %collective-permute-start.4 = (bf16[16,128,128]{2,1,0:T(8,128)(2,1)S(1)}, bf16[16,128,128]{2,1,0:T(8,128)(2,1)}, u32[]{:S(2)}, u32[]{:S(2)}) collective-permute-start(bf16[16,128,128]{2,1,0:T(8,128)(2,1)S(1)} %param.3), channel_id=1, source_target_pairs={{0,64},{32,96},{64,0},{96,32},{1,65},{33,97},{65,1},{97,33},{2,66}... | collective-permute-start | bytes 1572872 | tf_op jit(solution)/shard_map/cond/branch_1_fun/ppermute | solution.py:93
  111.5 15.6 %collective-permute-start.3 = (bf16[16,128,128]{2,1,0:T(8,128)(2,1)S(1)}, bf16[16,128,128]{2,1,0:T(8,128)(2,1)}, u32[]{:S(2)}, u32[]{:S(2)}) collective-permute-start(bf16[16,128,128]{2,1,0:T(8,128)(2,1)S(1)} %param.3), channel_id=1, source_target_pairs={{0,96},{32,0},{64,32},{96,64},{1,97},{33,1},{65,33},{97,65},{2,98}... | collective-permute-start | bytes 1572872 | tf_op jit(solution)/shard_map/cond/branch_1_fun/ppermute | solution.py:93
  127.2 12.0 %collective-permute-start.11 = (bf16[8,128,128]{2,1,0:T(8,128)(2,1)S(1)}, bf16[8,128,128]{2,1,0:T(8,128)(2,1)S(1)}, u32[]{:S(2)}, u32[]{:S(2)}) collective-permute-start(bf16[8,128,128]{2,1,0:T(8,128)(2,1)S(1)} %collective-permute-done.8.refs_8_), channel_id=1, source_target_pairs={{0,32},{32,64},{64,96},{96,0},{1,33},{33,65},{65,97},{97,1},{2,34}... | collective-permute-start | bytes 786440 | tf_op jit(solution)/shard_map/ppermute | solution.py:93
  132.7 9.0 %collective-permute-start.10 = (bf16[8,128,128]{2,1,0:T(8,128)(2,1)S(1)}, bf16[8,128,128]{2,1,0:T(8,128)(2,1)S(1)}, u32[]{:S(2)}, u32[]{:S(2)}) collective-permute-start(bf16[8,128,128]{2,1,0:T(8,128)(2,1)S(1)} %collective-permute-done.8.refs_8_), channel_id=1, source_target_pairs={{0,64},{32,96},{64,0},{96,32},{1,65},{33,97},{65,1},{97,33},{2,66}... | collective-permute-start | bytes 786440 | tf_op jit(solution)/shard_map/ppermute | solution.py:93
  135.2 7.5 %collective-permute-start.9 = (bf16[8,128,128]{2,1,0:T(8,128)(2,1)S(1)}, bf16[8,128,128]{2,1,0:T(8,128)(2,1)S(1)}, u32[]{:S(2)}, u32[]{:S(2)}) collective-permute-start(bf16[8,128,128]{2,1,0:T(8,128)(2,1)S(1)} %collective-permute-done.8.refs_8_), channel_id=1, source_target_pairs={{0,96},{32,0},{64,32},{96,64},{1,97},{33,1},{65,33},{97,65},{2,98}... | collective-permute-start | bytes 786440 | tf_op jit(solution)/shard_map/ppermute | solution.py:93
  149.0 1.6 copy-start
  154.7 8.6 %collective-permute-start.12 = (f32[8,128,128]{2,1,0:T(8,128)S(1)}, f32[8,128,128]{2,1,0:T(8,128)S(1)}, u32[]{:S(2)}, u32[]{:S(2)}) collective-permute-start(f32[8,128,128]{2,1,0:T(8,128)S(1)} %shard_map.39), channel_id=1, source_target_pairs={{0,1},{1,0},{2,3},{3,2},{4,5},{5,4},{6,7},{7,6},{8,9},{9,8},{10,11... | collective-permute-start | bytes 1572872 | tf_op jit(solution)/shard_map/ppermute | solution.py:131
Sparse Core Ops, SparseCore 0:
  59.0 89.8 all-gather.1

commit v10 on v9

--- a/solution.py
+++ b/solution.py
@@ -12,7 +12,7 @@
 S, SLOTS, R, BS = 8, 2, 16, 128
 COLS = X * ZH
 PER = R // (Y * CORE)
-WEIGHT = 36 * 10**9
+WEIGHT = 32 * 10**9
 
 
 def ring(n, k):
@@ -111,7 +111,6 @@
     n2 = along_z(own, -1)
     routed = lax.all_to_all(own, ("y", "core"), split_axis=0, concat_axis=0, tiled=True)
     own_x = fenced(over_x, own)
-    own_x, routed = together(own_x, routed)
     b = lax.all_gather(routed, "row", axis=0, tiled=True)
     n1, n2, own_x, routed = together(n1, n2, own_x, routed)
 

time: 185 us -> 181 us (0.978)
  starting transfers between devices: 102 us -> 82.4 us
  waiting for transfers between devices: 42.2 us -> 57.1 us
    ppermute x3, starting transfers between devices: 59.2 us -> 30.5 us  [along_z(): lax.ppermute(value, ('zh', 'core'), [(z * CORE + k, to * CORE + k) for to...]
    all_to_all x1, starting transfers between devices: 6.57 us -> 17.5 us  [on_device(): lax.all_to_all(own, ('y', 'core'), split_axis=0, concat_axis=0, tiled=True)]
    ppermute x9, waiting for transfers between devices: 25.7 us -> 34 us  [over_x(): two, one, three = (lax.ppermute(value, 'x', ring(X, -d)) for d in (2, 1, 3))]
    ppermute x3, waiting for transfers between devices: 10.2 us -> 17.1 us  [along_z(): lax.ppermute(value, ('zh', 'core'), [(z * CORE + k, to * CORE + k) for to...]
  transfers between devices with their start and end apart: 15 -> 15, of which waited for: 10 -> 11; matrix products, arithmetic and copies ran while one was open for 1% -> 1% of each run, Pallas kernels for 3% -> 3%
where the time goes in v10:
time: 181 us; the launch traced here: 180 us
  starting transfers between devices  82.4 us (46%)
  waiting for transfers between devices  57.1 us (32%)
  between operations  13.6 us (8%)
  blocking collectives  13.4 us (7%)
  Pallas kernels  9.44 us (5%)
  local copies, waits for them, and re-layouts  2.65 us (1%)
    ppermute x9, waiting for transfers between devices, over_x(): two, one, three = (lax.ppermute(value, 'x', ring(X, -d)) for d in (2, 1, 3))  34 us
    ppermute x9, starting transfers between devices, over_x(): two, one, three = (lax.ppermute(value, 'x', ring(X, -d)) for d in (2, 1, 3))  30.7 us
    ppermute x3, starting transfers between devices, along_z(): lax.ppermute(value, ('zh', 'core'), [(z * CORE + k, to * CORE + k) for to...  30.5 us
    all_to_all x1, starting transfers between devices, on_device(): lax.all_to_all(own, ('y', 'core'), split_axis=0, concat_axis=0, tiled=True)  17.5 us
    ppermute x3, waiting for transfers between devices, along_z(): lax.ppermute(value, ('zh', 'core'), [(z * CORE + k, to * CORE + k) for to...  17.1 us
    all_to_all x1, blocking collectives, on_device(): parts = lax.all_to_all(parts, 'y', split_axis=0, concat_axis=0, tiled=True)  13.4 us
    pallas_call x2, Pallas kernels, call(): pl.pallas_call(functools.partial(products, groups, other), out_shape=jax....  8.26 us
    all_gather x1, waiting for transfers between devices, on_device(): b = lax.all_gather(routed, 'row', axis=0, tiled=True)  5.96 us
  transfers between devices with their start and end apart: 15, of which 11 were waited for; matrix products, arithmetic and copies ran while one was open for 1% of the time, Pallas kernels for 3%

profile of v10, /device:TPU:1, one launch (start us, length us, event | category | flops | bytes accessed | tf_op | source)
XLA Modules:
  0.0 179.9 jit_solution(17214044849207011389)
XLA Ops:
  6.5 17.5 %all-to-all-start = ((bf16[8,128,128]{2,1,0:T(8,128)(2,1)}), bf16[8,128,128]{2,1,0:T(8,128)(2,1)S(1)}, u32[]{:S(2)}, u32[]{:S(2)}) async-start(bf16[8,128,128]{2,1,0:T(8,128)(2,1)} %bitcast.9), calls=%async_computation | async-start | bytes 524288 | tf_op jit(solution)/shard_map/all_to_all | solution.py:112
  24.0 0.0 all-gather.2.cloned.1.call-start
  24.0 11.2 %collective-permute-start.7 = (bf16[8,128,128]{2,1,0:T(8,128)(2,1)}, bf16[8,128,128]{2,1,0:T(8,128)(2,1)S(1)}, u32[]{:S(2)}, u32[]{:S(2)}) collective-permute-start(bf16[8,128,128]{2,1,0:T(8,128)(2,1)} %bitcast.10), channel_id=1, source_target_pairs={{0,8},{1,25},{8,16},{9,1},{16,24},{17,9},{24,0},{25,17},{2,10},{3,... | collective-permute-start | bytes 786440 | tf_op jit(solution)/shard_map/ppermute | solution.py:108
  35.2 2.8 %collective-permute-start.6 = (bf16[8,128,128]{2,1,0:T(8,128)(2,1)}, bf16[8,128,128]{2,1,0:T(8,128)(2,1)S(1)}, u32[]{:S(2)}, u32[]{:S(2)}) collective-permute-start(bf16[8,128,128]{2,1,0:T(8,128)(2,1)} %bitcast.11), channel_id=1, source_target_pairs={{0,24},{1,9},{8,0},{9,17},{16,8},{17,25},{24,16},{25,1},{2,26},{3,... | collective-permute-start | bytes 786440 | tf_op jit(solution)/shard_map/ppermute | solution.py:108
  38.0 0.0 all-to-all-done
  38.0 0.0 copy-start.3
  38.0 0.7 copy-done.3
  38.7 0.0 all-gather.2.cloned.1.call-update
  38.7 18.8 %conditional.2 = (bf16[8,128,128]{2,1,0:T(8,128)(2,1)}, bf16[8,128,128]{2,1,0:T(8,128)(2,1)}, bf16[8,128,128]{2,1,0:T(8,128)(2,1)}) conditional(s32[]{:T(128)} %convert_element_type.4, () %tuple.24, bf16[8,128,128]{2,1,0:T(8,128)(2,1)} %bitcast.12), branch_computations={%region_0.0_spmd, %region_1.0_spmd} | conditional | bytes 3145872 | solution.py:100
  38.7 2.3 %collective-permute-start.2 = (bf16[8,128,128]{2,1,0:T(8,128)(2,1)}, bf16[8,128,128]{2,1,0:T(8,128)(2,1)}, u32[]{:S(2)}, u32[]{:S(2)}) collective-permute-start(bf16[8,128,128]{2,1,0:T(8,128)(2,1)} %param.1), channel_id=1, source_target_pairs={{0,32},{32,64},{64,96},{96,0},{1,33},{33,65},{65,97},{97,1},{2,34}... | collective-permute-start | bytes 786440 | tf_op jit(solution)/shard_map/cond/branch_1_fun/ppermute | solution.py:93
  41.0 4.4 %collective-permute-start.1 = (bf16[8,128,128]{2,1,0:T(8,128)(2,1)}, bf16[8,128,128]{2,1,0:T(8,128)(2,1)}, u32[]{:S(2)}, u32[]{:S(2)}) collective-permute-start(bf16[8,128,128]{2,1,0:T(8,128)(2,1)} %param.1), channel_id=1, source_target_pairs={{0,64},{32,96},{64,0},{96,32},{1,65},{33,97},{65,1},{97,33},{2,66}... | collective-permute-start | bytes 786440 | tf_op jit(solution)/shard_map/cond/branch_1_fun/ppermute | solution.py:93
  45.4 3.1 %collective-permute-start = (bf16[8,128,128]{2,1,0:T(8,128)(2,1)}, bf16[8,128,128]{2,1,0:T(8,128)(2,1)}, u32[]{:S(2)}, u32[]{:S(2)}) collective-permute-start(bf16[8,128,128]{2,1,0:T(8,128)(2,1)} %param.1), channel_id=1, source_target_pairs={{0,96},{32,0},{64,32},{96,64},{1,97},{33,1},{65,33},{97,65},{2,98}... | collective-permute-start | bytes 786440 | tf_op jit(solution)/shard_map/cond/branch_1_fun/ppermute | solution.py:93
  48.5 0.8 collective-permute-done.2
  49.3 6.2 %collective-permute-done.1 = bf16[8,128,128]{2,1,0:T(8,128)(2,1)} collective-permute-done((bf16[8,128,128]{2,1,0:T(8,128)(2,1)}, bf16[8,128,128]{2,1,0:T(8,128)(2,1)}, u32[]{:S(2)}, u32[]{:S(2)}) %collective-permute-start.1) | collective-permute-done | bytes 262176 | tf_op jit(solution)/shard_map/cond/branch_1_fun/ppermute | solution.py:93
  55.5 2.0 %collective-permute-done = bf16[8,128,128]{2,1,0:T(8,128)(2,1)} collective-permute-done((bf16[8,128,128]{2,1,0:T(8,128)(2,1)}, bf16[8,128,128]{2,1,0:T(8,128)(2,1)}, u32[]{:S(2)}, u32[]{:S(2)}) %collective-permute-start) | collective-permute-done | bytes 262176 | tf_op jit(solution)/shard_map/cond/branch_1_fun/ppermute | solution.py:93
  57.5 0.6 pad_add_fusion.place_ref
  58.1 17.1 %collective-permute-done.7 = bf16[8,128,128]{2,1,0:T(8,128)(2,1)S(1)} collective-permute-done((bf16[8,128,128]{2,1,0:T(8,128)(2,1)}, bf16[8,128,128]{2,1,0:T(8,128)(2,1)S(1)}, u32[]{:S(2)}, u32[]{:S(2)}) %collective-permute-start.7) | collective-permute-done | bytes 262176 | tf_op jit(solution)/shard_map/ppermute | solution.py:108
  75.2 0.0 collective-permute-done.6
  75.2 16.5 %collective-permute-start.8 = (bf16[8,128,128]{2,1,0:T(8,128)(2,1)S(1)}, bf16[8,128,128]{2,1,0:T(8,128)(2,1)S(1)}, u32[]{:S(2)}, u32[]{:S(2)}) collective-permute-start(bf16[8,128,128]{2,1,0:T(8,128)(2,1)S(1)} %collective-permute-done.6), channel_id=1, source_target_pairs={{0,24},{1,9},{8,0},{9,17},{16,8},{17,25},{24,16},{25,1},{2,26},{3,... | collective-permute-start | bytes 786440 | tf_op jit(solution)/shard_map/ppermute | solution.py:108
  91.8 1.2 shard_map.37.place
  93.0 0.0 copy-start.4
  93.0 0.0 copy-start.5
  93.0 0.0 copy-start.1
  93.0 0.0 copy-start.2
  93.1 27.1 %conditional.3 = (bf16[16,128,128]{2,1,0:T(8,128)(2,1)}, bf16[16,128,128]{2,1,0:T(8,128)(2,1)}, bf16[16,128,128]{2,1,0:T(8,128)(2,1)}) conditional(s32[]{:T(128)} %convert_element_type.4, () %tuple.26, bf16[16,128,128]{2,1,0:T(8,128)(2,1)S(1)} %constant_dynamic-update-slice_fusion.refs_4_), branch_computations={%region_2.0_spmd, %region_3.0_spmd} | conditional | bytes 6291600 | solution.py:100
  93.1 2.9 %collective-permute-start.5 = (bf16[16,128,128]{2,1,0:T(8,128)(2,1)S(1)}, bf16[16,128,128]{2,1,0:T(8,128)(2,1)}, u32[]{:S(2)}, u32[]{:S(2)}) collective-permute-start(bf16[16,128,128]{2,1,0:T(8,128)(2,1)S(1)} %param.3), channel_id=1, source_target_pairs={{0,32},{32,64},{64,96},{96,0},{1,33},{33,65},{65,97},{97,1},{2,34}... | collective-permute-start | bytes 1572872 | tf_op jit(solution)/shard_map/cond/branch_1_fun/ppermute | solution.py:93
  96.0 4.4 %collective-permute-start.4 = (bf16[16,128,128]{2,1,0:T(8,128)(2,1)S(1)}, bf16[16,128,128]{2,1,0:T(8,128)(2,1)}, u32[]{:S(2)}, u32[]{:S(2)}) collective-permute-start(bf16[16,128,128]{2,1,0:T(8,128)(2,1)S(1)} %param.3), channel_id=1, source_target_pairs={{0,64},{32,96},{64,0},{96,32},{1,65},{33,97},{65,1},{97,33},{2,66}... | collective-permute-start | bytes 1572872 | tf_op jit(solution)/shard_map/cond/branch_1_fun/ppermute | solution.py:93
  100.3 3.1 %collective-permute-start.3 = (bf16[16,128,128]{2,1,0:T(8,128)(2,1)S(1)}, bf16[16,128,128]{2,1,0:T(8,128)(2,1)}, u32[]{:S(2)}, u32[]{:S(2)}) collective-permute-start(bf16[16,128,128]{2,1,0:T(8,128)(2,1)S(1)} %param.3), channel_id=1, source_target_pairs={{0,96},{32,0},{64,32},{96,64},{1,97},{33,1},{65,33},{97,65},{2,98}... | collective-permute-start | bytes 1572872 | tf_op jit(solution)/shard_map/cond/branch_1_fun/ppermute | solution.py:93
  103.4 5.3 %collective-permute-done.5 = bf16[16,128,128]{2,1,0:T(8,128)(2,1)} collective-permute-done((bf16[16,128,128]{2,1,0:T(8,128)(2,1)S(1)}, bf16[16,128,128]{2,1,0:T(8,128)(2,1)}, u32[]{:S(2)}, u32[]{:S(2)}) %collective-permute-start.5) | collective-permute-done | bytes 524320 | tf_op jit(solution)/shard_map/cond/branch_1_fun/ppermute | solution.py:93
  108.7 9.4 %collective-permute-done.4 = bf16[16,128,128]{2,1,0:T(8,128)(2,1)} collective-permute-done((bf16[16,128,128]{2,1,0:T(8,128)(2,1)S(1)}, bf16[16,128,128]{2,1,0:T(8,128)(2,1)}, u32[]{:S(2)}, u32[]{:S(2)}) %collective-permute-start.4) | collective-permute-done | bytes 524320 | tf_op jit(solution)/shard_map/cond/branch_1_fun/ppermute | solution.py:93
  118.2 2.0 %collective-permute-done.3 = bf16[16,128,128]{2,1,0:T(8,128)(2,1)} collective-permute-done((bf16[16,128,128]{2,1,0:T(8,128)(2,1)S(1)}, bf16[16,128,128]{2,1,0:T(8,128)(2,1)}, u32[]{:S(2)}, u32[]{:S(2)}) %collective-permute-start.3) | collective-permute-done | bytes 524320 | tf_op jit(solution)/shard_map/cond/branch_1_fun/ppermute | solution.py:93
  120.1 0.0 collective-permute-done.8.refs_8_
  120.1 4.2 %collective-permute-start.11 = (bf16[8,128,128]{2,1,0:T(8,128)(2,1)S(1)}, bf16[8,128,128]{2,1,0:T(8,128)(2,1)S(1)}, u32[]{:S(2)}, u32[]{:S(2)}) collective-permute-start(bf16[8,128,128]{2,1,0:T(8,128)(2,1)S(1)} %collective-permute-done.8.refs_8_), channel_id=1, source_target_pairs={{0,32},{32,64},{64,96},{96,0},{1,33},{33,65},{65,97},{97,1},{2,34}... | collective-permute-start | bytes 786440 | tf_op jit(solution)/shard_map/ppermute | solution.py:93
  124.3 3.2 %collective-permute-start.10 = (bf16[8,128,128]{2,1,0:T(8,128)(2,1)S(1)}, bf16[8,128,128]{2,1,0:T(8,128)(2,1)S(1)}, u32[]{:S(2)}, u32[]{:S(2)}) collective-permute-start(bf16[8,128,128]{2,1,0:T(8,128)(2,1)S(1)} %collective-permute-done.8.refs_8_), channel_id=1, source_target_pairs={{0,64},{32,96},{64,0},{96,32},{1,65},{33,97},{65,1},{97,33},{2,66}... | collective-permute-start | bytes 786440 | tf_op jit(solution)/shard_map/ppermute | solution.py:93
  127.5 3.4 %collective-permute-start.9 = (bf16[8,128,128]{2,1,0:T(8,128)(2,1)S(1)}, bf16[8,128,128]{2,1,0:T(8,128)(2,1)S(1)}, u32[]{:S(2)}, u32[]{:S(2)}) collective-permute-start(bf16[8,128,128]{2,1,0:T(8,128)(2,1)S(1)} %collective-permute-done.8.refs_8_), channel_id=1, source_target_pairs={{0,96},{32,0},{64,32},{96,64},{1,97},{33,1},{65,33},{97,65},{2,98}... | collective-permute-start | bytes 786440 | tf_op jit(solution)/shard_map/ppermute | solution.py:93
  130.9 0.0 copy-done.4
  130.9 0.1 copy.12
  131.0 0.1 copy.14.left
  131.0 0.0 copy-done.5
  131.0 0.1 copy.13
  131.1 0.1 copy.15.right
  131.2 0.3 collective-permute-done.11.refs_11_
  131.5 5.9 %collective-permute-done.10.refs_10_ = bf16[8,128,128]{2,1,0:T(8,128)(2,1)S(1)} collective-permute-done((bf16[8,128,128]{2,1,0:T(8,128)(2,1)S(1)}, bf16[8,128,128]{2,1,0:T(8,128)(2,1)S(1)}, u32[]{:S(2)}, u32[]{:S(2)}) %collective-permute-start.10) | collective-permute-done | bytes 262176 | tf_op jit(solution)/shard_map/ppermute | solution.py:93
  137.4 2.0 %collective-permute-done.9.refs_9_ = bf16[8,128,128]{2,1,0:T(8,128)(2,1)S(1)} collective-permute-done((bf16[8,128,128]{2,1,0:T(8,128)(2,1)S(1)}, bf16[8,128,128]{2,1,0:T(8,128)(2,1)S(1)}, u32[]{:S(2)}, u32[]{:S(2)}) %collective-permute-start.9) | collective-permute-done | bytes 262176 | tf_op jit(solution)/shard_map/ppermute | solution.py:93
  139.4 6.0 %all-gather.2.cloned.1.call-done.refs_12_ = bf16[64,128,128]{2,1,0:T(8,128)(2,1)} async-done(((bf16[8,128,128]{2,1,0:T(8,128)(2,1)}), bf16[64,128,128]{2,1,0:T(8,128)(2,1)}) %all-gather.2.cloned.1.call-update) | async-done | bytes 2097168 | tf_op jit(solution)/shard_map/all_gather | solution.py:114
  145.4 0.0 copy-done.1
  145.4 0.0 copy-done.2
  145.4 0.0 copy-start
  145.4 1.6 copy-done
  147.0 4.1 %shard_map.39 = f32[8,128,128]{2,1,0:T(8,128)S(1)} custom-call(s32[4]{0:T(128)S(1)} %copy-done.1, s32[16,32]{1,0:T(8,128)S(1)} %copy.14.left, s32[16,32]{1,0:T(8,128)S(1)} %copy.15.right, bf16[8,128,128]{2,1,0:T(8,128)(2,1)S(1)} %bitcast.13, bf16[8,128,128]{2,1,0:T(8,128)(2,1)} %get-tuple-element.34.refs_1_, bf16[8,128,128]{2,1,0:T(8,128)(2,1)} %get-tuple-element.35.refs_2_, ...), custom_call_target="tpu_custom_call" | custom-call | flops 1073741824 | bytes 8388608 | tf_op jit(solution)/shard_map/pallas_call | solution.py:57
  151.1 3.7 %collective-permute-start.12 = (f32[8,128,128]{2,1,0:T(8,128)S(1)}, f32[8,128,128]{2,1,0:T(8,128)S(1)}, u32[]{:S(2)}, u32[]{:S(2)}) collective-permute-start(f32[8,128,128]{2,1,0:T(8,128)S(1)} %shard_map.39), channel_id=1, source_target_pairs={{0,1},{1,0},{2,3},{3,2},{4,5},{5,4},{6,7},{7,6},{8,9},{9,8},{10,11... | collective-permute-start | bytes 1572872 | tf_op jit(solution)/shard_map/ppermute | solution.py:130
  154.8 4.1 %shard_map.38 = f32[8,128,128]{2,1,0:T(8,128)S(1)} custom-call(s32[4]{0:T(128)S(1)} %copy-done.1, s32[16,32]{1,0:T(8,128)S(1)} %copy.14.left, s32[16,32]{1,0:T(8,128)S(1)} %copy.15.right, bf16[8,128,128]{2,1,0:T(8,128)(2,1)S(1)} %bitcast.14, bf16[8,128,128]{2,1,0:T(8,128)(2,1)} %get-tuple-element.34.refs_1_, bf16[8,128,128]{2,1,0:T(8,128)(2,1)} %get-tuple-element.35.refs_2_, ...), custom_call_target="tpu_custom_call" | custom-call | flops 1073741824 | bytes 8388608 | tf_op jit(solution)/shard_map/pallas_call | solution.py:57
  159.0 0.0 collective-permute-done.12
  159.0 0.1 add.3
  159.1 13.4 %all_to_all.10 = f32[4,2,128,128]{3,2,1,0:T(8,128)S(1)} all-to-all(f32[4,2,128,128]{3,2,1,0:T(8,128)S(1)} %bitcast.15), channel_id=1, replica_groups=mesh['row'=8,'x'=4,'zh'=4,'y'=4,'core'=2] {'y'}, dimensions={0} | all-to-all | bytes 1048576 | tf_op jit(solution)/shard_map/all_to_all | solution.py:134
  172.4 0.7 reduce_sum.9
  (2 shorter events, 0.1 us)
Async XLA Ops:
  6.5 31.5 %all-to-all-start = ((bf16[8,128,128]{2,1,0:T(8,128)(2,1)}), bf16[8,128,128]{2,1,0:T(8,128)(2,1)S(1)}, u32[]{:S(2)}, u32[]{:S(2)}) async-start(bf16[8,128,128]{2,1,0:T(8,128)(2,1)} %bitcast.9), calls=%async_computation | async-start | bytes 524288 | tf_op jit(solution)/shard_map/all_to_all | solution.py:112
  24.0 121.4 %all-gather.2.cloned.1.call-start = ((), (), s32[]{:S(2)}) async-start(), calls=%async_computation.2 | async-start | bytes 2359296 | tf_op jit(solution)/shard_map/all_gather | solution.py:114
  24.0 51.2 %collective-permute-start.7 = (bf16[8,128,128]{2,1,0:T(8,128)(2,1)}, bf16[8,128,128]{2,1,0:T(8,128)(2,1)S(1)}, u32[]{:S(2)}, u32[]{:S(2)}) collective-permute-start(bf16[8,128,128]{2,1,0:T(8,128)(2,1)} %bitcast.10), channel_id=1, source_target_pairs={{0,8},{1,25},{8,16},{9,1},{16,24},{17,9},{24,0},{25,17},{2,10},{3,... | collective-permute-start | bytes 786440 | tf_op jit(solution)/shard_map/ppermute | solution.py:108
  35.2 40.0 %collective-permute-start.6 = (bf16[8,128,128]{2,1,0:T(8,128)(2,1)}, bf16[8,128,128]{2,1,0:T(8,128)(2,1)S(1)}, u32[]{:S(2)}, u32[]{:S(2)}) collective-permute-start(bf16[8,128,128]{2,1,0:T(8,128)(2,1)} %bitcast.11), channel_id=1, source_target_pairs={{0,24},{1,9},{8,0},{9,17},{16,8},{17,25},{24,16},{25,1},{2,26},{3,... | collective-permute-start | bytes 786440 | tf_op jit(solution)/shard_map/ppermute | solution.py:108
  38.0 0.7 copy-start.3
  38.7 10.5 %collective-permute-start.2 = (bf16[8,128,128]{2,1,0:T(8,128)(2,1)}, bf16[8,128,128]{2,1,0:T(8,128)(2,1)}, u32[]{:S(2)}, u32[]{:S(2)}) collective-permute-start(bf16[8,128,128]{2,1,0:T(8,128)(2,1)} %param.1), channel_id=1, source_target_pairs={{0,32},{32,64},{64,96},{96,0},{1,33},{33,65},{65,97},{97,1},{2,34}... | collective-permute-start | bytes 786440 | tf_op jit(solution)/shard_map/cond/branch_1_fun/ppermute | solution.py:93
  41.0 14.5 %collective-permute-start.1 = (bf16[8,128,128]{2,1,0:T(8,128)(2,1)}, bf16[8,128,128]{2,1,0:T(8,128)(2,1)}, u32[]{:S(2)}, u32[]{:S(2)}) collective-permute-start(bf16[8,128,128]{2,1,0:T(8,128)(2,1)} %param.1), channel_id=1, source_target_pairs={{0,64},{32,96},{64,0},{96,32},{1,65},{33,97},{65,1},{97,33},{2,66}... | collective-permute-start | bytes 786440 | tf_op jit(solution)/shard_map/cond/branch_1_fun/ppermute | solution.py:93
  45.4 12.1 %collective-permute-start = (bf16[8,128,128]{2,1,0:T(8,128)(2,1)}, bf16[8,128,128]{2,1,0:T(8,128)(2,1)}, u32[]{:S(2)}, u32[]{:S(2)}) collective-permute-start(bf16[8,128,128]{2,1,0:T(8,128)(2,1)} %param.1), channel_id=1, source_target_pairs={{0,96},{32,0},{64,32},{96,64},{1,97},{33,1},{65,33},{97,65},{2,98}... | collective-permute-start | bytes 786440 | tf_op jit(solution)/shard_map/cond/branch_1_fun/ppermute | solution.py:93
  75.2 44.9 %collective-permute-start.8 = (bf16[8,128,128]{2,1,0:T(8,128)(2,1)S(1)}, bf16[8,128,128]{2,1,0:T(8,128)(2,1)S(1)}, u32[]{:S(2)}, u32[]{:S(2)}) collective-permute-start(bf16[8,128,128]{2,1,0:T(8,128)(2,1)S(1)} %collective-permute-done.6), channel_id=1, source_target_pairs={{0,24},{1,9},{8,0},{9,17},{16,8},{17,25},{24,16},{25,1},{2,26},{3,... | collective-permute-start | bytes 786440 | tf_op jit(solution)/shard_map/ppermute | solution.py:108
  93.0 37.9 %copy-start.4 = (s32[1,1,1,16,16,2]{4,5,3,2,1,0:T(2,128)S(1)}, s32[1,1,1,16,16,2]{4,5,3,2,1,0:T(2,128)}, u32[]{:S(2)}) copy-start(s32[1,1,1,16,16,2]{4,5,3,2,1,0:T(2,128)} %param.8) | copy-start | bytes 6148
  93.0 38.1 %copy-start.5 = (s32[1,1,1,16,16,2]{4,5,3,2,1,0:T(2,128)S(1)}, s32[1,1,1,16,16,2]{4,5,3,2,1,0:T(2,128)}, u32[]{:S(2)}) copy-start(s32[1,1,1,16,16,2]{4,5,3,2,1,0:T(2,128)} %param.9) | copy-start | bytes 6148
  93.0 52.4 %copy-start.1 = (s32[4]{0:T(128)S(1)}, s32[4]{0:T(128)}, u32[]{:S(2)}) copy-start(s32[4]{0:T(128)} %shard_map.37.place) | copy-start | bytes 52
  93.0 52.4 %copy-start.2 = (bf16[1,1,1,8,1,128,128]{6,5,4,3,2,1,0:T(8,128)(2,1)S(1)}, bf16[1,1,1,8,1,128,128]{6,5,4,3,2,1,0:T(8,128)(2,1)}, u32[]{:S(2)}) copy-start(bf16[1,1,1,8,1,128,128]{6,5,4,3,2,1,0:T(8,128)(2,1)} %param.7) | copy-start | bytes 786436
  93.1 15.7 %collective-permute-start.5 = (bf16[16,128,128]{2,1,0:T(8,128)(2,1)S(1)}, bf16[16,128,128]{2,1,0:T(8,128)(2,1)}, u32[]{:S(2)}, u32[]{:S(2)}) collective-permute-start(bf16[16,128,128]{2,1,0:T(8,128)(2,1)S(1)} %param.3), channel_id=1, source_target_pairs={{0,32},{32,64},{64,96},{96,0},{1,33},{33,65},{65,97},{97,1},{2,34}... | collective-permute-start | bytes 1572872 | tf_op jit(solution)/shard_map/cond/branch_1_fun/ppermute | solution.py:93
  96.0 22.2 %collective-permute-start.4 = (bf16[16,128,128]{2,1,0:T(8,128)(2,1)S(1)}, bf16[16,128,128]{2,1,0:T(8,128)(2,1)}, u32[]{:S(2)}, u32[]{:S(2)}) collective-permute-start(bf16[16,128,128]{2,1,0:T(8,128)(2,1)S(1)} %param.3), channel_id=1, source_target_pairs={{0,64},{32,96},{64,0},{96,32},{1,65},{33,97},{65,1},{97,33},{2,66}... | collective-permute-start | bytes 1572872 | tf_op jit(solution)/shard_map/cond/branch_1_fun/ppermute | solution.py:93
  100.3 19.8 %collective-permute-start.3 = (bf16[16,128,128]{2,1,0:T(8,128)(2,1)S(1)}, bf16[16,128,128]{2,1,0:T(8,128)(2,1)}, u32[]{:S(2)}, u32[]{:S(2)}) collective-permute-start(bf16[16,128,128]{2,1,0:T(8,128)(2,1)S(1)} %param.3), channel_id=1, source_target_pairs={{0,96},{32,0},{64,32},{96,64},{1,97},{33,1},{65,33},{97,65},{2,98}... | collective-permute-start | bytes 1572872 | tf_op jit(solution)/shard_map/cond/branch_1_fun/ppermute | solution.py:93
  120.1 11.4 %collective-permute-start.11 = (bf16[8,128,128]{2,1,0:T(8,128)(2,1)S(1)}, bf16[8,128,128]{2,1,0:T(8,128)(2,1)S(1)}, u32[]{:S(2)}, u32[]{:S(2)}) collective-permute-start(bf16[8,128,128]{2,1,0:T(8,128)(2,1)S(1)} %collective-permute-done.8.refs_8_), channel_id=1, source_target_pairs={{0,32},{32,64},{64,96},{96,0},{1,33},{33,65},{65,97},{97,1},{2,34}... | collective-permute-start | bytes 786440 | tf_op jit(solution)/shard_map/ppermute | solution.py:93
  124.3 13.1 %collective-permute-start.10 = (bf16[8,128,128]{2,1,0:T(8,128)(2,1)S(1)}, bf16[8,128,128]{2,1,0:T(8,128)(2,1)S(1)}, u32[]{:S(2)}, u32[]{:S(2)}) collective-permute-start(bf16[8,128,128]{2,1,0:T(8,128)(2,1)S(1)} %collective-permute-done.8.refs_8_), channel_id=1, source_target_pairs={{0,64},{32,96},{64,0},{96,32},{1,65},{33,97},{65,1},{97,33},{2,66}... | collective-permute-start | bytes 786440 | tf_op jit(solution)/shard_map/ppermute | solution.py:93
  127.5 11.9 %collective-permute-start.9 = (bf16[8,128,128]{2,1,0:T(8,128)(2,1)S(1)}, bf16[8,128,128]{2,1,0:T(8,128)(2,1)S(1)}, u32[]{:S(2)}, u32[]{:S(2)}) collective-permute-start(bf16[8,128,128]{2,1,0:T(8,128)(2,1)S(1)} %collective-permute-done.8.refs_8_), channel_id=1, source_target_pairs={{0,96},{32,0},{64,32},{96,64},{1,97},{33,1},{65,33},{97,65},{2,98}... | collective-permute-start | bytes 786440 | tf_op jit(solution)/shard_map/ppermute | solution.py:93
  145.4 1.6 copy-start
  151.1 7.9 %collective-permute-start.12 = (f32[8,128,128]{2,1,0:T(8,128)S(1)}, f32[8,128,128]{2,1,0:T(8,128)S(1)}, u32[]{:S(2)}, u32[]{:S(2)}) collective-permute-start(f32[8,128,128]{2,1,0:T(8,128)S(1)} %shard_map.39), channel_id=1, source_target_pairs={{0,1},{1,0},{2,3},{3,2},{4,5},{5,4},{6,7},{7,6},{8,9},{9,8},{10,11... | collective-permute-start | bytes 1572872 | tf_op jit(solution)/shard_map/ppermute | solution.py:130
Sparse Core Ops, SparseCore 0:
  38.9 106.4 all-gather.1

commit v11 on v10

--- a/solution.py
+++ b/solution.py
@@ -12,7 +12,7 @@
 S, SLOTS, R, BS = 8, 2, 16, 128
 COLS = X * ZH
 PER = R // (Y * CORE)
-WEIGHT = 32 * 10**9
+WEIGHT = 26 * 10**9
 
 
 def ring(n, k):

time: 181 us -> 193 us (1.066)
  the two profiles are of different devices: /device:TPU:1 before, /device:TPU:98 now
where the time goes in v11:
time: 193 us; the launch traced here: 192 us
  waiting for transfers between devices  71.9 us (37%)
  starting transfers between devices  69 us (36%)
  blocking collectives  25 us (13%)
  between operations  13.6 us (7%)
  Pallas kernels  9.49 us (5%)
  local copies, waits for them, and re-layouts  1.97 us (1%)
    ppermute x9, waiting for transfers between devices, over_x(): two, one, three = (lax.ppermute(value, 'x', ring(X, -d)) for d in (2, 1, 3))  36.4 us
    ppermute x3, starting transfers between devices, along_z(): lax.ppermute(value, ('zh', 'core'), [(z * CORE + k, to * CORE + k) for to...  36.4 us
    ppermute x3, waiting for transfers between devices, along_z(): lax.ppermute(value, ('zh', 'core'), [(z * CORE + k, to * CORE + k) for to...  35.5 us
    ppermute x9, starting transfers between devices, over_x(): two, one, three = (lax.ppermute(value, 'x', ring(X, -d)) for d in (2, 1, 3))  30.6 us
    all_to_all x1, blocking collectives, on_device(): parts = lax.all_to_all(parts, 'y', split_axis=0, concat_axis=0, tiled=True)  12.9 us
    all_to_all x1, blocking collectives, on_device(): lax.all_to_all(own, ('y', 'core'), split_axis=0, concat_axis=0, tiled=True)  12.1 us
    pallas_call x2, Pallas kernels, call(): pl.pallas_call(functools.partial(products, groups, other), out_shape=jax....  8.31 us
  transfers between devices with their start and end apart: 14, of which 11 were waited for; matrix products, arithmetic and copies ran while one was open for 1% of the time, Pallas kernels for 3%

profile of v11, /device:TPU:98, one launch (start us, length us, event | category | flops | bytes accessed | tf_op | source)
XLA Modules:
  0.0 192.4 jit_solution(15263238427446760060)
XLA Ops:
  6.5 0.0 all-gather.2.cloned.1.call-start
  6.5 12.1 %all_to_all.10 = bf16[8,128,128]{2,1,0:T(8,128)(2,1)} all-to-all(bf16[8,128,128]{2,1,0:T(8,128)(2,1)} %bitcast.9), channel_id=1, replica_groups=mesh['row'=8,'x'=4,'zh'=4,'y'=4,'core'=2] {'y','core'}, dimensions={0} | all-to-all | bytes 524288 | tf_op jit(solution)/shard_map/all_to_all | solution.py:112
  18.6 0.0 all-gather.2.cloned.1.call-update
  18.7 15.7 %collective-permute-start.7 = (bf16[8,128,128]{2,1,0:T(8,128)(2,1)}, bf16[8,128,128]{2,1,0:T(8,128)(2,1)S(1)}, u32[]{:S(2)}, u32[]{:S(2)}) collective-permute-start(bf16[8,128,128]{2,1,0:T(8,128)(2,1)} %bitcast.10), channel_id=1, source_target_pairs={{0,8},{1,25},{8,16},{9,1},{16,24},{17,9},{24,0},{25,17},{2,10},{3,... | collective-permute-start | bytes 786440 | tf_op jit(solution)/shard_map/ppermute | solution.py:108
  34.4 6.5 %collective-permute-start.6 = (bf16[8,128,128]{2,1,0:T(8,128)(2,1)}, bf16[8,128,128]{2,1,0:T(8,128)(2,1)S(1)}, u32[]{:S(2)}, u32[]{:S(2)}) collective-permute-start(bf16[8,128,128]{2,1,0:T(8,128)(2,1)} %bitcast.11), channel_id=1, source_target_pairs={{0,24},{1,9},{8,0},{9,17},{16,8},{17,25},{24,16},{25,1},{2,26},{3,... | collective-permute-start | bytes 786440 | tf_op jit(solution)/shard_map/ppermute | solution.py:108
  40.9 19.9 %conditional.2 = (bf16[8,128,128]{2,1,0:T(8,128)(2,1)}, bf16[8,128,128]{2,1,0:T(8,128)(2,1)}, bf16[8,128,128]{2,1,0:T(8,128)(2,1)}) conditional(s32[]{:T(128)} %convert_element_type.4, () %tuple.24, bf16[8,128,128]{2,1,0:T(8,128)(2,1)} %bitcast.12), branch_computations={%region_0.0_spmd, %region_1.0_spmd} | conditional | bytes 3145872 | solution.py:100
  40.9 3.4 %collective-permute-start.2 = (bf16[8,128,128]{2,1,0:T(8,128)(2,1)}, bf16[8,128,128]{2,1,0:T(8,128)(2,1)}, u32[]{:S(2)}, u32[]{:S(2)}) collective-permute-start(bf16[8,128,128]{2,1,0:T(8,128)(2,1)} %param.1), channel_id=1, source_target_pairs={{0,32},{32,64},{64,96},{96,0},{1,33},{33,65},{65,97},{97,1},{2,34}... | collective-permute-start | bytes 786440 | tf_op jit(solution)/shard_map/cond/branch_1_fun/ppermute | solution.py:93
  44.3 3.0 %collective-permute-start.1 = (bf16[8,128,128]{2,1,0:T(8,128)(2,1)}, bf16[8,128,128]{2,1,0:T(8,128)(2,1)}, u32[]{:S(2)}, u32[]{:S(2)}) collective-permute-start(bf16[8,128,128]{2,1,0:T(8,128)(2,1)} %param.1), channel_id=1, source_target_pairs={{0,64},{32,96},{64,0},{96,32},{1,65},{33,97},{65,1},{97,33},{2,66}... | collective-permute-start | bytes 786440 | tf_op jit(solution)/shard_map/cond/branch_1_fun/ppermute | solution.py:93
  47.4 4.1 %collective-permute-start = (bf16[8,128,128]{2,1,0:T(8,128)(2,1)}, bf16[8,128,128]{2,1,0:T(8,128)(2,1)}, u32[]{:S(2)}, u32[]{:S(2)}) collective-permute-start(bf16[8,128,128]{2,1,0:T(8,128)(2,1)} %param.1), channel_id=1, source_target_pairs={{0,96},{32,0},{64,32},{96,64},{1,97},{33,1},{65,33},{97,65},{2,98}... | collective-permute-start | bytes 786440 | tf_op jit(solution)/shard_map/cond/branch_1_fun/ppermute | solution.py:93
  51.4 0.3 collective-permute-done.2
  51.7 5.6 %collective-permute-done.1 = bf16[8,128,128]{2,1,0:T(8,128)(2,1)} collective-permute-done((bf16[8,128,128]{2,1,0:T(8,128)(2,1)}, bf16[8,128,128]{2,1,0:T(8,128)(2,1)}, u32[]{:S(2)}, u32[]{:S(2)}) %collective-permute-start.1) | collective-permute-done | bytes 262176 | tf_op jit(solution)/shard_map/cond/branch_1_fun/ppermute | solution.py:93
  57.3 3.5 %collective-permute-done = bf16[8,128,128]{2,1,0:T(8,128)(2,1)} collective-permute-done((bf16[8,128,128]{2,1,0:T(8,128)(2,1)}, bf16[8,128,128]{2,1,0:T(8,128)(2,1)}, u32[]{:S(2)}, u32[]{:S(2)}) %collective-permute-start) | collective-permute-done | bytes 262176 | tf_op jit(solution)/shard_map/cond/branch_1_fun/ppermute | solution.py:93
  60.8 0.6 pad_add_fusion.place_ref
  61.4 29.0 %collective-permute-done.7 = bf16[8,128,128]{2,1,0:T(8,128)(2,1)S(1)} collective-permute-done((bf16[8,128,128]{2,1,0:T(8,128)(2,1)}, bf16[8,128,128]{2,1,0:T(8,128)(2,1)S(1)}, u32[]{:S(2)}, u32[]{:S(2)}) %collective-permute-start.7) | collective-permute-done | bytes 262176 | tf_op jit(solution)/shard_map/ppermute | solution.py:108
  90.4 6.5 %collective-permute-done.6 = bf16[8,128,128]{2,1,0:T(8,128)(2,1)S(1)} collective-permute-done((bf16[8,128,128]{2,1,0:T(8,128)(2,1)}, bf16[8,128,128]{2,1,0:T(8,128)(2,1)S(1)}, u32[]{:S(2)}, u32[]{:S(2)}) %collective-permute-start.6) | collective-permute-done | bytes 262176 | tf_op jit(solution)/shard_map/ppermute | solution.py:108
  96.9 14.2 %collective-permute-start.8 = (bf16[8,128,128]{2,1,0:T(8,128)(2,1)S(1)}, bf16[8,128,128]{2,1,0:T(8,128)(2,1)S(1)}, u32[]{:S(2)}, u32[]{:S(2)}) collective-permute-start(bf16[8,128,128]{2,1,0:T(8,128)(2,1)S(1)} %collective-permute-done.6), channel_id=1, source_target_pairs={{0,24},{1,9},{8,0},{9,17},{16,8},{17,25},{24,16},{25,1},{2,26},{3,... | collective-permute-start | bytes 786440 | tf_op jit(solution)/shard_map/ppermute | solution.py:108
  111.1 1.2 shard_map.37.place
  112.3 0.0 copy-start.3
  112.3 0.0 copy-start.4
  112.3 0.0 copy-start.1
  112.3 0.0 copy-start.2
  112.4 26.9 %conditional.3 = (bf16[16,128,128]{2,1,0:T(8,128)(2,1)}, bf16[16,128,128]{2,1,0:T(8,128)(2,1)}, bf16[16,128,128]{2,1,0:T(8,128)(2,1)}) conditional(s32[]{:T(128)} %convert_element_type.4, () %tuple.26, bf16[16,128,128]{2,1,0:T(8,128)(2,1)S(1)} %constant_dynamic-update-slice_fusion.refs_4_), branch_computations={%region_2.0_spmd, %region_3.0_spmd} | conditional | bytes 6291600 | solution.py:100
  112.4 3.4 %collective-permute-start.5 = (bf16[16,128,128]{2,1,0:T(8,128)(2,1)S(1)}, bf16[16,128,128]{2,1,0:T(8,128)(2,1)}, u32[]{:S(2)}, u32[]{:S(2)}) collective-permute-start(bf16[16,128,128]{2,1,0:T(8,128)(2,1)S(1)} %param.3), channel_id=1, source_target_pairs={{0,32},{32,64},{64,96},{96,0},{1,33},{33,65},{65,97},{97,1},{2,34}... | collective-permute-start | bytes 1572872 | tf_op jit(solution)/shard_map/cond/branch_1_fun/ppermute | solution.py:93
  115.8 5.1 %collective-permute-start.4 = (bf16[16,128,128]{2,1,0:T(8,128)(2,1)S(1)}, bf16[16,128,128]{2,1,0:T(8,128)(2,1)}, u32[]{:S(2)}, u32[]{:S(2)}) collective-permute-start(bf16[16,128,128]{2,1,0:T(8,128)(2,1)S(1)} %param.3), channel_id=1, source_target_pairs={{0,64},{32,96},{64,0},{96,32},{1,65},{33,97},{65,1},{97,33},{2,66}... | collective-permute-start | bytes 1572872 | tf_op jit(solution)/shard_map/cond/branch_1_fun/ppermute | solution.py:93
  120.9 2.0 %collective-permute-start.3 = (bf16[16,128,128]{2,1,0:T(8,128)(2,1)S(1)}, bf16[16,128,128]{2,1,0:T(8,128)(2,1)}, u32[]{:S(2)}, u32[]{:S(2)}) collective-permute-start(bf16[16,128,128]{2,1,0:T(8,128)(2,1)S(1)} %param.3), channel_id=1, source_target_pairs={{0,96},{32,0},{64,32},{96,64},{1,97},{33,1},{65,33},{97,65},{2,98}... | collective-permute-start | bytes 1572872 | tf_op jit(solution)/shard_map/cond/branch_1_fun/ppermute | solution.py:93
  122.9 6.2 %collective-permute-done.5 = bf16[16,128,128]{2,1,0:T(8,128)(2,1)} collective-permute-done((bf16[16,128,128]{2,1,0:T(8,128)(2,1)S(1)}, bf16[16,128,128]{2,1,0:T(8,128)(2,1)}, u32[]{:S(2)}, u32[]{:S(2)}) %collective-permute-start.5) | collective-permute-done | bytes 524320 | tf_op jit(solution)/shard_map/cond/branch_1_fun/ppermute | solution.py:93
  129.1 4.7 %collective-permute-done.4 = bf16[16,128,128]{2,1,0:T(8,128)(2,1)} collective-permute-done((bf16[16,128,128]{2,1,0:T(8,128)(2,1)S(1)}, bf16[16,128,128]{2,1,0:T(8,128)(2,1)}, u32[]{:S(2)}, u32[]{:S(2)}) %collective-permute-start.4) | collective-permute-done | bytes 524320 | tf_op jit(solution)/shard_map/cond/branch_1_fun/ppermute | solution.py:93
  133.8 5.5 %collective-permute-done.3 = bf16[16,128,128]{2,1,0:T(8,128)(2,1)} collective-permute-done((bf16[16,128,128]{2,1,0:T(8,128)(2,1)S(1)}, bf16[16,128,128]{2,1,0:T(8,128)(2,1)}, u32[]{:S(2)}, u32[]{:S(2)}) %collective-permute-start.3) | collective-permute-done | bytes 524320 | tf_op jit(solution)/shard_map/cond/branch_1_fun/ppermute | solution.py:93
  139.3 0.0 collective-permute-done.8.refs_8_
  139.3 2.5 %collective-permute-start.11 = (bf16[8,128,128]{2,1,0:T(8,128)(2,1)S(1)}, bf16[8,128,128]{2,1,0:T(8,128)(2,1)S(1)}, u32[]{:S(2)}, u32[]{:S(2)}) collective-permute-start(bf16[8,128,128]{2,1,0:T(8,128)(2,1)S(1)} %collective-permute-done.8.refs_8_), channel_id=1, source_target_pairs={{0,32},{32,64},{64,96},{96,0},{1,33},{33,65},{65,97},{97,1},{2,34}... | collective-permute-start | bytes 786440 | tf_op jit(solution)/shard_map/ppermute | solution.py:93
  141.9 3.3 %collective-permute-start.10 = (bf16[8,128,128]{2,1,0:T(8,128)(2,1)S(1)}, bf16[8,128,128]{2,1,0:T(8,128)(2,1)S(1)}, u32[]{:S(2)}, u32[]{:S(2)}) collective-permute-start(bf16[8,128,128]{2,1,0:T(8,128)(2,1)S(1)} %collective-permute-done.8.refs_8_), channel_id=1, source_target_pairs={{0,64},{32,96},{64,0},{96,32},{1,65},{33,97},{65,1},{97,33},{2,66}... | collective-permute-start | bytes 786440 | tf_op jit(solution)/shard_map/ppermute | solution.py:93
  145.1 3.9 %collective-permute-start.9 = (bf16[8,128,128]{2,1,0:T(8,128)(2,1)S(1)}, bf16[8,128,128]{2,1,0:T(8,128)(2,1)S(1)}, u32[]{:S(2)}, u32[]{:S(2)}) collective-permute-start(bf16[8,128,128]{2,1,0:T(8,128)(2,1)S(1)} %collective-permute-done.8.refs_8_), channel_id=1, source_target_pairs={{0,96},{32,0},{64,32},{96,64},{1,97},{33,1},{65,33},{97,65},{2,98}... | collective-permute-start | bytes 786440 | tf_op jit(solution)/shard_map/ppermute | solution.py:93
  149.0 0.0 copy-done.3
  149.0 0.1 copy.12
  149.1 0.1 copy.14.left
  149.2 0.0 copy-done.4
  149.2 0.1 copy.13
  149.3 0.1 copy.15.right
  149.3 0.6 collective-permute-done.11.refs_11_
  150.0 3.4 %collective-permute-done.10.refs_10_ = bf16[8,128,128]{2,1,0:T(8,128)(2,1)S(1)} collective-permute-done((bf16[8,128,128]{2,1,0:T(8,128)(2,1)S(1)}, bf16[8,128,128]{2,1,0:T(8,128)(2,1)S(1)}, u32[]{:S(2)}, u32[]{:S(2)}) %collective-permute-start.10) | collective-permute-done | bytes 262176 | tf_op jit(solution)/shard_map/ppermute | solution.py:93
  153.4 6.6 %collective-permute-done.9.refs_9_ = bf16[8,128,128]{2,1,0:T(8,128)(2,1)S(1)} collective-permute-done((bf16[8,128,128]{2,1,0:T(8,128)(2,1)S(1)}, bf16[8,128,128]{2,1,0:T(8,128)(2,1)S(1)}, u32[]{:S(2)}, u32[]{:S(2)}) %collective-permute-start.9) | collective-permute-done | bytes 262176 | tf_op jit(solution)/shard_map/ppermute | solution.py:93
  160.0 0.0 all-gather.2.cloned.1.call-done.refs_12_
  160.0 0.0 copy-done.1
  160.0 0.0 copy-done.2
  160.0 0.0 copy-start
  160.0 1.6 copy-done
  161.6 4.1 %shard_map.39 = f32[8,128,128]{2,1,0:T(8,128)S(1)} custom-call(s32[4]{0:T(128)S(1)} %copy-done.1, s32[16,32]{1,0:T(8,128)S(1)} %copy.14.left, s32[16,32]{1,0:T(8,128)S(1)} %copy.15.right, bf16[8,128,128]{2,1,0:T(8,128)(2,1)S(1)} %bitcast.13, bf16[8,128,128]{2,1,0:T(8,128)(2,1)} %get-tuple-element.34.refs_1_, bf16[8,128,128]{2,1,0:T(8,128)(2,1)} %get-tuple-element.35.refs_2_, ...), custom_call_target="tpu_custom_call" | custom-call | flops 1073741824 | bytes 8388608 | tf_op jit(solution)/shard_map/pallas_call | solution.py:57
  165.7 2.0 %collective-permute-start.12 = (f32[8,128,128]{2,1,0:T(8,128)S(1)}, f32[8,128,128]{2,1,0:T(8,128)S(1)}, u32[]{:S(2)}, u32[]{:S(2)}) collective-permute-start(f32[8,128,128]{2,1,0:T(8,128)S(1)} %shard_map.39), channel_id=1, source_target_pairs={{0,1},{1,0},{2,3},{3,2},{4,5},{5,4},{6,7},{7,6},{8,9},{9,8},{10,11... | collective-permute-start | bytes 1572872 | tf_op jit(solution)/shard_map/ppermute | solution.py:130
  167.8 4.2 %shard_map.38 = f32[8,128,128]{2,1,0:T(8,128)S(1)} custom-call(s32[4]{0:T(128)S(1)} %copy-done.1, s32[16,32]{1,0:T(8,128)S(1)} %copy.14.left, s32[16,32]{1,0:T(8,128)S(1)} %copy.15.right, bf16[8,128,128]{2,1,0:T(8,128)(2,1)S(1)} %bitcast.14, bf16[8,128,128]{2,1,0:T(8,128)(2,1)} %get-tuple-element.34.refs_1_, bf16[8,128,128]{2,1,0:T(8,128)(2,1)} %get-tuple-element.35.refs_2_, ...), custom_call_target="tpu_custom_call" | custom-call | flops 1073741824 | bytes 8388608 | tf_op jit(solution)/shard_map/pallas_call | solution.py:57
  172.0 0.0 collective-permute-done.12
  172.0 0.1 add.3
  172.0 12.9 %all_to_all.11 = f32[4,2,128,128]{3,2,1,0:T(8,128)S(1)} all-to-all(f32[4,2,128,128]{3,2,1,0:T(8,128)S(1)} %bitcast.15), channel_id=1, replica_groups=mesh['row'=8,'x'=4,'zh'=4,'y'=4,'core'=2] {'y'}, dimensions={0} | all-to-all | bytes 1048576 | tf_op jit(solution)/shard_map/all_to_all | solution.py:134
  184.9 0.7 reduce_sum.9
  (2 shorter events, 0.1 us)
Async XLA Ops:
  6.5 153.5 %all-gather.2.cloned.1.call-start = ((), (), s32[]{:S(2)}) async-start(), calls=%async_computation.2 | async-start | bytes 2359296 | tf_op jit(solution)/shard_map/all_gather | solution.py:114
  18.7 71.7 %collective-permute-start.7 = (bf16[8,128,128]{2,1,0:T(8,128)(2,1)}, bf16[8,128,128]{2,1,0:T(8,128)(2,1)S(1)}, u32[]{:S(2)}, u32[]{:S(2)}) collective-permute-start(bf16[8,128,128]{2,1,0:T(8,128)(2,1)} %bitcast.10), channel_id=1, source_target_pairs={{0,8},{1,25},{8,16},{9,1},{16,24},{17,9},{24,0},{25,17},{2,10},{3,... | collective-permute-start | bytes 786440 | tf_op jit(solution)/shard_map/ppermute | solution.py:108
  34.4 62.5 %collective-permute-start.6 = (bf16[8,128,128]{2,1,0:T(8,128)(2,1)}, bf16[8,128,128]{2,1,0:T(8,128)(2,1)S(1)}, u32[]{:S(2)}, u32[]{:S(2)}) collective-permute-start(bf16[8,128,128]{2,1,0:T(8,128)(2,1)} %bitcast.11), channel_id=1, source_target_pairs={{0,24},{1,9},{8,0},{9,17},{16,8},{17,25},{24,16},{25,1},{2,26},{3,... | collective-permute-start | bytes 786440 | tf_op jit(solution)/shard_map/ppermute | solution.py:108
  40.9 10.8 %collective-permute-start.2 = (bf16[8,128,128]{2,1,0:T(8,128)(2,1)}, bf16[8,128,128]{2,1,0:T(8,128)(2,1)}, u32[]{:S(2)}, u32[]{:S(2)}) collective-permute-start(bf16[8,128,128]{2,1,0:T(8,128)(2,1)} %param.1), channel_id=1, source_target_pairs={{0,32},{32,64},{64,96},{96,0},{1,33},{33,65},{65,97},{97,1},{2,34}... | collective-permute-start | bytes 786440 | tf_op jit(solution)/shard_map/cond/branch_1_fun/ppermute | solution.py:93
  44.3 13.0 %collective-permute-start.1 = (bf16[8,128,128]{2,1,0:T(8,128)(2,1)}, bf16[8,128,128]{2,1,0:T(8,128)(2,1)}, u32[]{:S(2)}, u32[]{:S(2)}) collective-permute-start(bf16[8,128,128]{2,1,0:T(8,128)(2,1)} %param.1), channel_id=1, source_target_pairs={{0,64},{32,96},{64,0},{96,32},{1,65},{33,97},{65,1},{97,33},{2,66}... | collective-permute-start | bytes 786440 | tf_op jit(solution)/shard_map/cond/branch_1_fun/ppermute | solution.py:93
  47.4 13.4 %collective-permute-start = (bf16[8,128,128]{2,1,0:T(8,128)(2,1)}, bf16[8,128,128]{2,1,0:T(8,128)(2,1)}, u32[]{:S(2)}, u32[]{:S(2)}) collective-permute-start(bf16[8,128,128]{2,1,0:T(8,128)(2,1)} %param.1), channel_id=1, source_target_pairs={{0,96},{32,0},{64,32},{96,64},{1,97},{33,1},{65,33},{97,65},{2,98}... | collective-permute-start | bytes 786440 | tf_op jit(solution)/shard_map/cond/branch_1_fun/ppermute | solution.py:93
  96.9 42.4 %collective-permute-start.8 = (bf16[8,128,128]{2,1,0:T(8,128)(2,1)S(1)}, bf16[8,128,128]{2,1,0:T(8,128)(2,1)S(1)}, u32[]{:S(2)}, u32[]{:S(2)}) collective-permute-start(bf16[8,128,128]{2,1,0:T(8,128)(2,1)S(1)} %collective-permute-done.6), channel_id=1, source_target_pairs={{0,24},{1,9},{8,0},{9,17},{16,8},{17,25},{24,16},{25,1},{2,26},{3,... | collective-permute-start | bytes 786440 | tf_op jit(solution)/shard_map/ppermute | solution.py:108
  112.3 36.7 %copy-start.3 = (s32[1,1,1,16,16,2]{4,5,3,2,1,0:T(2,128)S(1)}, s32[1,1,1,16,16,2]{4,5,3,2,1,0:T(2,128)}, u32[]{:S(2)}) copy-start(s32[1,1,1,16,16,2]{4,5,3,2,1,0:T(2,128)} %param.8) | copy-start | bytes 6148
  112.3 36.9 %copy-start.4 = (s32[1,1,1,16,16,2]{4,5,3,2,1,0:T(2,128)S(1)}, s32[1,1,1,16,16,2]{4,5,3,2,1,0:T(2,128)}, u32[]{:S(2)}) copy-start(s32[1,1,1,16,16,2]{4,5,3,2,1,0:T(2,128)} %param.9) | copy-start | bytes 6148
  112.3 47.7 %copy-start.1 = (s32[4]{0:T(128)S(1)}, s32[4]{0:T(128)}, u32[]{:S(2)}) copy-start(s32[4]{0:T(128)} %shard_map.37.place) | copy-start | bytes 52
  112.3 47.7 %copy-start.2 = (bf16[1,1,1,8,1,128,128]{6,5,4,3,2,1,0:T(8,128)(2,1)S(1)}, bf16[1,1,1,8,1,128,128]{6,5,4,3,2,1,0:T(8,128)(2,1)}, u32[]{:S(2)}) copy-start(bf16[1,1,1,8,1,128,128]{6,5,4,3,2,1,0:T(8,128)(2,1)} %param.7) | copy-start | bytes 786436
  112.4 16.7 %collective-permute-start.5 = (bf16[16,128,128]{2,1,0:T(8,128)(2,1)S(1)}, bf16[16,128,128]{2,1,0:T(8,128)(2,1)}, u32[]{:S(2)}, u32[]{:S(2)}) collective-permute-start(bf16[16,128,128]{2,1,0:T(8,128)(2,1)S(1)} %param.3), channel_id=1, source_target_pairs={{0,32},{32,64},{64,96},{96,0},{1,33},{33,65},{65,97},{97,1},{2,34}... | collective-permute-start | bytes 1572872 | tf_op jit(solution)/shard_map/cond/branch_1_fun/ppermute | solution.py:93
  115.8 18.0 %collective-permute-start.4 = (bf16[16,128,128]{2,1,0:T(8,128)(2,1)S(1)}, bf16[16,128,128]{2,1,0:T(8,128)(2,1)}, u32[]{:S(2)}, u32[]{:S(2)}) collective-permute-start(bf16[16,128,128]{2,1,0:T(8,128)(2,1)S(1)} %param.3), channel_id=1, source_target_pairs={{0,64},{32,96},{64,0},{96,32},{1,65},{33,97},{65,1},{97,33},{2,66}... | collective-permute-start | bytes 1572872 | tf_op jit(solution)/shard_map/cond/branch_1_fun/ppermute | solution.py:93
  120.9 18.4 %collective-permute-start.3 = (bf16[16,128,128]{2,1,0:T(8,128)(2,1)S(1)}, bf16[16,128,128]{2,1,0:T(8,128)(2,1)}, u32[]{:S(2)}, u32[]{:S(2)}) collective-permute-start(bf16[16,128,128]{2,1,0:T(8,128)(2,1)S(1)} %param.3), channel_id=1, source_target_pairs={{0,96},{32,0},{64,32},{96,64},{1,97},{33,1},{65,33},{97,65},{2,98}... | collective-permute-start | bytes 1572872 | tf_op jit(solution)/shard_map/cond/branch_1_fun/ppermute | solution.py:93
  139.3 10.6 %collective-permute-start.11 = (bf16[8,128,128]{2,1,0:T(8,128)(2,1)S(1)}, bf16[8,128,128]{2,1,0:T(8,128)(2,1)S(1)}, u32[]{:S(2)}, u32[]{:S(2)}) collective-permute-start(bf16[8,128,128]{2,1,0:T(8,128)(2,1)S(1)} %collective-permute-done.8.refs_8_), channel_id=1, source_target_pairs={{0,32},{32,64},{64,96},{96,0},{1,33},{33,65},{65,97},{97,1},{2,34}... | collective-permute-start | bytes 786440 | tf_op jit(solution)/shard_map/ppermute | solution.py:93
  141.9 11.5 %collective-permute-start.10 = (bf16[8,128,128]{2,1,0:T(8,128)(2,1)S(1)}, bf16[8,128,128]{2,1,0:T(8,128)(2,1)S(1)}, u32[]{:S(2)}, u32[]{:S(2)}) collective-permute-start(bf16[8,128,128]{2,1,0:T(8,128)(2,1)S(1)} %collective-permute-done.8.refs_8_), channel_id=1, source_target_pairs={{0,64},{32,96},{64,0},{96,32},{1,65},{33,97},{65,1},{97,33},{2,66}... | collective-permute-start | bytes 786440 | tf_op jit(solution)/shard_map/ppermute | solution.py:93
  145.1 14.9 %collective-permute-start.9 = (bf16[8,128,128]{2,1,0:T(8,128)(2,1)S(1)}, bf16[8,128,128]{2,1,0:T(8,128)(2,1)S(1)}, u32[]{:S(2)}, u32[]{:S(2)}) collective-permute-start(bf16[8,128,128]{2,1,0:T(8,128)(2,1)S(1)} %collective-permute-done.8.refs_8_), channel_id=1, source_target_pairs={{0,96},{32,0},{64,32},{96,64},{1,97},{33,1},{65,33},{97,65},{2,98}... | collective-permute-start | bytes 786440 | tf_op jit(solution)/shard_map/ppermute | solution.py:93
  160.0 1.6 copy-start
  165.7 6.2 %collective-permute-start.12 = (f32[8,128,128]{2,1,0:T(8,128)S(1)}, f32[8,128,128]{2,1,0:T(8,128)S(1)}, u32[]{:S(2)}, u32[]{:S(2)}) collective-permute-start(f32[8,128,128]{2,1,0:T(8,128)S(1)} %shard_map.39), channel_id=1, source_target_pairs={{0,1},{1,0},{2,3},{3,2},{4,5},{5,4},{6,7},{7,6},{8,9},{9,8},{10,11... | collective-permute-start | bytes 1572872 | tf_op jit(solution)/shard_map/ppermute | solution.py:130
Sparse Core Ops, SparseCore 0:
  18.8 121.8 all-gather.1

commit v12 on v11

--- a/solution.py
+++ b/solution.py
@@ -12,7 +12,7 @@
 S, SLOTS, R, BS = 8, 2, 16, 128
 COLS = X * ZH
 PER = R // (Y * CORE)
-WEIGHT = 26 * 10**9
+WEIGHT = 290 * 10**8
 
 
 def ring(n, k):
@@ -108,24 +108,23 @@
         return lax.ppermute(value, ("zh", "core"), [(z * CORE + k, to * CORE + k) for to, z, k in pairs])
 
     n1 = along_z(own, 1)
-    n2 = along_z(own, -1)
     routed = lax.all_to_all(own, ("y", "core"), split_axis=0, concat_axis=0, tiled=True)
+    b = lax.all_gather(routed, "row", axis=0, tiled=True)
     own_x = fenced(over_x, own)
-    b = lax.all_gather(routed, "row", axis=0, tiled=True)
-    n1, n2, own_x, routed = together(n1, n2, own_x, routed)
+    n1, own_x, again, _ = together(n1, own_x, own, routed)
 
+    n2 = along_z(again, -1)
     opposite = along_z(n1, 1)
-    both = jnp.concatenate([n1, n2])
-    near = fenced(over_x, both)
-    place, _ = passing(place, WEIGHT, n1, n2)
-    opposite, near, place = together(opposite, near, place)
-    far = over_x(opposite)
+    first = fenced(over_x, n1)
+    place, _ = passing(place, WEIGHT, n1)
+    n2, opposite, first, place = together(n2, opposite, first, place)
+    both = jnp.concatenate([n2, opposite])
+    last = over_x(both)
 
-    arrays = [own, *own_x, both, *near, opposite, *far]
+    arrays = [own, *own_x, n1, *first, both, *last]
     lists = (place, left, right)
-    groups = [(d, 0, d, 0) for d in range(X)]
-    groups += [(X + d, k * S, d, z) for k, z in enumerate((1, 2)) for d in range(X)]
-    groups += [(2 * X + d, 0, d, 3) for d in range(X)]
+    groups = [(z * X + d, 0, d, z) for z in (0, 1) for d in range(X)]
+    groups += [(2 * X + d, k * S, d, z) for k, z in enumerate((2, 3)) for d in range(X)]
     send = call(groups, 1, lists, arrays, b)
     got = lax.ppermute(send, "core", ring(CORE, 1))
     keep = call(groups, 0, lists, arrays, b)

time: 193 us -> 194 us (level)
  the two profiles are of different devices: /device:TPU:98 before, /device:TPU:32 now
where the time goes in v12:
time: 194 us; the launch traced here: 193 us
  starting transfers between devices  76.4 us (39%)
  waiting for transfers between devices  75 us (39%)
  blocking collectives  14.8 us (8%)
  between operations  13.5 us (7%)
  Pallas kernels  8.89 us (5%)
  local copies, waits for them, and re-layouts  3.32 us (2%)
    ppermute x3, waiting for transfers between devices, along_z(): lax.ppermute(value, ('zh', 'core'), [(z * CORE + k, to * CORE + k) for to...  45.1 us
    ppermute x3, starting transfers between devices, along_z(): lax.ppermute(value, ('zh', 'core'), [(z * CORE + k, to * CORE + k) for to...  37.7 us
    ppermute x9, starting transfers between devices, over_x(): two, one, three = (lax.ppermute(value, 'x', ring(X, -d)) for d in (2, 1, 3))  32.4 us
    ppermute x9, waiting for transfers between devices, over_x(): two, one, three = (lax.ppermute(value, 'x', ring(X, -d)) for d in (2, 1, 3))  29.9 us
    all_to_all x1, blocking collectives, on_device(): parts = lax.all_to_all(parts, 'y', split_axis=0, concat_axis=0, tiled=True)  14.8 us
    pallas_call x2, Pallas kernels, call(): pl.pallas_call(functools.partial(products, groups, other), out_shape=jax....  7.7 us
    all_to_all x1, starting transfers between devices, on_device(): lax.all_to_all(own, ('y', 'core'), split_axis=0, concat_axis=0, tiled=True)  4.47 us
  transfers between devices with their start and end apart: 15, of which 10 were waited for; matrix products, arithmetic and copies ran while one was open for 0% of the time, Pallas kernels for 3%

profile of v12, /device:TPU:32, one launch (start us, length us, event | category | flops | bytes accessed | tf_op | source)
XLA Modules:
  0.0 193.4 jit_solution(11371053236747465029)
XLA Ops:
  6.5 4.5 %all-to-all-start = ((bf16[8,128,128]{2,1,0:T(8,128)(2,1)}), bf16[8,128,128]{2,1,0:T(8,128)(2,1)S(1)}, u32[]{:S(2)}, u32[]{:S(2)}) async-start(bf16[8,128,128]{2,1,0:T(8,128)(2,1)} %bitcast.9), calls=%async_computation | async-start | bytes 524288 | tf_op jit(solution)/shard_map/all_to_all | solution.py:111
  11.0 0.0 all-gather.2.cloned.1.call-start
  11.0 22.1 %collective-permute-start.6 = (bf16[8,128,128]{2,1,0:T(8,128)(2,1)}, bf16[8,128,128]{2,1,0:T(8,128)(2,1)S(1)}, u32[]{:S(2)}, u32[]{:S(2)}) collective-permute-start(bf16[8,128,128]{2,1,0:T(8,128)(2,1)} %bitcast.10), channel_id=1, source_target_pairs={{0,24},{1,9},{8,0},{9,17},{16,8},{17,25},{24,16},{25,1},{2,26},{3,... | collective-permute-start | bytes 786440 | tf_op jit(solution)/shard_map/ppermute | solution.py:108
  33.2 0.0 all-to-all-done
  33.2 0.0 copy-start.3
  33.2 0.7 copy-done.3
  33.9 0.0 all-gather.2.cloned.1.call-update
  33.9 16.7 %conditional.2 = (bf16[8,128,128]{2,1,0:T(8,128)(2,1)}, bf16[8,128,128]{2,1,0:T(8,128)(2,1)}, bf16[8,128,128]{2,1,0:T(8,128)(2,1)}) conditional(s32[]{:T(128)} %convert_element_type.4, () %tuple.24, bf16[8,128,128]{2,1,0:T(8,128)(2,1)} %bitcast.11), branch_computations={%region_0.0_spmd, %region_1.0_spmd} | conditional | bytes 3145872 | solution.py:100
  33.9 3.4 %collective-permute-start.2 = (bf16[8,128,128]{2,1,0:T(8,128)(2,1)}, bf16[8,128,128]{2,1,0:T(8,128)(2,1)}, u32[]{:S(2)}, u32[]{:S(2)}) collective-permute-start(bf16[8,128,128]{2,1,0:T(8,128)(2,1)} %param.1), channel_id=1, source_target_pairs={{0,32},{32,64},{64,96},{96,0},{1,33},{33,65},{65,97},{97,1},{2,34}... | collective-permute-start | bytes 786440 | tf_op jit(solution)/shard_map/cond/branch_1_fun/ppermute | solution.py:93
  37.3 4.6 %collective-permute-start.1 = (bf16[8,128,128]{2,1,0:T(8,128)(2,1)}, bf16[8,128,128]{2,1,0:T(8,128)(2,1)}, u32[]{:S(2)}, u32[]{:S(2)}) collective-permute-start(bf16[8,128,128]{2,1,0:T(8,128)(2,1)} %param.1), channel_id=1, source_target_pairs={{0,64},{32,96},{64,0},{96,32},{1,65},{33,97},{65,1},{97,33},{2,66}... | collective-permute-start | bytes 786440 | tf_op jit(solution)/shard_map/cond/branch_1_fun/ppermute | solution.py:93
  42.0 3.3 %collective-permute-start = (bf16[8,128,128]{2,1,0:T(8,128)(2,1)}, bf16[8,128,128]{2,1,0:T(8,128)(2,1)}, u32[]{:S(2)}, u32[]{:S(2)}) collective-permute-start(bf16[8,128,128]{2,1,0:T(8,128)(2,1)} %param.1), channel_id=1, source_target_pairs={{0,96},{32,0},{64,32},{96,64},{1,97},{33,1},{65,33},{97,65},{2,98}... | collective-permute-start | bytes 786440 | tf_op jit(solution)/shard_map/cond/branch_1_fun/ppermute | solution.py:93
  45.3 0.0 collective-permute-done.2
  45.3 2.2 %collective-permute-done.1 = bf16[8,128,128]{2,1,0:T(8,128)(2,1)} collective-permute-done((bf16[8,128,128]{2,1,0:T(8,128)(2,1)}, bf16[8,128,128]{2,1,0:T(8,128)(2,1)}, u32[]{:S(2)}, u32[]{:S(2)}) %collective-permute-start.1) | collective-permute-done | bytes 262176 | tf_op jit(solution)/shard_map/cond/branch_1_fun/ppermute | solution.py:93
  47.5 3.1 %collective-permute-done = bf16[8,128,128]{2,1,0:T(8,128)(2,1)} collective-permute-done((bf16[8,128,128]{2,1,0:T(8,128)(2,1)}, bf16[8,128,128]{2,1,0:T(8,128)(2,1)}, u32[]{:S(2)}, u32[]{:S(2)}) %collective-permute-start) | collective-permute-done | bytes 262176 | tf_op jit(solution)/shard_map/cond/branch_1_fun/ppermute | solution.py:93
  50.6 0.6 pad_add_fusion.place_ref
  51.2 7.1 %collective-permute-done.6.refs_4_ = bf16[8,128,128]{2,1,0:T(8,128)(2,1)S(1)} collective-permute-done((bf16[8,128,128]{2,1,0:T(8,128)(2,1)}, bf16[8,128,128]{2,1,0:T(8,128)(2,1)S(1)}, u32[]{:S(2)}, u32[]{:S(2)}) %collective-permute-start.6) | collective-permute-done | bytes 262176 | tf_op jit(solution)/shard_map/ppermute | solution.py:108
  58.3 0.0 copy-start.4
  58.3 0.0 copy-start.5
  58.3 13.6 %collective-permute-start.8 = (bf16[8,128,128]{2,1,0:T(8,128)(2,1)S(1)}, bf16[8,128,128]{2,1,0:T(8,128)(2,1)S(1)}, u32[]{:S(2)}, u32[]{:S(2)}) collective-permute-start(bf16[8,128,128]{2,1,0:T(8,128)(2,1)S(1)} %collective-permute-done.6.refs_4_), channel_id=1, source_target_pairs={{0,24},{1,9},{8,0},{9,17},{16,8},{17,25},{24,16},{25,1},{2,26},{3,... | collective-permute-start | bytes 786440 | tf_op jit(solution)/shard_map/ppermute | solution.py:108
  71.9 1.9 collective-permute-start.7
  73.8 1.2 shard_map.37.place
  75.0 0.0 copy-start.2
  75.0 15.3 %conditional.3 = (bf16[8,128,128]{2,1,0:T(8,128)(2,1)}, bf16[8,128,128]{2,1,0:T(8,128)(2,1)}, bf16[8,128,128]{2,1,0:T(8,128)(2,1)}) conditional(s32[]{:T(128)} %convert_element_type.4, () %tuple.26, bf16[8,128,128]{2,1,0:T(8,128)(2,1)S(1)} %collective-permute-done.6.refs_4_), branch_computations={%region_2.0_spmd, %region_3.0_spmd} | conditional | bytes 3145872 | solution.py:100
  75.1 2.3 %collective-permute-start.5 = (bf16[8,128,128]{2,1,0:T(8,128)(2,1)S(1)}, bf16[8,128,128]{2,1,0:T(8,128)(2,1)}, u32[]{:S(2)}, u32[]{:S(2)}) collective-permute-start(bf16[8,128,128]{2,1,0:T(8,128)(2,1)S(1)} %param.3), channel_id=1, source_target_pairs={{0,32},{32,64},{64,96},{96,0},{1,33},{33,65},{65,97},{97,1},{2,34}... | collective-permute-start | bytes 786440 | tf_op jit(solution)/shard_map/cond/branch_1_fun/ppermute | solution.py:93
  77.3 4.6 %collective-permute-start.4 = (bf16[8,128,128]{2,1,0:T(8,128)(2,1)S(1)}, bf16[8,128,128]{2,1,0:T(8,128)(2,1)}, u32[]{:S(2)}, u32[]{:S(2)}) collective-permute-start(bf16[8,128,128]{2,1,0:T(8,128)(2,1)S(1)} %param.3), channel_id=1, source_target_pairs={{0,64},{32,96},{64,0},{96,32},{1,65},{33,97},{65,1},{97,33},{2,66}... | collective-permute-start | bytes 786440 | tf_op jit(solution)/shard_map/cond/branch_1_fun/ppermute | solution.py:93
  82.0 3.3 %collective-permute-start.3 = (bf16[8,128,128]{2,1,0:T(8,128)(2,1)S(1)}, bf16[8,128,128]{2,1,0:T(8,128)(2,1)}, u32[]{:S(2)}, u32[]{:S(2)}) collective-permute-start(bf16[8,128,128]{2,1,0:T(8,128)(2,1)S(1)} %param.3), channel_id=1, source_target_pairs={{0,96},{32,0},{64,32},{96,64},{1,97},{33,1},{65,33},{97,65},{2,98}... | collective-permute-start | bytes 786440 | tf_op jit(solution)/shard_map/cond/branch_1_fun/ppermute | solution.py:93
  85.3 2.2 %collective-permute-done.5 = bf16[8,128,128]{2,1,0:T(8,128)(2,1)} collective-permute-done((bf16[8,128,128]{2,1,0:T(8,128)(2,1)S(1)}, bf16[8,128,128]{2,1,0:T(8,128)(2,1)}, u32[]{:S(2)}, u32[]{:S(2)}) %collective-permute-start.5) | collective-permute-done | bytes 262176 | tf_op jit(solution)/shard_map/cond/branch_1_fun/ppermute | solution.py:93
  87.6 0.0 collective-permute-done.4
  87.6 2.8 %collective-permute-done.3 = bf16[8,128,128]{2,1,0:T(8,128)(2,1)} collective-permute-done((bf16[8,128,128]{2,1,0:T(8,128)(2,1)S(1)}, bf16[8,128,128]{2,1,0:T(8,128)(2,1)}, u32[]{:S(2)}, u32[]{:S(2)}) %collective-permute-start.3) | collective-permute-done | bytes 262176 | tf_op jit(solution)/shard_map/cond/branch_1_fun/ppermute | solution.py:93
  90.4 33.1 %collective-permute-done.7 = bf16[8,128,128]{2,1,0:T(8,128)(2,1)S(1)} collective-permute-done((bf16[8,128,128]{2,1,0:T(8,128)(2,1)}, bf16[8,128,128]{2,1,0:T(8,128)(2,1)S(1)}, u32[]{:S(2)}, u32[]{:S(2)}) %collective-permute-start.7) | collective-permute-done | bytes 262176 | tf_op jit(solution)/shard_map/ppermute | solution.py:108
  123.5 4.8 %collective-permute-done.8 = bf16[8,128,128]{2,1,0:T(8,128)(2,1)S(1)} collective-permute-done((bf16[8,128,128]{2,1,0:T(8,128)(2,1)S(1)}, bf16[8,128,128]{2,1,0:T(8,128)(2,1)S(1)}, u32[]{:S(2)}, u32[]{:S(2)}) %collective-permute-start.8) | collective-permute-done | bytes 262176 | tf_op jit(solution)/shard_map/ppermute | solution.py:108
  128.4 3.7 %collective-permute-start.11 = (bf16[16,128,128]{2,1,0:T(8,128)(2,1)S(1)}, bf16[16,128,128]{2,1,0:T(8,128)(2,1)S(1)}, u32[]{:S(2)}, u32[]{:S(2)}) collective-permute-start(bf16[16,128,128]{2,1,0:T(8,128)(2,1)S(1)} %constant_dynamic-update-slice_fusion.refs_8_), channel_id=1, source_target_pairs={{0,32},{32,64},{64,96},{96,0},{1,33},{33,65},{65,97},{97,1},{2,34}... | collective-permute-start | bytes 1572872 | tf_op jit(solution)/shard_map/ppermute | solution.py:93
  132.1 4.2 %collective-permute-start.10 = (bf16[16,128,128]{2,1,0:T(8,128)(2,1)S(1)}, bf16[16,128,128]{2,1,0:T(8,128)(2,1)S(1)}, u32[]{:S(2)}, u32[]{:S(2)}) collective-permute-start(bf16[16,128,128]{2,1,0:T(8,128)(2,1)S(1)} %constant_dynamic-update-slice_fusion.refs_8_), channel_id=1, source_target_pairs={{0,64},{32,96},{64,0},{96,32},{1,65},{33,97},{65,1},{97,33},{2,66}... | collective-permute-start | bytes 1572872 | tf_op jit(solution)/shard_map/ppermute | solution.py:93
  136.3 2.8 %collective-permute-start.9 = (bf16[16,128,128]{2,1,0:T(8,128)(2,1)S(1)}, bf16[16,128,128]{2,1,0:T(8,128)(2,1)S(1)}, u32[]{:S(2)}, u32[]{:S(2)}) collective-permute-start(bf16[16,128,128]{2,1,0:T(8,128)(2,1)S(1)} %constant_dynamic-update-slice_fusion.refs_8_), channel_id=1, source_target_pairs={{0,96},{32,0},{64,32},{96,64},{1,97},{33,1},{65,33},{97,65},{2,98}... | collective-permute-start | bytes 1572872 | tf_op jit(solution)/shard_map/ppermute | solution.py:93
  139.1 0.0 copy-done.4
  139.1 0.1 copy.12
  139.2 0.1 copy.14.left
  139.3 0.0 copy-done.5
  139.3 0.1 copy.13
  139.4 0.1 copy.15.right
  139.4 5.9 %collective-permute-done.11.refs_11_ = bf16[16,128,128]{2,1,0:T(8,128)(2,1)S(1)} collective-permute-done((bf16[16,128,128]{2,1,0:T(8,128)(2,1)S(1)}, bf16[16,128,128]{2,1,0:T(8,128)(2,1)S(1)}, u32[]{:S(2)}, u32[]{:S(2)}) %collective-permute-start.11) | collective-permute-done | bytes 524320 | tf_op jit(solution)/shard_map/ppermute | solution.py:93
  145.4 12.2 %collective-permute-done.10.refs_10_ = bf16[16,128,128]{2,1,0:T(8,128)(2,1)S(1)} collective-permute-done((bf16[16,128,128]{2,1,0:T(8,128)(2,1)S(1)}, bf16[16,128,128]{2,1,0:T(8,128)(2,1)S(1)}, u32[]{:S(2)}, u32[]{:S(2)}) %collective-permute-start.10) | collective-permute-done | bytes 524320 | tf_op jit(solution)/shard_map/ppermute | solution.py:93
  157.5 1.6 collective-permute-done.9.refs_9_
  159.1 0.0 all-gather.2.cloned.1.call-done.refs_12_
  159.1 0.0 copy-done.2
  159.1 0.0 copy-start
  159.1 1.6 copy-done
  160.7 0.0 copy-start.1
  160.7 0.7 copy-done.1
  161.4 3.8 %shard_map.39 = f32[8,128,128]{2,1,0:T(8,128)S(1)} custom-call(s32[4]{0:T(128)S(1)} %copy-done.1, s32[16,32]{1,0:T(8,128)S(1)} %copy.14.left, s32[16,32]{1,0:T(8,128)S(1)} %copy.15.right, bf16[8,128,128]{2,1,0:T(8,128)(2,1)S(1)} %bitcast.13, bf16[8,128,128]{2,1,0:T(8,128)(2,1)} %get-tuple-element.35.refs_1_, bf16[8,128,128]{2,1,0:T(8,128)(2,1)} %get-tuple-element.36.refs_2_, ...), custom_call_target="tpu_custom_call" | custom-call | flops 1073741824 | bytes 8388608 | tf_op jit(solution)/shard_map/pallas_call | solution.py:57
  165.2 1.9 collective-permute-start.12
  167.1 3.9 %shard_map.38 = f32[8,128,128]{2,1,0:T(8,128)S(1)} custom-call(s32[4]{0:T(128)S(1)} %copy-done.1, s32[16,32]{1,0:T(8,128)S(1)} %copy.14.left, s32[16,32]{1,0:T(8,128)S(1)} %copy.15.right, bf16[8,128,128]{2,1,0:T(8,128)(2,1)S(1)} %bitcast.14, bf16[8,128,128]{2,1,0:T(8,128)(2,1)} %get-tuple-element.35.refs_1_, bf16[8,128,128]{2,1,0:T(8,128)(2,1)} %get-tuple-element.36.refs_2_, ...), custom_call_target="tpu_custom_call" | custom-call | flops 1073741824 | bytes 8388608 | tf_op jit(solution)/shard_map/pallas_call | solution.py:57
  171.0 0.0 collective-permute-done.12
  171.0 0.1 add.3
  171.1 14.8 %all_to_all.10 = f32[4,2,128,128]{3,2,1,0:T(8,128)S(1)} all-to-all(f32[4,2,128,128]{3,2,1,0:T(8,128)S(1)} %bitcast.15), channel_id=1, replica_groups=mesh['row'=8,'x'=4,'zh'=4,'y'=4,'core'=2] {'y'}, dimensions={0} | all-to-all | bytes 1048576 | tf_op jit(solution)/shard_map/all_to_all | solution.py:133
  185.9 0.7 reduce_sum.9
  (2 shorter events, 0.1 us)
Async XLA Ops:
  6.5 26.6 %all-to-all-start = ((bf16[8,128,128]{2,1,0:T(8,128)(2,1)}), bf16[8,128,128]{2,1,0:T(8,128)(2,1)S(1)}, u32[]{:S(2)}, u32[]{:S(2)}) async-start(bf16[8,128,128]{2,1,0:T(8,128)(2,1)} %bitcast.9), calls=%async_computation | async-start | bytes 524288 | tf_op jit(solution)/shard_map/all_to_all | solution.py:111
  11.0 148.1 %all-gather.2.cloned.1.call-start = ((), (), s32[]{:S(2)}) async-start(), calls=%async_computation.2 | async-start | bytes 2359296 | tf_op jit(solution)/shard_map/all_gather | solution.py:112
  11.0 47.2 %collective-permute-start.6 = (bf16[8,128,128]{2,1,0:T(8,128)(2,1)}, bf16[8,128,128]{2,1,0:T(8,128)(2,1)S(1)}, u32[]{:S(2)}, u32[]{:S(2)}) collective-permute-start(bf16[8,128,128]{2,1,0:T(8,128)(2,1)} %bitcast.10), channel_id=1, source_target_pairs={{0,24},{1,9},{8,0},{9,17},{16,8},{17,25},{24,16},{25,1},{2,26},{3,... | collective-permute-start | bytes 786440 | tf_op jit(solution)/shard_map/ppermute | solution.py:108
  33.2 0.7 copy-start.3
  33.9 11.4 %collective-permute-start.2 = (bf16[8,128,128]{2,1,0:T(8,128)(2,1)}, bf16[8,128,128]{2,1,0:T(8,128)(2,1)}, u32[]{:S(2)}, u32[]{:S(2)}) collective-permute-start(bf16[8,128,128]{2,1,0:T(8,128)(2,1)} %param.1), channel_id=1, source_target_pairs={{0,32},{32,64},{64,96},{96,0},{1,33},{33,65},{65,97},{97,1},{2,34}... | collective-permute-start | bytes 786440 | tf_op jit(solution)/shard_map/cond/branch_1_fun/ppermute | solution.py:93
  37.3 10.2 %collective-permute-start.1 = (bf16[8,128,128]{2,1,0:T(8,128)(2,1)}, bf16[8,128,128]{2,1,0:T(8,128)(2,1)}, u32[]{:S(2)}, u32[]{:S(2)}) collective-permute-start(bf16[8,128,128]{2,1,0:T(8,128)(2,1)} %param.1), channel_id=1, source_target_pairs={{0,64},{32,96},{64,0},{96,32},{1,65},{33,97},{65,1},{97,33},{2,66}... | collective-permute-start | bytes 786440 | tf_op jit(solution)/shard_map/cond/branch_1_fun/ppermute | solution.py:93
  42.0 8.6 %collective-permute-start = (bf16[8,128,128]{2,1,0:T(8,128)(2,1)}, bf16[8,128,128]{2,1,0:T(8,128)(2,1)}, u32[]{:S(2)}, u32[]{:S(2)}) collective-permute-start(bf16[8,128,128]{2,1,0:T(8,128)(2,1)} %param.1), channel_id=1, source_target_pairs={{0,96},{32,0},{64,32},{96,64},{1,97},{33,1},{65,33},{97,65},{2,98}... | collective-permute-start | bytes 786440 | tf_op jit(solution)/shard_map/cond/branch_1_fun/ppermute | solution.py:93
  58.3 80.9 %copy-start.4 = (s32[1,1,1,16,16,2]{4,5,3,2,1,0:T(2,128)S(1)}, s32[1,1,1,16,16,2]{4,5,3,2,1,0:T(2,128)}, u32[]{:S(2)}) copy-start(s32[1,1,1,16,16,2]{4,5,3,2,1,0:T(2,128)} %param.8) | copy-start | bytes 6148
  58.3 81.0 %copy-start.5 = (s32[1,1,1,16,16,2]{4,5,3,2,1,0:T(2,128)S(1)}, s32[1,1,1,16,16,2]{4,5,3,2,1,0:T(2,128)}, u32[]{:S(2)}) copy-start(s32[1,1,1,16,16,2]{4,5,3,2,1,0:T(2,128)} %param.9) | copy-start | bytes 6148
  58.3 70.1 %collective-permute-start.8 = (bf16[8,128,128]{2,1,0:T(8,128)(2,1)S(1)}, bf16[8,128,128]{2,1,0:T(8,128)(2,1)S(1)}, u32[]{:S(2)}, u32[]{:S(2)}) collective-permute-start(bf16[8,128,128]{2,1,0:T(8,128)(2,1)S(1)} %collective-permute-done.6.refs_4_), channel_id=1, source_target_pairs={{0,24},{1,9},{8,0},{9,17},{16,8},{17,25},{24,16},{25,1},{2,26},{3,... | collective-permute-start | bytes 786440 | tf_op jit(solution)/shard_map/ppermute | solution.py:108
  71.9 51.6 %collective-permute-start.7 = (bf16[8,128,128]{2,1,0:T(8,128)(2,1)}, bf16[8,128,128]{2,1,0:T(8,128)(2,1)S(1)}, u32[]{:S(2)}, u32[]{:S(2)}) collective-permute-start(bf16[8,128,128]{2,1,0:T(8,128)(2,1)} %bitcast.12), channel_id=1, source_target_pairs={{0,8},{1,25},{8,16},{9,1},{16,24},{17,9},{24,0},{25,17},{2,10},{3,... | collective-permute-start | bytes 786440 | tf_op jit(solution)/shard_map/ppermute | solution.py:108
  75.0 84.1 %copy-start.2 = (bf16[1,1,1,8,1,128,128]{6,5,4,3,2,1,0:T(8,128)(2,1)S(1)}, bf16[1,1,1,8,1,128,128]{6,5,4,3,2,1,0:T(8,128)(2,1)}, u32[]{:S(2)}) copy-start(bf16[1,1,1,8,1,128,128]{6,5,4,3,2,1,0:T(8,128)(2,1)} %param.7) | copy-start | bytes 786436
  75.1 12.5 %collective-permute-start.5 = (bf16[8,128,128]{2,1,0:T(8,128)(2,1)S(1)}, bf16[8,128,128]{2,1,0:T(8,128)(2,1)}, u32[]{:S(2)}, u32[]{:S(2)}) collective-permute-start(bf16[8,128,128]{2,1,0:T(8,128)(2,1)S(1)} %param.3), channel_id=1, source_target_pairs={{0,32},{32,64},{64,96},{96,0},{1,33},{33,65},{65,97},{97,1},{2,34}... | collective-permute-start | bytes 786440 | tf_op jit(solution)/shard_map/cond/branch_1_fun/ppermute | solution.py:93
  77.3 10.2 %collective-permute-start.4 = (bf16[8,128,128]{2,1,0:T(8,128)(2,1)S(1)}, bf16[8,128,128]{2,1,0:T(8,128)(2,1)}, u32[]{:S(2)}, u32[]{:S(2)}) collective-permute-start(bf16[8,128,128]{2,1,0:T(8,128)(2,1)S(1)} %param.3), channel_id=1, source_target_pairs={{0,64},{32,96},{64,0},{96,32},{1,65},{33,97},{65,1},{97,33},{2,66}... | collective-permute-start | bytes 786440 | tf_op jit(solution)/shard_map/cond/branch_1_fun/ppermute | solution.py:93
  82.0 8.4 %collective-permute-start.3 = (bf16[8,128,128]{2,1,0:T(8,128)(2,1)S(1)}, bf16[8,128,128]{2,1,0:T(8,128)(2,1)}, u32[]{:S(2)}, u32[]{:S(2)}) collective-permute-start(bf16[8,128,128]{2,1,0:T(8,128)(2,1)S(1)} %param.3), channel_id=1, source_target_pairs={{0,96},{32,0},{64,32},{96,64},{1,97},{33,1},{65,33},{97,65},{2,98}... | collective-permute-start | bytes 786440 | tf_op jit(solution)/shard_map/cond/branch_1_fun/ppermute | solution.py:93
  128.4 16.9 %collective-permute-start.11 = (bf16[16,128,128]{2,1,0:T(8,128)(2,1)S(1)}, bf16[16,128,128]{2,1,0:T(8,128)(2,1)S(1)}, u32[]{:S(2)}, u32[]{:S(2)}) collective-permute-start(bf16[16,128,128]{2,1,0:T(8,128)(2,1)S(1)} %constant_dynamic-update-slice_fusion.refs_8_), channel_id=1, source_target_pairs={{0,32},{32,64},{64,96},{96,0},{1,33},{33,65},{65,97},{97,1},{2,34}... | collective-permute-start | bytes 1572872 | tf_op jit(solution)/shard_map/ppermute | solution.py:93
  132.1 25.4 %collective-permute-start.10 = (bf16[16,128,128]{2,1,0:T(8,128)(2,1)S(1)}, bf16[16,128,128]{2,1,0:T(8,128)(2,1)S(1)}, u32[]{:S(2)}, u32[]{:S(2)}) collective-permute-start(bf16[16,128,128]{2,1,0:T(8,128)(2,1)S(1)} %constant_dynamic-update-slice_fusion.refs_8_), channel_id=1, source_target_pairs={{0,64},{32,96},{64,0},{96,32},{1,65},{33,97},{65,1},{97,33},{2,66}... | collective-permute-start | bytes 1572872 | tf_op jit(solution)/shard_map/ppermute | solution.py:93
  136.3 22.8 %collective-permute-start.9 = (bf16[16,128,128]{2,1,0:T(8,128)(2,1)S(1)}, bf16[16,128,128]{2,1,0:T(8,128)(2,1)S(1)}, u32[]{:S(2)}, u32[]{:S(2)}) collective-permute-start(bf16[16,128,128]{2,1,0:T(8,128)(2,1)S(1)} %constant_dynamic-update-slice_fusion.refs_8_), channel_id=1, source_target_pairs={{0,96},{32,0},{64,32},{96,64},{1,97},{33,1},{65,33},{97,65},{2,98}... | collective-permute-start | bytes 1572872 | tf_op jit(solution)/shard_map/ppermute | solution.py:93
  159.1 1.6 copy-start
  160.7 0.7 copy-start.1
  165.2 5.8 %collective-permute-start.12 = (f32[8,128,128]{2,1,0:T(8,128)S(1)}, f32[8,128,128]{2,1,0:T(8,128)S(1)}, u32[]{:S(2)}, u32[]{:S(2)}) collective-permute-start(f32[8,128,128]{2,1,0:T(8,128)S(1)} %shard_map.39), channel_id=1, source_target_pairs={{0,1},{1,0},{2,3},{3,2},{4,5},{5,4},{6,7},{7,6},{8,9},{9,8},{10,11... | collective-permute-start | bytes 1572872 | tf_op jit(solution)/shard_map/ppermute | solution.py:129
Sparse Core Ops, SparseCore 0:
  34.0 109.0 all-gather.1

commit v13 on v11

--- a/solution.py
+++ b/solution.py
@@ -12,18 +12,18 @@
 S, SLOTS, R, BS = 8, 2, 16, 128
 COLS = X * ZH
 PER = R // (Y * CORE)
-WEIGHT = 26 * 10**9
+WEIGHT = 31 * 10**9
 
 
 def ring(n, k):
     return [(i, (i + k) % n) for i in range(n)]
 
 
-def products(groups, other, place, left, right, *refs):
+def products(groups, other, lists, *refs):
     n = 1 + max(g[0] for g in groups)
     a, refs = refs[:n], refs[n:]
     b, out = refs
-    x, zh, core, y = (place[k] for k in range(4))
+    x, zh, core, y = (lists[2 * R * COLS * SLOTS + k] for k in range(4))
     to_zh = (0, 1 + 2 * core, 3 - 2 * core, 2)
 
     def one(r):
@@ -32,10 +32,11 @@
             c = lax.rem(x + dx, X) * ZH + lax.rem(zh + to_zh[dz], ZH)
             lefts, rights = [], []
             for p in range(SLOTS):
-                m = left[r, c * SLOTS + p]
+                at = (r * COLS + c) * SLOTS + p
+                m = lists[at]
                 tile = a[array][start + jnp.minimum(m, S - 1)]
                 lefts.append(jnp.where(m < S, tile, jnp.zeros_like(tile)))
-                rights.append(b[jnp.minimum(right[r, c * SLOTS + p], ROW * S - 1)])
+                rights.append(b[jnp.minimum(lists[R * COLS * SLOTS + at], ROW * S - 1)])
             value = jnp.dot(
                 jnp.concatenate(lefts, axis=1),
                 jnp.concatenate(rights, axis=0),
@@ -57,13 +58,13 @@
     return pl.pallas_call(
         functools.partial(products, groups, other),
         out_shape=jax.ShapeDtypeStruct((R // 2, BS, BS), jnp.float32),
-        in_specs=[smem] * len(lists) + [vmem] * (len(arrays) + 1),
+        in_specs=[smem] + [vmem] * (len(arrays) + 1),
         out_specs=vmem,
         compiler_params=pltpu.CompilerParams(vmem_limit_bytes=24 * 1024 * 1024),
         cost_estimate=pl.CostEstimate(
             flops=R // 2 * len(groups) * SLOTS * 2 * BS**3, bytes_accessed=8 * 1024 * 1024, transcendentals=0
         ),
-    )(*lists, *arrays, b)
+    )(lists, *arrays, b)
 
 
 def passing(place, weight, *after):
@@ -85,8 +86,7 @@
 
 def on_device(tiles, pair_a, pair_b):
     own = tiles.reshape(S, BS, BS)
-    left = pair_a.reshape(R, COLS * SLOTS)
-    right = pair_b.reshape(R, COLS * SLOTS)
+    pairs = jnp.concatenate([pair_a.reshape(-1), pair_b.reshape(-1)])
     place = jnp.stack([lax.axis_index(n) for n in ("x", "zh", "core", "y")]).astype(jnp.int32)
 
     def over_x(value):
@@ -122,7 +122,7 @@
     far = over_x(opposite)
 
     arrays = [own, *own_x, both, *near, opposite, *far]
-    lists = (place, left, right)
+    lists = jnp.concatenate([pairs, place])
     groups = [(d, 0, d, 0) for d in range(X)]
     groups += [(X + d, k * S, d, z) for k, z in enumerate((1, 2)) for d in range(X)]
     groups += [(2 * X + d, 0, d, 3) for d in range(X)]

time: 193 us -> 181 us (0.938)
  the two profiles are of different devices: /device:TPU:98 before, /device:TPU:1 now
where the time goes in v13:
time: 181 us; the launch traced here: 180 us
  starting transfers between devices  82.2 us (45%)
  waiting for transfers between devices  56.4 us (31%)
  between operations  13.6 us (8%)
  blocking collectives  13.2 us (7%)
  Pallas kernels  9.55 us (5%)
  local copies, waits for them, and re-layouts  3.69 us (2%)
    ppermute x9, waiting for transfers between devices, over_x(): two, one, three = (lax.ppermute(value, 'x', ring(X, -d)) for d in (2, 1, 3))  33.9 us
    ppermute x9, starting transfers between devices, over_x(): two, one, three = (lax.ppermute(value, 'x', ring(X, -d)) for d in (2, 1, 3))  30.7 us
    ppermute x3, starting transfers between devices, along_z(): lax.ppermute(value, ('zh', 'core'), [(z * CORE + k, to * CORE + k) for to...  30.5 us
    all_to_all x1, starting transfers between devices, on_device(): lax.all_to_all(own, ('y', 'core'), split_axis=0, concat_axis=0, tiled=True)  17.5 us
    ppermute x3, waiting for transfers between devices, along_z(): lax.ppermute(value, ('zh', 'core'), [(z * CORE + k, to * CORE + k) for to...  16.1 us
    all_to_all x1, blocking collectives, on_device(): parts = lax.all_to_all(parts, 'y', split_axis=0, concat_axis=0, tiled=True)  13.2 us
    pallas_call x2, Pallas kernels, call(): pl.pallas_call(functools.partial(products, groups, other), out_shape=jax....  8.37 us
    all_gather x1, waiting for transfers between devices, on_device(): b = lax.all_gather(routed, 'row', axis=0, tiled=True)  6.31 us
  transfers between devices with their start and end apart: 15, of which 11 were waited for; matrix products, arithmetic and copies ran while one was open for 1% of the time, Pallas kernels for 3%

profile of v13, /device:TPU:1, one launch (start us, length us, event | category | flops | bytes accessed | tf_op | source)
XLA Modules:
  0.0 180.0 jit_solution(18356790169987053098)
XLA Ops:
  6.5 17.5 %all-to-all-start = ((bf16[8,128,128]{2,1,0:T(8,128)(2,1)}), bf16[8,128,128]{2,1,0:T(8,128)(2,1)S(1)}, u32[]{:S(2)}, u32[]{:S(2)}) async-start(bf16[8,128,128]{2,1,0:T(8,128)(2,1)} %bitcast.11), calls=%async_computation | async-start | bytes 524288 | tf_op jit(solution)/shard_map/all_to_all | solution.py:112
  24.0 0.0 all-gather.2.cloned.1.call-start
  24.0 11.2 %collective-permute-start.7 = (bf16[8,128,128]{2,1,0:T(8,128)(2,1)}, bf16[8,128,128]{2,1,0:T(8,128)(2,1)S(1)}, u32[]{:S(2)}, u32[]{:S(2)}) collective-permute-start(bf16[8,128,128]{2,1,0:T(8,128)(2,1)} %bitcast.12), channel_id=1, source_target_pairs={{0,8},{1,25},{8,16},{9,1},{16,24},{17,9},{24,0},{25,17},{2,10},{3,... | collective-permute-start | bytes 786440 | tf_op jit(solution)/shard_map/ppermute | solution.py:108
  35.2 2.8 %collective-permute-start.6 = (bf16[8,128,128]{2,1,0:T(8,128)(2,1)}, bf16[8,128,128]{2,1,0:T(8,128)(2,1)S(1)}, u32[]{:S(2)}, u32[]{:S(2)}) collective-permute-start(bf16[8,128,128]{2,1,0:T(8,128)(2,1)} %bitcast.13), channel_id=1, source_target_pairs={{0,24},{1,9},{8,0},{9,17},{16,8},{17,25},{24,16},{25,1},{2,26},{3,... | collective-permute-start | bytes 786440 | tf_op jit(solution)/shard_map/ppermute | solution.py:108
  38.0 0.0 all-to-all-done
  38.0 0.0 copy-start.2
  38.0 0.7 copy-done.2
  38.7 0.0 all-gather.2.cloned.1.call-update
  38.8 0.9 copy.6
  39.6 0.1 reshape.15
  39.8 18.8 %conditional.2 = (bf16[8,128,128]{2,1,0:T(8,128)(2,1)}, bf16[8,128,128]{2,1,0:T(8,128)(2,1)}, bf16[8,128,128]{2,1,0:T(8,128)(2,1)}) conditional(s32[]{:T(128)} %convert_element_type.4, () %tuple.24, bf16[8,128,128]{2,1,0:T(8,128)(2,1)} %bitcast.14), branch_computations={%region_0.0_spmd, %region_1.0_spmd} | conditional | bytes 3145872 | solution.py:100
  39.8 2.3 %collective-permute-start.2 = (bf16[8,128,128]{2,1,0:T(8,128)(2,1)}, bf16[8,128,128]{2,1,0:T(8,128)(2,1)}, u32[]{:S(2)}, u32[]{:S(2)}) collective-permute-start(bf16[8,128,128]{2,1,0:T(8,128)(2,1)} %param.1), channel_id=1, source_target_pairs={{0,32},{32,64},{64,96},{96,0},{1,33},{33,65},{65,97},{97,1},{2,34}... | collective-permute-start | bytes 786440 | tf_op jit(solution)/shard_map/cond/branch_1_fun/ppermute | solution.py:93
  42.1 4.4 %collective-permute-start.1 = (bf16[8,128,128]{2,1,0:T(8,128)(2,1)}, bf16[8,128,128]{2,1,0:T(8,128)(2,1)}, u32[]{:S(2)}, u32[]{:S(2)}) collective-permute-start(bf16[8,128,128]{2,1,0:T(8,128)(2,1)} %param.1), channel_id=1, source_target_pairs={{0,64},{32,96},{64,0},{96,32},{1,65},{33,97},{65,1},{97,33},{2,66}... | collective-permute-start | bytes 786440 | tf_op jit(solution)/shard_map/cond/branch_1_fun/ppermute | solution.py:93
  46.4 3.1 %collective-permute-start = (bf16[8,128,128]{2,1,0:T(8,128)(2,1)}, bf16[8,128,128]{2,1,0:T(8,128)(2,1)}, u32[]{:S(2)}, u32[]{:S(2)}) collective-permute-start(bf16[8,128,128]{2,1,0:T(8,128)(2,1)} %param.1), channel_id=1, source_target_pairs={{0,96},{32,0},{64,32},{96,64},{1,97},{33,1},{65,33},{97,65},{2,98}... | collective-permute-start | bytes 786440 | tf_op jit(solution)/shard_map/cond/branch_1_fun/ppermute | solution.py:93
  49.5 0.8 collective-permute-done.2
  50.3 6.2 %collective-permute-done.1 = bf16[8,128,128]{2,1,0:T(8,128)(2,1)} collective-permute-done((bf16[8,128,128]{2,1,0:T(8,128)(2,1)}, bf16[8,128,128]{2,1,0:T(8,128)(2,1)}, u32[]{:S(2)}, u32[]{:S(2)}) %collective-permute-start.1) | collective-permute-done | bytes 262176 | tf_op jit(solution)/shard_map/cond/branch_1_fun/ppermute | solution.py:93
  56.5 2.0 %collective-permute-done = bf16[8,128,128]{2,1,0:T(8,128)(2,1)} collective-permute-done((bf16[8,128,128]{2,1,0:T(8,128)(2,1)}, bf16[8,128,128]{2,1,0:T(8,128)(2,1)}, u32[]{:S(2)}, u32[]{:S(2)}) %collective-permute-start) | collective-permute-done | bytes 262176 | tf_op jit(solution)/shard_map/cond/branch_1_fun/ppermute | solution.py:93
  58.5 0.6 pad_add_fusion.place_ref
  59.1 16.1 %collective-permute-done.7 = bf16[8,128,128]{2,1,0:T(8,128)(2,1)S(1)} collective-permute-done((bf16[8,128,128]{2,1,0:T(8,128)(2,1)}, bf16[8,128,128]{2,1,0:T(8,128)(2,1)S(1)}, u32[]{:S(2)}, u32[]{:S(2)}) %collective-permute-start.7) | collective-permute-done | bytes 262176 | tf_op jit(solution)/shard_map/ppermute | solution.py:108
  75.2 0.0 collective-permute-done.6
  75.2 16.5 %collective-permute-start.8 = (bf16[8,128,128]{2,1,0:T(8,128)(2,1)S(1)}, bf16[8,128,128]{2,1,0:T(8,128)(2,1)S(1)}, u32[]{:S(2)}, u32[]{:S(2)}) collective-permute-start(bf16[8,128,128]{2,1,0:T(8,128)(2,1)S(1)} %collective-permute-done.6), channel_id=1, source_target_pairs={{0,24},{1,9},{8,0},{9,17},{16,8},{17,25},{24,16},{25,1},{2,26},{3,... | collective-permute-start | bytes 786440 | tf_op jit(solution)/shard_map/ppermute | solution.py:108
  91.8 1.2 shard_map.37
  93.0 0.0 copy-start.3
  93.0 0.0 copy-start.4
  93.0 0.0 copy-start.1
  93.1 27.1 %conditional.3 = (bf16[16,128,128]{2,1,0:T(8,128)(2,1)}, bf16[16,128,128]{2,1,0:T(8,128)(2,1)}, bf16[16,128,128]{2,1,0:T(8,128)(2,1)}) conditional(s32[]{:T(128)} %convert_element_type.4, () %tuple.26, bf16[16,128,128]{2,1,0:T(8,128)(2,1)S(1)} %constant_dynamic-update-slice_fusion.refs_4_), branch_computations={%region_2.0_spmd, %region_3.0_spmd} | conditional | bytes 6291600 | solution.py:100
  93.1 2.9 %collective-permute-start.5 = (bf16[16,128,128]{2,1,0:T(8,128)(2,1)S(1)}, bf16[16,128,128]{2,1,0:T(8,128)(2,1)}, u32[]{:S(2)}, u32[]{:S(2)}) collective-permute-start(bf16[16,128,128]{2,1,0:T(8,128)(2,1)S(1)} %param.3), channel_id=1, source_target_pairs={{0,32},{32,64},{64,96},{96,0},{1,33},{33,65},{65,97},{97,1},{2,34}... | collective-permute-start | bytes 1572872 | tf_op jit(solution)/shard_map/cond/branch_1_fun/ppermute | solution.py:93
  96.0 4.4 %collective-permute-start.4 = (bf16[16,128,128]{2,1,0:T(8,128)(2,1)S(1)}, bf16[16,128,128]{2,1,0:T(8,128)(2,1)}, u32[]{:S(2)}, u32[]{:S(2)}) collective-permute-start(bf16[16,128,128]{2,1,0:T(8,128)(2,1)S(1)} %param.3), channel_id=1, source_target_pairs={{0,64},{32,96},{64,0},{96,32},{1,65},{33,97},{65,1},{97,33},{2,66}... | collective-permute-start | bytes 1572872 | tf_op jit(solution)/shard_map/cond/branch_1_fun/ppermute | solution.py:93
  100.3 3.1 %collective-permute-start.3 = (bf16[16,128,128]{2,1,0:T(8,128)(2,1)S(1)}, bf16[16,128,128]{2,1,0:T(8,128)(2,1)}, u32[]{:S(2)}, u32[]{:S(2)}) collective-permute-start(bf16[16,128,128]{2,1,0:T(8,128)(2,1)S(1)} %param.3), channel_id=1, source_target_pairs={{0,96},{32,0},{64,32},{96,64},{1,97},{33,1},{65,33},{97,65},{2,98}... | collective-permute-start | bytes 1572872 | tf_op jit(solution)/shard_map/cond/branch_1_fun/ppermute | solution.py:93
  103.4 5.3 %collective-permute-done.5 = bf16[16,128,128]{2,1,0:T(8,128)(2,1)} collective-permute-done((bf16[16,128,128]{2,1,0:T(8,128)(2,1)S(1)}, bf16[16,128,128]{2,1,0:T(8,128)(2,1)}, u32[]{:S(2)}, u32[]{:S(2)}) %collective-permute-start.5) | collective-permute-done | bytes 524320 | tf_op jit(solution)/shard_map/cond/branch_1_fun/ppermute | solution.py:93
  108.7 9.4 %collective-permute-done.4 = bf16[16,128,128]{2,1,0:T(8,128)(2,1)} collective-permute-done((bf16[16,128,128]{2,1,0:T(8,128)(2,1)S(1)}, bf16[16,128,128]{2,1,0:T(8,128)(2,1)}, u32[]{:S(2)}, u32[]{:S(2)}) %collective-permute-start.4) | collective-permute-done | bytes 524320 | tf_op jit(solution)/shard_map/cond/branch_1_fun/ppermute | solution.py:93
  118.2 2.0 %collective-permute-done.3 = bf16[16,128,128]{2,1,0:T(8,128)(2,1)} collective-permute-done((bf16[16,128,128]{2,1,0:T(8,128)(2,1)S(1)}, bf16[16,128,128]{2,1,0:T(8,128)(2,1)}, u32[]{:S(2)}, u32[]{:S(2)}) %collective-permute-start.3) | collective-permute-done | bytes 524320 | tf_op jit(solution)/shard_map/cond/branch_1_fun/ppermute | solution.py:93
  120.1 0.0 collective-permute-done.8.refs_8_
  120.1 4.2 %collective-permute-start.11 = (bf16[8,128,128]{2,1,0:T(8,128)(2,1)S(1)}, bf16[8,128,128]{2,1,0:T(8,128)(2,1)S(1)}, u32[]{:S(2)}, u32[]{:S(2)}) collective-permute-start(bf16[8,128,128]{2,1,0:T(8,128)(2,1)S(1)} %collective-permute-done.8.refs_8_), channel_id=1, source_target_pairs={{0,32},{32,64},{64,96},{96,0},{1,33},{33,65},{65,97},{97,1},{2,34}... | collective-permute-start | bytes 786440 | tf_op jit(solution)/shard_map/ppermute | solution.py:93
  124.3 3.2 %collective-permute-start.10 = (bf16[8,128,128]{2,1,0:T(8,128)(2,1)S(1)}, bf16[8,128,128]{2,1,0:T(8,128)(2,1)S(1)}, u32[]{:S(2)}, u32[]{:S(2)}) collective-permute-start(bf16[8,128,128]{2,1,0:T(8,128)(2,1)S(1)} %collective-permute-done.8.refs_8_), channel_id=1, source_target_pairs={{0,64},{32,96},{64,0},{96,32},{1,65},{33,97},{65,1},{97,33},{2,66}... | collective-permute-start | bytes 786440 | tf_op jit(solution)/shard_map/ppermute | solution.py:93
  127.5 3.4 %collective-permute-start.9 = (bf16[8,128,128]{2,1,0:T(8,128)(2,1)S(1)}, bf16[8,128,128]{2,1,0:T(8,128)(2,1)S(1)}, u32[]{:S(2)}, u32[]{:S(2)}) collective-permute-start(bf16[8,128,128]{2,1,0:T(8,128)(2,1)S(1)} %collective-permute-done.8.refs_8_), channel_id=1, source_target_pairs={{0,96},{32,0},{64,32},{96,64},{1,97},{33,1},{65,33},{97,65},{2,98}... | collective-permute-start | bytes 786440 | tf_op jit(solution)/shard_map/ppermute | solution.py:93
  130.9 0.0 copy-done.3
  130.9 0.2 copy.7
  131.1 0.1 reshape.16
  131.2 0.0 copy-done.4
  131.2 0.3 collective-permute-done.11.refs_11_
  131.5 5.9 %collective-permute-done.10.refs_10_ = bf16[8,128,128]{2,1,0:T(8,128)(2,1)S(1)} collective-permute-done((bf16[8,128,128]{2,1,0:T(8,128)(2,1)S(1)}, bf16[8,128,128]{2,1,0:T(8,128)(2,1)S(1)}, u32[]{:S(2)}, u32[]{:S(2)}) %collective-permute-start.10) | collective-permute-done | bytes 262176 | tf_op jit(solution)/shard_map/ppermute | solution.py:93
  137.4 2.0 %collective-permute-done.9.refs_9_ = bf16[8,128,128]{2,1,0:T(8,128)(2,1)S(1)} collective-permute-done((bf16[8,128,128]{2,1,0:T(8,128)(2,1)S(1)}, bf16[8,128,128]{2,1,0:T(8,128)(2,1)S(1)}, u32[]{:S(2)}, u32[]{:S(2)}) %collective-permute-start.9) | collective-permute-done | bytes 262176 | tf_op jit(solution)/shard_map/ppermute | solution.py:93
  139.4 6.3 %all-gather.2.cloned.1.call-done.refs_12_ = bf16[64,128,128]{2,1,0:T(8,128)(2,1)} async-done(((bf16[8,128,128]{2,1,0:T(8,128)(2,1)}), bf16[64,128,128]{2,1,0:T(8,128)(2,1)}) %all-gather.2.cloned.1.call-update) | async-done | bytes 2097168 | tf_op jit(solution)/shard_map/all_gather | solution.py:114
  145.7 0.0 copy-done.1
  145.7 0.0 copy-start
  145.7 1.6 copy-done
  147.3 4.1 %shard_map.39 = f32[8,128,128]{2,1,0:T(8,128)S(1)} custom-call(s32[1028]{0:T(1024)S(1)} %constant_dynamic-update-slice_fusion.3.lists, bf16[8,128,128]{2,1,0:T(8,128)(2,1)S(1)} %bitcast.15, bf16[8,128,128]{2,1,0:T(8,128)(2,1)} %get-tuple-element.34.refs_1_, bf16[8,128,128]{2,1,0:T(8,128)(2,1)} %get-tuple-element.35.refs_2_, ...), custom_call_target="tpu_custom_call" | custom-call | flops 1073741824 | bytes 8388608 | tf_op jit(solution)/shard_map/pallas_call | solution.py:58
  151.5 3.5 %collective-permute-start.12 = (f32[8,128,128]{2,1,0:T(8,128)S(1)}, f32[8,128,128]{2,1,0:T(8,128)S(1)}, u32[]{:S(2)}, u32[]{:S(2)}) collective-permute-start(f32[8,128,128]{2,1,0:T(8,128)S(1)} %shard_map.39), channel_id=1, source_target_pairs={{0,1},{1,0},{2,3},{3,2},{4,5},{5,4},{6,7},{7,6},{8,9},{9,8},{10,11... | collective-permute-start | bytes 1572872 | tf_op jit(solution)/shard_map/ppermute | solution.py:130
  155.0 4.2 %shard_map.38 = f32[8,128,128]{2,1,0:T(8,128)S(1)} custom-call(s32[1028]{0:T(1024)S(1)} %constant_dynamic-update-slice_fusion.3.lists, bf16[8,128,128]{2,1,0:T(8,128)(2,1)S(1)} %bitcast.16, bf16[8,128,128]{2,1,0:T(8,128)(2,1)} %get-tuple-element.34.refs_1_, bf16[8,128,128]{2,1,0:T(8,128)(2,1)} %get-tuple-element.35.refs_2_, ...), custom_call_target="tpu_custom_call" | custom-call | flops 1073741824 | bytes 8388608 | tf_op jit(solution)/shard_map/pallas_call | solution.py:58
  159.2 0.0 collective-permute-done.12
  159.2 0.1 add.3
  159.3 13.2 %all_to_all.10 = f32[4,2,128,128]{3,2,1,0:T(8,128)S(1)} all-to-all(f32[4,2,128,128]{3,2,1,0:T(8,128)S(1)} %bitcast.17), channel_id=1, replica_groups=mesh['row'=8,'x'=4,'zh'=4,'y'=4,'core'=2] {'y'}, dimensions={0} | all-to-all | bytes 1048576 | tf_op jit(solution)/shard_map/all_to_all | solution.py:134
  172.5 0.7 reduce_sum.9
  (6 shorter events, 0.1 us)
Async XLA Ops:
  6.5 31.5 %all-to-all-start = ((bf16[8,128,128]{2,1,0:T(8,128)(2,1)}), bf16[8,128,128]{2,1,0:T(8,128)(2,1)S(1)}, u32[]{:S(2)}, u32[]{:S(2)}) async-start(bf16[8,128,128]{2,1,0:T(8,128)(2,1)} %bitcast.11), calls=%async_computation | async-start | bytes 524288 | tf_op jit(solution)/shard_map/all_to_all | solution.py:112
  24.0 121.7 %all-gather.2.cloned.1.call-start = ((), (), s32[]{:S(2)}) async-start(), calls=%async_computation.2 | async-start | bytes 2359296 | tf_op jit(solution)/shard_map/all_gather | solution.py:114
  24.0 51.2 %collective-permute-start.7 = (bf16[8,128,128]{2,1,0:T(8,128)(2,1)}, bf16[8,128,128]{2,1,0:T(8,128)(2,1)S(1)}, u32[]{:S(2)}, u32[]{:S(2)}) collective-permute-start(bf16[8,128,128]{2,1,0:T(8,128)(2,1)} %bitcast.12), channel_id=1, source_target_pairs={{0,8},{1,25},{8,16},{9,1},{16,24},{17,9},{24,0},{25,17},{2,10},{3,... | collective-permute-start | bytes 786440 | tf_op jit(solution)/shard_map/ppermute | solution.py:108
  35.2 40.0 %collective-permute-start.6 = (bf16[8,128,128]{2,1,0:T(8,128)(2,1)}, bf16[8,128,128]{2,1,0:T(8,128)(2,1)S(1)}, u32[]{:S(2)}, u32[]{:S(2)}) collective-permute-start(bf16[8,128,128]{2,1,0:T(8,128)(2,1)} %bitcast.13), channel_id=1, source_target_pairs={{0,24},{1,9},{8,0},{9,17},{16,8},{17,25},{24,16},{25,1},{2,26},{3,... | collective-permute-start | bytes 786440 | tf_op jit(solution)/shard_map/ppermute | solution.py:108
  38.0 0.7 copy-start.2
  39.8 10.5 %collective-permute-start.2 = (bf16[8,128,128]{2,1,0:T(8,128)(2,1)}, bf16[8,128,128]{2,1,0:T(8,128)(2,1)}, u32[]{:S(2)}, u32[]{:S(2)}) collective-permute-start(bf16[8,128,128]{2,1,0:T(8,128)(2,1)} %param.1), channel_id=1, source_target_pairs={{0,32},{32,64},{64,96},{96,0},{1,33},{33,65},{65,97},{97,1},{2,34}... | collective-permute-start | bytes 786440 | tf_op jit(solution)/shard_map/cond/branch_1_fun/ppermute | solution.py:93
  42.1 14.5 %collective-permute-start.1 = (bf16[8,128,128]{2,1,0:T(8,128)(2,1)}, bf16[8,128,128]{2,1,0:T(8,128)(2,1)}, u32[]{:S(2)}, u32[]{:S(2)}) collective-permute-start(bf16[8,128,128]{2,1,0:T(8,128)(2,1)} %param.1), channel_id=1, source_target_pairs={{0,64},{32,96},{64,0},{96,32},{1,65},{33,97},{65,1},{97,33},{2,66}... | collective-permute-start | bytes 786440 | tf_op jit(solution)/shard_map/cond/branch_1_fun/ppermute | solution.py:93
  46.4 12.1 %collective-permute-start = (bf16[8,128,128]{2,1,0:T(8,128)(2,1)}, bf16[8,128,128]{2,1,0:T(8,128)(2,1)}, u32[]{:S(2)}, u32[]{:S(2)}) collective-permute-start(bf16[8,128,128]{2,1,0:T(8,128)(2,1)} %param.1), channel_id=1, source_target_pairs={{0,96},{32,0},{64,32},{96,64},{1,97},{33,1},{65,33},{97,65},{2,98}... | collective-permute-start | bytes 786440 | tf_op jit(solution)/shard_map/cond/branch_1_fun/ppermute | solution.py:93
  75.2 44.9 %collective-permute-start.8 = (bf16[8,128,128]{2,1,0:T(8,128)(2,1)S(1)}, bf16[8,128,128]{2,1,0:T(8,128)(2,1)S(1)}, u32[]{:S(2)}, u32[]{:S(2)}) collective-permute-start(bf16[8,128,128]{2,1,0:T(8,128)(2,1)S(1)} %collective-permute-done.6), channel_id=1, source_target_pairs={{0,24},{1,9},{8,0},{9,17},{16,8},{17,25},{24,16},{25,1},{2,26},{3,... | collective-permute-start | bytes 786440 | tf_op jit(solution)/shard_map/ppermute | solution.py:108
  93.0 37.9 %copy-start.3 = (s32[1,1,1,16,16,2]{4,5,3,2,1,0:T(2,128)S(1)}, s32[1,1,1,16,16,2]{4,5,3,2,1,0:T(2,128)}, u32[]{:S(2)}) copy-start(s32[1,1,1,16,16,2]{4,5,3,2,1,0:T(2,128)} %param.9) | copy-start | bytes 6148
  93.0 38.2 %copy-start.4 = (s32[4]{0:T(128)S(1)}, s32[4]{0:T(128)}, u32[]{:S(2)}) copy-start(s32[4]{0:T(128)} %shard_map.37) | copy-start | bytes 52
  93.0 52.7 %copy-start.1 = (bf16[1,1,1,8,1,128,128]{6,5,4,3,2,1,0:T(8,128)(2,1)S(1)}, bf16[1,1,1,8,1,128,128]{6,5,4,3,2,1,0:T(8,128)(2,1)}, u32[]{:S(2)}) copy-start(bf16[1,1,1,8,1,128,128]{6,5,4,3,2,1,0:T(8,128)(2,1)} %param.7) | copy-start | bytes 786436
  93.1 15.6 %collective-permute-start.5 = (bf16[16,128,128]{2,1,0:T(8,128)(2,1)S(1)}, bf16[16,128,128]{2,1,0:T(8,128)(2,1)}, u32[]{:S(2)}, u32[]{:S(2)}) collective-permute-start(bf16[16,128,128]{2,1,0:T(8,128)(2,1)S(1)} %param.3), channel_id=1, source_target_pairs={{0,32},{32,64},{64,96},{96,0},{1,33},{33,65},{65,97},{97,1},{2,34}... | collective-permute-start | bytes 1572872 | tf_op jit(solution)/shard_map/cond/branch_1_fun/ppermute | solution.py:93
  96.0 22.2 %collective-permute-start.4 = (bf16[16,128,128]{2,1,0:T(8,128)(2,1)S(1)}, bf16[16,128,128]{2,1,0:T(8,128)(2,1)}, u32[]{:S(2)}, u32[]{:S(2)}) collective-permute-start(bf16[16,128,128]{2,1,0:T(8,128)(2,1)S(1)} %param.3), channel_id=1, source_target_pairs={{0,64},{32,96},{64,0},{96,32},{1,65},{33,97},{65,1},{97,33},{2,66}... | collective-permute-start | bytes 1572872 | tf_op jit(solution)/shard_map/cond/branch_1_fun/ppermute | solution.py:93
  100.3 19.8 %collective-permute-start.3 = (bf16[16,128,128]{2,1,0:T(8,128)(2,1)S(1)}, bf16[16,128,128]{2,1,0:T(8,128)(2,1)}, u32[]{:S(2)}, u32[]{:S(2)}) collective-permute-start(bf16[16,128,128]{2,1,0:T(8,128)(2,1)S(1)} %param.3), channel_id=1, source_target_pairs={{0,96},{32,0},{64,32},{96,64},{1,97},{33,1},{65,33},{97,65},{2,98}... | collective-permute-start | bytes 1572872 | tf_op jit(solution)/shard_map/cond/branch_1_fun/ppermute | solution.py:93
  120.1 11.4 %collective-permute-start.11 = (bf16[8,128,128]{2,1,0:T(8,128)(2,1)S(1)}, bf16[8,128,128]{2,1,0:T(8,128)(2,1)S(1)}, u32[]{:S(2)}, u32[]{:S(2)}) collective-permute-start(bf16[8,128,128]{2,1,0:T(8,128)(2,1)S(1)} %collective-permute-done.8.refs_8_), channel_id=1, source_target_pairs={{0,32},{32,64},{64,96},{96,0},{1,33},{33,65},{65,97},{97,1},{2,34}... | collective-permute-start | bytes 786440 | tf_op jit(solution)/shard_map/ppermute | solution.py:93
  124.3 13.1 %collective-permute-start.10 = (bf16[8,128,128]{2,1,0:T(8,128)(2,1)S(1)}, bf16[8,128,128]{2,1,0:T(8,128)(2,1)S(1)}, u32[]{:S(2)}, u32[]{:S(2)}) collective-permute-start(bf16[8,128,128]{2,1,0:T(8,128)(2,1)S(1)} %collective-permute-done.8.refs_8_), channel_id=1, source_target_pairs={{0,64},{32,96},{64,0},{96,32},{1,65},{33,97},{65,1},{97,33},{2,66}... | collective-permute-start | bytes 786440 | tf_op jit(solution)/shard_map/ppermute | solution.py:93
  127.5 11.9 %collective-permute-start.9 = (bf16[8,128,128]{2,1,0:T(8,128)(2,1)S(1)}, bf16[8,128,128]{2,1,0:T(8,128)(2,1)S(1)}, u32[]{:S(2)}, u32[]{:S(2)}) collective-permute-start(bf16[8,128,128]{2,1,0:T(8,128)(2,1)S(1)} %collective-permute-done.8.refs_8_), channel_id=1, source_target_pairs={{0,96},{32,0},{64,32},{96,64},{1,97},{33,1},{65,33},{97,65},{2,98}... | collective-permute-start | bytes 786440 | tf_op jit(solution)/shard_map/ppermute | solution.py:93
  145.7 1.6 copy-start
  151.5 7.7 %collective-permute-start.12 = (f32[8,128,128]{2,1,0:T(8,128)S(1)}, f32[8,128,128]{2,1,0:T(8,128)S(1)}, u32[]{:S(2)}, u32[]{:S(2)}) collective-permute-start(f32[8,128,128]{2,1,0:T(8,128)S(1)} %shard_map.39), channel_id=1, source_target_pairs={{0,1},{1,0},{2,3},{3,2},{4,5},{5,4},{6,7},{7,6},{8,9},{9,8},{10,11... | collective-permute-start | bytes 1572872 | tf_op jit(solution)/shard_map/ppermute | solution.py:130
Sparse Core Ops, SparseCore 0:
  38.9 106.8 all-gather.1

commit v14 on v13

--- a/solution.py
+++ b/solution.py
@@ -12,7 +12,7 @@
 S, SLOTS, R, BS = 8, 2, 16, 128
 COLS = X * ZH
 PER = R // (Y * CORE)
-WEIGHT = 31 * 10**9
+WEIGHT = 326 * 10**8
 
 
 def ring(n, k):
@@ -112,12 +112,13 @@
     routed = lax.all_to_all(own, ("y", "core"), split_axis=0, concat_axis=0, tiled=True)
     own_x = fenced(over_x, own)
     b = lax.all_gather(routed, "row", axis=0, tiled=True)
-    n1, n2, own_x, routed = together(n1, n2, own_x, routed)
+    n1, own_x, _ = together(n1, own_x, routed)
 
     opposite = along_z(n1, 1)
+    place, _ = passing(place, WEIGHT, n1)
+    n2, place = together(n2, place)
     both = jnp.concatenate([n1, n2])
     near = fenced(over_x, both)
-    place, _ = passing(place, WEIGHT, n1, n2)
     opposite, near, place = together(opposite, near, place)
     far = over_x(opposite)
 

time: 181 us -> 182 us (level)
  starting transfers between devices: 82.2 us -> 105 us
  waiting for transfers between devices: 56.4 us -> 34.4 us
    ppermute x3, starting transfers between devices: 30.5 us -> 56.4 us  [along_z(): lax.ppermute(value, ('zh', 'core'), [(z * CORE + k, to * CORE + k) for to...]
    ppermute x3, waiting for transfers between devices: 16.1 us -> 0.01 us  [along_z(): lax.ppermute(value, ('zh', 'core'), [(z * CORE + k, to * CORE + k) for to...]
    ppermute x9, starting transfers between devices: 30.7 us -> 27.1 us  [over_x(): two, one, three = (lax.ppermute(value, 'x', ring(X, -d)) for d in (2, 1, 3))]
    ppermute x9, waiting for transfers between devices: 33.9 us -> 30.7 us  [over_x(): two, one, three = (lax.ppermute(value, 'x', ring(X, -d)) for d in (2, 1, 3))]
    all_gather x1, waiting for transfers between devices: 6.31 us -> 3.67 us  [on_device(): b = lax.all_gather(routed, 'row', axis=0, tiled=True)]
  transfers between devices with their start and end apart: 15 -> 15, of which waited for: 11 -> 8; matrix products, arithmetic and copies ran while one was open for 1% -> 1% of each run, Pallas kernels for 3% -> 3%
where the time goes in v14:
time: 182 us; the launch traced here: 181 us
  starting transfers between devices  105 us (58%)
  waiting for transfers between devices  34.4 us (19%)
  blocking collectives  13.7 us (8%)
  between operations  13.6 us (7%)
  Pallas kernels  9.55 us (5%)
  local copies, waits for them, and re-layouts  3.69 us (2%)
    ppermute x3, starting transfers between devices, along_z(): lax.ppermute(value, ('zh', 'core'), [(z * CORE + k, to * CORE + k) for to...  56.4 us
    ppermute x9, waiting for transfers between devices, over_x(): two, one, three = (lax.ppermute(value, 'x', ring(X, -d)) for d in (2, 1, 3))  30.7 us
    ppermute x9, starting transfers between devices, over_x(): two, one, three = (lax.ppermute(value, 'x', ring(X, -d)) for d in (2, 1, 3))  27.1 us
    all_to_all x1, starting transfers between devices, on_device(): lax.all_to_all(own, ('y', 'core'), split_axis=0, concat_axis=0, tiled=True)  17.5 us
    all_to_all x1, blocking collectives, on_device(): parts = lax.all_to_all(parts, 'y', split_axis=0, concat_axis=0, tiled=True)  13.7 us
    pallas_call x2, Pallas kernels, call(): pl.pallas_call(functools.partial(products, groups, other), out_shape=jax....  8.37 us
    ppermute x1, starting transfers between devices, on_device(): got = lax.ppermute(send, 'core', ring(CORE, 1))  3.82 us
    all_gather x1, waiting for transfers between devices, on_device(): b = lax.all_gather(routed, 'row', axis=0, tiled=True)  3.67 us
  transfers between devices with their start and end apart: 15, of which 8 were waited for; matrix products, arithmetic and copies ran while one was open for 1% of the time, Pallas kernels for 3%

profile of v14, /device:TPU:1, one launch (start us, length us, event | category | flops | bytes accessed | tf_op | source)
XLA Modules:
  0.0 181.1 jit_solution(17523298672421686908)
XLA Ops:
  6.5 17.5 %all-to-all-start = ((bf16[8,128,128]{2,1,0:T(8,128)(2,1)}), bf16[8,128,128]{2,1,0:T(8,128)(2,1)S(1)}, u32[]{:S(2)}, u32[]{:S(2)}) async-start(bf16[8,128,128]{2,1,0:T(8,128)(2,1)} %bitcast.11), calls=%async_computation | async-start | bytes 524288 | tf_op jit(solution)/shard_map/all_to_all | solution.py:112
  24.0 0.0 all-gather.2.cloned.1.call-start
  24.0 3.9 %collective-permute-start.6 = (bf16[8,128,128]{2,1,0:T(8,128)(2,1)}, bf16[8,128,128]{2,1,0:T(8,128)(2,1)S(1)}, u32[]{:S(2)}, u32[]{:S(2)}) collective-permute-start(bf16[8,128,128]{2,1,0:T(8,128)(2,1)} %bitcast.12), channel_id=1, source_target_pairs={{0,24},{1,9},{8,0},{9,17},{16,8},{17,25},{24,16},{25,1},{2,26},{3,... | collective-permute-start | bytes 786440 | tf_op jit(solution)/shard_map/ppermute | solution.py:108
  27.9 10.1 %collective-permute-start.8 = (bf16[8,128,128]{2,1,0:T(8,128)(2,1)}, bf16[8,128,128]{2,1,0:T(8,128)(2,1)S(1)}, u32[]{:S(2)}, u32[]{:S(2)}) collective-permute-start(bf16[8,128,128]{2,1,0:T(8,128)(2,1)} %bitcast.13), channel_id=1, source_target_pairs={{0,8},{1,25},{8,16},{9,1},{16,24},{17,9},{24,0},{25,17},{2,10},{3,... | collective-permute-start | bytes 786440 | tf_op jit(solution)/shard_map/ppermute | solution.py:108
  38.0 0.0 all-to-all-done
  38.0 0.0 copy-start.2
  38.0 0.7 copy-done.2
  38.7 0.0 all-gather.2.cloned.1.call-update
  38.7 0.6 pad_add_fusion.place_ref
  39.3 0.9 copy.6
  40.2 0.1 reshape.15
  40.4 18.8 %conditional.2 = (bf16[8,128,128]{2,1,0:T(8,128)(2,1)}, bf16[8,128,128]{2,1,0:T(8,128)(2,1)}, bf16[8,128,128]{2,1,0:T(8,128)(2,1)}) conditional(s32[]{:T(128)} %convert_element_type.4, () %tuple.25, bf16[8,128,128]{2,1,0:T(8,128)(2,1)} %bitcast.14), branch_computations={%region_0.0_spmd, %region_1.0_spmd} | conditional | bytes 3145872 | solution.py:100
  40.4 2.3 %collective-permute-start.2 = (bf16[8,128,128]{2,1,0:T(8,128)(2,1)}, bf16[8,128,128]{2,1,0:T(8,128)(2,1)}, u32[]{:S(2)}, u32[]{:S(2)}) collective-permute-start(bf16[8,128,128]{2,1,0:T(8,128)(2,1)} %param.1), channel_id=1, source_target_pairs={{0,32},{32,64},{64,96},{96,0},{1,33},{33,65},{65,97},{97,1},{2,34}... | collective-permute-start | bytes 786440 | tf_op jit(solution)/shard_map/cond/branch_1_fun/ppermute | solution.py:93
  42.6 4.4 %collective-permute-start.1 = (bf16[8,128,128]{2,1,0:T(8,128)(2,1)}, bf16[8,128,128]{2,1,0:T(8,128)(2,1)}, u32[]{:S(2)}, u32[]{:S(2)}) collective-permute-start(bf16[8,128,128]{2,1,0:T(8,128)(2,1)} %param.1), channel_id=1, source_target_pairs={{0,64},{32,96},{64,0},{96,32},{1,65},{33,97},{65,1},{97,33},{2,66}... | collective-permute-start | bytes 786440 | tf_op jit(solution)/shard_map/cond/branch_1_fun/ppermute | solution.py:93
  47.0 3.1 %collective-permute-start = (bf16[8,128,128]{2,1,0:T(8,128)(2,1)}, bf16[8,128,128]{2,1,0:T(8,128)(2,1)}, u32[]{:S(2)}, u32[]{:S(2)}) collective-permute-start(bf16[8,128,128]{2,1,0:T(8,128)(2,1)} %param.1), channel_id=1, source_target_pairs={{0,96},{32,0},{64,32},{96,64},{1,97},{33,1},{65,33},{97,65},{2,98}... | collective-permute-start | bytes 786440 | tf_op jit(solution)/shard_map/cond/branch_1_fun/ppermute | solution.py:93
  50.1 0.8 collective-permute-done.2
  50.9 6.2 %collective-permute-done.1 = bf16[8,128,128]{2,1,0:T(8,128)(2,1)} collective-permute-done((bf16[8,128,128]{2,1,0:T(8,128)(2,1)}, bf16[8,128,128]{2,1,0:T(8,128)(2,1)}, u32[]{:S(2)}, u32[]{:S(2)}) %collective-permute-start.1) | collective-permute-done | bytes 262176 | tf_op jit(solution)/shard_map/cond/branch_1_fun/ppermute | solution.py:93
  57.1 2.0 %collective-permute-done = bf16[8,128,128]{2,1,0:T(8,128)(2,1)} collective-permute-done((bf16[8,128,128]{2,1,0:T(8,128)(2,1)}, bf16[8,128,128]{2,1,0:T(8,128)(2,1)}, u32[]{:S(2)}, u32[]{:S(2)}) %collective-permute-start) | collective-permute-done | bytes 262176 | tf_op jit(solution)/shard_map/cond/branch_1_fun/ppermute | solution.py:93
  59.1 0.0 collective-permute-done.6
  59.1 42.5 %collective-permute-start.7 = (bf16[8,128,128]{2,1,0:T(8,128)(2,1)S(1)}, bf16[8,128,128]{2,1,0:T(8,128)(2,1)S(1)}, u32[]{:S(2)}, u32[]{:S(2)}) collective-permute-start(bf16[8,128,128]{2,1,0:T(8,128)(2,1)S(1)} %collective-permute-done.6), channel_id=1, source_target_pairs={{0,24},{1,9},{8,0},{9,17},{16,8},{17,25},{24,16},{25,1},{2,26},{3,... | collective-permute-start | bytes 786440 | tf_op jit(solution)/shard_map/ppermute | solution.py:108
  101.6 1.2 shard_map.37
  102.8 0.0 copy-start.3
  102.8 0.0 copy-start.4
  102.8 0.0 copy-start.1
  102.8 0.0 collective-permute-done.8
  102.9 22.6 %conditional.3 = (bf16[16,128,128]{2,1,0:T(8,128)(2,1)}, bf16[16,128,128]{2,1,0:T(8,128)(2,1)}, bf16[16,128,128]{2,1,0:T(8,128)(2,1)}) conditional(s32[]{:T(128)} %convert_element_type.4, () %tuple.27, bf16[16,128,128]{2,1,0:T(8,128)(2,1)S(1)} %constant_dynamic-update-slice_fusion.refs_4_), branch_computations={%region_2.0_spmd, %region_3.0_spmd} | conditional | bytes 6291600 | solution.py:100
  102.9 1.9 %collective-permute-start.5 = (bf16[16,128,128]{2,1,0:T(8,128)(2,1)S(1)}, bf16[16,128,128]{2,1,0:T(8,128)(2,1)}, u32[]{:S(2)}, u32[]{:S(2)}) collective-permute-start(bf16[16,128,128]{2,1,0:T(8,128)(2,1)S(1)} %param.3), channel_id=1, source_target_pairs={{0,32},{32,64},{64,96},{96,0},{1,33},{33,65},{65,97},{97,1},{2,34}... | collective-permute-start | bytes 1572872 | tf_op jit(solution)/shard_map/cond/branch_1_fun/ppermute | solution.py:93
  104.8 1.9 %collective-permute-start.4 = (bf16[16,128,128]{2,1,0:T(8,128)(2,1)S(1)}, bf16[16,128,128]{2,1,0:T(8,128)(2,1)}, u32[]{:S(2)}, u32[]{:S(2)}) collective-permute-start(bf16[16,128,128]{2,1,0:T(8,128)(2,1)S(1)} %param.3), channel_id=1, source_target_pairs={{0,64},{32,96},{64,0},{96,32},{1,65},{33,97},{65,1},{97,33},{2,66}... | collective-permute-start | bytes 1572872 | tf_op jit(solution)/shard_map/cond/branch_1_fun/ppermute | solution.py:93
  106.8 4.6 %collective-permute-start.3 = (bf16[16,128,128]{2,1,0:T(8,128)(2,1)S(1)}, bf16[16,128,128]{2,1,0:T(8,128)(2,1)}, u32[]{:S(2)}, u32[]{:S(2)}) collective-permute-start(bf16[16,128,128]{2,1,0:T(8,128)(2,1)S(1)} %param.3), channel_id=1, source_target_pairs={{0,96},{32,0},{64,32},{96,64},{1,97},{33,1},{65,33},{97,65},{2,98}... | collective-permute-start | bytes 1572872 | tf_op jit(solution)/shard_map/cond/branch_1_fun/ppermute | solution.py:93
  111.3 14.2 %collective-permute-done.5 = bf16[16,128,128]{2,1,0:T(8,128)(2,1)} collective-permute-done((bf16[16,128,128]{2,1,0:T(8,128)(2,1)S(1)}, bf16[16,128,128]{2,1,0:T(8,128)(2,1)}, u32[]{:S(2)}, u32[]{:S(2)}) %collective-permute-start.5) | collective-permute-done | bytes 524320 | tf_op jit(solution)/shard_map/cond/branch_1_fun/ppermute | solution.py:93
  125.5 0.0 collective-permute-done.4
  125.5 0.0 collective-permute-done.3
  125.5 0.0 collective-permute-done.7.refs_8_
  125.5 2.4 %collective-permute-start.11 = (bf16[8,128,128]{2,1,0:T(8,128)(2,1)S(1)}, bf16[8,128,128]{2,1,0:T(8,128)(2,1)S(1)}, u32[]{:S(2)}, u32[]{:S(2)}) collective-permute-start(bf16[8,128,128]{2,1,0:T(8,128)(2,1)S(1)} %collective-permute-done.7.refs_8_), channel_id=1, source_target_pairs={{0,32},{32,64},{64,96},{96,0},{1,33},{33,65},{65,97},{97,1},{2,34}... | collective-permute-start | bytes 786440 | tf_op jit(solution)/shard_map/ppermute | solution.py:93
  127.9 4.5 %collective-permute-start.10 = (bf16[8,128,128]{2,1,0:T(8,128)(2,1)S(1)}, bf16[8,128,128]{2,1,0:T(8,128)(2,1)S(1)}, u32[]{:S(2)}, u32[]{:S(2)}) collective-permute-start(bf16[8,128,128]{2,1,0:T(8,128)(2,1)S(1)} %collective-permute-done.7.refs_8_), channel_id=1, source_target_pairs={{0,64},{32,96},{64,0},{96,32},{1,65},{33,97},{65,1},{97,33},{2,66}... | collective-permute-start | bytes 786440 | tf_op jit(solution)/shard_map/ppermute | solution.py:93
  132.4 2.1 %collective-permute-start.9 = (bf16[8,128,128]{2,1,0:T(8,128)(2,1)S(1)}, bf16[8,128,128]{2,1,0:T(8,128)(2,1)S(1)}, u32[]{:S(2)}, u32[]{:S(2)}) collective-permute-start(bf16[8,128,128]{2,1,0:T(8,128)(2,1)S(1)} %collective-permute-done.7.refs_8_), channel_id=1, source_target_pairs={{0,96},{32,0},{64,32},{96,64},{1,97},{33,1},{65,33},{97,65},{2,98}... | collective-permute-start | bytes 786440 | tf_op jit(solution)/shard_map/ppermute | solution.py:93
  134.5 0.0 copy-done.3
  134.5 0.2 copy.7
  134.7 0.1 reshape.16
  134.8 0.0 copy-done.4
  134.9 2.1 %collective-permute-done.11.refs_11_ = bf16[8,128,128]{2,1,0:T(8,128)(2,1)S(1)} collective-permute-done((bf16[8,128,128]{2,1,0:T(8,128)(2,1)S(1)}, bf16[8,128,128]{2,1,0:T(8,128)(2,1)S(1)}, u32[]{:S(2)}, u32[]{:S(2)}) %collective-permute-start.11) | collective-permute-done | bytes 262176 | tf_op jit(solution)/shard_map/ppermute | solution.py:93
  136.9 2.8 %collective-permute-done.10.refs_10_ = bf16[8,128,128]{2,1,0:T(8,128)(2,1)S(1)} collective-permute-done((bf16[8,128,128]{2,1,0:T(8,128)(2,1)S(1)}, bf16[8,128,128]{2,1,0:T(8,128)(2,1)S(1)}, u32[]{:S(2)}, u32[]{:S(2)}) %collective-permute-start.10) | collective-permute-done | bytes 262176 | tf_op jit(solution)/shard_map/ppermute | solution.py:93
  139.8 2.6 %collective-permute-done.9.refs_9_ = bf16[8,128,128]{2,1,0:T(8,128)(2,1)S(1)} collective-permute-done((bf16[8,128,128]{2,1,0:T(8,128)(2,1)S(1)}, bf16[8,128,128]{2,1,0:T(8,128)(2,1)S(1)}, u32[]{:S(2)}, u32[]{:S(2)}) %collective-permute-start.9) | collective-permute-done | bytes 262176 | tf_op jit(solution)/shard_map/ppermute | solution.py:93
  142.4 3.7 %all-gather.2.cloned.1.call-done.refs_12_ = bf16[64,128,128]{2,1,0:T(8,128)(2,1)} async-done(((bf16[8,128,128]{2,1,0:T(8,128)(2,1)}), bf16[64,128,128]{2,1,0:T(8,128)(2,1)}) %all-gather.2.cloned.1.call-update) | async-done | bytes 2097168 | tf_op jit(solution)/shard_map/all_gather | solution.py:114
  146.0 0.0 copy-done.1
  146.0 0.0 copy-start
  146.0 1.6 copy-done
  147.6 4.1 %shard_map.39 = f32[8,128,128]{2,1,0:T(8,128)S(1)} custom-call(s32[1028]{0:T(1024)S(1)} %constant_dynamic-update-slice_fusion.3.lists, bf16[8,128,128]{2,1,0:T(8,128)(2,1)S(1)} %bitcast.15, bf16[8,128,128]{2,1,0:T(8,128)(2,1)} %get-tuple-element.36.refs_1_, bf16[8,128,128]{2,1,0:T(8,128)(2,1)} %get-tuple-element.37.refs_2_, ...), custom_call_target="tpu_custom_call" | custom-call | flops 1073741824 | bytes 8388608 | tf_op jit(solution)/shard_map/pallas_call | solution.py:58
  151.8 3.8 %collective-permute-start.12 = (f32[8,128,128]{2,1,0:T(8,128)S(1)}, f32[8,128,128]{2,1,0:T(8,128)S(1)}, u32[]{:S(2)}, u32[]{:S(2)}) collective-permute-start(f32[8,128,128]{2,1,0:T(8,128)S(1)} %shard_map.39), channel_id=1, source_target_pairs={{0,1},{1,0},{2,3},{3,2},{4,5},{5,4},{6,7},{7,6},{8,9},{9,8},{10,11... | collective-permute-start | bytes 1572872 | tf_op jit(solution)/shard_map/ppermute | solution.py:131
  155.6 4.2 %shard_map.38 = f32[8,128,128]{2,1,0:T(8,128)S(1)} custom-call(s32[1028]{0:T(1024)S(1)} %constant_dynamic-update-slice_fusion.3.lists, bf16[8,128,128]{2,1,0:T(8,128)(2,1)S(1)} %bitcast.16, bf16[8,128,128]{2,1,0:T(8,128)(2,1)} %get-tuple-element.36.refs_1_, bf16[8,128,128]{2,1,0:T(8,128)(2,1)} %get-tuple-element.37.refs_2_, ...), custom_call_target="tpu_custom_call" | custom-call | flops 1073741824 | bytes 8388608 | tf_op jit(solution)/shard_map/pallas_call | solution.py:58
  159.8 0.0 collective-permute-done.12
  159.8 0.1 add.3
  159.9 13.7 %all_to_all.10 = f32[4,2,128,128]{3,2,1,0:T(8,128)S(1)} all-to-all(f32[4,2,128,128]{3,2,1,0:T(8,128)S(1)} %bitcast.17), channel_id=1, replica_groups=mesh['row'=8,'x'=4,'zh'=4,'y'=4,'core'=2] {'y'}, dimensions={0} | all-to-all | bytes 1048576 | tf_op jit(solution)/shard_map/all_to_all | solution.py:135
  173.6 0.7 reduce_sum.9
  (6 shorter events, 0.1 us)
Async XLA Ops:
  6.5 31.5 %all-to-all-start = ((bf16[8,128,128]{2,1,0:T(8,128)(2,1)}), bf16[8,128,128]{2,1,0:T(8,128)(2,1)S(1)}, u32[]{:S(2)}, u32[]{:S(2)}) async-start(bf16[8,128,128]{2,1,0:T(8,128)(2,1)} %bitcast.11), calls=%async_computation | async-start | bytes 524288 | tf_op jit(solution)/shard_map/all_to_all | solution.py:112
  24.0 122.0 %all-gather.2.cloned.1.call-start = ((), (), s32[]{:S(2)}) async-start(), calls=%async_computation.2 | async-start | bytes 2359296 | tf_op jit(solution)/shard_map/all_gather | solution.py:114
  24.0 35.1 %collective-permute-start.6 = (bf16[8,128,128]{2,1,0:T(8,128)(2,1)}, bf16[8,128,128]{2,1,0:T(8,128)(2,1)S(1)}, u32[]{:S(2)}, u32[]{:S(2)}) collective-permute-start(bf16[8,128,128]{2,1,0:T(8,128)(2,1)} %bitcast.12), channel_id=1, source_target_pairs={{0,24},{1,9},{8,0},{9,17},{16,8},{17,25},{24,16},{25,1},{2,26},{3,... | collective-permute-start | bytes 786440 | tf_op jit(solution)/shard_map/ppermute | solution.py:108
  27.9 74.9 %collective-permute-start.8 = (bf16[8,128,128]{2,1,0:T(8,128)(2,1)}, bf16[8,128,128]{2,1,0:T(8,128)(2,1)S(1)}, u32[]{:S(2)}, u32[]{:S(2)}) collective-permute-start(bf16[8,128,128]{2,1,0:T(8,128)(2,1)} %bitcast.13), channel_id=1, source_target_pairs={{0,8},{1,25},{8,16},{9,1},{16,24},{17,9},{24,0},{25,17},{2,10},{3,... | collective-permute-start | bytes 786440 | tf_op jit(solution)/shard_map/ppermute | solution.py:108
  38.0 0.7 copy-start.2
  40.4 10.5 %collective-permute-start.2 = (bf16[8,128,128]{2,1,0:T(8,128)(2,1)}, bf16[8,128,128]{2,1,0:T(8,128)(2,1)}, u32[]{:S(2)}, u32[]{:S(2)}) collective-permute-start(bf16[8,128,128]{2,1,0:T(8,128)(2,1)} %param.1), channel_id=1, source_target_pairs={{0,32},{32,64},{64,96},{96,0},{1,33},{33,65},{65,97},{97,1},{2,34}... | collective-permute-start | bytes 786440 | tf_op jit(solution)/shard_map/cond/branch_1_fun/ppermute | solution.py:93
  42.6 14.5 %collective-permute-start.1 = (bf16[8,128,128]{2,1,0:T(8,128)(2,1)}, bf16[8,128,128]{2,1,0:T(8,128)(2,1)}, u32[]{:S(2)}, u32[]{:S(2)}) collective-permute-start(bf16[8,128,128]{2,1,0:T(8,128)(2,1)} %param.1), channel_id=1, source_target_pairs={{0,64},{32,96},{64,0},{96,32},{1,65},{33,97},{65,1},{97,33},{2,66}... | collective-permute-start | bytes 786440 | tf_op jit(solution)/shard_map/cond/branch_1_fun/ppermute | solution.py:93
  47.0 12.1 %collective-permute-start = (bf16[8,128,128]{2,1,0:T(8,128)(2,1)}, bf16[8,128,128]{2,1,0:T(8,128)(2,1)}, u32[]{:S(2)}, u32[]{:S(2)}) collective-permute-start(bf16[8,128,128]{2,1,0:T(8,128)(2,1)} %param.1), channel_id=1, source_target_pairs={{0,96},{32,0},{64,32},{96,64},{1,97},{33,1},{65,33},{97,65},{2,98}... | collective-permute-start | bytes 786440 | tf_op jit(solution)/shard_map/cond/branch_1_fun/ppermute | solution.py:93
  59.1 66.4 %collective-permute-start.7 = (bf16[8,128,128]{2,1,0:T(8,128)(2,1)S(1)}, bf16[8,128,128]{2,1,0:T(8,128)(2,1)S(1)}, u32[]{:S(2)}, u32[]{:S(2)}) collective-permute-start(bf16[8,128,128]{2,1,0:T(8,128)(2,1)S(1)} %collective-permute-done.6), channel_id=1, source_target_pairs={{0,24},{1,9},{8,0},{9,17},{16,8},{17,25},{24,16},{25,1},{2,26},{3,... | collective-permute-start | bytes 786440 | tf_op jit(solution)/shard_map/ppermute | solution.py:108
  102.8 31.7 %copy-start.3 = (s32[1,1,1,16,16,2]{4,5,3,2,1,0:T(2,128)S(1)}, s32[1,1,1,16,16,2]{4,5,3,2,1,0:T(2,128)}, u32[]{:S(2)}) copy-start(s32[1,1,1,16,16,2]{4,5,3,2,1,0:T(2,128)} %param.9) | copy-start | bytes 6148
  102.8 32.1 %copy-start.4 = (s32[4]{0:T(128)S(1)}, s32[4]{0:T(128)}, u32[]{:S(2)}) copy-start(s32[4]{0:T(128)} %shard_map.37) | copy-start | bytes 52
  102.8 43.2 %copy-start.1 = (bf16[1,1,1,8,1,128,128]{6,5,4,3,2,1,0:T(8,128)(2,1)S(1)}, bf16[1,1,1,8,1,128,128]{6,5,4,3,2,1,0:T(8,128)(2,1)}, u32[]{:S(2)}) copy-start(bf16[1,1,1,8,1,128,128]{6,5,4,3,2,1,0:T(8,128)(2,1)} %param.7) | copy-start | bytes 786436
  102.9 22.6 %collective-permute-start.5 = (bf16[16,128,128]{2,1,0:T(8,128)(2,1)S(1)}, bf16[16,128,128]{2,1,0:T(8,128)(2,1)}, u32[]{:S(2)}, u32[]{:S(2)}) collective-permute-start(bf16[16,128,128]{2,1,0:T(8,128)(2,1)S(1)} %param.3), channel_id=1, source_target_pairs={{0,32},{32,64},{64,96},{96,0},{1,33},{33,65},{65,97},{97,1},{2,34}... | collective-permute-start | bytes 1572872 | tf_op jit(solution)/shard_map/cond/branch_1_fun/ppermute | solution.py:93
  104.8 20.7 %collective-permute-start.4 = (bf16[16,128,128]{2,1,0:T(8,128)(2,1)S(1)}, bf16[16,128,128]{2,1,0:T(8,128)(2,1)}, u32[]{:S(2)}, u32[]{:S(2)}) collective-permute-start(bf16[16,128,128]{2,1,0:T(8,128)(2,1)S(1)} %param.3), channel_id=1, source_target_pairs={{0,64},{32,96},{64,0},{96,32},{1,65},{33,97},{65,1},{97,33},{2,66}... | collective-permute-start | bytes 1572872 | tf_op jit(solution)/shard_map/cond/branch_1_fun/ppermute | solution.py:93
  106.8 18.8 %collective-permute-start.3 = (bf16[16,128,128]{2,1,0:T(8,128)(2,1)S(1)}, bf16[16,128,128]{2,1,0:T(8,128)(2,1)}, u32[]{:S(2)}, u32[]{:S(2)}) collective-permute-start(bf16[16,128,128]{2,1,0:T(8,128)(2,1)S(1)} %param.3), channel_id=1, source_target_pairs={{0,96},{32,0},{64,32},{96,64},{1,97},{33,1},{65,33},{97,65},{2,98}... | collective-permute-start | bytes 1572872 | tf_op jit(solution)/shard_map/cond/branch_1_fun/ppermute | solution.py:93
  125.5 11.4 %collective-permute-start.11 = (bf16[8,128,128]{2,1,0:T(8,128)(2,1)S(1)}, bf16[8,128,128]{2,1,0:T(8,128)(2,1)S(1)}, u32[]{:S(2)}, u32[]{:S(2)}) collective-permute-start(bf16[8,128,128]{2,1,0:T(8,128)(2,1)S(1)} %collective-permute-done.7.refs_8_), channel_id=1, source_target_pairs={{0,32},{32,64},{64,96},{96,0},{1,33},{33,65},{65,97},{97,1},{2,34}... | collective-permute-start | bytes 786440 | tf_op jit(solution)/shard_map/ppermute | solution.py:93
  127.9 11.9 %collective-permute-start.10 = (bf16[8,128,128]{2,1,0:T(8,128)(2,1)S(1)}, bf16[8,128,128]{2,1,0:T(8,128)(2,1)S(1)}, u32[]{:S(2)}, u32[]{:S(2)}) collective-permute-start(bf16[8,128,128]{2,1,0:T(8,128)(2,1)S(1)} %collective-permute-done.7.refs_8_), channel_id=1, source_target_pairs={{0,64},{32,96},{64,0},{96,32},{1,65},{33,97},{65,1},{97,33},{2,66}... | collective-permute-start | bytes 786440 | tf_op jit(solution)/shard_map/ppermute | solution.py:93
  132.4 10.0 %collective-permute-start.9 = (bf16[8,128,128]{2,1,0:T(8,128)(2,1)S(1)}, bf16[8,128,128]{2,1,0:T(8,128)(2,1)S(1)}, u32[]{:S(2)}, u32[]{:S(2)}) collective-permute-start(bf16[8,128,128]{2,1,0:T(8,128)(2,1)S(1)} %collective-permute-done.7.refs_8_), channel_id=1, source_target_pairs={{0,96},{32,0},{64,32},{96,64},{1,97},{33,1},{65,33},{97,65},{2,98}... | collective-permute-start | bytes 786440 | tf_op jit(solution)/shard_map/ppermute | solution.py:93
  146.0 1.6 copy-start
  151.8 8.1 %collective-permute-start.12 = (f32[8,128,128]{2,1,0:T(8,128)S(1)}, f32[8,128,128]{2,1,0:T(8,128)S(1)}, u32[]{:S(2)}, u32[]{:S(2)}) collective-permute-start(f32[8,128,128]{2,1,0:T(8,128)S(1)} %shard_map.39), channel_id=1, source_target_pairs={{0,1},{1,0},{2,3},{3,2},{4,5},{5,4},{6,7},{7,6},{8,9},{9,8},{10,11... | collective-permute-start | bytes 1572872 | tf_op jit(solution)/shard_map/ppermute | solution.py:131
Sparse Core Ops, SparseCore 0:
  38.9 107.1 all-gather.1

commit v15 on v14

--- a/solution.py
+++ b/solution.py
@@ -12,7 +12,7 @@
 S, SLOTS, R, BS = 8, 2, 16, 128
 COLS = X * ZH
 PER = R // (Y * CORE)
-WEIGHT = 326 * 10**8
+WEIGHT = 31 * 10**9
 
 
 def ring(n, k):

time: 182 us -> 183 us (level)
    ppermute x9, waiting for transfers between devices: 30.7 us -> 25.6 us  [over_x(): two, one, three = (lax.ppermute(value, 'x', ring(X, -d)) for d in (2, 1, 3))]
    ppermute x9, starting transfers between devices: 27.1 us -> 31.2 us  [over_x(): two, one, three = (lax.ppermute(value, 'x', ring(X, -d)) for d in (2, 1, 3))]
    ppermute x3, starting transfers between devices: 56.4 us -> 53.4 us  [along_z(): lax.ppermute(value, ('zh', 'core'), [(z * CORE + k, to * CORE + k) for to...]
    all_to_all x1, waiting for transfers between devices: 0.01 us -> 2.58 us  [on_device(): lax.all_to_all(own, ('y', 'core'), split_axis=0, concat_axis=0, tiled=True)]
    all_gather x1, waiting for transfers between devices: 3.67 us -> 5.61 us  [on_device(): b = lax.all_gather(routed, 'row', axis=0, tiled=True)]
  transfers between devices with their start and end apart: 15 -> 15, of which waited for: 8 -> 9; matrix products, arithmetic and copies ran while one was open for 1% -> 1% of each run, Pallas kernels for 3% -> 3%
where the time goes in v15:
time: 183 us; the launch traced here: 182 us
  starting transfers between devices  106 us (58%)
  waiting for transfers between devices  33.8 us (18%)
  blocking collectives  13.7 us (7%)
  between operations  13.6 us (7%)
  Pallas kernels  9.56 us (5%)
  local copies, waits for them, and re-layouts  3.7 us (2%)
    ppermute x3, starting transfers between devices, along_z(): lax.ppermute(value, ('zh', 'core'), [(z * CORE + k, to * CORE + k) for to...  53.4 us
    ppermute x9, starting transfers between devices, over_x(): two, one, three = (lax.ppermute(value, 'x', ring(X, -d)) for d in (2, 1, 3))  31.2 us
    ppermute x9, waiting for transfers between devices, over_x(): two, one, three = (lax.ppermute(value, 'x', ring(X, -d)) for d in (2, 1, 3))  25.6 us
    all_to_all x1, starting transfers between devices, on_device(): lax.all_to_all(own, ('y', 'core'), split_axis=0, concat_axis=0, tiled=True)  17.5 us
    all_to_all x1, blocking collectives, on_device(): parts = lax.all_to_all(parts, 'y', split_axis=0, concat_axis=0, tiled=True)  13.7 us
    pallas_call x2, Pallas kernels, call(): pl.pallas_call(functools.partial(products, groups, other), out_shape=jax....  8.37 us
    all_gather x1, waiting for transfers between devices, on_device(): b = lax.all_gather(routed, 'row', axis=0, tiled=True)  5.61 us
  transfers between devices with their start and end apart: 15, of which 9 were waited for; matrix products, arithmetic and copies ran while one was open for 1% of the time, Pallas kernels for 3%

profile of v15, /device:TPU:1, one launch (start us, length us, event | category | flops | bytes accessed | tf_op | source)
XLA Modules:
  0.0 181.6 jit_solution(6619964720865901252)
XLA Ops:
  6.5 17.5 %all-to-all-start = ((bf16[8,128,128]{2,1,0:T(8,128)(2,1)}), bf16[8,128,128]{2,1,0:T(8,128)(2,1)S(1)}, u32[]{:S(2)}, u32[]{:S(2)}) async-start(bf16[8,128,128]{2,1,0:T(8,128)(2,1)} %bitcast.11), calls=%async_computation | async-start | bytes 524288 | tf_op jit(solution)/shard_map/all_to_all | solution.py:112
  24.0 0.0 all-gather.2.cloned.1.call-start
  24.0 3.9 %collective-permute-start.6 = (bf16[8,128,128]{2,1,0:T(8,128)(2,1)}, bf16[8,128,128]{2,1,0:T(8,128)(2,1)S(1)}, u32[]{:S(2)}, u32[]{:S(2)}) collective-permute-start(bf16[8,128,128]{2,1,0:T(8,128)(2,1)} %bitcast.12), channel_id=1, source_target_pairs={{0,24},{1,9},{8,0},{9,17},{16,8},{17,25},{24,16},{25,1},{2,26},{3,... | collective-permute-start | bytes 786440 | tf_op jit(solution)/shard_map/ppermute | solution.py:108
  27.9 2.6 %all-to-all-done = bf16[8,128,128]{2,1,0:T(8,128)(2,1)S(1)} async-done(((bf16[8,128,128]{2,1,0:T(8,128)(2,1)}), bf16[8,128,128]{2,1,0:T(8,128)(2,1)S(1)}, u32[]{:S(2)}, u32[]{:S(2)}) %all-to-all-start) | async-done | bytes 262176 | tf_op jit(solution)/shard_map/all_to_all | solution.py:112
  30.5 0.0 copy-start.2
  30.5 0.7 copy-done.2
  31.2 0.0 all-gather.2.cloned.1.call-update
  31.2 11.2 %collective-permute-start.8 = (bf16[8,128,128]{2,1,0:T(8,128)(2,1)}, bf16[8,128,128]{2,1,0:T(8,128)(2,1)S(1)}, u32[]{:S(2)}, u32[]{:S(2)}) collective-permute-start(bf16[8,128,128]{2,1,0:T(8,128)(2,1)} %bitcast.13), channel_id=1, source_target_pairs={{0,8},{1,25},{8,16},{9,1},{16,24},{17,9},{24,0},{25,17},{2,10},{3,... | collective-permute-start | bytes 786440 | tf_op jit(solution)/shard_map/ppermute | solution.py:108
  42.5 0.9 copy.6
  43.4 0.1 reshape.15
  43.5 17.6 %conditional.2 = (bf16[8,128,128]{2,1,0:T(8,128)(2,1)}, bf16[8,128,128]{2,1,0:T(8,128)(2,1)}, bf16[8,128,128]{2,1,0:T(8,128)(2,1)}) conditional(s32[]{:T(128)} %convert_element_type.4, () %tuple.25, bf16[8,128,128]{2,1,0:T(8,128)(2,1)} %bitcast.14), branch_computations={%region_0.0_spmd, %region_1.0_spmd} | conditional | bytes 3145872 | solution.py:100
  43.5 3.1 %collective-permute-start.2 = (bf16[8,128,128]{2,1,0:T(8,128)(2,1)}, bf16[8,128,128]{2,1,0:T(8,128)(2,1)}, u32[]{:S(2)}, u32[]{:S(2)}) collective-permute-start(bf16[8,128,128]{2,1,0:T(8,128)(2,1)} %param.1), channel_id=1, source_target_pairs={{0,32},{32,64},{64,96},{96,0},{1,33},{33,65},{65,97},{97,1},{2,34}... | collective-permute-start | bytes 786440 | tf_op jit(solution)/shard_map/cond/branch_1_fun/ppermute | solution.py:93
  46.6 4.4 %collective-permute-start.1 = (bf16[8,128,128]{2,1,0:T(8,128)(2,1)}, bf16[8,128,128]{2,1,0:T(8,128)(2,1)}, u32[]{:S(2)}, u32[]{:S(2)}) collective-permute-start(bf16[8,128,128]{2,1,0:T(8,128)(2,1)} %param.1), channel_id=1, source_target_pairs={{0,64},{32,96},{64,0},{96,32},{1,65},{33,97},{65,1},{97,33},{2,66}... | collective-permute-start | bytes 786440 | tf_op jit(solution)/shard_map/cond/branch_1_fun/ppermute | solution.py:93
  51.0 3.1 %collective-permute-start = (bf16[8,128,128]{2,1,0:T(8,128)(2,1)}, bf16[8,128,128]{2,1,0:T(8,128)(2,1)}, u32[]{:S(2)}, u32[]{:S(2)}) collective-permute-start(bf16[8,128,128]{2,1,0:T(8,128)(2,1)} %param.1), channel_id=1, source_target_pairs={{0,96},{32,0},{64,32},{96,64},{1,97},{33,1},{65,33},{97,65},{2,98}... | collective-permute-start | bytes 786440 | tf_op jit(solution)/shard_map/cond/branch_1_fun/ppermute | solution.py:93
  54.1 4.2 %collective-permute-done.2 = bf16[8,128,128]{2,1,0:T(8,128)(2,1)} collective-permute-done((bf16[8,128,128]{2,1,0:T(8,128)(2,1)}, bf16[8,128,128]{2,1,0:T(8,128)(2,1)}, u32[]{:S(2)}, u32[]{:S(2)}) %collective-permute-start.2) | collective-permute-done | bytes 262176 | tf_op jit(solution)/shard_map/cond/branch_1_fun/ppermute | solution.py:93
  58.2 0.0 collective-permute-done.1
  58.2 2.9 %collective-permute-done = bf16[8,128,128]{2,1,0:T(8,128)(2,1)} collective-permute-done((bf16[8,128,128]{2,1,0:T(8,128)(2,1)}, bf16[8,128,128]{2,1,0:T(8,128)(2,1)}, u32[]{:S(2)}, u32[]{:S(2)}) %collective-permute-start) | collective-permute-done | bytes 262176 | tf_op jit(solution)/shard_map/cond/branch_1_fun/ppermute | solution.py:93
  61.1 0.6 pad_add_fusion.place_ref
  61.7 0.0 collective-permute-done.6
  61.7 38.3 %collective-permute-start.7 = (bf16[8,128,128]{2,1,0:T(8,128)(2,1)S(1)}, bf16[8,128,128]{2,1,0:T(8,128)(2,1)S(1)}, u32[]{:S(2)}, u32[]{:S(2)}) collective-permute-start(bf16[8,128,128]{2,1,0:T(8,128)(2,1)S(1)} %collective-permute-done.6), channel_id=1, source_target_pairs={{0,24},{1,9},{8,0},{9,17},{16,8},{17,25},{24,16},{25,1},{2,26},{3,... | collective-permute-start | bytes 786440 | tf_op jit(solution)/shard_map/ppermute | solution.py:108
  100.0 1.2 shard_map.37
  101.2 0.0 copy-start.3
  101.2 0.0 copy-start.4
  101.2 0.0 copy-start.1
  101.3 0.0 collective-permute-done.8
  101.3 22.9 %conditional.3 = (bf16[16,128,128]{2,1,0:T(8,128)(2,1)}, bf16[16,128,128]{2,1,0:T(8,128)(2,1)}, bf16[16,128,128]{2,1,0:T(8,128)(2,1)}) conditional(s32[]{:T(128)} %convert_element_type.4, () %tuple.27, bf16[16,128,128]{2,1,0:T(8,128)(2,1)S(1)} %constant_dynamic-update-slice_fusion.refs_4_), branch_computations={%region_2.0_spmd, %region_3.0_spmd} | conditional | bytes 6291600 | solution.py:100
  101.4 2.8 %collective-permute-start.5 = (bf16[16,128,128]{2,1,0:T(8,128)(2,1)S(1)}, bf16[16,128,128]{2,1,0:T(8,128)(2,1)}, u32[]{:S(2)}, u32[]{:S(2)}) collective-permute-start(bf16[16,128,128]{2,1,0:T(8,128)(2,1)S(1)} %param.3), channel_id=1, source_target_pairs={{0,32},{32,64},{64,96},{96,0},{1,33},{33,65},{65,97},{97,1},{2,34}... | collective-permute-start | bytes 1572872 | tf_op jit(solution)/shard_map/cond/branch_1_fun/ppermute | solution.py:93
  104.2 4.2 %collective-permute-start.4 = (bf16[16,128,128]{2,1,0:T(8,128)(2,1)S(1)}, bf16[16,128,128]{2,1,0:T(8,128)(2,1)}, u32[]{:S(2)}, u32[]{:S(2)}) collective-permute-start(bf16[16,128,128]{2,1,0:T(8,128)(2,1)S(1)} %param.3), channel_id=1, source_target_pairs={{0,64},{32,96},{64,0},{96,32},{1,65},{33,97},{65,1},{97,33},{2,66}... | collective-permute-start | bytes 1572872 | tf_op jit(solution)/shard_map/cond/branch_1_fun/ppermute | solution.py:93
  108.4 3.1 %collective-permute-start.3 = (bf16[16,128,128]{2,1,0:T(8,128)(2,1)S(1)}, bf16[16,128,128]{2,1,0:T(8,128)(2,1)}, u32[]{:S(2)}, u32[]{:S(2)}) collective-permute-start(bf16[16,128,128]{2,1,0:T(8,128)(2,1)S(1)} %param.3), channel_id=1, source_target_pairs={{0,96},{32,0},{64,32},{96,64},{1,97},{33,1},{65,33},{97,65},{2,98}... | collective-permute-start | bytes 1572872 | tf_op jit(solution)/shard_map/cond/branch_1_fun/ppermute | solution.py:93
  111.5 5.1 %collective-permute-done.5 = bf16[16,128,128]{2,1,0:T(8,128)(2,1)} collective-permute-done((bf16[16,128,128]{2,1,0:T(8,128)(2,1)S(1)}, bf16[16,128,128]{2,1,0:T(8,128)(2,1)}, u32[]{:S(2)}, u32[]{:S(2)}) %collective-permute-start.5) | collective-permute-done | bytes 524320 | tf_op jit(solution)/shard_map/cond/branch_1_fun/ppermute | solution.py:93
  116.6 5.6 %collective-permute-done.4 = bf16[16,128,128]{2,1,0:T(8,128)(2,1)} collective-permute-done((bf16[16,128,128]{2,1,0:T(8,128)(2,1)S(1)}, bf16[16,128,128]{2,1,0:T(8,128)(2,1)}, u32[]{:S(2)}, u32[]{:S(2)}) %collective-permute-start.4) | collective-permute-done | bytes 524320 | tf_op jit(solution)/shard_map/cond/branch_1_fun/ppermute | solution.py:93
  122.2 2.0 %collective-permute-done.3 = bf16[16,128,128]{2,1,0:T(8,128)(2,1)} collective-permute-done((bf16[16,128,128]{2,1,0:T(8,128)(2,1)S(1)}, bf16[16,128,128]{2,1,0:T(8,128)(2,1)}, u32[]{:S(2)}, u32[]{:S(2)}) %collective-permute-start.3) | collective-permute-done | bytes 524320 | tf_op jit(solution)/shard_map/cond/branch_1_fun/ppermute | solution.py:93
  124.2 0.0 collective-permute-done.7.refs_8_
  124.2 4.0 %collective-permute-start.11 = (bf16[8,128,128]{2,1,0:T(8,128)(2,1)S(1)}, bf16[8,128,128]{2,1,0:T(8,128)(2,1)S(1)}, u32[]{:S(2)}, u32[]{:S(2)}) collective-permute-start(bf16[8,128,128]{2,1,0:T(8,128)(2,1)S(1)} %collective-permute-done.7.refs_8_), channel_id=1, source_target_pairs={{0,32},{32,64},{64,96},{96,0},{1,33},{33,65},{65,97},{97,1},{2,34}... | collective-permute-start | bytes 786440 | tf_op jit(solution)/shard_map/ppermute | solution.py:93
  128.2 3.4 %collective-permute-start.10 = (bf16[8,128,128]{2,1,0:T(8,128)(2,1)S(1)}, bf16[8,128,128]{2,1,0:T(8,128)(2,1)S(1)}, u32[]{:S(2)}, u32[]{:S(2)}) collective-permute-start(bf16[8,128,128]{2,1,0:T(8,128)(2,1)S(1)} %collective-permute-done.7.refs_8_), channel_id=1, source_target_pairs={{0,64},{32,96},{64,0},{96,32},{1,65},{33,97},{65,1},{97,33},{2,66}... | collective-permute-start | bytes 786440 | tf_op jit(solution)/shard_map/ppermute | solution.py:93
  131.6 3.2 %collective-permute-start.9 = (bf16[8,128,128]{2,1,0:T(8,128)(2,1)S(1)}, bf16[8,128,128]{2,1,0:T(8,128)(2,1)S(1)}, u32[]{:S(2)}, u32[]{:S(2)}) collective-permute-start(bf16[8,128,128]{2,1,0:T(8,128)(2,1)S(1)} %collective-permute-done.7.refs_8_), channel_id=1, source_target_pairs={{0,96},{32,0},{64,32},{96,64},{1,97},{33,1},{65,33},{97,65},{2,98}... | collective-permute-start | bytes 786440 | tf_op jit(solution)/shard_map/ppermute | solution.py:93
  134.8 0.0 copy-done.3
  134.8 0.2 copy.7
  135.0 0.1 reshape.16
  135.1 0.0 copy-done.4
  135.1 0.0 collective-permute-done.11.refs_11_
  135.2 4.2 %collective-permute-done.10.refs_10_ = bf16[8,128,128]{2,1,0:T(8,128)(2,1)S(1)} collective-permute-done((bf16[8,128,128]{2,1,0:T(8,128)(2,1)S(1)}, bf16[8,128,128]{2,1,0:T(8,128)(2,1)S(1)}, u32[]{:S(2)}, u32[]{:S(2)}) %collective-permute-start.10) | collective-permute-done | bytes 262176 | tf_op jit(solution)/shard_map/ppermute | solution.py:93
  139.4 1.6 collective-permute-done.9.refs_9_
  141.0 5.6 %all-gather.2.cloned.1.call-done.refs_12_ = bf16[64,128,128]{2,1,0:T(8,128)(2,1)} async-done(((bf16[8,128,128]{2,1,0:T(8,128)(2,1)}), bf16[64,128,128]{2,1,0:T(8,128)(2,1)}) %all-gather.2.cloned.1.call-update) | async-done | bytes 2097168 | tf_op jit(solution)/shard_map/all_gather | solution.py:114
  146.7 0.0 copy-done.1
  146.7 0.0 copy-start
  146.7 1.6 copy-done
  148.2 4.1 %shard_map.39 = f32[8,128,128]{2,1,0:T(8,128)S(1)} custom-call(s32[1028]{0:T(1024)S(1)} %constant_dynamic-update-slice_fusion.3.lists, bf16[8,128,128]{2,1,0:T(8,128)(2,1)S(1)} %bitcast.15, bf16[8,128,128]{2,1,0:T(8,128)(2,1)} %get-tuple-element.36.refs_1_, bf16[8,128,128]{2,1,0:T(8,128)(2,1)} %get-tuple-element.37.refs_2_, ...), custom_call_target="tpu_custom_call" | custom-call | flops 1073741824 | bytes 8388608 | tf_op jit(solution)/shard_map/pallas_call | solution.py:58
  152.4 3.6 %collective-permute-start.12 = (f32[8,128,128]{2,1,0:T(8,128)S(1)}, f32[8,128,128]{2,1,0:T(8,128)S(1)}, u32[]{:S(2)}, u32[]{:S(2)}) collective-permute-start(f32[8,128,128]{2,1,0:T(8,128)S(1)} %shard_map.39), channel_id=1, source_target_pairs={{0,1},{1,0},{2,3},{3,2},{4,5},{5,4},{6,7},{7,6},{8,9},{9,8},{10,11... | collective-permute-start | bytes 1572872 | tf_op jit(solution)/shard_map/ppermute | solution.py:131
  156.0 4.2 %shard_map.38 = f32[8,128,128]{2,1,0:T(8,128)S(1)} custom-call(s32[1028]{0:T(1024)S(1)} %constant_dynamic-update-slice_fusion.3.lists, bf16[8,128,128]{2,1,0:T(8,128)(2,1)S(1)} %bitcast.16, bf16[8,128,128]{2,1,0:T(8,128)(2,1)} %get-tuple-element.36.refs_1_, bf16[8,128,128]{2,1,0:T(8,128)(2,1)} %get-tuple-element.37.refs_2_, ...), custom_call_target="tpu_custom_call" | custom-call | flops 1073741824 | bytes 8388608 | tf_op jit(solution)/shard_map/pallas_call | solution.py:58
  160.3 0.0 collective-permute-done.12
  160.3 0.1 add.3
  160.4 13.7 %all_to_all.10 = f32[4,2,128,128]{3,2,1,0:T(8,128)S(1)} all-to-all(f32[4,2,128,128]{3,2,1,0:T(8,128)S(1)} %bitcast.17), channel_id=1, replica_groups=mesh['row'=8,'x'=4,'zh'=4,'y'=4,'core'=2] {'y'}, dimensions={0} | all-to-all | bytes 1048576 | tf_op jit(solution)/shard_map/all_to_all | solution.py:135
  174.1 0.7 reduce_sum.9
  (6 shorter events, 0.1 us)
Async XLA Ops:
  6.5 24.0 %all-to-all-start = ((bf16[8,128,128]{2,1,0:T(8,128)(2,1)}), bf16[8,128,128]{2,1,0:T(8,128)(2,1)S(1)}, u32[]{:S(2)}, u32[]{:S(2)}) async-start(bf16[8,128,128]{2,1,0:T(8,128)(2,1)} %bitcast.11), calls=%async_computation | async-start | bytes 524288 | tf_op jit(solution)/shard_map/all_to_all | solution.py:112
  24.0 122.6 %all-gather.2.cloned.1.call-start = ((), (), s32[]{:S(2)}) async-start(), calls=%async_computation.2 | async-start | bytes 2359296 | tf_op jit(solution)/shard_map/all_gather | solution.py:114
  24.0 37.7 %collective-permute-start.6 = (bf16[8,128,128]{2,1,0:T(8,128)(2,1)}, bf16[8,128,128]{2,1,0:T(8,128)(2,1)S(1)}, u32[]{:S(2)}, u32[]{:S(2)}) collective-permute-start(bf16[8,128,128]{2,1,0:T(8,128)(2,1)} %bitcast.12), channel_id=1, source_target_pairs={{0,24},{1,9},{8,0},{9,17},{16,8},{17,25},{24,16},{25,1},{2,26},{3,... | collective-permute-start | bytes 786440 | tf_op jit(solution)/shard_map/ppermute | solution.py:108
  30.5 0.7 copy-start.2
  31.2 70.0 %collective-permute-start.8 = (bf16[8,128,128]{2,1,0:T(8,128)(2,1)}, bf16[8,128,128]{2,1,0:T(8,128)(2,1)S(1)}, u32[]{:S(2)}, u32[]{:S(2)}) collective-permute-start(bf16[8,128,128]{2,1,0:T(8,128)(2,1)} %bitcast.13), channel_id=1, source_target_pairs={{0,8},{1,25},{8,16},{9,1},{16,24},{17,9},{24,0},{25,17},{2,10},{3,... | collective-permute-start | bytes 786440 | tf_op jit(solution)/shard_map/ppermute | solution.py:108
  43.5 14.7 %collective-permute-start.2 = (bf16[8,128,128]{2,1,0:T(8,128)(2,1)}, bf16[8,128,128]{2,1,0:T(8,128)(2,1)}, u32[]{:S(2)}, u32[]{:S(2)}) collective-permute-start(bf16[8,128,128]{2,1,0:T(8,128)(2,1)} %param.1), channel_id=1, source_target_pairs={{0,32},{32,64},{64,96},{96,0},{1,33},{33,65},{65,97},{97,1},{2,34}... | collective-permute-start | bytes 786440 | tf_op jit(solution)/shard_map/cond/branch_1_fun/ppermute | solution.py:93
  46.6 11.6 %collective-permute-start.1 = (bf16[8,128,128]{2,1,0:T(8,128)(2,1)}, bf16[8,128,128]{2,1,0:T(8,128)(2,1)}, u32[]{:S(2)}, u32[]{:S(2)}) collective-permute-start(bf16[8,128,128]{2,1,0:T(8,128)(2,1)} %param.1), channel_id=1, source_target_pairs={{0,64},{32,96},{64,0},{96,32},{1,65},{33,97},{65,1},{97,33},{2,66}... | collective-permute-start | bytes 786440 | tf_op jit(solution)/shard_map/cond/branch_1_fun/ppermute | solution.py:93
  51.0 10.1 %collective-permute-start = (bf16[8,128,128]{2,1,0:T(8,128)(2,1)}, bf16[8,128,128]{2,1,0:T(8,128)(2,1)}, u32[]{:S(2)}, u32[]{:S(2)}) collective-permute-start(bf16[8,128,128]{2,1,0:T(8,128)(2,1)} %param.1), channel_id=1, source_target_pairs={{0,96},{32,0},{64,32},{96,64},{1,97},{33,1},{65,33},{97,65},{2,98}... | collective-permute-start | bytes 786440 | tf_op jit(solution)/shard_map/cond/branch_1_fun/ppermute | solution.py:93
  61.7 62.5 %collective-permute-start.7 = (bf16[8,128,128]{2,1,0:T(8,128)(2,1)S(1)}, bf16[8,128,128]{2,1,0:T(8,128)(2,1)S(1)}, u32[]{:S(2)}, u32[]{:S(2)}) collective-permute-start(bf16[8,128,128]{2,1,0:T(8,128)(2,1)S(1)} %collective-permute-done.6), channel_id=1, source_target_pairs={{0,24},{1,9},{8,0},{9,17},{16,8},{17,25},{24,16},{25,1},{2,26},{3,... | collective-permute-start | bytes 786440 | tf_op jit(solution)/shard_map/ppermute | solution.py:108
  101.2 33.6 %copy-start.3 = (s32[1,1,1,16,16,2]{4,5,3,2,1,0:T(2,128)S(1)}, s32[1,1,1,16,16,2]{4,5,3,2,1,0:T(2,128)}, u32[]{:S(2)}) copy-start(s32[1,1,1,16,16,2]{4,5,3,2,1,0:T(2,128)} %param.9) | copy-start | bytes 6148
  101.2 33.9 %copy-start.4 = (s32[4]{0:T(128)S(1)}, s32[4]{0:T(128)}, u32[]{:S(2)}) copy-start(s32[4]{0:T(128)} %shard_map.37) | copy-start | bytes 52
  101.2 45.4 %copy-start.1 = (bf16[1,1,1,8,1,128,128]{6,5,4,3,2,1,0:T(8,128)(2,1)S(1)}, bf16[1,1,1,8,1,128,128]{6,5,4,3,2,1,0:T(8,128)(2,1)}, u32[]{:S(2)}) copy-start(bf16[1,1,1,8,1,128,128]{6,5,4,3,2,1,0:T(8,128)(2,1)} %param.7) | copy-start | bytes 786436
  101.4 15.2 %collective-permute-start.5 = (bf16[16,128,128]{2,1,0:T(8,128)(2,1)S(1)}, bf16[16,128,128]{2,1,0:T(8,128)(2,1)}, u32[]{:S(2)}, u32[]{:S(2)}) collective-permute-start(bf16[16,128,128]{2,1,0:T(8,128)(2,1)S(1)} %param.3), channel_id=1, source_target_pairs={{0,32},{32,64},{64,96},{96,0},{1,33},{33,65},{65,97},{97,1},{2,34}... | collective-permute-start | bytes 1572872 | tf_op jit(solution)/shard_map/cond/branch_1_fun/ppermute | solution.py:93
  104.2 18.0 %collective-permute-start.4 = (bf16[16,128,128]{2,1,0:T(8,128)(2,1)S(1)}, bf16[16,128,128]{2,1,0:T(8,128)(2,1)}, u32[]{:S(2)}, u32[]{:S(2)}) collective-permute-start(bf16[16,128,128]{2,1,0:T(8,128)(2,1)S(1)} %param.3), channel_id=1, source_target_pairs={{0,64},{32,96},{64,0},{96,32},{1,65},{33,97},{65,1},{97,33},{2,66}... | collective-permute-start | bytes 1572872 | tf_op jit(solution)/shard_map/cond/branch_1_fun/ppermute | solution.py:93
  108.4 15.8 %collective-permute-start.3 = (bf16[16,128,128]{2,1,0:T(8,128)(2,1)S(1)}, bf16[16,128,128]{2,1,0:T(8,128)(2,1)}, u32[]{:S(2)}, u32[]{:S(2)}) collective-permute-start(bf16[16,128,128]{2,1,0:T(8,128)(2,1)S(1)} %param.3), channel_id=1, source_target_pairs={{0,96},{32,0},{64,32},{96,64},{1,97},{33,1},{65,33},{97,65},{2,98}... | collective-permute-start | bytes 1572872 | tf_op jit(solution)/shard_map/cond/branch_1_fun/ppermute | solution.py:93
  124.2 10.9 %collective-permute-start.11 = (bf16[8,128,128]{2,1,0:T(8,128)(2,1)S(1)}, bf16[8,128,128]{2,1,0:T(8,128)(2,1)S(1)}, u32[]{:S(2)}, u32[]{:S(2)}) collective-permute-start(bf16[8,128,128]{2,1,0:T(8,128)(2,1)S(1)} %collective-permute-done.7.refs_8_), channel_id=1, source_target_pairs={{0,32},{32,64},{64,96},{96,0},{1,33},{33,65},{65,97},{97,1},{2,34}... | collective-permute-start | bytes 786440 | tf_op jit(solution)/shard_map/ppermute | solution.py:93
  128.2 11.2 %collective-permute-start.10 = (bf16[8,128,128]{2,1,0:T(8,128)(2,1)S(1)}, bf16[8,128,128]{2,1,0:T(8,128)(2,1)S(1)}, u32[]{:S(2)}, u32[]{:S(2)}) collective-permute-start(bf16[8,128,128]{2,1,0:T(8,128)(2,1)S(1)} %collective-permute-done.7.refs_8_), channel_id=1, source_target_pairs={{0,64},{32,96},{64,0},{96,32},{1,65},{33,97},{65,1},{97,33},{2,66}... | collective-permute-start | bytes 786440 | tf_op jit(solution)/shard_map/ppermute | solution.py:93
  131.6 9.5 %collective-permute-start.9 = (bf16[8,128,128]{2,1,0:T(8,128)(2,1)S(1)}, bf16[8,128,128]{2,1,0:T(8,128)(2,1)S(1)}, u32[]{:S(2)}, u32[]{:S(2)}) collective-permute-start(bf16[8,128,128]{2,1,0:T(8,128)(2,1)S(1)} %collective-permute-done.7.refs_8_), channel_id=1, source_target_pairs={{0,96},{32,0},{64,32},{96,64},{1,97},{33,1},{65,33},{97,65},{2,98}... | collective-permute-start | bytes 786440 | tf_op jit(solution)/shard_map/ppermute | solution.py:93
  146.7 1.6 copy-start
  152.4 7.9 %collective-permute-start.12 = (f32[8,128,128]{2,1,0:T(8,128)S(1)}, f32[8,128,128]{2,1,0:T(8,128)S(1)}, u32[]{:S(2)}, u32[]{:S(2)}) collective-permute-start(f32[8,128,128]{2,1,0:T(8,128)S(1)} %shard_map.39), channel_id=1, source_target_pairs={{0,1},{1,0},{2,3},{3,2},{4,5},{5,4},{6,7},{7,6},{8,9},{9,8},{10,11... | collective-permute-start | bytes 1572872 | tf_op jit(solution)/shard_map/ppermute | solution.py:131
Sparse Core Ops, SparseCore 0:
  31.4 115.2 all-gather.1
